TPU v7x, 32 devices: a whole 2x2x4 slice. The times are simulated.
32 devices in a mesh: rep: 4 (over z), shard: 8 (over y, x, core).
Axes of the slice: x: 2, y: 2, z: 4, core: 2. Of those that a mesh axis runs over, the one named last changes fastest.
Arguments:
- tokens: bfloat16 [2, 64, 128, 2048], P(None, ('rep', 'shard')), may hold values from -6 to 6
- cotangent: bfloat16 [2, 64, 128, 2048], P(None, 'rep', None, 'shard'), may hold values from -6 to 6
- seq_blocks: int32 [2, 4, 4], P(None, 'rep'), may hold values from 1 to 8, 16 in all within a row
- seq_pad: int32 [2, 4, 4], P(None, 'rep'), may hold values from 0 to 63
- deal_order: int32 [2, 4, 16], P(None, 'rep'), may hold values from 0 to 15, each once within a row
- ln1_gain: bfloat16 [2048], P('shard'), may hold values from 0.5 to 1.5
- ln1_bias: bfloat16 [2048], P('shard'), may hold values from -1.25 to 1.25
- ln2_gain: bfloat16 [2048], P('shard'), may hold values from 0.5 to 1.5
- ln2_bias: bfloat16 [2048], P('shard'), may hold values from -1.25 to 1.25
- qkv_weight: bfloat16 [2048, 6144], P('shard'), may hold values from -0.125 to 0.125
- qkv_bias: bfloat16 [6144], P('shard'), may hold values from -1.25 to 1.25
- out_weight: bfloat16 [2048, 2048], P('shard'), may hold values from -1 to 1
- out_bias: bfloat16 [2048], P('shard'), may hold values from -1.25 to 1.25
- up_weight: bfloat16 [2048, 8192], P('shard'), may hold values from -0.125 to 0.125
- up_bias: bfloat16 [8192], P('shard'), may hold values from -3 to 3
- down_weight: bfloat16 [8192, 2048], P('shard'), may hold values from -0.0625 to 0.0625
- down_bias: bfloat16 [2048], P('shard'), may hold values from -1.25 to 1.25
Outputs:
- out: bfloat16 [2, 64, 128, 2048], P(None, 'rep', None, 'shard')
- tokens_grad: bfloat16 [2, 64, 128, 2048], P(None, ('rep', 'shard'))
- ln1_gain_grad: float32 [2048], P('shard')
- ln1_bias_grad: float32 [2048], P('shard')
- ln2_gain_grad: float32 [2048], P('shard')
- ln2_bias_grad: float32 [2048], P('shard')
- qkv_weight_grad: float32 [2048, 6144], P('shard')
- qkv_bias_grad: float32 [6144], P('shard')
- out_weight_grad: float32 [2048, 2048], P('shard')
- out_bias_grad: float32 [2048], P('shard')
- up_weight_grad: float32 [2048, 8192], P('shard')
- up_bias_grad: float32 [8192], P('shard')
- down_weight_grad: float32 [8192, 2048], P('shard')
- down_bias_grad: float32 [2048], P('shard')
Inputs may be any that keep to these rules, and one draw needn't show every extreme that they name: `seq_blocks`: each row of 4 counts sums to 16, and its largest count is exactly 8. `deal_order`: each row is a permutation of the 16 block indices of one group.
All inputs are finite; a program needn't handle non-finite values.
Results may differ from a plain program's by a relative error of at most 0.014.
Values may be sent and summed in bfloat16 or wider, within the bound.
No kernel may reach another device: no remote copies, remote signals or barrier semaphores. Data moves between devices by JAX's collectives and lax.ppermute only.
A program may use at most 640 MiB of HBM per device.

v0:
```python
import jax
import jax.numpy as jnp
from jax import lax
from jax.sharding import PartitionSpec as P

D = 2048
HEADS = 8
HD = 256
ROT = 64
FF = 8192
BLK = 128
SEQ_MOST = 8
MB = 2


EPS = 1e-05


def rotary_tables(positions):
    half = ROT // 2
    freqs = 10000.0 ** (-2.0 * jnp.arange(half, dtype=jnp.float32) / ROT)
    angles = positions.astype(jnp.float32)[:, None] * freqs[None, :]
    cosine = jnp.concatenate([jnp.cos(angles), jnp.cos(angles)], axis=-1)
    sine = jnp.concatenate([jnp.sin(angles), jnp.sin(angles)], axis=-1)
    return (cosine, sine)


def rotate(values, cosine, sine):
    half = ROT // 2
    front = values[..., :ROT]
    turned = jnp.concatenate([-front[..., half:], front[..., :half]], axis=-1)
    moved = front * cosine[:, None, :] + turned * sine[:, None, :]
    return jnp.concatenate([moved, values[..., ROT:]], axis=-1)


def times_transposed(left_mat, right_mat):
    return lax.dot_general(
        left_mat, right_mat, (((1,), (1,)), ((), ())), preferred_element_type=jnp.float32
    )


def transposed_times(left_mat, right_mat):
    return lax.dot_general(
        left_mat, right_mat, (((0,), (0,)), ((), ())), preferred_element_type=jnp.float32
    )


def pick_rows(table, chosen):
    return table[chosen]


def block_spans(blocks, pad_counts, given):
    ends = jnp.cumsum(blocks)
    starts = ends - blocks
    inside = (given[..., None] >= starts) & (given[..., None] < ends)
    seq_first = jnp.sum(jnp.where(inside, starts, 0), axis=-1)
    seq_valid = jnp.sum(jnp.where(inside, blocks * BLK - pad_counts, 0), axis=-1)
    return (seq_first, seq_valid)


def attention_scores(queries, keys_window, allowed, score_scale):
    scores = (
        jnp.einsum("bqhd,bkhd->bhqk", queries, keys_window, preferred_element_type=jnp.float32)
        * score_scale
    )
    return jnp.where(allowed[:, None], scores, -jnp.inf)


def local(
    tokens,
    cotangent,
    seq_blocks,
    seq_pad,
    deal_order,
    ln1_gain,
    ln1_bias,
    ln2_gain,
    ln2_bias,
    qkv_weight,
    qkv_bias,
    out_weight,
    out_bias,
    up_weight,
    up_bias,
    down_weight,
    down_bias,
):
    shards = lax.axis_size("shard")
    shard_place = lax.axis_index("shard")
    own_blocks = tokens.shape[1]
    group_blocks = deal_order.shape[2]
    query_blocks = MB * own_blocks
    row_count = query_blocks * BLK
    key_span = SEQ_MOST * BLK
    up_ratio = FF // D
    score_scale = HD ** (-0.5)
    deal_slots = deal_order[:, 0, :]
    block_counts = seq_blocks[:, 0, :]
    pad_counts = seq_pad[:, 0, :]
    slot_ids = jnp.arange(group_blocks, dtype=jnp.int32)
    inverse = jnp.sum(
        jnp.where(deal_slots[:, None, :] == slot_ids[None, :, None], slot_ids[None, None, :], 0),
        axis=-1,
    )
    own_given = lax.dynamic_slice_in_dim(deal_slots, shard_place * own_blocks, own_blocks, 1)
    seq_first, seq_valid = jax.vmap(block_spans)(block_counts, pad_counts, own_given)
    inner_pos = jnp.arange(BLK, dtype=jnp.int32)
    query_tok = own_given[:, :, None] * BLK + inner_pos
    positions = query_tok - seq_first[:, :, None] * BLK
    window = jnp.minimum(seq_first, group_blocks - SEQ_MOST)[:, :, None] + jnp.arange(
        SEQ_MOST, dtype=jnp.int32
    )
    window_slots = jax.vmap(pick_rows)(inverse, window)
    key_tok = (window[:, :, :, None] * BLK + inner_pos).reshape(MB, own_blocks, 1, key_span)
    lower = (seq_first * BLK)[:, :, None, None]
    upper = lower + seq_valid[:, :, None, None]
    allowed = (key_tok >= lower) & (key_tok <= query_tok[:, :, :, None]) & (key_tok < upper)
    allowed = allowed.reshape(query_blocks, BLK, key_span)
    small_params = (
        lax.all_gather(ln1_gain, "shard", axis=0, tiled=True),
        lax.all_gather(ln1_bias, "shard", axis=0, tiled=True),
        lax.all_gather(ln2_gain, "shard", axis=0, tiled=True),
        lax.all_gather(ln2_bias, "shard", axis=0, tiled=True),
        lax.all_gather(qkv_bias, "shard", axis=0, tiled=True),
        lax.all_gather(out_bias, "shard", axis=0, tiled=True),
        lax.all_gather(up_bias, "shard", axis=0, tiled=True),
        lax.all_gather(down_bias, "shard", axis=0, tiled=True),
    )
    (
        gain_first,
        offset_first,
        gain_second,
        offset_second,
        bias_mixed,
        bias_attend,
        bias_upward,
        bias_downward,
    ) = [item.astype(jnp.float32) for item in small_params]
    flat_tokens = tokens.reshape(row_count, D).astype(jnp.float32)
    center = flat_tokens - jnp.mean(flat_tokens, axis=-1, keepdims=True)
    inv_std = lax.rsqrt(jnp.mean(center * center, axis=-1, keepdims=True) + EPS)
    normed = center * inv_std
    in_one = (normed * gain_first + offset_first).astype(jnp.bfloat16)
    in_two = (normed * gain_second + offset_second).astype(jnp.bfloat16)
    pieces = (
        lax.all_gather(qkv_weight, "shard", axis=0, tiled=True),
        lax.all_gather(up_weight, "shard", axis=0, tiled=True),
    )
    one_part = in_one
    two_part = in_two
    mixed_sum = jnp.dot(one_part, pieces[0], preferred_element_type=jnp.float32)
    up_sum = jnp.dot(two_part, pieces[1], preferred_element_type=jnp.float32)
    mixed = mixed_sum + bias_mixed
    hidden = up_sum + bias_upward
    active_low = jax.nn.gelu(hidden, approximate=False).astype(jnp.bfloat16)
    cosine, sine = rotary_tables(positions.reshape(row_count))
    query_low = rotate(mixed[:, :D].reshape(row_count, HEADS, HD), cosine, sine).astype(
        jnp.bfloat16
    )
    key_low = rotate(mixed[:, D : 2 * D].reshape(row_count, HEADS, HD), cosine, sine).astype(
        jnp.bfloat16
    )
    value_low = mixed[:, 2 * D :].astype(jnp.bfloat16)
    key_all, value_all = (
        lax.all_gather(key_low.reshape(MB, own_blocks, BLK, D), "shard", axis=1, tiled=True),
        lax.all_gather(value_low.reshape(MB, own_blocks, BLK, D), "shard", axis=1, tiled=True),
    )
    keys_window = jax.vmap(pick_rows)(key_all, window_slots).reshape(
        query_blocks, key_span, HEADS, HD
    )
    values_window = jax.vmap(pick_rows)(value_all, window_slots).reshape(
        query_blocks, key_span, HEADS, HD
    )
    queries = query_low.reshape(query_blocks, BLK, HEADS, HD)
    scores = attention_scores(queries, keys_window, allowed, score_scale)
    row_top = jnp.max(scores, axis=-1, keepdims=True)
    exponent = jnp.exp(scores - row_top)
    denominator = jnp.sum(exponent, axis=-1, keepdims=True)
    log_total = row_top + jnp.log(denominator)
    prob_low = (exponent / denominator).astype(jnp.bfloat16)
    context = jnp.einsum(
        "bhqk,bkhd->bqhd", prob_low, values_window, preferred_element_type=jnp.float32
    )
    context_low = context.reshape(row_count, D).astype(jnp.bfloat16)
    down_rows = down_weight.reshape(D // shards, up_ratio * D)
    pieces = (
        lax.all_gather(out_weight, "shard", axis=0, tiled=True),
        lax.all_gather(down_rows, "shard", axis=0, tiled=True),
    )
    piece_rows = pieces[0].shape[0]
    ctx_part = context_low
    act_part = active_low
    attended = jnp.dot(ctx_part, pieces[0], preferred_element_type=jnp.float32)
    fed = jnp.dot(
        act_part, pieces[1].reshape(up_ratio * piece_rows, D), preferred_element_type=jnp.float32
    )
    branch_sum = attended + fed
    result = flat_tokens + branch_sum + bias_attend + bias_downward
    result_low = result.astype(jnp.bfloat16).reshape(MB, own_blocks, BLK, D)
    returned = lax.all_to_all(result_low, "shard", split_axis=3, concat_axis=1, tiled=True)
    out_given = jax.vmap(pick_rows)(returned, inverse)
    dealt_cot = jax.vmap(pick_rows)(cotangent, deal_slots)
    grad_blocks = lax.all_to_all(dealt_cot, "shard", split_axis=1, concat_axis=3, tiled=True)
    grad_out = grad_blocks.reshape(row_count, D)
    pieces = (
        lax.all_gather(out_weight, "shard", axis=0, tiled=True),
        lax.all_gather(down_rows, "shard", axis=0, tiled=True),
    )
    piece_rows = pieces[0].shape[0]
    ctx_part = times_transposed(grad_out, pieces[0])
    act_part = times_transposed(grad_out, pieces[1].reshape(up_ratio * piece_rows, D))
    context_grad = ctx_part
    active_grad = act_part
    context_grad_low = context_grad.astype(jnp.bfloat16)
    active_grad_low = active_grad.astype(jnp.bfloat16)
    _, gelu_back = jax.vjp(lambda inside_vals: jax.nn.gelu(inside_vals, approximate=False), hidden)
    hidden_grad_low = gelu_back(active_grad_low.astype(jnp.float32))[0].astype(jnp.bfloat16)
    scores = attention_scores(queries, keys_window, allowed, score_scale)
    attention = jnp.exp(scores - log_total)
    attention_low = attention.astype(jnp.bfloat16)
    grad_heads = context_grad_low.reshape(query_blocks, BLK, HEADS, HD)
    prob_grad = jnp.einsum(
        "bqhd,bkhd->bhqk", grad_heads, values_window, preferred_element_type=jnp.float32
    )
    row_delta = jnp.sum(attention * prob_grad, axis=-1, keepdims=True)
    score_grad = (attention * (prob_grad - row_delta)).astype(jnp.bfloat16)
    query_grad = (
        jnp.einsum("bhqk,bkhd->bqhd", score_grad, keys_window, preferred_element_type=jnp.float32)
        * score_scale
    )
    key_window_grad = (
        jnp.einsum("bhqk,bqhd->bkhd", score_grad, queries, preferred_element_type=jnp.float32)
        * score_scale
    ).reshape(MB, own_blocks * SEQ_MOST, BLK, D)
    value_window_grad = jnp.einsum(
        "bhqk,bqhd->bkhd", attention_low, grad_heads, preferred_element_type=jnp.float32
    ).reshape(MB, own_blocks * SEQ_MOST, BLK, D)
    key_parts = []
    value_parts = []
    for micro_index in range(MB):
        term_slots = window_slots[micro_index].reshape(own_blocks * SEQ_MOST)
        key_term = (
            jnp.zeros((group_blocks, BLK, D), jnp.float32)
            .at[term_slots]
            .add(key_window_grad[micro_index])
        )
        value_term = (
            jnp.zeros((group_blocks, BLK, D), jnp.float32)
            .at[term_slots]
            .add(value_window_grad[micro_index])
        )
        key_summed, value_summed = (
            lax.psum_scatter(
                key_term.astype(jnp.bfloat16), "shard", scatter_dimension=0, tiled=True
            ).astype(jnp.float32),
            lax.psum_scatter(
                value_term.astype(jnp.bfloat16), "shard", scatter_dimension=0, tiled=True
            ).astype(jnp.float32),
        )
        key_parts.append(key_summed)
        value_parts.append(value_summed)
    key_grad = jnp.stack(key_parts).reshape(row_count, HEADS, HD)
    value_grad = jnp.stack(value_parts).reshape(row_count, D)
    _, unrotate = jax.vjp(
        lambda turned_vals: rotate(turned_vals, cosine, sine),
        jnp.zeros((row_count, HEADS, HD), jnp.float32),
    )
    query_pre = unrotate(query_grad.reshape(row_count, HEADS, HD))[0].reshape(row_count, D)
    key_pre = unrotate(key_grad)[0].reshape(row_count, D)
    mixed_grad = jnp.concatenate([query_pre, key_pre, value_grad], axis=1).astype(jnp.bfloat16)
    pieces = (
        lax.all_gather(qkv_weight, "shard", axis=0, tiled=True),
        lax.all_gather(up_weight, "shard", axis=0, tiled=True),
    )
    one_part = times_transposed(mixed_grad, pieces[0])
    two_part = times_transposed(hidden_grad_low, pieces[1])
    in_one_grad = one_part
    in_two_grad = two_part
    grad_out_f = grad_out.astype(jnp.float32)
    normed_grad = in_one_grad * gain_first + in_two_grad * gain_second
    mean_grad = jnp.mean(normed_grad, axis=-1, keepdims=True)
    mean_proj = jnp.mean(normed_grad * normed, axis=-1, keepdims=True)
    tokens_grad = (
        (grad_out_f + inv_std * (normed_grad - mean_grad - normed * mean_proj))
        .astype(jnp.bfloat16)
        .reshape(MB, own_blocks, BLK, D)
    )
    bias_out_grad = jnp.sum(grad_out, axis=0, dtype=jnp.float32)
    small_grads = lax.psum(
        (
            jnp.sum(in_one_grad * normed, axis=0),
            jnp.sum(in_one_grad, axis=0),
            jnp.sum(in_two_grad * normed, axis=0),
            jnp.sum(in_two_grad, axis=0),
            jnp.sum(mixed_grad, axis=0, dtype=jnp.float32),
            bias_out_grad,
            jnp.sum(hidden_grad_low, axis=0, dtype=jnp.float32),
        ),
        ("rep", "shard"),
    )

    def own_share(vector):
        share_len = vector.shape[0] // shards
        return lax.dynamic_slice_in_dim(vector, shard_place * share_len, share_len, 0)

    (
        gain_one_grad,
        shift_one_grad,
        gain_two_grad,
        shift_two_grad,
        mixed_bias_grad,
        attend_bias_grad,
        upward_bias_grad,
    ) = [own_share(item) for item in small_grads]
    one_cols, two_cols, ctx_cols, act_cols = (
        lax.all_to_all(in_one, "shard", split_axis=1, concat_axis=0, tiled=True),
        lax.all_to_all(in_two, "shard", split_axis=1, concat_axis=0, tiled=True),
        lax.all_to_all(context_low, "shard", split_axis=1, concat_axis=0, tiled=True),
        lax.all_to_all(active_low, "shard", split_axis=1, concat_axis=0, tiled=True),
    )
    own_rows = D // shards
    pieces = (
        lax.all_gather(mixed_grad, "shard", axis=0, tiled=True),
        lax.all_gather(hidden_grad_low, "shard", axis=0, tiled=True),
        lax.all_gather(grad_out, "shard", axis=0, tiled=True),
    )
    one_part = one_cols
    two_part = two_cols
    ctx_part = ctx_cols
    act_part = act_cols
    terms = [
        transposed_times(one_part, pieces[0]),
        transposed_times(two_part, pieces[1]),
        transposed_times(ctx_part, pieces[2]),
        transposed_times(act_part, pieces[2]).reshape(own_rows, up_ratio * D),
    ]
    local_rows = jnp.concatenate(terms, axis=1)
    summed_rows = lax.psum(local_rows.astype(jnp.bfloat16), "rep").astype(jnp.float32)
    qkv_weight_grad = summed_rows[:, : 3 * D]
    up_weight_grad = summed_rows[:, 3 * D : 3 * D + FF]
    out_weight_grad = summed_rows[:, 3 * D + FF : 4 * D + FF]
    down_weight_grad = summed_rows[:, 4 * D + FF :].reshape(FF // shards, D)
    return (
        out_given,
        tokens_grad,
        gain_one_grad,
        shift_one_grad,
        gain_two_grad,
        shift_two_grad,
        qkv_weight_grad,
        mixed_bias_grad,
        out_weight_grad,
        attend_bias_grad,
        up_weight_grad,
        upward_bias_grad,
        down_weight_grad,
        attend_bias_grad,
    )


def solution(mesh):
    in_specs = (
        P(None, ("rep", "shard"), None, None),
        P(None, "rep", None, "shard"),
        P(None, "rep", None),
        P(None, "rep", None),
        P(None, "rep", None),
        P("shard"),
        P("shard"),
        P("shard"),
        P("shard"),
        P("shard", None),
        P("shard"),
        P("shard", None),
        P("shard"),
        P("shard", None),
        P("shard"),
        P("shard", None),
        P("shard"),
    )
    out_specs = (
        P(None, "rep", None, "shard"),
        P(None, ("rep", "shard"), None, None),
        P("shard"),
        P("shard"),
        P("shard"),
        P("shard"),
        P("shard", None),
        P("shard"),
        P("shard", None),
        P("shard"),
        P("shard", None),
        P("shard"),
        P("shard", None),
        P("shard"),
    )
    return jax.shard_map(local, mesh=mesh, in_specs=in_specs, out_specs=out_specs, check_vma=False)
```

profile of v0, /device:TPU:0, one launch (start us, length us, event | category | flops | bytes accessed | tf_op | source)
XLA Modules:
  0.0 2670.1 jit_solution(9088882856725699455)
XLA Ops:
  71.5 66.6 %all-gather.17.cloned.1.call-done = bf16[2048,6144]{1,0:T(8,128)(2,1)} async-done(((bf16[256,6144]{1,0:T(8,128)(2,1)}), bf16[2048,6144]{1,0:T(8,128)(2,1)}) %all-gather.17.cloned.1.call-update) | async-done | bytes 25165840 | tf_op jit(solution)/shard_map/all_gather | solution.py:146
  138.1 21.3 convolution_add_fusion
  196.0 32.2 %all-to-all-done.1 = bf16[2,16,128,256]{3,2,0,1:T(8,128)(2,1)} async-done(((bf16[2,16,128,256]{3,2,0,1:T(8,128)(2,1)}), bf16[2,16,128,256]{3,2,0,1:T(8,128)(2,1)}, u32[]{:S(2)}, u32[]{:S(2)}) %all-to-all-start.1) | async-done | bytes 2097184 | tf_op jit(solution)/shard_map/all_to_all | solution.py:203
  254.4 41.1 %all-gather.21.cloned.1.call-done = bf16[2,16,128,2048]{3,2,1,0:T(8,128)(2,1)} async-done(((bf16[2,2,128,2048]{3,2,1,0:T(8,128)(2,1)}), bf16[2,16,128,2048]{3,2,1,0:T(8,128)(2,1)}) %all-gather.21.cloned.1.call-update) | async-done | bytes 16777232 | tf_op jit(solution)/shard_map/all_gather | solution.py:165
  295.5 14.7 gather_fusion.2
  310.2 16.3 copy.183
  326.5 20.0 fusion.88
  354.9 32.8 %all-gather.19.cloned.1.call-done = bf16[2,16,128,2048]{3,2,1,0:T(8,128)(2,1)} async-done(((bf16[2,2,128,2048]{3,2,1,0:T(8,128)(2,1)}), bf16[2,16,128,2048]{3,2,1,0:T(8,128)(2,1)}) %all-gather.19.cloned.1.call-update) | async-done | bytes 16777232 | tf_op jit(solution)/shard_map/all_gather | solution.py:166
  387.7 13.2 gather_fusion.1
  400.9 16.4 copy.184
  417.4 21.6 multiply_reduce_fusion
  439.0 15.2 multiply_convert_fusion
  454.1 19.7 multiply_bitcast_fusion
  473.8 21.9 fusion.81
  495.7 17.6 copy.159
  513.4 18.3 reshape.524
  539.6 34.4 %scatter_fusion = f32[16,128,2048]{2,1,0:T(8,128)} fusion(f32[16,128,2048]{2,1,0:T(8,128)} %broadcast.460.clone.3, s32[16]{0:T(128)S(1)} %copy-done.37, f32[16,128,2048]{2,1,0:T(8,128)} %reshape.524), kind=kCustom, calls=%fused_computation.5 | custom fusion | flops 4194304 | bytes 50331712 | tf_op jit(solution)/shard_map/scatter-add | solution.py:245
  583.1 18.4 copy.160
  601.5 18.3 reshape.532
  627.8 34.6 %scatter_fusion.1 = f32[16,128,2048]{2,1,0:T(8,128)} fusion(f32[16,128,2048]{2,1,0:T(8,128)} %broadcast.460.clone.2, s32[16]{0:T(128)S(1)} %copy-done.36, f32[16,128,2048]{2,1,0:T(8,128)} %reshape.532), kind=kCustom, calls=%fused_computation.6 | custom fusion | flops 4194304 | bytes 50331712 | tf_op jit(solution)/shard_map/scatter-add | solution.py:245
  671.6 20.0 convolution_bitcast_fusion
  691.6 22.5 fusion.82
  714.1 17.8 copy.162
  731.8 18.0 reshape.540
  757.7 34.4 %scatter_fusion.2 = f32[16,128,2048]{2,1,0:T(8,128)} fusion(f32[16,128,2048]{2,1,0:T(8,128)} %broadcast.460.clone.1, s32[16]{0:T(128)S(1)} %copy-done.37, f32[16,128,2048]{2,1,0:T(8,128)} %reshape.540), kind=kCustom, calls=%fused_computation.7 | custom fusion | flops 4194304 | bytes 50331712 | tf_op jit(solution)/shard_map/scatter-add | solution.py:250
  801.2 18.5 copy.163
  819.7 17.8 reshape.548
  845.6 34.6 %scatter_fusion.3 = f32[16,128,2048]{2,1,0:T(8,128)} fusion(f32[16,128,2048]{2,1,0:T(8,128)} %broadcast.460.clone, s32[16]{0:T(128)S(1)} %copy-done.36, f32[16,128,2048]{2,1,0:T(8,128)} %reshape.548), kind=kCustom, calls=%fused_computation.8 | custom fusion | flops 4194304 | bytes 50331712 | tf_op jit(solution)/shard_map/scatter-add | solution.py:250
  899.1 16.3 multiply_bitcast_fusion.1
  946.1 15.4 reduce-scatter.11.cloned.1.call-done
  977.7 146.4 %all-gather.27.cloned.1.call-done = bf16[2048,8192]{1,0:T(8,128)(2,1)} async-done(((bf16[256,8192]{1,0:T(8,128)(2,1)}), bf16[2048,8192]{1,0:T(8,128)(2,1)}) %all-gather.27.cloned.1.call-update) | async-done | bytes 33554448 | tf_op jit(solution)/shard_map/all_gather | solution.py:188
  1124.2 55.7 %reshape.473 = bf16[8192,2048]{1,0:T(8,128)(2,1)} reshape(bf16[2048,8192]{1,0:T(8,128)(2,1)} %all-gather.27.cloned.1.call-done) | data formatting | bytes 67108864 | tf_op jit(solution)/shard_map/reshape | solution.py:195
  1179.8 106.9 %all-gather.25.cloned.1.call-done = bf16[2048,8192]{1,0:T(8,128)(2,1)} async-done(((bf16[256,8192]{1,0:T(8,128)(2,1)}), bf16[2048,8192]{1,0:T(8,128)(2,1)}) %all-gather.25.cloned.1.call-update) | async-done | bytes 33554448 | tf_op jit(solution)/shard_map/all_gather | solution.py:147
  1286.7 58.2 %multiply_convert_fusion.1 = (bf16[512,8192]{1,0:T(8,128)(2,1)}, f32[512,8192]{1,0:T(8,128)}, f32[512,8192]{1,0:T(8,128)}) fusion(f32[8192]{0:T(1024)S(1)} %convert_element_type.166, bf16[512,2048]{1,0:T(8,128)(2,1)} %get-tuple-element.57, bf16[2048,8192]{1,0:T(8,128)(2,1)} %all-gather.25.cloned.1.call-done), kind=kOutput, calls=%fused_computation.25 | convolution fusion | flops 17456693248 | bytes 77627392 | tf_op jit(solution)/shard_map/dot_general | solution.py:152
  1344.9 32.6 %convert_reduce_fusion = (f32[8192]{0:T(1024)}, bf16[512,8192]{1,0:T(8,128)(2,1)}) fusion(f32[512,8192]{1,0:T(8,128)} %get-tuple-element.33, bf16[512,2048]{1,0:T(8,128)(2,1)S(1)} %bitcast.252, bf16[8192,2048]{1,0:T(8,128)(2,1)} %reshape.473, f32[512,8192]{1,0:T(8,128)} %get-tuple-element.79, f32[8192]{0:T(1024)S(1)} %convert_element_type.166), kind=kOutput, calls=%fused_computation.21 | convolution fusion | flops 17259552768 | bytes 77660160 | tf_op jit(solution)/shard_map/dot_general | solution.py:37
  1400.5 15.6 convert_bitcast_fusion
  1421.9 130.5 %all-to-all-done.5 = bf16[512,8,1024]{2,0,1:T(8,128)(2,1)} async-done(((bf16[512,8,1024]{2,0,1:T(8,128)(2,1)}), bf16[512,8,1024]{2,0,1:T(8,128)(2,1)}, u32[]{:S(2)}, u32[]{:S(2)}) %all-to-all-start.5) | async-done | bytes 8388640 | tf_op jit(solution)/shard_map/all_to_all | solution.py:319
  1557.0 27.5 %convolution_convert_fusion.3 = bf16[1024,2048]{1,0:T(8,128)(2,1)} fusion(bf16[4096,1024]{1,0:T(8,128)(2,1)} %bitcast.56, bf16[4096,2048]{1,0:T(8,128)(2,1)} %all-gather.33.cloned.1.call-done), kind=kOutput, calls=%fused_computation.102 | convolution fusion | flops 17181966336 | bytes 29360128 | tf_op jit(solution)/shard_map/dot_general | solution.py:43
  1592.5 13.7 all-to-all-done.4
  1621.5 21.5 fusion.90
  1643.0 27.3 %fusion.77 = (f32[2048]{0:T(1024)}, f32[2048]{0:T(1024)}, f32[512]{0:T(512)S(1)}, f32[512]{0:T(512)S(1)}, f32[512,2048]{1,0:T(8,128)}, /*index=5*/f32[2048]{0:T(1024)}, f32[2048]{0:T(1024)}) fusion(f32[512]{0:T(512)S(1)} %bitcast.301, f32[512]{0:T(512)S(1)} %bitcast.285, bf16[2,2,128,2048]{3,2,1,0:T(8,128)(2,1)S(1)} %copy-done.4, f32[2048]{0:T(1024)S(1)} %bitcast.288, ...), kind=kOutput, calls=%fused_computation.185 | convolution fusion | flops 17195589632 | bytes 52486144 | tf_op jit(solution)/shard_map/dot_general | solution.py:37
  1674.9 91.2 %all-gather.29.cloned.1.call-done = bf16[4096,6144]{1,0:T(8,128)(2,1)} async-done(((bf16[512,6144]{1,0:T(8,128)(2,1)}), bf16[4096,6144]{1,0:T(8,128)(2,1)}) %all-gather.29.cloned.1.call-update) | async-done | bytes 50331664 | tf_op jit(solution)/shard_map/all_gather | solution.py:323
  1766.1 28.7 %convolution_convert_fusion.2 = bf16[256,6144]{1,0:T(8,128)(2,1)} fusion(bf16[4096,256]{1,0:T(8,128)(2,1)} %bitcast.49, bf16[4096,6144]{1,0:T(8,128)(2,1)} %all-gather.29.cloned.1.call-done), kind=kOutput, calls=%fused_computation.61 | convolution fusion | flops 12886474752 | bytes 55574528 | tf_op jit(solution)/shard_map/dot_general | solution.py:43
  1794.8 276.6 %all-gather.31.cloned.1.call-done = bf16[4096,8192]{1,0:T(8,128)(2,1)} async-done(((bf16[512,8192]{1,0:T(8,128)(2,1)}), bf16[4096,8192]{1,0:T(8,128)(2,1)}) %all-gather.31.cloned.1.call-update) | async-done | bytes 67108880 | tf_op jit(solution)/shard_map/all_gather | solution.py:324
  2071.4 29.4 %convolution_convert_fusion.1 = bf16[256,8192]{1,0:T(8,128)(2,1)} fusion(bf16[4096,256]{1,0:T(8,128)(2,1)} %bitcast.51, bf16[4096,8192]{1,0:T(8,128)(2,1)} %all-gather.31.cloned.1.call-done), kind=kOutput, calls=%fused_computation.56 | convolution fusion | flops 17181966336 | bytes 73400320 | tf_op jit(solution)/shard_map/dot_general | solution.py:43
  2138.6 24.9 fusion.32
  2174.2 27.5 %all-to-all-done = bf16[2,2,128,2048]{2,1,0,3:T(2,128)(2,1)} async-done(((bf16[2,2,128,2048]{2,1,0,3:T(2,128)(2,1)}), bf16[2,2,128,2048]{2,1,0,3:T(2,128)(2,1)}, u32[]{:S(2)}, u32[]{:S(2)}) %all-to-all-start) | async-done | bytes 2097184 | tf_op jit(solution)/shard_map/all_to_all | solution.py:200
  2224.8 408.1 %all-reduce.12.cloned.1.call-done = bf16[256,24576]{1,0:T(8,128)(2,1)} async-done(((bf16[256,24576]{1,0:T(8,128)(2,1)}), bf16[256,24576]{1,0:T(8,128)(2,1)}) %all-reduce.12.cloned.1.call-update) | async-done | bytes 12582928 | tf_op jit(solution)/shard_map/psum | solution.py:338
  (273 shorter events, 423.0 us)
Async XLA Ops:
  7.2 175.4 %copy-start = (bf16[2,16,128,256]{3,2,1,0:T(8,128)(2,1)S(1)}, bf16[2,16,128,256]{3,2,1,0:T(8,128)(2,1)}, u32[]{:S(2)}) copy-start(bf16[2,16,128,256]{3,2,1,0:T(8,128)(2,1)} %param.18) | copy-start | bytes 6291460
  7.2 130.9 %all-gather.17.cloned.1.call-start = ((), (), s32[]{:S(2)}) async-start(), calls=%async_computation.10 | async-start | bytes 28311552 | tf_op jit(solution)/shard_map/all_gather | solution.py:146
  7.9 225.0 %all-gather.23.cloned.1.call-start = ((), (), s32[]{:S(2)}) async-start(), calls=%async_computation.13 | async-start | bytes 9437184 | tf_op jit(solution)/shard_map/all_gather | solution.py:187
  8.7 286.8 %all-gather.21.cloned.1.call-start = ((), (), s32[]{:S(2)}) async-start(), calls=%async_computation.12 | async-start | bytes 18874368 | tf_op jit(solution)/shard_map/all_gather | solution.py:165
  20.6 27.7 %copy-start.15 = (bf16[8,1,256]{2,1,0:T(2,128)(2,1)}, bf16[8,1,256]{2,1,0:T(2,128)(2,1)S(1)}, u32[]{:S(2)}) copy-start(bf16[8,1,256]{2,1,0:T(2,128)(2,1)S(1)} %all-gather.3) | copy-start | bytes 12292
  20.6 138.8 %copy-start.29 = (f32[8,1,256]{2,1,0:T(1,128)}, f32[8,1,256]{2,1,0:T(1,128)S(1)}, u32[]{:S(2)}) copy-start(f32[8,1,256]{2,1,0:T(1,128)S(1)} %convert_element_type.197) | copy-start | bytes 24580
  30.1 18.2 copy-start.17
  30.2 129.2 %copy-start.31 = (f32[8,1,256]{2,1,0:T(1,128)}, f32[8,1,256]{2,1,0:T(1,128)S(1)}, u32[]{:S(2)}) copy-start(f32[8,1,256]{2,1,0:T(1,128)S(1)} %convert_element_type.194) | copy-start | bytes 24580
  38.7 9.6 copy-start.19
  60.8 108.8 %copy-start.12 = (f32[512,64]{1,0:T(8,128)}, f32[512,64]{1,0:T(8,128)S(1)}, u32[]{:S(2)}) copy-start(f32[512,64]{1,0:T(8,128)S(1)} %pad_maximum_fusion.7) | copy-start | bytes 393220
  60.9 108.7 %copy-start.13 = (f32[512,64]{1,0:T(8,128)}, f32[512,64]{1,0:T(8,128)S(1)}, u32[]{:S(2)}) copy-start(f32[512,64]{1,0:T(8,128)S(1)} %pad_maximum_fusion.8) | copy-start | bytes 393220
  172.0 10.5 copy-start.35
  178.5 209.2 %all-gather.19.cloned.1.call-start = ((), (), s32[]{:S(2)}) async-start(), calls=%async_computation.11 | async-start | bytes 18874368 | tf_op jit(solution)/shard_map/all_gather | solution.py:166
  187.8 40.4 %all-to-all-start.1 = ((bf16[2,16,128,256]{3,2,0,1:T(8,128)(2,1)}), bf16[2,16,128,256]{3,2,0,1:T(8,128)(2,1)}, u32[]{:S(2)}, u32[]{:S(2)}) async-start(bf16[2,16,128,256]{3,2,0,1:T(8,128)(2,1)} %copy.151), calls=%async_computation.1 | async-start | bytes 4194304 | tf_op jit(solution)/shard_map/all_to_all | solution.py:203
  192.1 733.2 %reduce-scatter.5.cloned.1.call-start = ((), (), s32[]{:S(2)}) async-start(), calls=%async_computation.16 | async-start | bytes 9437184 | tf_op jit(solution)/shard_map/reduce_scatter | solution.py:253
  192.5 49.0 %copy-start.2 = (s32[2,16]{1,0:T(2,128)}, s32[2,16]{1,0:T(2,128)S(1)}, u32[]{:S(2)}) copy-start(s32[2,16]{1,0:T(2,128)S(1)} %select_reduce_fusion) | copy-start | bytes 388
  346.5 7.8 copy-start.23
  531.7 7.9 copy-start.37
  583.1 342.3 %reduce-scatter.7.cloned.1.call-start = ((), (), s32[]{:S(2)}) async-start(), calls=%async_computation.17 | async-start | bytes 9437184 | tf_op jit(solution)/shard_map/reduce_scatter | solution.py:253
  619.8 8.0 copy-start.36
  671.6 274.5 %reduce-scatter.9.cloned.1.call-start = ((), (), s32[]{:S(2)}) async-start(), calls=%async_computation.18 | async-start | bytes 9437184 | tf_op jit(solution)/shard_map/reduce_scatter | solution.py:256
  801.2 160.3 %reduce-scatter.11.cloned.1.call-start = ((), (), s32[]{:S(2)}) async-start(), calls=%async_computation.19 | async-start | bytes 9437184 | tf_op jit(solution)/shard_map/reduce_scatter | solution.py:256
  889.4 234.8 %all-gather.27.cloned.1.call-start = ((), (), s32[]{:S(2)}) async-start(), calls=%async_computation.15 | async-start | bytes 37748736 | tf_op jit(solution)/shard_map/all_gather | solution.py:188
  897.5 389.2 %all-gather.25.cloned.1.call-start = ((), (), s32[]{:S(2)}) async-start(), calls=%async_computation.14 | async-start | bytes 37748736 | tf_op jit(solution)/shard_map/all_gather | solution.py:147
  898.1 658.9 %all-gather.33.cloned.1.call-start = ((), (), s32[]{:S(2)}) async-start(), calls=%async_computation.22 | async-start | bytes 18874368 | tf_op jit(solution)/shard_map/all_gather | solution.py:325
  898.9 867.2 %all-gather.29.cloned.1.call-start = ((), (), s32[]{:S(2)}) async-start(), calls=%async_computation.20 | async-start | bytes 56623104 | tf_op jit(solution)/shard_map/all_gather | solution.py:323
  935.8 5.7 copy-start.10
  963.2 5.8 copy-start.39
  968.9 1102.5 %all-gather.31.cloned.1.call-start = ((), (), s32[]{:S(2)}) async-start(), calls=%async_computation.21 | async-start | bytes 75497472 | tf_op jit(solution)/shard_map/all_gather | solution.py:324
  1286.7 58.2 %copy-start.9 = (bf16[64,8,8,256]{3,1,2,0:T(8,128)(2,1)S(1)}, bf16[64,8,8,256]{3,1,2,0:T(8,128)(2,1)}, u32[]{:S(2)}) copy-start(bf16[64,8,8,256]{3,1,2,0:T(8,128)(2,1)} %copy.186) | copy-start | bytes 6291460
  1385.5 5.5 copy-start.4
  1385.6 6.0 copy-start.28
  1385.6 6.0 copy-start.34
  1385.6 166.8 %all-to-all-start.5 = ((bf16[512,8,1024]{2,0,1:T(8,128)(2,1)}), bf16[512,8,1024]{2,0,1:T(8,128)(2,1)}, u32[]{:S(2)}, u32[]{:S(2)}) async-start(bf16[512,8,1024]{2,0,1:T(8,128)(2,1)} %bitcast.246), calls=%async_computation.9 | async-start | bytes 16777216 | tf_op jit(solution)/shard_map/all_to_all | solution.py:319
  1393.6 6.8 copy-start.24
  1393.6 6.8 copy-start.26
  1552.4 53.8 %all-to-all-start.4 = ((bf16[512,8,256]{2,0,1:T(8,128)(2,1)}), bf16[512,8,256]{2,0,1:T(8,128)(2,1)}, u32[]{:S(2)}, u32[]{:S(2)}) async-start(bf16[512,8,256]{2,0,1:T(8,128)(2,1)} %copy.167), calls=%async_computation.8 | async-start | bytes 4194304 | tf_op jit(solution)/shard_map/all_to_all | solution.py:318
  1606.2 64.2 %all-to-all-start.2 = ((bf16[512,8,256]{2,0,1:T(8,128)(2,1)}), bf16[512,8,256]{2,0,1:T(8,128)(2,1)}, u32[]{:S(2)}, u32[]{:S(2)}) async-start(bf16[512,8,256]{2,0,1:T(8,128)(2,1)} %copy.164), calls=%async_computation.6 | async-start | bytes 4194304 | tf_op jit(solution)/shard_map/all_to_all | solution.py:316
  1610.5 605.7 %all-reduce.14.cloned.1.call-start = ((), (), s32[]{:S(2)}) async-start(), calls=%async_computation.24 | async-start | bytes 196608 | tf_op jit(solution)/shard_map/psum | solution.py:289
  1621.5 21.5 copy-start.30
  1621.5 21.5 copy-start.32
  1670.4 124.4 %all-to-all-start.3 = ((bf16[512,8,256]{2,0,1:T(8,128)(2,1)}), bf16[512,8,256]{2,0,1:T(8,128)(2,1)}, u32[]{:S(2)}, u32[]{:S(2)}) async-start(bf16[512,8,256]{2,0,1:T(8,128)(2,1)} %copy.165), calls=%async_computation.7 | async-start | bytes 4194304 | tf_op jit(solution)/shard_map/all_to_all | solution.py:317
  1674.8 958.1 %all-reduce.12.cloned.1.call-start = ((), (), s32[]{:S(2)}) async-start(), calls=%async_computation.23 | async-start | bytes 25165824 | tf_op jit(solution)/shard_map/psum | solution.py:338
  2111.8 9.5 copy-start.41
  2163.5 10.5 copy-start.3
  2169.7 32.0 %all-to-all-start = ((bf16[2,2,128,2048]{2,1,0,3:T(2,128)(2,1)}), bf16[2,2,128,2048]{2,1,0,3:T(2,128)(2,1)}, u32[]{:S(2)}, u32[]{:S(2)}) async-start(bf16[2,2,128,2048]{2,1,0,3:T(2,128)(2,1)} %copy.148), calls=%async_computation | async-start | bytes 4194304 | tf_op jit(solution)/shard_map/all_to_all | solution.py:200
  2217.0 445.8 %copy-start.38 = (f32[256]{0:T(256)}, f32[256]{0:T(256)S(1)}, u32[]{:S(2)}) copy-start(f32[256]{0:T(256)S(1)} %dynamic_slice.30) | copy-start | bytes 3076
  2644.7 18.6 copy-start.1
  (15 other events, 42.3 us)
Sparse Core Ops, SparseCore 0:
  9.9 128.1 all-gather.16
  140.0 54.3 all-gather.22
  196.9 98.5 all-gather.20
  297.8 89.8 all-gather.18
  583.2 71.3 reduce-scatter.4
  671.7 71.1 reduce-scatter.6
  801.3 71.8 reduce-scatter.8
  889.5 71.9 reduce-scatter.10
  963.3 160.7 all-gather.26
  1125.9 160.7 all-gather.24
  1288.6 89.8 all-gather.32
  1380.8 385.1 all-gather.28
  1768.5 302.8 all-gather.30
  2077.7 126.7 all-reduce.13
  2206.9 425.9 all-reduce.11
where the time goes:
time: 2680 us; the launch traced here: 2670 us
  waiting for transfers between devices  1390 us (52%)
  local copies, waits for them, and re-layouts  492 us (18%)
  matrix products  411 us (15%)
  other arithmetic  262 us (10%)
  blocking collectives  69.6 us (3%)
  starting transfers between devices  28.2 us (1%)
    psum x1, waiting for transfers between devices, local(): lax.psum(local_rows.astype(jnp.bfloat16), 'rep').astype(jnp.float32)  408 us
    all_gather x1, waiting for transfers between devices, local(): lax.all_gather(hidden_grad_low, 'shard', axis=0, tiled=True)  277 us
    all_gather x1, waiting for transfers between devices, local(): lax.all_gather(down_rows, 'shard', axis=0, tiled=True)  146 us
    all_to_all x1, waiting for transfers between devices, local(): lax.all_to_all(active_low, 'shard', split_axis=1, concat_axis=0, tiled=True)  130 us
    all_gather x1, waiting for transfers between devices, local(): lax.all_gather(up_weight, 'shard', axis=0, tiled=True)  107 us
    dot_general x4, matrix products, transposed_times(): lax.dot_general(left_mat, right_mat, (((0,), (0,)), ((), ())), preferred_...  96.5 us
    all_gather x1, waiting for transfers between devices, local(): lax.all_gather(mixed_grad, 'shard', axis=0, tiled=True)  91.2 us
    dot_general x4, matrix products, times_transposed(): lax.dot_general(left_mat, right_mat, (((1,), (1,)), ((), ())), preferred_...  90 us
  transfers between devices with their start and end apart: 21, of which 13 were waited for; matrix products, arithmetic and copies ran while one was open for 35% of the time, Pallas kernels for 0%

commit v1 on v0

v1 whole, which is shorter than its diff:
```python
import jax
import jax.numpy as jnp
from jax import lax
from jax.experimental import pallas as pl
from jax.experimental.pallas import tpu as pltpu
from jax.sharding import PartitionSpec as P

D = 2048
HEADS = 8
HD = 256
ROT = 64
FF = 8192
BLK = 128
SEQ_MOST = 8
MB = 2
EPS = 1e-05
SCALE = HD ** (-0.5)

bf16 = jnp.bfloat16
f32 = jnp.float32

ORDER = (0, 2, 4, 6, 1, 3, 5, 7)
SPOT = tuple(ORDER.index(r) for r in range(8))


def dot(a, b, ca, cb):
    return lax.dot_general(a, b, (((ca,), (cb,)), ((), ())), preferred_element_type=f32)


def flip(value, bit):
    return lax.ppermute(value, "shard", [(i, i ^ bit) for i in range(8)])


def gather_pieces(own):
    x_got = [flip(h, 2) for h in own]
    y_got = [flip(h, 4) for h in own]
    core = [flip(h, 1) for h in own]
    far = [flip(x_got[0], 4), flip(y_got[1], 2)]
    x_core = [flip(h, 1) for h in x_got]
    y_core = [flip(h, 1) for h in y_got]
    far_core = [flip(h, 1) for h in far]
    return [own, core, x_got, x_core, y_got, y_core, far, far_core]


def turn_rows(value, bit):
    lead, n, c = value.shape[:-2], value.shape[-2], value.shape[-1]
    if bit == 1:
        return lax.rev(value, (value.ndim - 3,))
    value = value.reshape(lead + (2, 2, n // 4, c))
    value = lax.rev(value, (value.ndim - (3 if bit == 2 else 4),))
    return value.reshape(lead + (n, c))


def reduce_pieces(odd, even_of, turn=lambda value, bit: value):
    even = even_of(turn(flip(odd, 1), 1))
    one, two = even[:, 0], even[:, 1]
    got_one = turn(flip(one[1::2], 2), 2)
    got_two = turn(flip(two[2:], 4), 4)
    mid_one = [(one[2 * i].astype(f32) + got_one[i].astype(f32)).astype(bf16) for i in range(2)]
    mid_two = [(two[i].astype(f32) + got_two[i].astype(f32)).astype(bf16) for i in range(2)]
    last_one = turn(flip(mid_one[1], 4), 4)
    last_two = turn(flip(mid_two[1], 2), 2)
    return [
        mid_one[0].astype(f32) + last_one.astype(f32),
        mid_two[0].astype(f32) + last_two.astype(f32),
    ]


def rep_sum(value):
    if lax.axis_size("rep") != 4:
        return lax.psum(value, "rep")
    spot = lax.axis_index("rep")
    inner = (spot == 1) | (spot == 2)
    came = lax.ppermute(value, "rep", [(0, 1), (3, 2)])
    pair = (value.astype(f32) + came.astype(f32)).astype(bf16)
    other = lax.ppermute(pair, "rep", [(1, 2), (2, 1)])
    total = (pair.astype(f32) + other.astype(f32)).astype(bf16)
    back = lax.ppermute(total, "rep", [(1, 0), (2, 3)])
    return jnp.where(inner, total, back)


def rotary_tables():
    half = ROT // 2
    freqs = 10000.0 ** (-2.0 * jnp.arange(half, dtype=f32) / ROT)
    angles = jnp.arange(SEQ_MOST * BLK, dtype=f32)[:, None] * freqs[None, :]
    rest = 128 - ROT
    cosine = jnp.concatenate(
        [jnp.cos(angles), jnp.cos(angles), jnp.ones((SEQ_MOST * BLK, rest), f32)], axis=-1
    )
    sine = jnp.concatenate(
        [-jnp.sin(angles), jnp.sin(angles), jnp.zeros((SEQ_MOST * BLK, rest), f32)], axis=-1
    )
    return cosine.reshape(SEQ_MOST, BLK, 128), sine.reshape(SEQ_MOST, BLK, 128)


def attention_kernel(
    piece_of, inner_of, first_of, end_of,
    qkv_ref, grad_ref, cos_ref, sin_ref,
    ctx_ref, out_ref,
    q_buf, k_buf, v_buf, dk_buf, dv_buf,
):
    m = pl.program_id(0)
    blocks = piece_of.shape[1]
    lane = lax.broadcasted_iota(jnp.int32, (BLK, 128), 1)

    def turned(x):
        return jnp.where(lane < ROT // 2, pltpu.roll(x, 128 - ROT // 2, 1), pltpu.roll(x, ROT // 2, 1))

    def load(g, carry):
        p, i = piece_of[m, g], inner_of[m, g]
        at = g - first_of[m, g]
        cosine, sine = cos_ref[at], sin_ref[at]
        rows = pl.ds(pl.multiple_of(g * BLK, BLK), BLK)
        for buf, start in ((q_buf, 0), (k_buf, HD)):
            front = qkv_ref[p, 0, i, :, start:start + 128]
            buf[rows, 0:128] = (front * cosine + turned(front) * sine).astype(bf16)
            buf[rows, 128:HD] = qkv_ref[p, 0, i, :, start + 128:start + HD].astype(bf16)
        v_buf[rows, :] = qkv_ref[p, 0, i, :, 2 * HD:].astype(bf16)
        return carry

    lax.fori_loop(0, blocks, load, 0)
    k_buf[blocks * BLK:, :] = jnp.zeros((BLK, HD), bf16)
    v_buf[blocks * BLK:, :] = jnp.zeros((BLK, HD), bf16)
    dk_buf[...] = jnp.zeros(dk_buf.shape, f32)
    dv_buf[...] = jnp.zeros(dv_buf.shape, f32)

    def attend(g, span):
        p, i = piece_of[m, g], inner_of[m, g]
        first = first_of[m, g]
        rows = pl.ds(pl.multiple_of(g * BLK, BLK), BLK)
        keys = pl.ds(pl.multiple_of(first * BLK, BLK), span)
        query, key, value = q_buf[rows, :], k_buf[keys, :], v_buf[keys, :]
        grad = grad_ref[p, 0, i]
        scores = dot(query, key, 1, 1) * SCALE
        key_tok = first * BLK + lax.broadcasted_iota(jnp.int32, (BLK, span), 1)
        query_tok = g * BLK + lax.broadcasted_iota(jnp.int32, (BLK, span), 0)
        allowed = (key_tok <= query_tok) & (key_tok < end_of[m, g])
        scores = jnp.where(allowed, scores, -jnp.inf)
        exponent = jnp.exp(scores - jnp.max(scores, axis=1, keepdims=True))
        prob = exponent * (1.0 / jnp.sum(exponent, axis=1, keepdims=True))
        prob_low = prob.astype(bf16)
        ctx_ref[p, 0, i] = dot(prob_low, value, 1, 0).astype(bf16)
        prob_grad = dot(grad, value, 1, 1)
        delta = jnp.sum(prob * prob_grad, axis=1, keepdims=True)
        score_grad = (prob * (prob_grad - delta)).astype(bf16)
        dk_buf[keys, :] += dot(score_grad, query, 0, 0)
        dv_buf[keys, :] += dot(prob_low, grad, 0, 0)
        query_grad = dot(score_grad, key, 1, 0) * SCALE
        at = g - first
        front = query_grad[:, 0:128]
        out_ref[p, 0, i, :, 0:128] = (front * cos_ref[at] - turned(front) * sin_ref[at]).astype(bf16)
        out_ref[p, 0, i, :, 128:HD] = query_grad[:, 128:].astype(bf16)

    def one_block(g, carry):
        pairs = (g - first_of[m, g]) // 2
        for count in range(SEQ_MOST // 2):
            pl.when(pairs == count)(lambda: attend(g, (count + 1) * 2 * BLK))
        return carry

    lax.fori_loop(0, blocks, one_block, 0)

    def store(g, carry):
        p, i = piece_of[m, g], inner_of[m, g]
        at = g - first_of[m, g]
        rows = pl.ds(pl.multiple_of(g * BLK, BLK), BLK)
        front = dk_buf[rows, 0:128] * SCALE
        out_ref[p, 0, i, :, HD:HD + 128] = (
            front * cos_ref[at] - turned(front) * sin_ref[at]
        ).astype(bf16)
        out_ref[p, 0, i, :, HD + 128:2 * HD] = (dk_buf[rows, 128:HD] * SCALE).astype(bf16)
        out_ref[p, 0, i, :, 2 * HD:] = dv_buf[rows, :].astype(bf16)
        return carry

    lax.fori_loop(0, blocks, store, 0)


def attention(tables, qkv, grad, cosine, sine):
    pieces, _, own = qkv.shape[:3]
    blocks = tables[0].shape[1]

    def part(width):
        return pl.BlockSpec((pieces, 1, own, BLK, width), lambda m, *_: (0, m, 0, 0, 0))

    whole = pl.BlockSpec((SEQ_MOST, BLK, 128), lambda m, *_: (0, 0, 0))
    rows = (blocks + 1) * BLK
    return pl.pallas_call(
        attention_kernel,
        grid_spec=pltpu.PrefetchScalarGridSpec(
            num_scalar_prefetch=4,
            grid=(MB,),
            in_specs=[part(3 * HD), part(HD), whole, whole],
            out_specs=[part(HD), part(3 * HD)],
            scratch_shapes=[
                pltpu.VMEM((rows, HD), bf16),
                pltpu.VMEM((rows, HD), bf16),
                pltpu.VMEM((rows, HD), bf16),
                pltpu.VMEM((rows, HD), f32),
                pltpu.VMEM((rows, HD), f32),
            ],
        ),
        out_shape=[
            jax.ShapeDtypeStruct((pieces, MB, own, BLK, HD), bf16),
            jax.ShapeDtypeStruct((pieces, MB, own, BLK, 3 * HD), bf16),
        ],
        compiler_params=pltpu.CompilerParams(vmem_limit_bytes=52 * 2**20),
        cost_estimate=pl.CostEstimate(
            flops=MB * blocks * 6 * BLK * 640 * HD * 2, bytes_accessed=30 * 2**20, transcendentals=2**21
        ),
    )(*tables, qkv, grad, cosine, sine)


def local(
    tokens, cotangent, seq_blocks, seq_pad, deal_order,
    ln1_gain, ln1_bias, ln2_gain, ln2_bias,
    qkv_weight, qkv_bias, out_weight, out_bias, up_weight, up_bias, down_weight, down_bias,
):
    shards = lax.axis_size("shard")
    place = lax.axis_index("shard")
    cube = shards == 8
    own = tokens.shape[1]
    blocks = deal_order.shape[2]
    own_rows = MB * own * BLK
    rows = shards * own_rows
    cols = D // shards
    wide = FF // shards
    split = shards // HEADS
    head, share = place // split, place % split
    share_cols = 3 * HD // split

    if cube:
        owners = jnp.bitwise_xor(place, jnp.array(ORDER, jnp.int32))
        spots = jnp.array(SPOT, jnp.int32)[jnp.bitwise_xor(place, jnp.arange(8))]
    else:
        owners = jnp.arange(shards, dtype=jnp.int32)
    deal = deal_order[:, 0, :]
    counts = seq_blocks[:, 0, :]
    pads = seq_pad[:, 0, :]
    ids = jnp.arange(blocks, dtype=jnp.int32)
    inverse = jnp.sum(
        jnp.where(deal[:, None, :] == ids[None, :, None], ids[None, None, :], 0), axis=-1
    )
    owner_of = inverse // own
    piece_of = jnp.sum(
        jnp.where(
            owner_of[:, :, None] == owners, jnp.arange(shards, dtype=jnp.int32)[None, None, :], 0
        ),
        axis=-1,
    )
    inner_of = inverse % own
    ends = jnp.cumsum(counts, axis=1)
    starts = ends - counts
    inside = (ids[None, :, None] >= starts[:, None, :]) & (ids[None, :, None] < ends[:, None, :])
    first_of = jnp.sum(jnp.where(inside, starts[:, None, :], 0), axis=-1)
    valid = jnp.sum(jnp.where(inside, (counts * BLK - pads)[:, None, :], 0), axis=-1)
    tables = [t.astype(jnp.int32) for t in (piece_of, inner_of, first_of, first_of * BLK + valid)]
    given = jnp.take(deal.reshape(MB, shards, own), owners, axis=1)

    cot_own = jnp.stack([cotangent[m][given[m]] for m in range(MB)], axis=1)
    if cube:
        cot_own = cot_own.reshape(2, 4, own_rows, cols)
        got = gather_pieces([cot_own[0], cot_own[1]])
        got = [jnp.concatenate(g, axis=0) for g in got]
        parts = []
        for r in ORDER:
            parts.append(jnp.concatenate([got[r][SPOT[o ^ r]] for o in ORDER], axis=0))
        grad_out = jnp.stack(parts)
        out_w = jnp.take(out_weight.reshape(-1, shards, cols), owners, axis=1)
        down_w = jnp.take(down_weight.reshape(-1, shards, cols), owners, axis=1)
    else:
        grad_out = lax.all_gather(cot_own.reshape(rows, cols), "shard", axis=0)
        out_w = out_weight.reshape(-1, shards, cols)
        down_w = down_weight.reshape(-1, shards, cols)

    params = jnp.concatenate([ln1_gain, ln1_bias, ln2_gain, ln2_bias, qkv_bias])
    params = lax.all_gather(params, "shard", axis=0).astype(f32)
    gain_one, shift_one, gain_two, shift_two = [
        params[:, i * cols:(i + 1) * cols].reshape(D) for i in range(4)
    ]
    bias_qkv = params[:, 4 * cols:].reshape(3, HEADS, HD)
    bias_qkv = lax.dynamic_index_in_dim(bias_qkv, head, 1, keepdims=False).reshape(3 * HD)

    up_send = up_weight.astype(f32) * ln2_gain.astype(f32)[:, None]
    up_send = up_send.astype(bf16).reshape(cols, shards, wide).transpose(1, 0, 2)
    up_w = lax.all_to_all(up_send, "shard", split_axis=0, concat_axis=0, tiled=True).reshape(D, wide)
    qkv_send = qkv_weight.astype(f32) * ln1_gain.astype(f32)[:, None]
    qkv_send = qkv_send.astype(bf16).reshape(cols, 3, HEADS, HD).transpose(2, 0, 1, 3)
    qkv_send = jnp.repeat(qkv_send.reshape(HEADS, cols, 3 * HD), split, axis=0)
    qkv_w = lax.all_to_all(qkv_send, "shard", split_axis=0, concat_axis=0, tiled=True)
    qkv_w = qkv_w.reshape(D, 3 * HD)

    bias_up = up_bias.astype(f32) + jnp.sum(up_w.astype(f32) * (shift_two / gain_two)[:, None], axis=0)
    bias_qkv = bias_qkv + jnp.sum(qkv_w.astype(f32) * (shift_one / gain_one)[:, None], axis=0)

    flat = tokens.reshape(own_rows, D).astype(f32)
    center = flat - jnp.mean(flat, axis=-1, keepdims=True)
    inv_std = lax.rsqrt(jnp.mean(center * center, axis=-1, keepdims=True) + EPS)
    normed_own = center * inv_std
    normed_low = normed_own.astype(bf16)
    if cube:
        half = own_rows // 2
        got = gather_pieces([normed_low[:half], normed_low[half:]])
        normed = jnp.concatenate([h for r in ORDER for h in got[r]], axis=0)
    else:
        normed = lax.all_gather(normed_low, "shard", axis=0, tiled=True)

    def back(weights):
        return lax.dot_general(
            grad_out, weights, (((0, 2), (1, 2)), ((), ())), preferred_element_type=f32
        ).astype(bf16)

    active_grad = back(down_w)
    hidden = dot(normed, up_w, 1, 0) + bias_up
    cdf = 0.5 + 0.5 * lax.erf(hidden * (0.5 ** 0.5))
    density = jnp.exp(-0.5 * hidden * hidden) * 0.3989422804014327
    active = (hidden * cdf).astype(bf16)
    hidden_grad = (active_grad.astype(f32) * (cdf + hidden * density)).astype(bf16)

    def spread(grads):
        return lax.all_to_all(
            grads.reshape(shards, cols, grads.shape[-1]), "shard", split_axis=0, concat_axis=0, tiled=True
        )

    def grad_dot(left):
        return lax.dot_general(
            left, grad_out, (((0,), (1,)), ((), ())), preferred_element_type=f32
        ).astype(bf16)

    down_sum = rep_sum(grad_dot(active))
    up_sum = rep_sum(spread(dot(normed, hidden_grad, 0, 0).astype(bf16)))

    context_w = out_w
    if split > 1:
        groups = [list(range(h * split, (h + 1) * split)) for h in range(HEADS)]
        context_w = lax.all_gather(out_w, "shard", axis=0, tiled=True, axis_index_groups=groups)
    context_grad = back(context_w)
    mixed = dot(normed, qkv_w, 1, 0) + bias_qkv
    cosine, sine = rotary_tables()
    context, mixed_grad = attention(
        tables,
        mixed.reshape(shards, MB, own, BLK, 3 * HD),
        context_grad.reshape(shards, MB, own, BLK, HD),
        cosine,
        sine,
    )
    context = context.reshape(rows, HD)
    mixed_grad = mixed_grad.reshape(rows, 3 * HD)
    if split > 1:
        context = lax.dynamic_slice_in_dim(context, share * (HD // split), HD // split, 1)
        mixed_grad = lax.dynamic_slice_in_dim(mixed_grad, share * share_cols, share_cols, 1)
        qkv_w = lax.dynamic_slice_in_dim(qkv_w, share * share_cols, share_cols, 1)
    qkv_sum = rep_sum(spread(dot(normed, mixed_grad, 0, 0).astype(bf16)))
    out_sum = rep_sum(grad_dot(context))

    both = jnp.concatenate([context, active], axis=1)
    both_w = jnp.concatenate([out_w, down_w], axis=0)
    resid = flat.reshape(own_rows, shards, cols)
    resid = jnp.take(resid, owners, axis=1) if cube else resid

    def out_terms(lo, hi):
        sums = lax.dot_general(both, both_w[:, lo:hi], (((1,), (0,)), ((), ())), preferred_element_type=f32)
        if cube:
            add = jnp.pad(resid[:, lo:hi], ((0, rows - own_rows), (0, 0), (0, 0)))
            sums = sums + add
        return sums.transpose(1, 0, 2)

    if cube:
        odd = out_terms(4, 8).astype(bf16).reshape(4, 2, rows // 2, cols)
        even = out_terms(0, 4).reshape(4, 2, rows // 2, cols)
        out_own = jnp.concatenate(
            reduce_pieces(odd, lambda came: (even + came.astype(f32)).astype(bf16), turn_rows), axis=0
        )
    else:
        terms = out_terms(0, shards)
        terms = lax.dynamic_update_slice(
            terms,
            lax.dynamic_slice(terms, (0, place * own_rows, 0), (shards, own_rows, cols))
            + resid.transpose(1, 0, 2),
            (0, place * own_rows, 0),
        )
        out_own = lax.psum_scatter(terms.astype(bf16), "shard", scatter_dimension=0, tiled=True)
        out_own = out_own.reshape(rows, cols).astype(f32)
    out_own = out_own + (out_bias.astype(f32) + down_bias.astype(f32))
    out_own = out_own.astype(bf16).reshape(shards, MB, own, BLK, cols)
    out_given = jnp.stack([out_own[piece_of[m], m, inner_of[m]] for m in range(MB)])

    both_grad = jnp.concatenate([mixed_grad, hidden_grad], axis=1)
    both_w = jnp.concatenate([qkv_w, up_w], axis=1)
    if cube:
        half = rows // 2
        odd = dot(both_grad[half:], both_w, 1, 1).astype(bf16).reshape(4, 2, -1, D)
        even = dot(both_grad[:half], both_w, 1, 1).reshape(4, 2, -1, D)
        normed_grad = jnp.concatenate(
            reduce_pieces(odd, lambda came: (even + came.astype(f32)).astype(bf16)), axis=0
        )
        grad_rows = jnp.take(grad_out[:, :own_rows], spots, axis=0)
    else:
        terms = dot(both_grad, both_w, 1, 1).astype(bf16)
        normed_grad = lax.psum_scatter(terms, "shard", scatter_dimension=0, tiled=True).astype(f32)
        grad_rows = lax.dynamic_slice_in_dim(grad_out, place * own_rows, own_rows, 1)
    grad_rows = grad_rows.transpose(1, 0, 2).reshape(own_rows, D).astype(f32)
    mean_grad = jnp.mean(normed_grad, axis=-1, keepdims=True)
    mean_proj = jnp.mean(normed_grad * normed_own, axis=-1, keepdims=True)
    tokens_grad = grad_rows + inv_std * (normed_grad - mean_grad - normed_own * mean_proj)
    tokens_grad = tokens_grad.astype(bf16).reshape(MB, own, BLK, D)

    small = jnp.concatenate(
        [
            jnp.sum(mixed_grad, axis=0, dtype=f32),
            jnp.sum(hidden_grad, axis=0, dtype=f32),
            jnp.sum(cot_own, axis=tuple(range(cot_own.ndim - 1)), dtype=f32),
        ]
    )
    small = jnp.sum(lax.all_gather(lax.all_gather(small, "rep"), "shard"), axis=1)
    sum_qkv = small[:, :share_cols].reshape(HEADS, 3, HD).transpose(1, 0, 2).reshape(3 * D)
    sum_up = small[:, share_cols:share_cols + wide].reshape(FF)
    out_bias_grad = lax.dynamic_index_in_dim(small[:, share_cols + wide:], place, 0, keepdims=False)
    qkv_bias_grad = lax.dynamic_slice_in_dim(sum_qkv, place * 3 * cols, 3 * cols)
    up_bias_grad = lax.dynamic_slice_in_dim(sum_up, place * wide, wide)

    qkv_rows = qkv_sum.reshape(HEADS, split, cols, share_cols).transpose(2, 0, 1, 3)
    qkv_rows = qkv_rows.reshape(cols, HEADS, 3, HD).transpose(0, 2, 1, 3).reshape(cols, 3 * D).astype(f32)
    up_rows = up_sum.transpose(1, 0, 2).reshape(cols, FF).astype(f32)

    def finish(sums, weight, gain, shift, total):
        weight_f = weight.astype(f32)
        grads = gain.astype(f32)[:, None] * sums + shift.astype(f32)[:, None] * total
        return grads, jnp.sum(weight_f * sums, axis=1), jnp.sum(weight_f * total, axis=1)

    qkv_grad, gain_one_grad, shift_one_grad = finish(qkv_rows, qkv_weight, ln1_gain, ln1_bias, sum_qkv)
    up_grad, gain_two_grad, shift_two_grad = finish(up_rows, up_weight, ln2_gain, ln2_bias, sum_up)

    def in_order(sums):
        sums = jnp.take(sums, spots, axis=1) if cube else sums
        return sums.reshape(-1, D).astype(f32)

    return (
        out_given,
        tokens_grad,
        gain_one_grad,
        shift_one_grad,
        gain_two_grad,
        shift_two_grad,
        qkv_grad,
        qkv_bias_grad,
        in_order(out_sum),
        out_bias_grad,
        up_grad,
        up_bias_grad,
        in_order(down_sum),
        out_bias_grad,
    )


def solution(mesh):
    in_specs = (
        P(None, ("rep", "shard"), None, None),
        P(None, "rep", None, "shard"),
        P(None, "rep", None),
        P(None, "rep", None),
        P(None, "rep", None),
        P("shard"),
        P("shard"),
        P("shard"),
        P("shard"),
        P("shard", None),
        P("shard"),
        P("shard", None),
        P("shard"),
        P("shard", None),
        P("shard"),
        P("shard", None),
        P("shard"),
    )
    out_specs = (
        P(None, "rep", None, "shard"),
        P(None, ("rep", "shard"), None, None),
        P("shard"),
        P("shard"),
        P("shard"),
        P("shard"),
        P("shard", None),
        P("shard"),
        P("shard", None),
        P("shard"),
        P("shard", None),
        P("shard"),
        P("shard", None),
        P("shard"),
    )
    return jax.shard_map(local, mesh=mesh, in_specs=in_specs, out_specs=out_specs, check_vma=False)
```

time: 2680 us -> 1230 us (0.46)
  waiting for transfers between devices: 1390 us -> 345 us
  local copies, waits for them, and re-layouts: 492 us -> 246 us
  matrix products: 411 us -> 239 us
  other arithmetic: 262 us -> 168 us
  Pallas kernels: 0 us -> 53.4 us
  starting transfers between devices: 28.2 us -> 76.8 us
    all_gather x9 -> x0, waiting for transfers between devices: 762 us -> none  [the longest x1 277 us: local(): lax.all_gather(hidden_grad_low, 'shard', axis=0, tiled=True)]
    psum x2 -> x0, waiting for transfers between devices: 408 us -> none  [the longest x1 408 us: local(): lax.psum(local_rows.astype(jnp.bfloat16), 'rep').astype(jnp.float32)]
    ppermute x0 -> x50, waiting for transfers between devices: none -> 340 us  [the longest x38 168 us: flip(): return lax.ppermute(value, 'shard', [(i, i ^ bit) for i in range(8)])]
    all_to_all x6 -> x4, waiting for transfers between devices: 204 us -> 4.29 us  [the longest x2 4.29 us: spread(): lax.all_to_all(grads.reshape(shards, cols, grads.shape[-1]), 'shard', spl...]
    dot_general x18 -> x12, matrix products: 411 us -> 239 us  [the longest x6 129 us: dot(): lax.dot_general(a, b, (((ca,), (cb,)), ((), ())), preferred_element_type=...]
    scatter-add x4 -> x0, other arithmetic: 138 us -> none  [the longest x2 69 us: local(): value_term = jnp.zeros((group_blocks, BLK, D), jnp.float32).at[term_slots...]
    slice x13 -> x19, local copies, waits for them, and re-layouts: 149 us -> 16.3 us  [the longest x1 3.13 us: local(): grad_rows = jnp.take(grad_out[:, :own_rows], spots, axis=0)]
    squeeze x4 -> x3, local copies, waits for them, and re-layouts: 72.5 us -> 2.26 us  [the longest x1 1.68 us: local(): cot_own = jnp.stack([cotangent[m][given[m]] for m in range(MB)], axis=1)]
  transfers between devices with their start and end apart: 21 -> 54, of which waited for: 13 -> 14; matrix products, arithmetic and copies ran while one was open for 35% -> 49% of each run, Pallas kernels for 0% -> 4%
where the time goes in v1:
time: 1230 us; the launch traced here: 1220 us
  waiting for transfers between devices  345 us (28%)
  local copies, waits for them, and re-layouts  246 us (20%)
  matrix products  239 us (19%)
  other arithmetic  168 us (14%)
  blocking collectives  92.3 us (8%)
  starting transfers between devices  76.8 us (6%)
  Pallas kernels  53.4 us (4%)
    ppermute x38, waiting for transfers between devices, flip(): return lax.ppermute(value, 'shard', [(i, i ^ bit) for i in range(8)])  168 us
    dot_general x6, matrix products, dot(): lax.dot_general(a, b, (((ca,), (cb,)), ((), ())), preferred_element_type=...  129 us
    unnamed x231, local copies, waits for them, and re-layouts  112 us
    ppermute x4, waiting for transfers between devices, rep_sum(): came = lax.ppermute(value, 'rep', [(0, 1), (3, 2)])  107 us
    all_gather x1, blocking collectives, local(): params = lax.all_gather(params, 'shard', axis=0).astype(f32)  69 us
    ppermute x4, waiting for transfers between devices, rep_sum(): back = lax.ppermute(total, 'rep', [(1, 0), (2, 3)])  65.5 us
    pallas_call x1, Pallas kernels, attention(): pl.pallas_call(attention_kernel, grid_spec=pltpu.PrefetchScalarGridSpec(n...  53.4 us
    dot_general x2, matrix products, out_terms(): lax.dot_general(both, both_w[:, lo:hi], (((1,), (0,)), ((), ())), preferr...  37.1 us
  transfers between devices with their start and end apart: 54, of which 14 were waited for; matrix products, arithmetic and copies ran while one was open for 49% of the time, Pallas kernels for 4%

profile of v1, /device:TPU:0, one launch (start us, length us, event | category | flops | bytes accessed | tf_op | source)
XLA Modules:
  0.0 1221.5 jit_solution(6833950677779936798)
XLA Ops:
  30.3 69.0 %all-gather.3 = bf16[8,1,1792]{2,1,0:T(2,128)(2,1)S(1)} all-gather(bf16[1,1,1792]{2,1,0:T(2,128)(2,1)S(1)} %reshape.793), channel_id=2, replica_groups=mesh['rep'=4,'shard'=8] {'shard'}, dimensions={0}, use_global_device_ids=true | all-gather | bytes 32256 | tf_op jit(solution)/shard_map/all_gather | solution.py:275
  107.3 6.4 copy.159
  124.5 6.4 copy.162
  130.9 6.4 copy.163
  202.5 6.0 collective-permute-done
  209.6 20.7 %collective-permute-done.1 = bf16[256,2048]{1,0:T(8,128)(2,1)S(1)} collective-permute-done((bf16[256,2048]{1,0:T(8,128)(2,1)S(1)}, bf16[256,2048]{1,0:T(8,128)(2,1)S(1)}, u32[]{:S(2)}, u32[]{:S(2)}) %collective-permute-start.1) | collective-permute-done | bytes 1048608 | tf_op jit(solution)/shard_map/ppermute | solution.py:31
  238.5 18.4 %collective-permute-done.18 = bf16[4,512,256]{2,1,0:T(8,128)(2,1)S(1)} collective-permute-done((bf16[4,512,256]{2,1,0:T(8,128)(2,1)}, bf16[4,512,256]{2,1,0:T(8,128)(2,1)S(1)}, u32[]{:S(2)}, u32[]{:S(2)}) %collective-permute-start.18) | collective-permute-done | bytes 1048608 | tf_op jit(solution)/shard_map/ppermute | solution.py:31
  261.6 21.4 %collective-permute-done.4 = bf16[256,2048]{1,0:T(8,128)(2,1)} collective-permute-done((bf16[256,2048]{1,0:T(8,128)(2,1)S(1)}, bf16[256,2048]{1,0:T(8,128)(2,1)}, u32[]{:S(2)}, u32[]{:S(2)}) %collective-permute-start.4) | collective-permute-done | bytes 1048608 | tf_op jit(solution)/shard_map/ppermute | solution.py:31
  329.3 9.9 fusion.20
  341.9 15.8 %convolution_add_fusion = f32[4096,768]{1,0:T(8,128)} fusion(bf16[4096,2048]{1,0:T(8,128)(2,1)S(1)} %constant_dynamic-update-slice_fusion, bf16[2048,768]{1,0:T(8,128)(2,1)S(1)} %bitcast.562, f32[768]{0:T(1024)S(1)} %add.279), kind=kOutput, calls=%fused_computation.51 | convolution fusion | flops 12888047616 | bytes 32508928 | tf_op jit(solution)/shard_map/dot_general | solution.py:27
  357.8 53.4 %shard_map.290 = (bf16[8,2,2,128,256]{4,3,2,1,0:T(8,128)(2,1)}, bf16[8,2,2,128,768]{4,3,2,1,0:T(8,128)(2,1)}) custom-call(s32[2,16]{1,0:T(2,128)S(1)} %select_reduce_fusion.1.piece_of, s32[2,16]{1,0:T(2,128)S(1)} %get-tuple-element.121.inner_of, s32[2,16]{1,0:T(2,128)S(1)} %get-tuple-element.81.first_of, s32[2,16]{1,0:T(2,128)S(1)} %multiply_add_fusion.2.end_of, ...), custom_call_target="tpu_custom_call" | custom-call | flops 8053063680 | bytes 31457280 | tf_op jit(solution)/shard_map/pallas_call | solution.py:186
  411.1 11.9 convolution_convert_fusion.3
  428.0 8.7 copy.169
  436.6 19.0 %convolution_convert_fusion.2 = bf16[2048,768]{1,0:T(8,128)(2,1)S(1)} fusion(bf16[4096,2048]{1,0:T(8,128)(2,1)} %copy-done.28, bf16[4096,768]{1,0:T(8,128)(2,1)} %bitcast.532), kind=kOutput, calls=%fused_computation.109 | convolution fusion | flops 12886474752 | bytes 26214400 | tf_op jit(solution)/shard_map/dot_general | solution.py:27
  465.6 5.0 reshape.672
  481.5 6.4 copy.160
  488.0 25.9 %multiply_convert_fusion = (bf16[4096,1024]{0,1:T(8,128)(2,1)S(1)}, f32[4096,1024]{0,1:T(8,128)}) fusion(f32[1024]{0:T(1024)S(1)} %convert_add_fusion.12, bf16[4096,2048]{1,0:T(8,128)(2,1)} %copy-done.28, bf16[2048,1024]{1,0:T(8,128)(2,1)} %bitcast.550), kind=kOutput, calls=%fused_computation.25 | convolution fusion | flops 17205035008 | bytes 46141440 | tf_op jit(solution)/shard_map/dot_general | solution.py:27
  513.9 24.3 %fusion.23 = bf16[1024,8,256]{2,0,1:T(8,128)(2,1)} fusion(bf16[8,4096,256]{2,1,0:T(8,128)(2,1)} %bitcast_dynamic-update-slice_fusion, bf16[4096,1024]{0,1:T(8,128)(2,1)S(1)} %get-tuple-element.125), kind=kOutput, calls=%fused_computation.111 | convolution fusion | flops 17181966336 | bytes 29360128 | tf_op jit(solution)/shard_map/dot_general | solution.py:324
  541.5 26.7 %convert_reduce_fusion = (f32[1024]{0:T(1024)S(1)}, bf16[4096,1024]{0,1:T(8,128)(2,1)}) fusion(f32[4096,1024]{0,1:T(8,128)} %get-tuple-element.126, f32[1024]{0:T(1024)S(1)} %convert_add_fusion.12, bf16[8,4096,256]{2,1,0:T(8,128)(2,1)} %bitcast_dynamic-update-slice_fusion, bf16[1024,8,256]{2,0,1:T(8,128)(2,1)S(1)} %copy-done.12), kind=kOutput, calls=%fused_computation.20 | convolution fusion | flops 17242783744 | bytes 46145536 | tf_op jit(solution)/shard_map/dot_general | solution.py:307
  568.2 24.2 %convolution_convert_fusion.1 = bf16[2048,1024]{1,0:T(8,128)(2,1)} fusion(bf16[4096,2048]{1,0:T(8,128)(2,1)S(1)} %bitcast.576, bf16[4096,1024]{0,1:T(8,128)(2,1)} %get-tuple-element.128), kind=kOutput, calls=%fused_computation.107 | convolution fusion | flops 17181966336 | bytes 29360128 | tf_op jit(solution)/shard_map/dot_general | solution.py:27
  597.4 20.9 %convolution_convert_fusion = bf16[2048,2048]{1,0:T(8,128)(2,1)} fusion(bf16[4096,1024]{0,1:T(8,128)(2,1)} %get-tuple-element.128, bf16[4096,768]{0,1:T(8,128)(2,1)} %copy.169, bf16[2048,1024]{1,0:T(8,128)(2,1)} %bitcast.551, bf16[2048,768]{1,0:T(8,128)(2,1)S(1)} %bitcast.563), kind=kOutput, calls=%fused_computation.50 | convolution fusion | flops 15065939968 | bytes 30408704 | tf_op jit(solution)/shard_map/dot_general | solution.py:27
  621.3 18.4 %add_convert_fusion.2 = bf16[4096,4,256]{2,0,1:T(8,128)(2,1)} fusion(f32[512,4,256]{2,0,1:T(8,128)} %get-tuple-element.92, bf16[4096,1024]{0,1:T(8,128)(2,1)} %copy-done.62, bf16[4096,256]{0,1:T(8,128)(2,1)} %copy.161, bf16[1024,8,256]{2,0,1:T(8,128)(2,1)} %select_bitcast_fusion, bf16[256,8,256]{2,0,1:T(8,128)(2,1)} %select_bitcast_fusion.2), kind=kOutput, calls=%fused_computation.23 | convolution fusion | flops 10772021248 | bytes 26214400 | tf_op jit(solution)/shard_map/dot_general | solution.py:360
  650.2 18.7 %pad_add_fusion = f32[4096,4,256]{2,0,1:T(8,128)} fusion(f32[512,4,256]{2,0,1:T(8,128)} %get-tuple-element.93, bf16[4096,1024]{0,1:T(8,128)(2,1)} %copy-done.62, bf16[4096,256]{0,1:T(8,128)(2,1)} %copy.161, bf16[256,8,256]{2,0,1:T(8,128)(2,1)} %select_bitcast_fusion.2, bf16[1024,8,256]{2,0,1:T(8,128)(2,1)} %select_bitcast_fusion), kind=kOutput, calls=%fused_computation.24 | convolution fusion | flops 10767826944 | bytes 34603008 | tf_op jit(solution)/shard_map/dot_general | solution.py:360
  669.0 13.2 %all-gather.1 = f32[8192]{0:T(1024)S(1)} all-gather(f32[2048]{0:T(1024)S(1)} %pad_maximum_fusion.11), channel_id=3, replica_groups=mesh['rep'=4,'shard'=8] {'rep'}, dimensions={0}, use_global_device_ids=true | all-gather | bytes 40960 | tf_op jit(solution)/shard_map/all_gather | solution.py:413
  682.2 10.1 all-gather.4
  702.3 23.2 %fusion.13 = f32[2048,2048]{1,0:T(8,128)} fusion(bf16[4096,768]{0,1:T(8,128)(2,1)} %copy.169, bf16[4096,1024]{0,1:T(8,128)(2,1)} %get-tuple-element.128, bf16[2048,1024]{1,0:T(8,128)(2,1)} %bitcast.552, bf16[2048,768]{1,0:T(8,128)(2,1)} %bitcast.561), kind=kOutput, calls=%fused_computation.53 | convolution fusion | flops 15061745664 | bytes 38797312 | tf_op jit(solution)/shard_map/dot_general | solution.py:27
  746.4 107.0 %collective-permute-done.38 = bf16[8,256,768]{1,2,0:T(8,128)(2,1)} collective-permute-done((bf16[8,256,768]{1,2,0:T(8,128)(2,1)S(1)}, bf16[8,256,768]{1,2,0:T(8,128)(2,1)}, u32[]{:S(2)}, u32[]{:S(2)}) %collective-permute-start.38) | collective-permute-done | bytes 3145760 | tf_op jit(solution)/shard_map/ppermute | solution.py:74
  858.5 7.8 add_convert_fusion.6
  866.4 9.2 add_convert_fusion
  877.6 9.9 add_convert_fusion.1
  896.0 5.4 add_convert_fusion.3
  908.5 16.3 %collective-permute-done.34 = bf16[2,256,2048]{2,1,0:T(8,128)(2,1)} collective-permute-done((bf16[2,256,2048]{2,1,0:T(8,128)(2,1)S(1)}, bf16[2,256,2048]{2,1,0:T(8,128)(2,1)}, u32[]{:S(2)}, u32[]{:S(2)}) %collective-permute-start.34) | collective-permute-done | bytes 2097184 | tf_op jit(solution)/shard_map/ppermute | solution.py:31
  928.7 39.5 %collective-permute-done.29 = bf16[2,2048,256]{2,1,0:T(8,128)(2,1)S(1)} collective-permute-done((bf16[2,2048,256]{2,1,0:T(8,128)(2,1)}, bf16[2,2048,256]{2,1,0:T(8,128)(2,1)S(1)}, u32[]{:S(2)}, u32[]{:S(2)}) %collective-permute-start.29) | collective-permute-done | bytes 2097184 | tf_op jit(solution)/shard_map/ppermute | solution.py:31
  974.9 11.5 collective-permute-done.31
  990.3 18.5 %collective-permute-done.35 = bf16[256,2048]{1,0:T(8,128)(2,1)} collective-permute-done((bf16[256,2048]{1,0:T(8,128)(2,1)}, bf16[256,2048]{1,0:T(8,128)(2,1)}, u32[]{:S(2)}, u32[]{:S(2)}) %collective-permute-start.35) | collective-permute-done | bytes 1048608 | tf_op jit(solution)/shard_map/ppermute | solution.py:31
  1014.5 15.0 %collective-permute-done.30 = bf16[2048,256]{1,0:T(8,128)(2,1)} collective-permute-done((bf16[2048,256]{1,0:T(8,128)(2,1)}, bf16[2048,256]{1,0:T(8,128)(2,1)}, u32[]{:S(2)}, u32[]{:S(2)}) %collective-permute-start.30) | collective-permute-done | bytes 1048608 | tf_op jit(solution)/shard_map/ppermute | solution.py:31
  1046.6 6.6 copy.178
  1053.1 7.8 add_convert_fusion.5
  1062.5 35.6 %collective-permute-done.49 = bf16[1024,8,256]{2,0,1:T(8,128)(2,1)} collective-permute-done((bf16[1024,8,256]{2,0,1:T(8,128)(2,1)}, bf16[1024,8,256]{2,0,1:T(8,128)(2,1)}, u32[]{:S(2)}, u32[]{:S(2)}) %collective-permute-start.49) | collective-permute-done | bytes 4194336 | tf_op jit(solution)/shard_map/ppermute | solution.py:78
  1102.7 5.2 gather_fusion.11
  1107.9 6.2 bitcast_convert_fusion.1
  1114.1 9.1 copy.177
  1123.2 9.1 copy.181
  1155.6 29.9 %collective-permute-done.43 = bf16[8,256,1024]{2,1,0:T(8,128)(2,1)} collective-permute-done((bf16[8,256,1024]{2,1,0:T(8,128)(2,1)}, bf16[8,256,1024]{2,1,0:T(8,128)(2,1)}, u32[]{:S(2)}, u32[]{:S(2)}) %collective-permute-start.43) | collective-permute-done | bytes 4194336 | tf_op jit(solution)/shard_map/ppermute | solution.py:78
  1185.6 6.1 convert_bitcast_fusion
  1191.7 9.1 copy.174
  1200.9 10.9 fusion.8
  1211.8 8.9 copy.180
  (474 shorter events, 344.1 us)
Async XLA Ops:
  11.0 167.2 %collective-permute-start.14 = (bf16[4,512,256]{2,1,0:T(8,128)(2,1)}, bf16[4,512,256]{2,1,0:T(8,128)(2,1)}, u32[]{:S(2)}, u32[]{:S(2)}) collective-permute-start(bf16[4,512,256]{2,1,0:T(8,128)(2,1)} %bitcast.32), channel_id=1, source_target_pairs={{0,2},{1,3},{2,0},{3,1},{4,6},{5,7},{6,4},{7,5},{8,10},{9,11},{10,... | collective-permute-start | bytes 3145736 | tf_op jit(solution)/shard_map/ppermute | solution.py:31
  14.0 173.0 %collective-permute-start.16 = (bf16[4,512,256]{2,1,0:T(8,128)(2,1)}, bf16[4,512,256]{2,1,0:T(8,128)(2,1)}, u32[]{:S(2)}, u32[]{:S(2)}) collective-permute-start(bf16[4,512,256]{2,1,0:T(8,128)(2,1)} %bitcast.32), channel_id=1, source_target_pairs={{0,4},{1,5},{2,6},{3,7},{4,0},{5,1},{6,2},{7,3},{8,12},{9,13},{10,... | collective-permute-start | bytes 3145736 | tf_op jit(solution)/shard_map/ppermute | solution.py:31
  15.5 167.0 %collective-permute-start.15 = (bf16[4,512,256]{2,1,0:T(8,128)(2,1)}, bf16[4,512,256]{2,1,0:T(8,128)(2,1)}, u32[]{:S(2)}, u32[]{:S(2)}) collective-permute-start(bf16[4,512,256]{2,1,0:T(8,128)(2,1)} %bitcast.37), channel_id=1, source_target_pairs={{0,2},{1,3},{2,0},{3,1},{4,6},{5,7},{6,4},{7,5},{8,10},{9,11},{10,... | collective-permute-start | bytes 3145736 | tf_op jit(solution)/shard_map/ppermute | solution.py:31
  16.0 176.5 %collective-permute-start.17 = (bf16[4,512,256]{2,1,0:T(8,128)(2,1)}, bf16[4,512,256]{2,1,0:T(8,128)(2,1)}, u32[]{:S(2)}, u32[]{:S(2)}) collective-permute-start(bf16[4,512,256]{2,1,0:T(8,128)(2,1)} %bitcast.37), channel_id=1, source_target_pairs={{0,4},{1,5},{2,6},{3,7},{4,0},{5,1},{6,2},{7,3},{8,12},{9,13},{10,... | collective-permute-start | bytes 3145736 | tf_op jit(solution)/shard_map/ppermute | solution.py:31
  16.0 180.9 %collective-permute-start.20 = (bf16[4,512,256]{2,1,0:T(8,128)(2,1)}, bf16[4,512,256]{2,1,0:T(8,128)(2,1)}, u32[]{:S(2)}, u32[]{:S(2)}) collective-permute-start(bf16[4,512,256]{2,1,0:T(8,128)(2,1)} %bitcast.37), channel_id=1, source_target_pairs={{0,1},{1,0},{2,3},{3,2},{4,5},{5,4},{6,7},{7,6},{8,9},{9,8},{10,11... | collective-permute-start | bytes 3145736 | tf_op jit(solution)/shard_map/ppermute | solution.py:31
  22.1 280.5 %all-to-all-start = ((bf16[8,256,768]{1,2,0:T(8,128)(2,1)}), bf16[8,256,768]{1,2,0:T(8,128)(2,1)}, u32[]{:S(2)}, u32[]{:S(2)}) async-start(bf16[8,256,768]{1,2,0:T(8,128)(2,1)} %bitcast.547), calls=%async_computation | async-start | bytes 6291456 | tf_op jit(solution)/shard_map/all_to_all | solution.py:288
  178.2 24.1 %collective-permute-start.21 = (bf16[4,512,256]{2,1,0:T(8,128)(2,1)}, bf16[4,512,256]{2,1,0:T(8,128)(2,1)S(1)}, u32[]{:S(2)}, u32[]{:S(2)}) collective-permute-start(bf16[4,512,256]{2,1,0:T(8,128)(2,1)} %bitcast.32), channel_id=1, source_target_pairs={{0,1},{1,0},{2,3},{3,2},{4,5},{5,4},{6,7},{7,6},{8,9},{9,8},{10,11... | collective-permute-start | bytes 3145736 | tf_op jit(solution)/shard_map/ppermute | solution.py:31
  182.5 26.1 %collective-permute-start = (bf16[256,2048]{1,0:T(8,128)(2,1)S(1)}, bf16[256,2048]{1,0:T(8,128)(2,1)S(1)}, u32[]{:S(2)}, u32[]{:S(2)}) collective-permute-start(bf16[256,2048]{1,0:T(8,128)(2,1)S(1)} %copy-done.26), channel_id=1, source_target_pairs={{0,2},{1,3},{2,0},{3,1},{4,6},{5,7},{6,4},{7,5},{8,10},{9,11},{10,... | collective-permute-start | bytes 3145736 | tf_op jit(solution)/shard_map/ppermute | solution.py:31
  186.9 44.9 %collective-permute-start.2 = (bf16[256,2048]{1,0:T(8,128)(2,1)S(1)}, bf16[256,2048]{1,0:T(8,128)(2,1)S(1)}, u32[]{:S(2)}, u32[]{:S(2)}) collective-permute-start(bf16[256,2048]{1,0:T(8,128)(2,1)S(1)} %copy-done.26), channel_id=1, source_target_pairs={{0,4},{1,5},{2,6},{3,7},{4,0},{5,1},{6,2},{7,3},{8,12},{9,13},{10,... | collective-permute-start | bytes 3145736 | tf_op jit(solution)/shard_map/ppermute | solution.py:31
  192.5 37.8 %collective-permute-start.1 = (bf16[256,2048]{1,0:T(8,128)(2,1)S(1)}, bf16[256,2048]{1,0:T(8,128)(2,1)S(1)}, u32[]{:S(2)}, u32[]{:S(2)}) collective-permute-start(bf16[256,2048]{1,0:T(8,128)(2,1)S(1)} %copy-done.25), channel_id=1, source_target_pairs={{0,2},{1,3},{2,0},{3,1},{4,6},{5,7},{6,4},{7,5},{8,10},{9,11},{10,... | collective-permute-start | bytes 3145736 | tf_op jit(solution)/shard_map/ppermute | solution.py:31
  196.9 39.1 %collective-permute-start.3 = (bf16[256,2048]{1,0:T(8,128)(2,1)S(1)}, bf16[256,2048]{1,0:T(8,128)(2,1)S(1)}, u32[]{:S(2)}, u32[]{:S(2)}) collective-permute-start(bf16[256,2048]{1,0:T(8,128)(2,1)S(1)} %copy-done.25), channel_id=1, source_target_pairs={{0,4},{1,5},{2,6},{3,7},{4,0},{5,1},{6,2},{7,3},{8,12},{9,13},{10,... | collective-permute-start | bytes 3145736 | tf_op jit(solution)/shard_map/ppermute | solution.py:31
  202.4 86.1 %collective-permute-start.6 = (bf16[256,2048]{1,0:T(8,128)(2,1)S(1)}, bf16[256,2048]{1,0:T(8,128)(2,1)S(1)}, u32[]{:S(2)}, u32[]{:S(2)}) collective-permute-start(bf16[256,2048]{1,0:T(8,128)(2,1)S(1)} %copy-done.26), channel_id=1, source_target_pairs={{0,1},{1,0},{2,3},{3,2},{4,5},{5,4},{6,7},{7,6},{8,9},{9,8},{10,11... | collective-permute-start | bytes 3145736 | tf_op jit(solution)/shard_map/ppermute | solution.py:31
  208.5 81.6 %collective-permute-start.7 = (bf16[256,2048]{1,0:T(8,128)(2,1)S(1)}, bf16[256,2048]{1,0:T(8,128)(2,1)S(1)}, u32[]{:S(2)}, u32[]{:S(2)}) collective-permute-start(bf16[256,2048]{1,0:T(8,128)(2,1)S(1)} %copy-done.25), channel_id=1, source_target_pairs={{0,1},{1,0},{2,3},{3,2},{4,5},{5,4},{6,7},{7,6},{8,9},{9,8},{10,11... | collective-permute-start | bytes 3145736 | tf_op jit(solution)/shard_map/ppermute | solution.py:31
  230.3 26.7 %collective-permute-start.18 = (bf16[4,512,256]{2,1,0:T(8,128)(2,1)}, bf16[4,512,256]{2,1,0:T(8,128)(2,1)S(1)}, u32[]{:S(2)}, u32[]{:S(2)}) collective-permute-start(bf16[4,512,256]{2,1,0:T(8,128)(2,1)} %collective-permute-done.14), channel_id=1, source_target_pairs={{0,4},{1,5},{2,6},{3,7},{4,0},{5,1},{6,2},{7,3},{8,12},{9,13},{10,... | collective-permute-start | bytes 3145736 | tf_op jit(solution)/shard_map/ppermute | solution.py:31
  231.9 25.2 %collective-permute-start.19 = (bf16[4,512,256]{2,1,0:T(8,128)(2,1)}, bf16[4,512,256]{2,1,0:T(8,128)(2,1)S(1)}, u32[]{:S(2)}, u32[]{:S(2)}) collective-permute-start(bf16[4,512,256]{2,1,0:T(8,128)(2,1)} %collective-permute-done.17), channel_id=1, source_target_pairs={{0,2},{1,3},{2,0},{3,1},{4,6},{5,7},{6,4},{7,5},{8,10},{9,11},{10,... | collective-permute-start | bytes 3145736 | tf_op jit(solution)/shard_map/ppermute | solution.py:31
  236.0 21.7 %collective-permute-start.22 = (bf16[4,512,256]{2,1,0:T(8,128)(2,1)}, bf16[4,512,256]{2,1,0:T(8,128)(2,1)S(1)}, u32[]{:S(2)}, u32[]{:S(2)}) collective-permute-start(bf16[4,512,256]{2,1,0:T(8,128)(2,1)} %collective-permute-done.15), channel_id=1, source_target_pairs={{0,1},{1,0},{2,3},{3,2},{4,5},{5,4},{6,7},{7,6},{8,9},{9,8},{10,11... | collective-permute-start | bytes 3145736 | tf_op jit(solution)/shard_map/ppermute | solution.py:31
  257.7 25.3 %collective-permute-start.4 = (bf16[256,2048]{1,0:T(8,128)(2,1)S(1)}, bf16[256,2048]{1,0:T(8,128)(2,1)}, u32[]{:S(2)}, u32[]{:S(2)}) collective-permute-start(bf16[256,2048]{1,0:T(8,128)(2,1)S(1)} %collective-permute-done), channel_id=1, source_target_pairs={{0,4},{1,5},{2,6},{3,7},{4,0},{5,1},{6,2},{7,3},{8,12},{9,13},{10,... | collective-permute-start | bytes 3145736 | tf_op jit(solution)/shard_map/ppermute | solution.py:31
  259.8 25.6 %collective-permute-start.5 = (bf16[256,2048]{1,0:T(8,128)(2,1)S(1)}, bf16[256,2048]{1,0:T(8,128)(2,1)}, u32[]{:S(2)}, u32[]{:S(2)}) collective-permute-start(bf16[256,2048]{1,0:T(8,128)(2,1)S(1)} %collective-permute-done.3), channel_id=1, source_target_pairs={{0,2},{1,3},{2,0},{3,1},{4,6},{5,7},{6,4},{7,5},{8,10},{9,11},{10,... | collective-permute-start | bytes 3145736 | tf_op jit(solution)/shard_map/ppermute | solution.py:31
  261.4 26.9 %collective-permute-start.25 = (bf16[4,512,256]{2,1,0:T(8,128)(2,1)}, bf16[4,512,256]{2,1,0:T(8,128)(2,1)S(1)}, u32[]{:S(2)}, u32[]{:S(2)}) collective-permute-start(bf16[4,512,256]{2,1,0:T(8,128)(2,1)} %collective-permute-done.16), channel_id=1, source_target_pairs={{0,1},{1,0},{2,3},{3,2},{4,5},{5,4},{6,7},{7,6},{8,9},{9,8},{10,11... | collective-permute-start | bytes 3145736 | tf_op jit(solution)/shard_map/ppermute | solution.py:31
  290.2 24.5 %collective-permute-start.26 = (bf16[4,512,256]{2,1,0:T(8,128)(2,1)S(1)}, bf16[4,512,256]{2,1,0:T(8,128)(2,1)}, u32[]{:S(2)}, u32[]{:S(2)}) collective-permute-start(bf16[4,512,256]{2,1,0:T(8,128)(2,1)S(1)} %collective-permute-done.19), channel_id=1, source_target_pairs={{0,1},{1,0},{2,3},{3,2},{4,5},{5,4},{6,7},{7,6},{8,9},{9,8},{10,11... | collective-permute-start | bytes 3145736 | tf_op jit(solution)/shard_map/ppermute | solution.py:31
  291.2 27.3 %collective-permute-start.27 = (bf16[4,512,256]{2,1,0:T(8,128)(2,1)S(1)}, bf16[4,512,256]{2,1,0:T(8,128)(2,1)}, u32[]{:S(2)}, u32[]{:S(2)}) collective-permute-start(bf16[4,512,256]{2,1,0:T(8,128)(2,1)S(1)} %collective-permute-done.18), channel_id=1, source_target_pairs={{0,1},{1,0},{2,3},{3,2},{4,5},{5,4},{6,7},{7,6},{8,9},{9,8},{10,11... | collective-permute-start | bytes 3145736 | tf_op jit(solution)/shard_map/ppermute | solution.py:31
  292.8 34.2 %collective-permute-start.12 = (bf16[256,2048]{1,0:T(8,128)(2,1)}, bf16[256,2048]{1,0:T(8,128)(2,1)}, u32[]{:S(2)}, u32[]{:S(2)}) collective-permute-start(bf16[256,2048]{1,0:T(8,128)(2,1)} %collective-permute-done.4), channel_id=1, source_target_pairs={{0,1},{1,0},{2,3},{3,2},{4,5},{5,4},{6,7},{7,6},{8,9},{9,8},{10,11... | collective-permute-start | bytes 3145736 | tf_op jit(solution)/shard_map/ppermute | solution.py:31
  293.9 45.3 %collective-permute-start.13 = (bf16[256,2048]{1,0:T(8,128)(2,1)}, bf16[256,2048]{1,0:T(8,128)(2,1)}, u32[]{:S(2)}, u32[]{:S(2)}) collective-permute-start(bf16[256,2048]{1,0:T(8,128)(2,1)} %collective-permute-done.5), channel_id=1, source_target_pairs={{0,1},{1,0},{2,3},{3,2},{4,5},{5,4},{6,7},{7,6},{8,9},{9,8},{10,11... | collective-permute-start | bytes 3145736 | tf_op jit(solution)/shard_map/ppermute | solution.py:31
  302.6 175.9 %all-to-all-start.1 = ((bf16[8,256,1024]{1,2,0:T(8,128)(2,1)}), bf16[8,256,1024]{1,2,0:T(8,128)(2,1)}, u32[]{:S(2)}, u32[]{:S(2)}) async-start(bf16[8,256,1024]{1,2,0:T(8,128)(2,1)} %bitcast.537), calls=%async_computation.1 | async-start | bytes 8388608 | tf_op jit(solution)/shard_map/all_to_all | solution.py:284
  423.1 195.7 %collective-permute-start.44 = (bf16[256,8,256]{2,0,1:T(8,128)(2,1)}, bf16[256,8,256]{2,0,1:T(8,128)(2,1)}, u32[]{:S(2)}, u32[]{:S(2)}) collective-permute-start(bf16[256,8,256]{2,0,1:T(8,128)(2,1)} %convolution_convert_fusion.3), channel_id=1, source_target_pairs={{0,8},{24,16},{1,9},{25,17},{2,10},{26,18},{3,11},{27,19},{4,12},{... | collective-permute-start | bytes 3145736 | tf_op jit(solution)/shard_map/ppermute | solution.py:74
  538.2 201.1 %collective-permute-start.47 = (bf16[1024,8,256]{2,0,1:T(8,128)(2,1)}, bf16[1024,8,256]{2,0,1:T(8,128)(2,1)}, u32[]{:S(2)}, u32[]{:S(2)}) collective-permute-start(bf16[1024,8,256]{2,0,1:T(8,128)(2,1)} %fusion.23), channel_id=1, source_target_pairs={{0,8},{24,16},{1,9},{25,17},{2,10},{26,18},{3,11},{27,19},{4,12},{... | collective-permute-start | bytes 12582920 | tf_op jit(solution)/shard_map/ppermute | solution.py:74
  592.4 54.1 %all-to-all-start.3 = ((bf16[8,256,1024]{2,1,0:T(8,128)(2,1)}), bf16[8,256,1024]{2,1,0:T(8,128)(2,1)}, u32[]{:S(2)}, u32[]{:S(2)}) async-start(bf16[8,256,1024]{2,1,0:T(8,128)(2,1)} %bitcast.553), calls=%async_computation.3 | async-start | bytes 8388608 | tf_op jit(solution)/shard_map/all_to_all | solution.py:319
  618.3 248.0 %collective-permute-start.33 = (bf16[4,2,256,2048]{3,2,1,0:T(8,128)(2,1)}, bf16[4,2,256,2048]{3,2,1,0:T(8,128)(2,1)}, u32[]{:S(2)}, u32[]{:S(2)}) collective-permute-start(bf16[4,2,256,2048]{3,2,1,0:T(8,128)(2,1)} %bitcast.593), channel_id=1, source_target_pairs={{0,1},{1,0},{2,3},{3,2},{4,5},{5,4},{6,7},{7,6},{8,9},{9,8},{10,11... | collective-permute-start | bytes 25165832 | tf_op jit(solution)/shard_map/ppermute | solution.py:31
  620.6 19.2 %collective-permute-start.45 = (bf16[256,8,256]{2,0,1:T(8,128)(2,1)S(1)}, bf16[256,8,256]{2,0,1:T(8,128)(2,1)S(1)}, u32[]{:S(2)}, u32[]{:S(2)}) collective-permute-start(bf16[256,8,256]{2,0,1:T(8,128)(2,1)S(1)} %add_convert_fusion.12), channel_id=1, source_target_pairs={{8,16},{16,8},{9,17},{17,9},{10,18},{18,10},{11,19},{19,11},{12,20... | collective-permute-start | bytes 3145736 | tf_op jit(solution)/shard_map/ppermute | solution.py:76
  639.7 237.9 %collective-permute-start.28 = (bf16[4,2,2048,256]{3,2,1,0:T(8,128)(2,1)}, bf16[4,2,2048,256]{3,2,1,0:T(8,128)(2,1)}, u32[]{:S(2)}, u32[]{:S(2)}) collective-permute-start(bf16[4,2,2048,256]{3,2,1,0:T(8,128)(2,1)} %bitcast.594), channel_id=1, source_target_pairs={{0,1},{1,0},{2,3},{3,2},{4,5},{5,4},{6,7},{7,6},{8,9},{9,8},{10,11... | collective-permute-start | bytes 25165832 | tf_op jit(solution)/shard_map/ppermute | solution.py:31
  641.0 58.3 %collective-permute-start.46 = (bf16[256,8,256]{2,0,1:T(8,128)(2,1)}, bf16[256,8,256]{2,0,1:T(8,128)(2,1)}, u32[]{:S(2)}, u32[]{:S(2)}) collective-permute-start(bf16[256,8,256]{2,0,1:T(8,128)(2,1)} %add_convert_fusion.11), channel_id=1, source_target_pairs={{8,0},{16,24},{9,1},{17,25},{10,2},{18,26},{11,3},{19,27},{12,4},{... | collective-permute-start | bytes 3145736 | tf_op jit(solution)/shard_map/ppermute | solution.py:78
  646.6 52.7 %all-to-all-start.2 = ((bf16[8,256,768]{1,2,0:T(8,128)(2,1)}), bf16[8,256,768]{1,2,0:T(8,128)(2,1)S(1)}, u32[]{:S(2)}, u32[]{:S(2)}) async-start(bf16[8,256,768]{1,2,0:T(8,128)(2,1)} %copy.172), calls=%async_computation.2 | async-start | bytes 6291456 | tf_op jit(solution)/shard_map/all_to_all | solution.py:319
  692.4 166.1 %collective-permute-start.41 = (bf16[8,256,1024]{2,1,0:T(8,128)(2,1)}, bf16[8,256,1024]{2,1,0:T(8,128)(2,1)}, u32[]{:S(2)}, u32[]{:S(2)}) collective-permute-start(bf16[8,256,1024]{2,1,0:T(8,128)(2,1)} %all-to-all-done.3), channel_id=1, source_target_pairs={{0,8},{24,16},{1,9},{25,17},{2,10},{26,18},{3,11},{27,19},{4,12},{... | collective-permute-start | bytes 12582920 | tf_op jit(solution)/shard_map/ppermute | solution.py:74
  699.3 154.1 %collective-permute-start.38 = (bf16[8,256,768]{1,2,0:T(8,128)(2,1)S(1)}, bf16[8,256,768]{1,2,0:T(8,128)(2,1)}, u32[]{:S(2)}, u32[]{:S(2)}) collective-permute-start(bf16[8,256,768]{1,2,0:T(8,128)(2,1)S(1)} %all-to-all-done.2), channel_id=1, source_target_pairs={{0,8},{24,16},{1,9},{25,17},{2,10},{26,18},{3,11},{27,19},{4,12},{... | collective-permute-start | bytes 9437192 | tf_op jit(solution)/shard_map/ppermute | solution.py:74
  743.8 151.3 %collective-permute-start.48 = (bf16[1024,8,256]{2,0,1:T(8,128)(2,1)S(1)}, bf16[1024,8,256]{2,0,1:T(8,128)(2,1)}, u32[]{:S(2)}, u32[]{:S(2)}) collective-permute-start(bf16[1024,8,256]{2,0,1:T(8,128)(2,1)S(1)} %add_convert_fusion.4), channel_id=1, source_target_pairs={{8,16},{16,8},{9,17},{17,9},{10,18},{18,10},{11,19},{19,11},{12,20... | collective-permute-start | bytes 12582920 | tf_op jit(solution)/shard_map/ppermute | solution.py:76
  856.0 45.3 %collective-permute-start.39 = (bf16[8,256,768]{1,2,0:T(8,128)(2,1)S(1)}, bf16[8,256,768]{1,2,0:T(8,128)(2,1)}, u32[]{:S(2)}, u32[]{:S(2)}) collective-permute-start(bf16[8,256,768]{1,2,0:T(8,128)(2,1)S(1)} %add_convert_fusion.8), channel_id=1, source_target_pairs={{8,16},{16,8},{9,17},{17,9},{10,18},{18,10},{11,19},{19,11},{12,20... | collective-permute-start | bytes 9437192 | tf_op jit(solution)/shard_map/ppermute | solution.py:76
  876.1 48.7 %collective-permute-start.34 = (bf16[2,256,2048]{2,1,0:T(8,128)(2,1)S(1)}, bf16[2,256,2048]{2,1,0:T(8,128)(2,1)}, u32[]{:S(2)}, u32[]{:S(2)}) collective-permute-start(bf16[2,256,2048]{2,1,0:T(8,128)(2,1)S(1)} %slice.522), channel_id=1, source_target_pairs={{0,2},{1,3},{2,0},{3,1},{4,6},{5,7},{6,4},{7,5},{8,10},{9,11},{10,... | collective-permute-start | bytes 6291464 | tf_op jit(solution)/shard_map/ppermute | solution.py:31
  889.5 78.6 %collective-permute-start.29 = (bf16[2,2048,256]{2,1,0:T(8,128)(2,1)}, bf16[2,2048,256]{2,1,0:T(8,128)(2,1)S(1)}, u32[]{:S(2)}, u32[]{:S(2)}) collective-permute-start(bf16[2,2048,256]{2,1,0:T(8,128)(2,1)} %slice.495), channel_id=1, source_target_pairs={{0,2},{1,3},{2,0},{3,1},{4,6},{5,7},{6,4},{7,5},{8,10},{9,11},{10,... | collective-permute-start | bytes 6291464 | tf_op jit(solution)/shard_map/ppermute | solution.py:31
  892.5 78.5 %collective-permute-start.36 = (bf16[2,256,2048]{2,1,0:T(8,128)(2,1)}, bf16[2,256,2048]{2,1,0:T(8,128)(2,1)}, u32[]{:S(2)}, u32[]{:S(2)}) collective-permute-start(bf16[2,256,2048]{2,1,0:T(8,128)(2,1)} %slice_bitcast_fusion.2), channel_id=1, source_target_pairs={{0,4},{1,5},{2,6},{3,7},{4,0},{5,1},{6,2},{7,3},{8,12},{9,13},{10,... | collective-permute-start | bytes 6291464 | tf_op jit(solution)/shard_map/ppermute | solution.py:31
  895.1 91.2 %collective-permute-start.31 = (bf16[2,2048,256]{2,1,0:T(8,128)(2,1)}, bf16[2,2048,256]{2,1,0:T(8,128)(2,1)}, u32[]{:S(2)}, u32[]{:S(2)}) collective-permute-start(bf16[2,2048,256]{2,1,0:T(8,128)(2,1)} %slice_bitcast_fusion.3), channel_id=1, source_target_pairs={{0,4},{1,5},{2,6},{3,7},{4,0},{5,1},{6,2},{7,3},{8,12},{9,13},{10,... | collective-permute-start | bytes 6291464 | tf_op jit(solution)/shard_map/ppermute | solution.py:31
  901.4 151.8 %collective-permute-start.42 = (bf16[8,256,1024]{2,1,0:T(8,128)(2,1)}, bf16[8,256,1024]{2,1,0:T(8,128)(2,1)}, u32[]{:S(2)}, u32[]{:S(2)}) collective-permute-start(bf16[8,256,1024]{2,1,0:T(8,128)(2,1)} %add_convert_fusion.6), channel_id=1, source_target_pairs={{8,16},{16,8},{9,17},{17,9},{10,18},{18,10},{11,19},{19,11},{12,20... | collective-permute-start | bytes 12582920 | tf_op jit(solution)/shard_map/ppermute | solution.py:76
  924.8 112.8 %collective-permute-start.40 = (bf16[8,256,768]{1,2,0:T(8,128)(2,1)}, bf16[8,256,768]{1,2,0:T(8,128)(2,1)}, u32[]{:S(2)}, u32[]{:S(2)}) collective-permute-start(bf16[8,256,768]{1,2,0:T(8,128)(2,1)} %add_convert_fusion.7), channel_id=1, source_target_pairs={{8,0},{16,24},{9,1},{17,25},{10,2},{18,26},{11,3},{19,27},{12,4},{... | collective-permute-start | bytes 9437192 | tf_op jit(solution)/shard_map/ppermute | solution.py:78
  968.2 129.9 %collective-permute-start.49 = (bf16[1024,8,256]{2,0,1:T(8,128)(2,1)}, bf16[1024,8,256]{2,0,1:T(8,128)(2,1)}, u32[]{:S(2)}, u32[]{:S(2)}) collective-permute-start(bf16[1024,8,256]{2,0,1:T(8,128)(2,1)} %add_convert_fusion.3), channel_id=1, source_target_pairs={{8,0},{16,24},{9,1},{17,25},{10,2},{18,26},{11,3},{19,27},{12,4},{... | collective-permute-start | bytes 12582920 | tf_op jit(solution)/shard_map/ppermute | solution.py:78
  971.0 37.8 %collective-permute-start.35 = (bf16[256,2048]{1,0:T(8,128)(2,1)}, bf16[256,2048]{1,0:T(8,128)(2,1)}, u32[]{:S(2)}, u32[]{:S(2)}) collective-permute-start(bf16[256,2048]{1,0:T(8,128)(2,1)} %fusion.31), channel_id=1, source_target_pairs={{0,4},{1,5},{2,6},{3,7},{4,0},{5,1},{6,2},{7,3},{8,12},{9,13},{10,... | collective-permute-start | bytes 3145736 | tf_op jit(solution)/shard_map/ppermute | solution.py:31
  986.3 43.2 %collective-permute-start.30 = (bf16[2048,256]{1,0:T(8,128)(2,1)}, bf16[2048,256]{1,0:T(8,128)(2,1)}, u32[]{:S(2)}, u32[]{:S(2)}) collective-permute-start(bf16[2048,256]{1,0:T(8,128)(2,1)} %fusion.35), channel_id=1, source_target_pairs={{0,4},{1,5},{2,6},{3,7},{4,0},{5,1},{6,2},{7,3},{8,12},{9,13},{10,... | collective-permute-start | bytes 3145736 | tf_op jit(solution)/shard_map/ppermute | solution.py:31
  1013.3 134.2 %collective-permute-start.37 = (bf16[256,2048]{1,0:T(8,128)(2,1)}, bf16[256,2048]{1,0:T(8,128)(2,1)}, u32[]{:S(2)}, u32[]{:S(2)}) collective-permute-start(bf16[256,2048]{1,0:T(8,128)(2,1)} %get-tuple-element.86), channel_id=1, source_target_pairs={{0,2},{1,3},{2,0},{3,1},{4,6},{5,7},{6,4},{7,5},{8,10},{9,11},{10,... | collective-permute-start | bytes 3145736 | tf_op jit(solution)/shard_map/ppermute | solution.py:31
  1036.5 95.8 %collective-permute-start.32 = (bf16[2048,256]{1,0:T(8,128)(2,1)}, bf16[2048,256]{1,0:T(8,128)(2,1)}, u32[]{:S(2)}, u32[]{:S(2)}) collective-permute-start(bf16[2048,256]{1,0:T(8,128)(2,1)} %get-tuple-element.88), channel_id=1, source_target_pairs={{0,2},{1,3},{2,0},{3,1},{4,6},{5,7},{6,4},{7,5},{8,10},{9,11},{10,... | collective-permute-start | bytes 3145736 | tf_op jit(solution)/shard_map/ppermute | solution.py:31
  1061.0 124.6 %collective-permute-start.43 = (bf16[8,256,1024]{2,1,0:T(8,128)(2,1)}, bf16[8,256,1024]{2,1,0:T(8,128)(2,1)}, u32[]{:S(2)}, u32[]{:S(2)}) collective-permute-start(bf16[8,256,1024]{2,1,0:T(8,128)(2,1)} %add_convert_fusion.5), channel_id=1, source_target_pairs={{8,0},{16,24},{9,1},{17,25},{10,2},{18,26},{11,3},{19,27},{12,4},{... | collective-permute-start | bytes 12582920 | tf_op jit(solution)/shard_map/ppermute | solution.py:78
  (73 other events, 1365.9 us)

commit v2 on v1

v2 whole, which is shorter than its diff:
```python
import jax
import jax.numpy as jnp
from jax import lax
from jax.experimental import pallas as pl
from jax.experimental.pallas import tpu as pltpu
from jax.sharding import PartitionSpec as P

D = 2048
HEADS = 8
HD = 256
ROT = 64
FF = 8192
BLK = 128
SEQ_MOST = 8
MB = 2
EPS = 1e-05
SCALE = HD ** (-0.5)

bf16 = jnp.bfloat16
f32 = jnp.float32

ORDER = (0, 2, 4, 6, 1, 3, 5, 7)


def dot(a, b, ca, cb):
    return lax.dot_general(a, b, (((ca,), (cb,)), ((), ())), preferred_element_type=f32)


def flip(value, bit):
    return lax.ppermute(value, "shard", [(i, i ^ bit) for i in range(8)])


def tie(*values):
    return lax.optimization_barrier(values)


def plus(a, b):
    return a.astype(f32) + b.astype(f32)


def rep_in(value):
    return lax.ppermute(value, "rep", [(0, 1), (3, 2)])


def rep_over(value):
    return lax.ppermute(value, "rep", [(1, 2), (2, 1)])


def rep_out(value):
    return lax.ppermute(value, "rep", [(1, 0), (2, 3)])


def rotary_tables():
    half = ROT // 2
    freqs = 10000.0 ** (-2.0 * jnp.arange(half, dtype=f32) / ROT)
    angles = jnp.arange(SEQ_MOST * BLK, dtype=f32)[:, None] * freqs[None, :]
    rest = 128 - ROT
    cosine = jnp.concatenate(
        [jnp.cos(angles), jnp.cos(angles), jnp.ones((SEQ_MOST * BLK, rest), f32)], axis=-1
    )
    sine = jnp.concatenate(
        [-jnp.sin(angles), jnp.sin(angles), jnp.zeros((SEQ_MOST * BLK, rest), f32)], axis=-1
    )
    return cosine.reshape(SEQ_MOST, BLK, 128), sine.reshape(SEQ_MOST, BLK, 128)


def params_of(vmem=52):
    return pltpu.CompilerParams(vmem_limit_bytes=vmem * 2**20)


def cost(us):
    return pl.CostEstimate(flops=int(us * 1.1e9) + 1024, bytes_accessed=1024, transcendentals=0)


def tick(token, *arrays):
    def body(*refs):
        refs[-1][...] = refs[0][...]

    return pl.pallas_call(
        body,
        in_specs=[pl.BlockSpec(memory_space=pltpu.VMEM)] + [pl.BlockSpec(memory_space=pl.ANY)] * len(arrays),
        out_specs=pl.BlockSpec(memory_space=pltpu.VMEM),
        out_shape=jax.ShapeDtypeStruct(token.shape, token.dtype),
        compiler_params=params_of(16), cost_estimate=cost(2000),
    )(token, *arrays)


def spec(shape, index):
    return pl.BlockSpec(shape, index)


def attention_kernel(
    piece_of, inner_of, first_of, end_of,
    qkv_ref, grad_ref, cos_ref, sin_ref,
    ctx_ref, out_ref,
    q_buf, k_buf, v_buf, g_buf, dk_buf, dv_buf,
):
    m = pl.program_id(0)
    blocks = piece_of.shape[1]
    lane = lax.broadcasted_iota(jnp.int32, (BLK, 128), 1)
    tile = 2 * BLK

    def turned(x):
        return jnp.where(lane < ROT // 2, pltpu.roll(x, 128 - ROT // 2, 1), pltpu.roll(x, ROT // 2, 1))

    def block_rows(g):
        return pl.ds(pl.multiple_of(g * BLK, BLK), BLK)

    def load(g, carry):
        p, i = piece_of[m, g], inner_of[m, g]
        at = g - first_of[m, g]
        cosine, sine = cos_ref[at], sin_ref[at]
        rows = block_rows(g)
        for buf, start in ((q_buf, 0), (k_buf, HD)):
            front = qkv_ref[p, 0, i, :, start:start + 128]
            buf[rows, 0:128] = (front * cosine + turned(front) * sine).astype(bf16)
            buf[rows, 128:HD] = qkv_ref[p, 0, i, :, start + 128:start + HD].astype(bf16)
        v_buf[rows, :] = qkv_ref[p, 0, i, :, 2 * HD:].astype(bf16)
        g_buf[rows, :] = grad_ref[p, 0, i]
        return carry

    lax.fori_loop(0, blocks, load, 0)
    for buf in (q_buf, k_buf, v_buf, g_buf):
        buf[blocks * BLK:, :] = jnp.zeros((BLK, HD), bf16)
    dk_buf[...] = jnp.zeros(dk_buf.shape, f32)
    dv_buf[...] = jnp.zeros(dv_buf.shape, f32)

    def attend(g, span):
        first = first_of[m, g]
        rows = pl.ds(pl.multiple_of(g * BLK, BLK), tile)
        keys = pl.ds(pl.multiple_of(first * BLK, BLK), span)
        query, grad = q_buf[rows, :], g_buf[rows, :]
        key, value = k_buf[keys, :], v_buf[keys, :]
        after_g = jnp.minimum(g + 1, blocks - 1)
        second = (g + 1 < blocks) & (first_of[m, after_g] == first)
        scores = dot(query, key, 1, 1) * SCALE
        key_tok = first * BLK + lax.broadcasted_iota(jnp.int32, (tile, span), 1)
        query_tok = g * BLK + lax.broadcasted_iota(jnp.int32, (tile, span), 0)
        allowed = (key_tok <= query_tok) & (key_tok < end_of[m, g])
        scores = jnp.where(allowed, scores, -jnp.inf)
        exponent = jnp.exp(scores - jnp.max(scores, axis=1, keepdims=True))
        scale = 1.0 / jnp.sum(exponent, axis=1, keepdims=True)
        last_row = jnp.where(second, tile, BLK)
        row = lax.broadcasted_iota(jnp.int32, (tile, 1), 0)
        prob = exponent * jnp.where(row < last_row, scale, 0.0)
        prob_low = prob.astype(bf16)
        ctx = dot(prob_low, value, 1, 0).astype(bf16)
        prob_grad = dot(grad, value, 1, 1)
        delta = jnp.sum(prob * prob_grad, axis=1, keepdims=True)
        score_grad = (prob * (prob_grad - delta)).astype(bf16)
        dk_buf[keys, :] += dot(score_grad, query, 0, 0)
        dv_buf[keys, :] += dot(prob_low, grad, 0, 0)
        query_grad = dot(score_grad, key, 1, 0) * SCALE

        def put(block, lo):
            p, i = piece_of[m, block], inner_of[m, block]
            at = block - first
            ctx_ref[p, 0, i] = ctx[lo:lo + BLK]
            front = query_grad[lo:lo + BLK, 0:128]
            out_ref[p, 0, i, :, 0:128] = (
                front * cos_ref[at] - turned(front) * sin_ref[at]
            ).astype(bf16)
            out_ref[p, 0, i, :, 128:HD] = query_grad[lo:lo + BLK, 128:].astype(bf16)

        put(g, 0)
        pl.when(second)(lambda: put(after_g, BLK))

    def one_block(g, carry):
        at = g - first_of[m, g]
        for count in range(SEQ_MOST // 2):
            pl.when(at == 2 * count)(lambda: attend(g, (count + 1) * tile))
        return carry

    lax.fori_loop(0, blocks, one_block, 0)

    def store(g, carry):
        p, i = piece_of[m, g], inner_of[m, g]
        at = g - first_of[m, g]
        rows = block_rows(g)
        front = dk_buf[rows, 0:128] * SCALE
        out_ref[p, 0, i, :, HD:HD + 128] = (
            front * cos_ref[at] - turned(front) * sin_ref[at]
        ).astype(bf16)
        out_ref[p, 0, i, :, HD + 128:2 * HD] = (dk_buf[rows, 128:HD] * SCALE).astype(bf16)
        out_ref[p, 0, i, :, 2 * HD:] = dv_buf[rows, :].astype(bf16)
        return carry

    lax.fori_loop(0, blocks, store, 0)


def attention(tables, qkv, grad, cosine, sine):
    pieces, _, own = qkv.shape[:3]
    blocks = tables[0].shape[1]

    def part(width):
        return pl.BlockSpec((pieces, 1, own, BLK, width), lambda m, *_: (0, m, 0, 0, 0))

    whole = pl.BlockSpec((SEQ_MOST, BLK, 128), lambda m, *_: (0, 0, 0))
    rows = (blocks + 1) * BLK
    return pl.pallas_call(
        attention_kernel,
        grid_spec=pltpu.PrefetchScalarGridSpec(
            num_scalar_prefetch=4,
            grid=(MB,),
            in_specs=[part(3 * HD), part(HD), whole, whole],
            out_specs=[part(HD), part(3 * HD)],
            scratch_shapes=[
                pltpu.VMEM((rows, HD), bf16),
                pltpu.VMEM((rows, HD), bf16),
                pltpu.VMEM((rows, HD), bf16),
                pltpu.VMEM((rows, HD), bf16),
                pltpu.VMEM((rows, HD), f32),
                pltpu.VMEM((rows, HD), f32),
            ],
        ),
        out_shape=[
            jax.ShapeDtypeStruct((pieces, MB, own, BLK, HD), bf16),
            jax.ShapeDtypeStruct((pieces, MB, own, BLK, 3 * HD), bf16),
        ],
        compiler_params=params_of(),
        cost_estimate=cost(0),
    )(*tables, qkv, grad, cosine, sine)


def plus_low(a, b, index=None):
    shape = a.shape if index is None else a.shape[1:]
    if index is None:
        a, b, index = a[None], b[None], 0
    a, b = [x.reshape(x.shape[0], -1, x.shape[-1]) for x in (a, b)]
    rows, cols = a.shape[1:]
    block = spec((1, rows // 4, cols), lambda i: (index, i, 0))

    def body(a_ref, b_ref, out_ref):
        out_ref[...] = plus(a_ref[0], b_ref[0]).astype(bf16)

    return pl.pallas_call(
        body, grid=(4,), in_specs=[block, block],
        out_specs=spec((rows // 4, cols), lambda i: (i, 0)),
        out_shape=jax.ShapeDtypeStruct((rows, cols), bf16),
        compiler_params=params_of(32), cost_estimate=cost(0),
    )(a, b).reshape(shape)


def out_terms(owners, place, context, active, out_w, down_w, resid, came=None):
    rows, inner = active.shape
    n = resid.shape[0]
    cols = D // 8
    first = 4 if came is None else 0

    def terms(place_ref, refs):
        ctx, act = refs[0][...], refs[1][...]
        own = pl.program_id(0) == place_ref[0]
        return [
            dot(ctx, refs[2 + b][...], 1, 0)
            + dot(act, refs[6 + b][...], 1, 0)
            + jnp.where(own, refs[10 + b][...].astype(f32), 0.0)
            for b in range(4)
        ]

    def odd_body(owners_ref, place_ref, *refs):
        for b, part in enumerate(terms(place_ref, refs)):
            refs[14][b] = part.astype(bf16)

    def even_body(owners_ref, place_ref, *refs):
        got, send_one, keep_one, send_two, keep_two = refs[14:]
        parts = [(p + got[b].astype(f32)).astype(bf16) for b, p in enumerate(terms(place_ref, refs))]

        @pl.when(pl.program_id(0) < 4)
        def _():
            send_one[0], send_one[1] = parts[1], parts[3]
            keep_one[0], keep_one[1] = parts[0], parts[2]

        @pl.when(pl.program_id(0) >= 4)
        def _():
            send_two[0], send_two[1] = parts[2], parts[3]
            keep_two[0], keep_two[1] = parts[0], parts[1]

    def columns(height, b):
        return spec((height, cols), lambda i, o, p: (0, o[first + b]))

    in_specs = [
        spec((n, context.shape[1]), lambda i, o, p: (i, 0)),
        spec((n, inner), lambda i, o, p: (i, 0)),
        *[columns(context.shape[1], b) for b in range(4)],
        *[columns(inner, b) for b in range(4)],
        *[columns(n, b) for b in range(4)],
    ]
    args = [context, active, *[out_w] * 4, *[down_w] * 4, *[resid] * 4]
    if came is None:
        body = odd_body
        out_specs = spec((4, n, cols), lambda i, o, p: (0, i, 0))
        out_shape = jax.ShapeDtypeStruct((4, rows, cols), bf16)
    else:
        body = even_body
        in_specs.append(spec((4, n, cols), lambda i, o, p: (0, i, 0)))
        args.append(came)
        low = spec((2, n, cols), lambda i, o, p: (0, jnp.minimum(i, 3), 0))
        high = spec((2, n, cols), lambda i, o, p: (0, jnp.maximum(i - 4, 0), 0))
        out_specs = [low, low, high, high]
        out_shape = [jax.ShapeDtypeStruct((2, rows // 2, cols), bf16)] * 4
    return pl.pallas_call(
        body,
        grid_spec=pltpu.PrefetchScalarGridSpec(
            num_scalar_prefetch=2, grid=(8,), in_specs=in_specs, out_specs=out_specs
        ),
        out_shape=out_shape, compiler_params=params_of(), cost_estimate=cost(0),
    )(owners, place.reshape(1), *args)


def norm_terms(owners, mixed_grad, hidden_grad, qkv_w, up_w, came=None):
    rows = mixed_grad.shape[0]
    n = rows // 16
    first = 4 if came is None else 0

    def terms(refs):
        one, two, w_one, w_two = refs
        return dot(one[...], w_one[...], 1, 1) + dot(two[...], w_two[...], 1, 1)

    def odd_body(owners_ref, *refs):
        refs[4][0, 0] = terms(refs[:4]).astype(bf16)

    def even_body(owners_ref, *refs):
        got, send_one, keep_one, send_two, keep_two = refs[4:]
        sums = (terms(refs[:4]) + got[0, 0].astype(f32)).astype(bf16)
        i = pl.program_id(0)
        for ref, steps in (
            (keep_one, (0, 4)), (send_one, (2, 6)), (keep_two, (1, 3)), (send_two, (5, 7)),
        ):
            @pl.when((i == steps[0]) | (i == steps[1]))
            def _():
                ref[0] = sums

    def own_rows(i, o):
        return (o[first + i // 2] * 2 + i % 2, 0)

    in_specs = [
        spec((n, mixed_grad.shape[1]), own_rows),
        spec((n, hidden_grad.shape[1]), own_rows),
        spec(qkv_w.shape, lambda i, o: (0, 0)),
        spec(up_w.shape, lambda i, o: (0, 0)),
    ]
    args = [mixed_grad, hidden_grad, qkv_w, up_w]
    if came is None:
        body = odd_body
        out_specs = spec((1, 1, n, D), lambda i, o: (i // 2, i % 2, 0, 0))
        out_shape = jax.ShapeDtypeStruct((4, 2, n, D), bf16)
    else:
        body = even_body
        in_specs.append(spec((1, 1, n, D), lambda i, o: (i // 2, i % 2, 0, 0)))
        args.append(came)
        out_specs = [
            spec((1, n, D), lambda i, o: (i // 4, 0, 0)),
            spec((1, n, D), lambda i, o: (i // 4, 0, 0)),
            spec((1, n, D), lambda i, o: (jnp.maximum(i - 4, 0) // 2, 0, 0)),
            spec((1, n, D), lambda i, o: (jnp.minimum(i // 2, 1), 0, 0)),
        ]
        out_shape = [jax.ShapeDtypeStruct((2, n, D), bf16)] * 4
    return pl.pallas_call(
        body,
        grid_spec=pltpu.PrefetchScalarGridSpec(
            num_scalar_prefetch=1, grid=(8,), in_specs=in_specs, out_specs=out_specs
        ),
        out_shape=out_shape, compiler_params=params_of(), cost_estimate=cost(0),
    )(owners, *args)


def token_dot(left, right, part=0, parts=1):
    rows, width = left.shape[0], left.shape[1] // parts
    blocks, _, cols = right.shape
    step = 512 // cols

    def body(left_ref, right_ref, out_ref):
        for b in range(step):
            out_ref[:, b * cols:(b + 1) * cols] = dot(left_ref[...], right_ref[b], 0, 0).astype(bf16)

    return pl.pallas_call(
        body, grid=(blocks // step,),
        in_specs=[
            spec((rows, width), lambda i: (0, part)),
            spec((step, rows, cols), lambda i: (i, 0, 0)),
        ],
        out_specs=spec((width, step * cols), lambda i: (0, i)),
        out_shape=jax.ShapeDtypeStruct((width, blocks * cols), bf16),
        compiler_params=params_of(56), cost_estimate=cost(0),
    )(left, right)


def normed_dot(normed, right, sums=False, part=0, parts=1):
    rows, tile = normed.shape[0], 512

    def body(left_ref, right_ref, out_ref, *rest):
        out_ref[...] = dot(left_ref[...], right_ref[...], 0, 0).astype(bf16)
        if sums:
            @pl.when(pl.program_id(0) == 0)
            def _():
                rest[0][...] = jnp.sum(right_ref[...].astype(f32), axis=0, keepdims=True)

    width = right.shape[1] // parts
    out_specs = [spec((tile, width), lambda i: (i, 0))]
    out_shape = [jax.ShapeDtypeStruct((D, width), bf16)]
    if sums:
        out_specs.append(spec((1, width), lambda i: (0, 0)))
        out_shape.append(jax.ShapeDtypeStruct((1, width), f32))
    found = pl.pallas_call(
        body, grid=(D // tile,),
        in_specs=[spec((rows, tile), lambda i: (0, i)), spec((rows, width), lambda i: (0, part))],
        out_specs=out_specs, out_shape=out_shape,
        compiler_params=params_of(56), cost_estimate=cost(0),
    )(normed, right)
    return found if sums else found[0]


def whole_rows(ref):
    return jnp.concatenate([ref[b] for b in range(ref.shape[0])], axis=1)


def hidden_back(grad_out, down_w, slope):
    rows, wide = slope.shape
    n = rows // 8

    def body(grad_ref, w_ref, slope_ref, out_ref, sum_ref):
        active_grad = dot(whole_rows(grad_ref), w_ref[...], 1, 1).astype(bf16).astype(f32)
        value = (active_grad * slope_ref[...]).astype(bf16)
        out_ref[...] = value
        total = jnp.sum(value.astype(f32), axis=0, keepdims=True)

        @pl.when(pl.program_id(0) == 0)
        def _():
            sum_ref[...] = total

        @pl.when(pl.program_id(0) > 0)
        def _():
            sum_ref[...] += total

    return pl.pallas_call(
        body, grid=(8,),
        in_specs=[
            spec((grad_out.shape[0], n, grad_out.shape[2]), lambda i: (0, i, 0)),
            spec((wide, D), lambda i: (0, 0)),
            spec((n, wide), lambda i: (i, 0)),
        ],
        out_specs=[spec((n, wide), lambda i: (i, 0)), spec((1, wide), lambda i: (0, 0))],
        out_shape=[
            jax.ShapeDtypeStruct((rows, wide), bf16), jax.ShapeDtypeStruct((1, wide), f32),
        ],
        compiler_params=params_of(), cost_estimate=cost(0),
    )(grad_out, down_w, slope)


def head_back(grad_out, out_w):
    blocks, rows, cols = grad_out.shape
    n = rows // 8

    def body(grad_ref, w_ref, out_ref):
        out_ref[...] = dot(whole_rows(grad_ref), w_ref[...], 1, 1).astype(bf16)

    return pl.pallas_call(
        body, grid=(8,),
        in_specs=[
            spec((blocks, n, cols), lambda i: (0, i, 0)),
            spec((HD, D), lambda i: (0, 0)),
        ],
        out_specs=spec((n, HD), lambda i: (i, 0)),
        out_shape=jax.ShapeDtypeStruct((rows, HD), bf16),
        compiler_params=params_of(), cost_estimate=cost(0),
    )(grad_out, out_w)


def row_grads(inner, chunks):
    rows = [c[0].shape[0] for c in chunks]
    total, cols = sum(rows), 512

    def body(inner_ref, *refs):
        at = 0
        for c, n in enumerate(rows):
            one, two = refs[2 * c][...].astype(f32), refs[2 * c + 1][...].astype(f32)
            refs[-1][at:at + n, :] = jnp.where(inner_ref[0] == 1, one, two)
            at += n

    return pl.pallas_call(
        body,
        grid_spec=pltpu.PrefetchScalarGridSpec(
            num_scalar_prefetch=1, grid=(D // cols,),
            in_specs=[spec((n, cols), lambda i, *_: (0, i)) for n in rows for _ in range(2)],
            out_specs=spec((total, cols), lambda i, *_: (0, i)),
        ),
        out_shape=jax.ShapeDtypeStruct((total, D), f32),
        compiler_params=params_of(32), cost_estimate=cost(0),
    )(inner, *[a for c in chunks for a in c])


def column_grads(inner, chunks, weight, gain, shift, totals, run, step, by_run, token=None):
    rows, each = weight.shape[0], len(chunks[0])
    if by_run:
        groups, per = len(chunks), chunks[0][0].shape[0] // step
        steps = per
    else:
        groups, per = chunks[0][0].shape[2] // run, chunks[0][0].shape[0] // step
        steps = per * len(chunks)

    tokens = [] if token is None else [token]

    def body(inner_ref, *refs):
        pairs, refs = refs[:each * len(chunks)], refs[each * len(chunks) + len(tokens):]
        w_ref, t_ref, gain_ref, shift_ref, grads, gain_out, shift_out = refs[-7:]
        i, k = pl.program_id(0), pl.program_id(1)

        @pl.when((i == 0) & (k == 0))
        def _():
            gain_out[...] = jnp.zeros_like(gain_out)
            shift_out[...] = jnp.zeros_like(shift_out)

        for c in range(len(chunks)):
            @pl.when((k if by_run else i // per) == c)
            def _():
                for j in range(step):
                    value = pairs[each * c][j].astype(f32)
                    if each == 2:
                        other = pairs[2 * c + 1][j].astype(f32)
                        value = jnp.where(inner_ref[0] == 1, value, other)
                    at = slice(j * run, (j + 1) * run)
                    w, t = w_ref[:, at].astype(f32), t_ref[:, at]
                    grads[:, at] = gain_ref[...] * value + shift_ref[...] * t
                    for out, terms in ((gain_out, w * value), (shift_out, w * t)):
                        out[...] += sum(terms[:, lo:lo + 128] for lo in range(0, run, 128))

    def part_index(c):
        if by_run:
            return lambda i, k, *_: (i, 0, 0)
        return lambda i, k, *_: (jnp.clip(i - c * per, 0, per - 1), 0, k)

    def columns(i, k, *_):
        return (0, i * groups + k if by_run else k * steps + i)

    column = spec((rows, 1), lambda i, k, *_: (0, 0))
    wide_column = spec((rows, 128), lambda i, k, *_: (0, 0))
    grads, gain_grad, shift_grad = pl.pallas_call(
        body,
        grid_spec=pltpu.PrefetchScalarGridSpec(
            num_scalar_prefetch=1, grid=(steps, groups),
            in_specs=[spec((step, rows, run), part_index(c)) for c in range(len(chunks)) for _ in range(each)]
            + [pl.BlockSpec(memory_space=pl.ANY)] * len(tokens)
            + [spec((rows, step * run), columns), spec((1, step * run), columns), column, column],
            out_specs=[spec((rows, step * run), columns), wide_column, wide_column],
        ),
        out_shape=[
            jax.ShapeDtypeStruct(weight.shape, f32),
            jax.ShapeDtypeStruct((rows, 128), f32),
            jax.ShapeDtypeStruct((rows, 128), f32),
        ],
        compiler_params=params_of(32), cost_estimate=cost(0),
    )(
        inner, *[a for c in chunks for a in c], *tokens, weight, totals[None],
        gain.astype(f32)[:, None], shift.astype(f32)[:, None],
    )
    return grads, jnp.sum(gain_grad, axis=1), jnp.sum(shift_grad, axis=1)


def local(
    tokens, cotangent, seq_blocks, seq_pad, deal_order,
    ln1_gain, ln1_bias, ln2_gain, ln2_bias,
    qkv_weight, qkv_bias, out_weight, out_bias, up_weight, up_bias, down_weight, down_bias,
):
    shards = lax.axis_size("shard")
    place = lax.axis_index("shard")
    cube = shards == 8 and lax.axis_size("rep") == 4
    own = tokens.shape[1]
    blocks = deal_order.shape[2]
    own_rows = MB * own * BLK
    rows = shards * own_rows
    cols = D // shards
    wide = FF // shards
    split = shards // HEADS
    head, share = place // split, place % split
    share_cols = 3 * HD // split

    if cube:
        owners = jnp.bitwise_xor(place, jnp.array(ORDER, jnp.int32))
    deal = deal_order[:, 0, :]
    counts = seq_blocks[:, 0, :]
    pads = seq_pad[:, 0, :]
    ids = jnp.arange(blocks, dtype=jnp.int32)
    inverse = jnp.sum(
        jnp.where(deal[:, None, :] == ids[None, :, None], ids[None, None, :], 0), axis=-1
    )
    piece_of, inner_of = inverse // own, inverse % own
    ends = jnp.cumsum(counts, axis=1)
    starts = ends - counts
    inside = (ids[None, :, None] >= starts[:, None, :]) & (ids[None, :, None] < ends[:, None, :])
    first_of = jnp.sum(jnp.where(inside, starts[:, None, :], 0), axis=-1)
    valid = jnp.sum(jnp.where(inside, (counts * BLK - pads)[:, None, :], 0), axis=-1)
    tables = [t.astype(jnp.int32) for t in (piece_of, inner_of, first_of, first_of * BLK + valid)]
    given = deal.reshape(MB, shards, own)

    cot_own = jnp.stack([cotangent[m][given[m]] for m in range(MB)], axis=1)

    def swap(value):
        return lax.all_to_all(value, "shard", split_axis=0, concat_axis=0, tiled=True)

    token = jnp.zeros((8, 128), f32)

    def gate(*arrays):
        nonlocal token
        if cube:
            token = tick(token, *arrays)

    def late(value):
        nonlocal token
        if cube:
            value, token = tie(value, token)
        return value

    flat = tokens.reshape(own_rows, D).astype(f32)
    center = flat - jnp.mean(flat, axis=-1, keepdims=True)
    inv_std = lax.rsqrt(jnp.mean(center * center, axis=-1, keepdims=True) + EPS)
    normed_own = center * inv_std
    normed_low = normed_own.astype(bf16)
    normed = lax.all_gather(normed_low, "shard", axis=0, tiled=True)
    gate(normed_low)

    shares = lax.axis_size("rep") if cube else 1
    part_rows = cols // shares
    spot = lax.axis_index("rep") if cube else 0
    up_late, qkv_late = late((up_weight, qkv_weight))

    def part_of(array):
        return lax.dynamic_slice_in_dim(array, spot * part_rows, part_rows, 0).astype(f32)

    def with_shift(weight, gain, shift):
        high = lax.reduce_precision(shift, 8, 7)
        low = lax.reduce_precision(shift - high, 8, 7)
        tail = jnp.zeros((14, shift.shape[0]), bf16)
        scaled = (part_of(weight) * part_of(gain)[:, None]).astype(bf16)
        return jnp.concatenate([scaled, high.astype(bf16)[None], low.astype(bf16)[None], tail], axis=0)

    shift_up = jnp.sum(up_late.astype(f32) * ln2_bias.astype(f32)[:, None], axis=0)
    shift_qkv = jnp.sum(qkv_late.astype(f32) * ln1_bias.astype(f32)[:, None], axis=0)
    own_bias = lax.dynamic_slice_in_dim(shift_qkv, place * 3 * cols, 3 * cols) + qkv_bias.astype(f32)
    shift_qkv = lax.dynamic_update_slice_in_dim(shift_qkv, own_bias, place * 3 * cols, 0)
    sent_rows = part_rows + 16
    up_send = with_shift(up_late, ln2_gain, shift_up).reshape(sent_rows, shards, wide).transpose(1, 0, 2)
    qkv_send = with_shift(qkv_late, ln1_gain, shift_qkv).reshape(sent_rows, 3, HEADS, HD)
    qkv_send = qkv_send.transpose(2, 0, 1, 3).reshape(HEADS, sent_rows, 3 * HD)
    if split > 1:
        qkv_send = jnp.repeat(qkv_send, split, axis=0)
    found = swap(jnp.concatenate([up_send, qkv_send], axis=2))
    cot_late = late(cot_own)
    grad_out = lax.all_gather(cot_late.reshape(rows, cols), "shard", axis=0)
    gate(up_send, qkv_send, cot_late)
    found = late(found)
    biases = jnp.sum(found[:, part_rows:part_rows + 2].astype(f32), axis=(0, 1))
    bias_up, bias_qkv = biases[:wide] + up_bias.astype(f32), biases[wide:]

    def exchange(part):
        return [part] + [
            lax.ppermute(part, "rep", [(i, (i + k) % shares) for i in range(shares)])
            for k in range(1, shares)
        ]

    def whole(parts):
        if shares == 1:
            return parts[0].reshape(D, parts[0].shape[-1])
        width = parts[0].shape[-1]
        array = jnp.zeros((shards, shares, part_rows, width), bf16)
        for k, part in enumerate(parts):
            at = lax.rem(spot - k + shares, shares)
            array = lax.dynamic_update_slice(array, part[:, None], (0, at, 0, 0))
        return array.reshape(D, width)

    up_parts = exchange(found[:, :part_rows, :wide])
    gate(up_parts[0], biases)
    qkv_parts = exchange(late(found)[:, :part_rows, wide:])
    normed, up_parts = late((normed, up_parts))
    up_w = whole(up_parts)
    out_w, down_w, resid = out_weight, down_weight, tokens.reshape(own_rows, D)

    hidden = dot(normed, up_w, 1, 0) + bias_up
    cdf = 0.5 + 0.5 * lax.erf(hidden * (0.5 ** 0.5))
    density = jnp.exp(-0.5 * hidden * hidden) * 0.3989422804014327
    active = (hidden * cdf).astype(bf16)
    slope = cdf + hidden * density
    grad_out, active = tie(grad_out, active)

    def spread(grads):
        return swap(grads.reshape(shards, cols, grads.shape[-1]))

    down_parts = [token_dot(active, grad_out, 0, 2)]
    down_came = [rep_in(down_parts[0])]
    gate(down_parts[0])
    down_parts.append(token_dot(late(active), grad_out, 1, 2))
    grad_out, down_parts[1] = tie(grad_out, down_parts[1])
    hidden_grad, sum_hidden = hidden_back(grad_out, down_w, slope)
    up_terms = [normed_dot(normed, hidden_grad, False, 0, 2)]
    up_found = [spread(up_terms[0])]
    down_came[0], up_terms[0] = tie(down_came[0], up_terms[0])
    down_pair = [plus_low(down_parts[0], down_came[0])]
    down_other = [rep_over(down_pair[0])]
    down_came.append(rep_in(down_parts[1]))
    gate(down_pair[0], up_terms[0])

    context_w = out_w
    if split > 1:
        pairs = [list(range(h * split, (h + 1) * split)) for h in range(HEADS)]
        context_w = lax.all_gather(out_w, "shard", axis=0, tiled=True, axis_index_groups=pairs)
    up_terms.append(normed_dot(late(normed), hidden_grad, False, 1, 2))
    grad_out, up_terms[1] = tie(grad_out, up_terms[1])
    context_grad = head_back(grad_out, context_w)
    qkv_parts, context_grad = tie(qkv_parts, context_grad)
    qkv_w = whole(qkv_parts)
    mixed = dot(normed, qkv_w, 1, 0) + bias_qkv
    down_other[0], down_came[1], up_found[0], mixed = tie(down_other[0], down_came[1], up_found[0], mixed)
    down_total = [plus_low(down_pair[0], down_other[0])]
    down_back = [rep_out(down_total[0])]
    down_pair.append(plus_low(down_parts[1], down_came[1]))
    down_other.append(rep_over(down_pair[1]))
    up_came = [rep_in(up_found[0])]
    up_terms[1], up_found[0] = tie(up_terms[1], up_found[0])
    up_found.append(spread(up_terms[1]))
    gate(down_total[0], down_pair[1], up_found[0])
    cosine, sine = rotary_tables()
    context, mixed_grad = attention(
        tables,
        late(mixed).reshape(shards, MB, own, BLK, 3 * HD),
        context_grad.reshape(shards, MB, own, BLK, HD),
        cosine,
        sine,
    )
    context = context.reshape(rows, HD)
    mixed_grad = mixed_grad.reshape(rows, 3 * HD)
    down_back[0], down_other[1], up_came[0], up_found[1], context = tie(
        down_back[0], down_other[1], up_came[0], up_found[1], context
    )
    down_total.append(plus_low(down_pair[1], down_other[1]))
    down_back.append(rep_out(down_total[1]))
    up_pair = [plus_low(up_found[0], up_came[0])]
    up_other = [rep_over(up_pair[0])]
    up_came.append(rep_in(up_found[1]))
    gate(down_back[0], down_total[1], up_pair[0], up_found[1])
    mixed_grad = late(mixed_grad)
    if split > 1:
        context = lax.dynamic_slice_in_dim(context, share * (HD // split), HD // split, 1)
        mixed_grad = lax.dynamic_slice_in_dim(mixed_grad, share * share_cols, share_cols, 1)
        qkv_w = lax.dynamic_slice_in_dim(qkv_w, share * share_cols, share_cols, 1)
    qkv_terms, sum_mixed = normed_dot(normed, mixed_grad, True)
    qkv_found = spread(qkv_terms)
    sum_cot = jnp.sum(cot_own, axis=tuple(range(cot_own.ndim - 1)), dtype=f32)
    small = jnp.concatenate([sum_mixed[0], sum_hidden[0], sum_cot])

    def bias_grads(small):
        sum_qkv = small[:, :share_cols].reshape(HEADS, 3, HD).transpose(1, 0, 2).reshape(3 * D)
        sum_up = small[:, share_cols:share_cols + wide].reshape(FF)
        out_bias_grad = lax.dynamic_index_in_dim(small[:, share_cols + wide:], place, 0, keepdims=False)
        qkv_bias_grad = lax.dynamic_slice_in_dim(sum_qkv, place * 3 * cols, 3 * cols)
        up_bias_grad = lax.dynamic_slice_in_dim(sum_up, place * wide, wide)
        return sum_qkv, sum_up, out_bias_grad, qkv_bias_grad, up_bias_grad

    if cube:
        small_came = lax.ppermute(small, "rep", [(i, i ^ 1) for i in range(4)])
        context, qkv_terms = tie(context, qkv_terms)
        out_part = token_dot(context, grad_out)
        out_came = rep_in(out_part)

        context, out_part = tie(context, out_part)
        odd = out_terms(owners, place, context, active, out_w, down_w, resid)
        odd_came = flip(odd, 1)
        down_back[1], up_other[0], up_came[1], odd = tie(down_back[1], up_other[0], up_came[1], odd)
        up_total = [plus_low(up_pair[0], up_other[0])]
        up_back = [rep_out(up_total[0])]
        up_pair.append(plus_low(up_found[1], up_came[1]))
        up_other.append(rep_over(up_pair[1]))
        gate(down_back[1], up_total[0], up_pair[1], small, qkv_terms, odd)

        norm_odd = norm_terms(owners, late(mixed_grad), hidden_grad, qkv_w, up_w)
        norm_odd_came = flip(norm_odd, 1)
        odd_came, norm_odd = tie(odd_came, norm_odd)
        send_one, keep_one, send_two, keep_two = out_terms(
            owners, place, context, active, out_w, down_w, resid, odd_came
        )
        got_one, got_two = flip(send_one, 2), flip(send_two, 4)
        up_back[0], up_other[1], out_came, qkv_found, keep_one = tie(
            up_back[0], up_other[1], out_came, qkv_found, keep_one
        )
        up_total.append(plus_low(up_pair[1], up_other[1]))
        up_back.append(rep_out(up_total[1]))
        out_pair = plus_low(out_part, out_came)
        out_other = rep_over(out_pair)
        qkv_parts = [qkv_found[:shards // 2], qkv_found[shards // 2:]]
        qkv_came = [rep_in(part) for part in qkv_parts]
        gate(up_back[0], up_total[1], out_pair, *qkv_parts, norm_odd, send_one)

        norm_send_one, norm_keep_one, norm_send_two, norm_keep_two = norm_terms(
            owners, mixed_grad, hidden_grad, qkv_w, up_w, late(norm_odd_came)
        )
        norm_got_one, norm_got_two = flip(norm_send_one, 2), flip(norm_send_two, 4)

        out_other, qkv_came[0], norm_keep_one = tie(out_other, qkv_came[0], norm_keep_one)
        out_total = plus_low(out_pair, out_other)
        out_back = rep_out(out_total)
        qkv_pair = [plus_low(qkv_parts[0], qkv_came[0])]
        qkv_other = [rep_over(qkv_pair[0])]
        got_one, got_two, up_back[1], out_total, qkv_pair[0] = tie(
            got_one, got_two, up_back[1], out_total, qkv_pair[0]
        )
        last_one = plus_low(keep_one, got_one, 1)
        last_two = plus_low(keep_two, got_two, 1)
        qkv_came[1], last_one, last_two, up_back[1] = tie(qkv_came[1], last_one, last_two, up_back[1])
        last_one, last_two = flip(last_one, 4), flip(last_two, 2)
        qkv_pair.append(plus_low(qkv_parts[1], qkv_came[1]))
        qkv_other.append(rep_over(qkv_pair[1]))
        down_late, small_came, qkv_pair[1] = tie(
            list(zip(down_total, down_back)), small_came, qkv_pair[1]
        )
        inner = ((spot == 1) | (spot == 2)).astype(jnp.int32).reshape(1)
        down_grad = row_grads(inner, down_late)
        small_pair = small + small_came
        small_other = lax.ppermute(small_pair, "rep", [(i, i ^ 2) for i in range(4)])
        qkv_other[0], out_back, down_grad, small_pair = tie(qkv_other[0], out_back, down_grad, small_pair)
        qkv_total = [plus_low(qkv_pair[0], qkv_other[0])]
        qkv_back = [rep_out(qkv_total[0])]
        out_back, grad_late, qkv_total[0] = tie(out_back, grad_out, qkv_total[0])
        out_grad = row_grads(inner, [(out_total, out_back)])
        grad_rows = lax.dynamic_slice_in_dim(grad_late, place * own_rows, own_rows, 1)
        grad_rows = grad_rows.transpose(1, 0, 2).reshape(own_rows, D)
        norm_got_one, norm_got_two, out_grad, grad_rows = tie(
            norm_got_one, norm_got_two, out_grad, grad_rows
        )
        norm_last_one = plus_low(norm_keep_one, norm_got_one, 1)
        norm_last_two = plus_low(norm_keep_two, norm_got_two, 1)
        qkv_other[1], small_other, norm_last_one, norm_last_two = tie(
            qkv_other[1], small_other, norm_last_one, norm_last_two
        )
        norm_last_one, norm_last_two = flip(norm_last_one, 4), flip(norm_last_two, 2)
        qkv_total.append(plus_low(qkv_pair[1], qkv_other[1]))
        qkv_back.append(rep_out(qkv_total[1]))
        small_pair = small_pair + small_other
        small = swap(jnp.broadcast_to(small_pair[None], (shards,) + small_pair.shape))
        last_one, last_two, qkv_total[1], small_pair = tie(last_one, last_two, qkv_total[1], small_pair)
        out_own = jnp.concatenate(
            [
                plus(keep_one[0], got_one[0]) + last_one.astype(f32),
                plus(keep_two[0], got_two[0]) + last_two.astype(f32),
            ],
            axis=0,
        )
        norm_last_one, norm_last_two, qkv_back[0], out_own = tie(
            norm_last_one, norm_last_two, qkv_back[0], out_own
        )
        normed_grad = jnp.concatenate(
            [
                plus(norm_keep_one[0], norm_got_one[0]) + norm_last_one.astype(f32),
                plus(norm_keep_two[0], norm_got_two[0]) + norm_last_two.astype(f32),
            ],
            axis=0,
        )
    else:
        small = lax.all_gather(lax.psum(small, "rep"), "shard")
        sum_qkv, sum_up, out_bias_grad, qkv_bias_grad, up_bias_grad = bias_grads(small)
        out_sum, qkv_sum, up_sum, down_sum = lax.psum(
            (token_dot(context, grad_out), qkv_found, jnp.concatenate(up_found, axis=2), jnp.concatenate(down_parts)), "rep"
        )
        terms = dot(context, out_w, 1, 0) + dot(active, down_w, 1, 0)
        terms = lax.dynamic_update_slice_in_dim(
            terms,
            lax.dynamic_slice_in_dim(terms, place * own_rows, own_rows, 0) + resid.astype(f32),
            place * own_rows,
            0,
        )
        out_own = lax.psum_scatter(terms.astype(bf16), "shard", scatter_dimension=1, tiled=True)
        out_own = out_own.astype(f32)
        terms = dot(mixed_grad, qkv_w, 1, 1) + dot(hidden_grad, up_w, 1, 1)
        normed_grad = lax.psum_scatter(terms.astype(bf16), "shard", scatter_dimension=0, tiled=True)
        normed_grad = normed_grad.astype(f32)
        grad_rows = lax.dynamic_slice_in_dim(grad_out, place * own_rows, own_rows, 1)
        grad_rows = grad_rows.transpose(1, 0, 2).reshape(own_rows, D)

    out_own = out_own + (out_bias.astype(f32) + down_bias.astype(f32))
    out_own = out_own.astype(bf16).reshape(shards, MB, own, BLK, cols)
    out_given = jnp.stack([out_own[piece_of[m], m, inner_of[m]] for m in range(MB)])

    mean_grad = jnp.mean(normed_grad, axis=-1, keepdims=True)
    mean_proj = jnp.mean(normed_grad * normed_own, axis=-1, keepdims=True)
    tokens_grad = inv_std * (normed_grad - mean_grad - normed_own * mean_proj)
    tokens_grad = grad_rows.astype(f32) + tokens_grad
    tokens_grad = tokens_grad.astype(bf16).reshape(MB, own, BLK, D)

    if cube:
        small, tokens_grad = tie(small, tokens_grad)
        sum_qkv, sum_up, out_bias_grad, qkv_bias_grad, up_bias_grad = bias_grads(small)
        up_grad, gain_two_grad, shift_two_grad = column_grads(
            inner, list(zip(up_total, up_back)), up_weight, ln2_gain, ln2_bias, sum_up, wide // 2, 1, True
        )
        qkv_back, up_grad = tie(qkv_back, up_grad)
        qkv_grad, gain_one_grad, shift_one_grad = column_grads(
            inner, list(zip(qkv_total, qkv_back)), qkv_weight, ln1_gain, ln1_bias, sum_qkv, HD, 2, False, token
        )
    else:
        def finish(sums, weight, gain, shift, total):
            sums = sums.astype(f32)
            grads = gain.astype(f32)[:, None] * sums + shift.astype(f32)[:, None] * total
            weight = weight.astype(f32)
            return grads, jnp.sum(weight * sums, axis=1), jnp.sum(weight * total, axis=1)

        qkv_rows = qkv_sum.reshape(HEADS, split, cols, share_cols).transpose(2, 0, 1, 3)
        qkv_rows = qkv_rows.reshape(cols, HEADS, 3, HD).transpose(0, 2, 1, 3).reshape(cols, 3 * D)
        up_rows = up_sum.transpose(1, 0, 2).reshape(cols, FF)
        qkv_grad, gain_one_grad, shift_one_grad = finish(
            qkv_rows, qkv_weight, ln1_gain, ln1_bias, sum_qkv
        )
        out_grad = out_sum.astype(f32)
        down_grad = down_sum.astype(f32)
        up_grad, gain_two_grad, shift_two_grad = finish(
            up_rows, up_weight, ln2_gain, ln2_bias, sum_up
        )

    return (
        out_given,
        tokens_grad,
        gain_one_grad.reshape(cols),
        shift_one_grad.reshape(cols),
        gain_two_grad.reshape(cols),
        shift_two_grad.reshape(cols),
        qkv_grad,
        qkv_bias_grad,
        out_grad,
        out_bias_grad,
        up_grad,
        up_bias_grad,
        down_grad,
        out_bias_grad,
    )


def solution(mesh):
    in_specs = (
        P(None, ("rep", "shard"), None, None),
        P(None, "rep", None, "shard"),
        P(None, "rep", None),
        P(None, "rep", None),
        P(None, "rep", None),
        P("shard"),
        P("shard"),
        P("shard"),
        P("shard"),
        P("shard", None),
        P("shard"),
        P("shard", None),
        P("shard"),
        P("shard", None),
        P("shard"),
        P("shard", None),
        P("shard"),
    )
    out_specs = (
        P(None, "rep", None, "shard"),
        P(None, ("rep", "shard"), None, None),
        P("shard"),
        P("shard"),
        P("shard"),
        P("shard"),
        P("shard", None),
        P("shard"),
        P("shard", None),
        P("shard"),
        P("shard", None),
        P("shard"),
        P("shard", None),
        P("shard"),
    )
    return jax.shard_map(local, mesh=mesh, in_specs=in_specs, out_specs=out_specs, check_vma=False)
```

time: 1230 us -> 842 us (0.68)
  Pallas kernels: 53.4 us -> 336 us
  matrix products: 239 us -> 46.4 us
  local copies, waits for them, and re-layouts: 246 us -> 65 us
  waiting for transfers between devices: 345 us -> 183 us
  other arithmetic: 168 us -> 49.8 us
  blocking collectives: 92.3 us -> 0 us
  starting transfers between devices: 76.8 us -> 133 us
  between operations: 2.42 us -> 16 us
    pallas_call x0 -> x43, Pallas kernels: none -> 299 us  [the longest x18 58.7 us: plus_low(): pl.pallas_call(body, grid=(4,), in_specs=[block, block], out_specs=spec((...]
    ppermute x38 -> x10, waiting for transfers between devices: 168 us -> 1.26 us  [flip(): return lax.ppermute(value, 'shard', [(i, i ^ bit) for i in range(8)])]
    dot_general x6 -> x0, matrix products: 110 us -> none  [the longest x2 37.1 us: out_terms(): lax.dot_general(both, both_w[:, lo:hi], (((1,), (0,)), ((), ())), preferr...]
    all_gather x3 -> x0, blocking collectives: 92.3 us -> none  [the longest x1 69 us: local(): params = lax.all_gather(params, 'shard', axis=0).astype(f32)]
    unnamed x231 -> x170, local copies, waits for them, and re-layouts: 112 us -> 25.2 us
    dot_general x6 -> x2, matrix products: 129 us -> 46.4 us  [dot(): lax.dot_general(a, b, (((ca,), (cb,)), ((), ())), preferred_element_type=...]
    convert_element_type x23 -> x8, other arithmetic: 82.2 us -> 4.07 us  [the longest x2 2.04 us: with_shift(): scaled = (part_of(weight) * part_of(gain)[:, None]).astype(bf16)]
    ppermute x12 -> x29, starting transfers between devices: 30.3 us -> 99.1 us  [the longest x7 61.4 us: rep_in(): return lax.ppermute(value, 'rep', [(0, 1), (3, 2)])]
  transfers between devices with their start and end apart: 54 -> 46, of which waited for: 14 -> 13; matrix products, arithmetic and copies ran while one was open for 49% -> 16% of each run, Pallas kernels for 4% -> 39%
where the time goes in v2:
time: 842 us; the launch traced here: 829 us
  Pallas kernels  336 us (40%)
  waiting for transfers between devices  183 us (22%)
  starting transfers between devices  133 us (16%)
  local copies, waits for them, and re-layouts  65 us (8%)
  other arithmetic  49.8 us (6%)
  matrix products  46.4 us (6%)
  between operations  16 us (2%)
    ppermute x7, starting transfers between devices, rep_in(): return lax.ppermute(value, 'rep', [(0, 1), (3, 2)])  61.4 us
    ppermute x6, waiting for transfers between devices, exchange(): lax.ppermute(part, 'rep', [(i, (i + k) % shares) for i in range(shares)])  60.9 us
    pallas_call x18, Pallas kernels, plus_low(): pl.pallas_call(body, grid=(4,), in_specs=[block, block], out_specs=spec((...  58.7 us
    pallas_call x3, Pallas kernels, normed_dot(): pl.pallas_call(body, grid=(D // tile,), in_specs=[spec((rows, tile), lamb...  47.5 us
    pallas_call x2, Pallas kernels, norm_terms(): pl.pallas_call(body, grid_spec=pltpu.PrefetchScalarGridSpec(num_scalar_pr...  47.3 us
    dot_general x2, matrix products, dot(): lax.dot_general(a, b, (((ca,), (cb,)), ((), ())), preferred_element_type=...  46.4 us
    pallas_call x3, Pallas kernels, token_dot(): pl.pallas_call(body, grid=(blocks // step,), in_specs=[spec((rows, width)...  37.9 us
    pallas_call x1, Pallas kernels, attention(): pl.pallas_call(attention_kernel, grid_spec=pltpu.PrefetchScalarGridSpec(n...  36.6 us
  transfers between devices with their start and end apart: 46, of which 13 were waited for; matrix products, arithmetic and copies ran while one was open for 16% of the time, Pallas kernels for 39%

profile of v2, /device:TPU:0, one launch (start us, length us, event | category | flops | bytes accessed | tf_op | source)
XLA Modules:
  0.0 829.2 jit_solution(2121795684804815176)
XLA Ops:
  29.0 5.1 all-to-all-start
  54.1 21.1 %all-to-all-done = bf16[8,80,1792]{2,1,0:T(8,128)(2,1)} async-done(((bf16[8,80,1792]{2,1,0:T(8,128)(2,1)}), bf16[8,80,1792]{2,1,0:T(8,128)(2,1)}, u32[]{:S(2)}, u32[]{:S(2)}) %all-to-all-start) | async-done | bytes 2293792 | tf_op jit(solution)/shard_map/all_to_all | solution.py:598
  87.6 19.3 %collective-permute-done = bf16[8,64,1024]{2,1,0:T(8,128)(2,1)} collective-permute-done((bf16[8,64,1024]{2,1,0:T(8,128)(2,1)}, bf16[8,64,1024]{2,1,0:T(8,128)(2,1)}, u32[]{:S(2)}, u32[]{:S(2)}) %collective-permute-start) | collective-permute-done | bytes 1048608 | tf_op jit(solution)/shard_map/ppermute | solution.py:656
  110.2 41.6 %collective-permute-done.1 = bf16[8,64,1024]{2,1,0:T(8,128)(2,1)} collective-permute-done((bf16[8,64,1024]{2,1,0:T(8,128)(2,1)}, bf16[8,64,1024]{2,1,0:T(8,128)(2,1)}, u32[]{:S(2)}, u32[]{:S(2)}) %collective-permute-start.1) | collective-permute-done | bytes 1048608 | tf_op jit(solution)/shard_map/ppermute | solution.py:656
  159.8 27.9 %fusion.3 = (f32[4096,1024]{1,0:T(8,128)}, bf16[4096,1024]{1,0:T(8,128)(2,1)}) fusion(f32[1024]{0:T(1024)S(1)} %slice_add_fusion, bf16[4096,2048]{1,0:T(8,128)(2,1)} %all-gather.5.cloned.1.call-done.left_ref, bf16[2048,1024]{1,0:T(8,128)(2,1)S(1)} %bitcast.213), kind=kOutput, calls=%fused_computation.8 | convolution fusion | flops 17226006528 | bytes 46141440 | tf_op jit(solution)/shard_map/dot_general | solution.py:26
  187.7 34.5 %all-gather.3.cloned.1.call-done.right_ref.grad_ref = bf16[8,4096,256]{2,1,0:T(8,128)(2,1)} async-done(((bf16[1,4096,256]{2,1,0:T(8,128)(2,1)}), bf16[8,4096,256]{2,1,0:T(8,128)(2,1)}) %all-gather.3.cloned.1.call-update) | async-done | bytes 16777232 | tf_op jit(solution)/shard_map/all_gather | solution.py:648
  222.2 13.8 %shard_map.284.refs_1_ = bf16[512,2048]{1,0:T(8,128)(2,1)} custom-call(bf16[4096,1024]{1,0:T(8,128)(2,1)} %get-tuple-element.161.left_ref.refs_1_, bf16[8,4096,256]{2,1,0:T(8,128)(2,1)} %all-gather.3.cloned.1.call-done.right_ref.grad_ref), custom_call_target="tpu_custom_call" | custom-call | flops 1024 | bytes 1024 | tf_op jit(solution)/shard_map/pallas_call | solution.py:376
  236.0 23.7 %collective-permute-start.3 = (bf16[512,2048]{1,0:T(8,128)(2,1)}, bf16[512,2048]{1,0:T(8,128)(2,1)}, u32[]{:S(2)}, u32[]{:S(2)}) collective-permute-start(bf16[512,2048]{1,0:T(8,128)(2,1)} %shard_map.284.refs_1_), channel_id=1, source_target_pairs={{0,8},{24,16},{1,9},{25,17},{2,10},{26,18},{3,11},{27,19},{4,12},{... | collective-permute-start | bytes 6291464 | tf_op jit(solution)/shard_map/ppermute | solution.py:42
  261.3 13.8 %shard_map.286 = bf16[512,2048]{1,0:T(8,128)(2,1)} custom-call(bf16[4096,1024]{1,0:T(8,128)(2,1)} %get-tuple-element.161.left_ref.refs_1_, bf16[8,4096,256]{2,1,0:T(8,128)(2,1)} %all-gather.3.cloned.1.call-done.right_ref.grad_ref), custom_call_target="tpu_custom_call" | custom-call | flops 1024 | bytes 1024 | tf_op jit(solution)/shard_map/pallas_call | solution.py:376
  275.2 24.9 %shard_map.287 = (bf16[4096,1024]{1,0:T(8,128)(2,1)}, f32[1,1024]{1,0:T(1,128)S(1)}) custom-call(bf16[8,4096,256]{2,1,0:T(8,128)(2,1)} %all-gather.3.cloned.1.call-done.right_ref.grad_ref, bf16[1024,2048]{1,0:T(8,128)(2,1)} %refs_9_.3, f32[4096,1024]{1,0:T(8,128)} %get-tuple-element.280.slope_ref), custom_call_target="tpu_custom_call" | custom-call | flops 1024 | bytes 1024 | tf_op jit(solution)/shard_map/pallas_call | solution.py:435
  300.1 13.7 %shard_map.288.refs_2_ = bf16[2048,512]{1,0:T(8,128)(2,1)} custom-call(bf16[4096,2048]{1,0:T(8,128)(2,1)} %all-gather.5.cloned.1.call-done.left_ref, bf16[4096,1024]{1,0:T(8,128)(2,1)} %get-tuple-element.164.right_ref.refs_1_), custom_call_target="tpu_custom_call" | custom-call | flops 1024 | bytes 1024 | tf_op jit(solution)/shard_map/pallas_call | solution.py:404
  313.9 4.5 all-to-all-start.1
  321.0 4.1 shard_map.289.refs_1_
  327.6 13.8 %shard_map.291 = bf16[2048,512]{1,0:T(8,128)(2,1)} custom-call(bf16[4096,2048]{1,0:T(8,128)(2,1)} %all-gather.5.cloned.1.call-done.left_ref, bf16[4096,1024]{1,0:T(8,128)(2,1)} %get-tuple-element.164.right_ref.refs_1_), custom_call_target="tpu_custom_call" | custom-call | flops 1024 | bytes 1024 | tf_op jit(solution)/shard_map/pallas_call | solution.py:404
  341.4 11.6 %shard_map.292 = bf16[4096,256]{1,0:T(8,128)(2,1)} custom-call(bf16[8,4096,256]{2,1,0:T(8,128)(2,1)} %all-gather.3.cloned.1.call-done.right_ref.grad_ref, bf16[256,2048]{1,0:T(8,128)(2,1)S(1)} %copy-done), custom_call_target="tpu_custom_call" | custom-call | flops 1024 | bytes 1024 | tf_op jit(solution)/shard_map/pallas_call | solution.py:457
  359.9 18.5 %convolution_add_fusion = f32[4096,768]{1,0:T(8,128)} fusion(bf16[4096,2048]{1,0:T(8,128)(2,1)} %all-gather.5.cloned.1.call-done.left_ref, bf16[2048,768]{1,0:T(8,128)(2,1)S(1)} %bitcast.216, f32[768]{0:T(1024)S(1)} %slice-done), kind=kOutput, calls=%fused_computation.12 | convolution fusion | flops 12888047616 | bytes 32508928 | tf_op jit(solution)/shard_map/dot_general | solution.py:26
  381.1 4.3 shard_map.294.refs_2_
  387.3 4.3 shard_map.293.refs_1_.refs_0_
  392.9 4.5 all-to-all-start.2
  398.1 36.6 %shard_map.296 = (bf16[8,2,2,128,256]{4,3,2,1,0:T(8,128)(2,1)}, bf16[8,2,2,128,768]{4,3,2,1,0:T(8,128)(2,1)}) custom-call(s32[2,16]{1,0:T(2,128)S(1)} %get-tuple-element.300.piece_of, s32[2,16]{1,0:T(2,128)S(1)} %get-tuple-element.299.inner_of, s32[2,16]{1,0:T(2,128)S(1)} %copy-done.43, s32[2,16]{1,0:T(2,128)S(1)} %get-tuple-element.307.end_of, ...), custom_call_target="tpu_custom_call" | custom-call | flops 1024 | bytes 1024 | tf_op jit(solution)/shard_map/pallas_call | solution.py:200
  434.7 7.0 collective-permute-done.9.refs_1_
  441.7 4.4 shard_map.298.refs_2_
  447.4 4.3 shard_map.297
  453.7 8.9 %collective-permute-start.14 = (bf16[8,256,512]{2,1,0:T(8,128)(2,1)}, bf16[8,256,512]{2,1,0:T(8,128)(2,1)}, u32[]{:S(2)}, u32[]{:S(2)}) collective-permute-start(bf16[8,256,512]{2,1,0:T(8,128)(2,1)} %all-to-all-done.2.refs_4_), channel_id=1, source_target_pairs={{0,8},{24,16},{1,9},{25,17},{2,10},{26,18},{3,11},{27,19},{4,12},{... | collective-permute-start | bytes 6291464 | tf_op jit(solution)/shard_map/ppermute | solution.py:42
  462.6 20.0 %shard_map.300 = (bf16[2048,768]{1,0:T(8,128)(2,1)}, f32[1,768]{1,0:T(1,128)}) custom-call(bf16[4096,2048]{1,0:T(8,128)(2,1)} %all-gather.5.cloned.1.call-done.left_ref, bf16[4096,768]{1,0:T(8,128)(2,1)} %bitcast.210), custom_call_target="tpu_custom_call" | custom-call | flops 1024 | bytes 1024 | tf_op jit(solution)/shard_map/pallas_call | solution.py:404
  482.5 10.2 %shard_map.301 = bf16[256,2048]{1,0:T(8,128)(2,1)} custom-call(bf16[4096,256]{1,0:T(8,128)(2,1)} %bitcast.219, bf16[8,4096,256]{2,1,0:T(8,128)(2,1)} %all-gather.3.cloned.1.call-done.right_ref.grad_ref), custom_call_target="tpu_custom_call" | custom-call | flops 1024 | bytes 1024 | tf_op jit(solution)/shard_map/pallas_call | solution.py:376
  492.7 16.8 %shard_map.302.refs_6_ = bf16[4,4096,256]{2,1,0:T(8,128)(2,1)} custom-call(s32[8]{0:T(128)S(1)} %broadcast_xor_fusion.owners_ref, s32[1]{0:T(128)} %bitcast.52.place_ref, bf16[4096,256]{1,0:T(8,128)(2,1)} %bitcast.220, bf16[4096,1024]{1,0:T(8,128)(2,1)} %get-tuple-element.161.left_ref.refs_1_, bf16[256,2048]{1,0:T(8,128)(2,1)S(1)} %copy-done.1, ...), custom_call_target="tpu_custom_call" | custom-call | flops 1024 | bytes 1024 | tf_op jit(solution)/shard_map/pallas_call | solution.py:301
  513.0 4.2 shard_map.303
  517.3 22.2 %shard_map.306.refs_6_ = bf16[4,2,256,2048]{3,2,1,0:T(8,128)(2,1)} custom-call(s32[8]{0:T(128)S(1)} %broadcast_xor_fusion.owners_ref, bf16[4096,768]{1,0:T(8,128)(2,1)} %bitcast.211, bf16[4096,1024]{1,0:T(8,128)(2,1)} %get-tuple-element.164.right_ref.refs_1_, bf16[2048,768]{1,0:T(8,128)(2,1)} %bitcast.217, bf16[2048,1024]{1,0:T(8,128)(2,1)} %bitcast.214), custom_call_target="tpu_custom_call" | custom-call | flops 1024 | bytes 1024 | tf_op jit(solution)/shard_map/pallas_call | solution.py:358
  540.0 4.5 all-to-all-start.3
  547.7 6.0 collective-permute-start.17
  553.8 19.1 %shard_map.307 = (bf16[2,2048,256]{2,1,0:T(8,128)(2,1)}, bf16[2,2048,256]{2,1,0:T(8,128)(2,1)}, bf16[2,2048,256]{2,1,0:T(8,128)(2,1)}, bf16[2,2048,256]{2,1,0:T(8,128)(2,1)}) custom-call(s32[8]{0:T(128)S(1)} %broadcast_xor_fusion.owners_ref, s32[1]{0:T(128)} %bitcast.52.place_ref, bf16[4096,256]{1,0:T(8,128)(2,1)} %bitcast.221, ...), custom_call_target="tpu_custom_call" | custom-call | flops 1024 | bytes 1024 | tf_op jit(solution)/shard_map/pallas_call | solution.py:301
  577.6 4.7 all-to-all-done.3
  582.3 14.0 %collective-permute-done.15.refs_1_ = bf16[8,256,512]{2,1,0:T(8,128)(2,1)} collective-permute-done((bf16[8,256,512]{2,1,0:T(8,128)(2,1)S(1)}, bf16[8,256,512]{2,1,0:T(8,128)(2,1)}, u32[]{:S(2)}, u32[]{:S(2)}) %collective-permute-start.15) | collective-permute-done | bytes 2097184 | tf_op jit(solution)/shard_map/ppermute | solution.py:50
  600.0 3.9 fusion.31
  603.9 4.3 collective-permute-start.24
  608.2 4.0 shard_map.308
  617.7 13.2 %collective-permute-start.19 = (bf16[4,256,768]{2,1,0:T(8,128)(2,1)}, bf16[4,256,768]{2,1,0:T(8,128)(2,1)}, u32[]{:S(2)}, u32[]{:S(2)}) collective-permute-start(bf16[4,256,768]{2,1,0:T(8,128)(2,1)} %get-tuple-element.285.refs_5_), channel_id=1, source_target_pairs={{0,8},{24,16},{1,9},{25,17},{2,10},{26,18},{3,11},{27,19},{4,12},{... | collective-permute-start | bytes 4718600 | tf_op jit(solution)/shard_map/ppermute | solution.py:42
  631.0 25.1 %shard_map.311 = (bf16[2,256,2048]{2,1,0:T(8,128)(2,1)}, bf16[2,256,2048]{2,1,0:T(8,128)(2,1)}, bf16[2,256,2048]{2,1,0:T(8,128)(2,1)}, bf16[2,256,2048]{2,1,0:T(8,128)(2,1)}) custom-call(s32[8]{0:T(128)S(1)} %broadcast_xor_fusion.owners_ref, bf16[4096,768]{1,0:T(8,128)(2,1)} %bitcast.212, bf16[4096,1024]{1,0:T(8,128)(2,1)} %get-tuple-element.164.right_ref.refs_1_, ...), custom_call_target="tpu_custom_call" | custom-call | flops 1024 | bytes 1024 | tf_op jit(solution)/shard_map/pallas_call | solution.py:358
  659.9 14.3 %collective-permute-done.19 = bf16[4,256,768]{2,1,0:T(8,128)(2,1)} collective-permute-done((bf16[4,256,768]{2,1,0:T(8,128)(2,1)}, bf16[4,256,768]{2,1,0:T(8,128)(2,1)}, u32[]{:S(2)}, u32[]{:S(2)}) %collective-permute-start.19) | collective-permute-done | bytes 1572896 | tf_op jit(solution)/shard_map/ppermute | solution.py:42
  688.6 4.0 shard_map.316
  692.6 9.7 %collective-permute-done.27 = f32[2048]{0:T(1024)S(1)} collective-permute-done((f32[2048]{0:T(1024)S(1)}, f32[2048]{0:T(1024)S(1)}, u32[]{:S(2)}, u32[]{:S(2)}) %collective-permute-start.27) | collective-permute-done | bytes 8224 | tf_op jit(solution)/shard_map/ppermute | solution.py:758
  712.1 7.1 shard_map.317
  738.9 4.0 shard_map.322
  747.9 4.3 all-to-all-start.4
  759.0 8.8 %all-to-all-done.4 = f32[8,1,2048]{2,1,0:T(1,128)} async-done(((f32[8,1,2048]{2,1,0:T(1,128)}), f32[8,1,2048]{2,1,0:T(1,128)}, u32[]{:S(2)}, u32[]{:S(2)}) %all-to-all-start.4) | async-done | bytes 65568 | tf_op jit(solution)/shard_map/all_to_all | solution.py:598
  781.8 14.5 %shard_map.323 = (f32[256,8192]{1,0:T(8,128)}, f32[256,128]{1,0:T(8,128)S(1)}, f32[256,128]{1,0:T(8,128)S(1)}) custom-call(s32[1]{0:T(128)} %bitcast.74.inner_ref, bf16[8,256,512]{2,1,0:T(8,128)(2,1)S(1)} %bitcast.184, bf16[8,256,512]{2,1,0:T(8,128)(2,1)} %collective-permute-done.15.refs_1_, bf16[8,256,512]{2,1,0:T(8,128)(2,1)} %bitcast.64.refs_2_, ...), custom_call_target="tpu_custom_call" | custom-call | flops 1024 | bytes 1024 | tf_op jit(solution)/shard_map/pallas_call | solution.py:537
  808.0 11.9 %shard_map.324 = (f32[256,6144]{1,0:T(8,128)}, f32[256,128]{1,0:T(8,128)S(1)}, f32[256,128]{1,0:T(8,128)S(1)}) custom-call(s32[1]{0:T(128)} %bitcast.74.inner_ref, bf16[4,256,768]{2,1,0:T(8,128)(2,1)} %bitcast.77.refs_0_, bf16[4,256,768]{2,1,0:T(8,128)(2,1)} %collective-permute-done.35.refs_1_, bf16[4,256,768]{2,1,0:T(8,128)(2,1)} %bitcast.82.refs_2_, ...), custom_call_target="tpu_custom_call" | custom-call | flops 1024 | bytes 1024 | tf_op jit(solution)/shard_map/pallas_call | solution.py:537
  (373 shorter events, 196.1 us)
Async XLA Ops:
  7.2 144.7 %all-gather.5.cloned.1.call-start = ((), (), s32[]{:S(2)}) async-start(), calls=%async_computation.6 | async-start | bytes 18874368 | tf_op jit(solution)/shard_map/all_gather | solution.py:618
  29.0 46.3 %all-to-all-start = ((bf16[8,80,1792]{2,1,0:T(8,128)(2,1)}), bf16[8,80,1792]{2,1,0:T(8,128)(2,1)}, u32[]{:S(2)}, u32[]{:S(2)}) async-start(bf16[8,80,1792]{2,1,0:T(8,128)(2,1)} %pad_maximum_fusion.2), calls=%async_computation | async-start | bytes 4587520 | tf_op jit(solution)/shard_map/all_to_all | solution.py:598
  34.0 188.2 %all-gather.3.cloned.1.call-start = ((), (), s32[]{:S(2)}) async-start(), calls=%async_computation.5 | async-start | bytes 18874368 | tf_op jit(solution)/shard_map/all_gather | solution.py:648
  51.8 345.7 %copy-start.38 = (s32[2,16]{1,0:T(2,128)}, s32[2,16]{1,0:T(2,128)S(1)}, u32[]{:S(2)}) copy-start(s32[2,16]{1,0:T(2,128)S(1)} %get-tuple-element.299.inner_of) | copy-start | bytes 388
  51.8 345.7 %copy-start.40 = (s32[2,16]{1,0:T(2,128)}, s32[2,16]{1,0:T(2,128)S(1)}, u32[]{:S(2)}) copy-start(s32[2,16]{1,0:T(2,128)S(1)} %get-tuple-element.300.piece_of) | copy-start | bytes 388
  78.5 28.4 %collective-permute-start = (bf16[8,64,1024]{2,1,0:T(8,128)(2,1)}, bf16[8,64,1024]{2,1,0:T(8,128)(2,1)}, u32[]{:S(2)}, u32[]{:S(2)}) collective-permute-start(bf16[8,64,1024]{2,1,0:T(8,128)(2,1)} %slice.84.refs_1_), channel_id=1, source_target_pairs={{0,8},{8,16},{16,24},{24,0},{1,9},{9,17},{17,25},{25,1},{2,10},{10... | collective-permute-start | bytes 3145736 | tf_op jit(solution)/shard_map/ppermute | solution.py:656
  80.1 71.8 %collective-permute-start.1 = (bf16[8,64,1024]{2,1,0:T(8,128)(2,1)}, bf16[8,64,1024]{2,1,0:T(8,128)(2,1)}, u32[]{:S(2)}, u32[]{:S(2)}) collective-permute-start(bf16[8,64,1024]{2,1,0:T(8,128)(2,1)} %slice.84.refs_1_), channel_id=1, source_target_pairs={{0,16},{8,24},{16,0},{24,8},{1,17},{9,25},{17,1},{25,9},{2,18},{10... | collective-permute-start | bytes 3145736 | tf_op jit(solution)/shard_map/ppermute | solution.py:656
  82.5 69.4 %collective-permute-start.2 = (bf16[8,64,1024]{2,1,0:T(8,128)(2,1)}, bf16[8,64,1024]{2,1,0:T(8,128)(2,1)}, u32[]{:S(2)}, u32[]{:S(2)}) collective-permute-start(bf16[8,64,1024]{2,1,0:T(8,128)(2,1)} %slice.84.refs_1_), channel_id=1, source_target_pairs={{0,24},{8,0},{16,8},{24,16},{1,25},{9,1},{17,9},{25,17},{2,26},{10... | collective-permute-start | bytes 3145736 | tf_op jit(solution)/shard_map/ppermute | solution.py:656
  86.0 267.0 %collective-permute-start.6 = (bf16[8,64,768]{2,1,0:T(8,128)(2,1)}, bf16[8,64,768]{2,1,0:T(8,128)(2,1)}, u32[]{:S(2)}, u32[]{:S(2)}) collective-permute-start(bf16[8,64,768]{2,1,0:T(8,128)(2,1)} %slice.87), channel_id=1, source_target_pairs={{0,8},{8,16},{16,24},{24,0},{1,9},{9,17},{17,25},{25,1},{2,10},{10... | collective-permute-start | bytes 2359304 | tf_op jit(solution)/shard_map/ppermute | solution.py:656
  86.8 266.2 %collective-permute-start.7 = (bf16[8,64,768]{2,1,0:T(8,128)(2,1)}, bf16[8,64,768]{2,1,0:T(8,128)(2,1)}, u32[]{:S(2)}, u32[]{:S(2)}) collective-permute-start(bf16[8,64,768]{2,1,0:T(8,128)(2,1)} %slice.87), channel_id=1, source_target_pairs={{0,16},{8,24},{16,0},{24,8},{1,17},{9,25},{17,1},{25,9},{2,18},{10... | collective-permute-start | bytes 2359304 | tf_op jit(solution)/shard_map/ppermute | solution.py:656
  106.9 246.1 %collective-permute-start.8 = (bf16[8,64,768]{2,1,0:T(8,128)(2,1)}, bf16[8,64,768]{2,1,0:T(8,128)(2,1)}, u32[]{:S(2)}, u32[]{:S(2)}) collective-permute-start(bf16[8,64,768]{2,1,0:T(8,128)(2,1)} %slice.87), channel_id=1, source_target_pairs={{0,24},{8,0},{16,8},{24,16},{1,25},{9,1},{17,9},{25,17},{2,26},{10... | collective-permute-start | bytes 2359304 | tf_op jit(solution)/shard_map/ppermute | solution.py:656
  236.0 84.9 %collective-permute-start.3 = (bf16[512,2048]{1,0:T(8,128)(2,1)}, bf16[512,2048]{1,0:T(8,128)(2,1)}, u32[]{:S(2)}, u32[]{:S(2)}) collective-permute-start(bf16[512,2048]{1,0:T(8,128)(2,1)} %shard_map.284.refs_1_), channel_id=1, source_target_pairs={{0,8},{24,16},{1,9},{25,17},{2,10},{26,18},{3,11},{27,19},{4,12},{... | collective-permute-start | bytes 6291464 | tf_op jit(solution)/shard_map/ppermute | solution.py:42
  313.9 64.5 %all-to-all-start.1 = ((bf16[8,256,512]{2,1,0:T(8,128)(2,1)}), bf16[8,256,512]{2,1,0:T(8,128)(2,1)}, u32[]{:S(2)}, u32[]{:S(2)}) async-start(bf16[8,256,512]{2,1,0:T(8,128)(2,1)} %bitcast.190), calls=%async_computation.1 | async-start | bytes 4194304 | tf_op jit(solution)/shard_map/all_to_all | solution.py:598
  318.4 60.0 %collective-permute-start.5 = (bf16[512,2048]{1,0:T(8,128)(2,1)}, bf16[512,2048]{1,0:T(8,128)(2,1)}, u32[]{:S(2)}, u32[]{:S(2)}) collective-permute-start(bf16[512,2048]{1,0:T(8,128)(2,1)} %shard_map.286), channel_id=1, source_target_pairs={{0,8},{24,16},{1,9},{25,17},{2,10},{26,18},{3,11},{27,19},{4,12},{... | collective-permute-start | bytes 6291464 | tf_op jit(solution)/shard_map/ppermute | solution.py:42
  325.1 53.3 %collective-permute-start.4 = (bf16[512,2048]{1,0:T(8,128)(2,1)}, bf16[512,2048]{1,0:T(8,128)(2,1)}, u32[]{:S(2)}, u32[]{:S(2)}) collective-permute-start(bf16[512,2048]{1,0:T(8,128)(2,1)} %shard_map.289.refs_1_), channel_id=1, source_target_pairs={{8,16},{16,8},{9,17},{17,9},{10,18},{18,10},{11,19},{19,11},{12,20... | collective-permute-start | bytes 6291464 | tf_op jit(solution)/shard_map/ppermute | solution.py:46
  378.4 63.4 %collective-permute-start.11 = (bf16[8,256,512]{2,1,0:T(8,128)(2,1)}, bf16[8,256,512]{2,1,0:T(8,128)(2,1)}, u32[]{:S(2)}, u32[]{:S(2)}) collective-permute-start(bf16[8,256,512]{2,1,0:T(8,128)(2,1)} %all-to-all-done.1.refs_3_), channel_id=1, source_target_pairs={{0,8},{24,16},{1,9},{25,17},{2,10},{26,18},{3,11},{27,19},{4,12},{... | collective-permute-start | bytes 6291464 | tf_op jit(solution)/shard_map/ppermute | solution.py:42
  385.4 49.4 %collective-permute-start.10 = (bf16[512,2048]{1,0:T(8,128)(2,1)}, bf16[512,2048]{1,0:T(8,128)(2,1)}, u32[]{:S(2)}, u32[]{:S(2)}) collective-permute-start(bf16[512,2048]{1,0:T(8,128)(2,1)} %shard_map.294.refs_2_), channel_id=1, source_target_pairs={{8,16},{16,8},{9,17},{17,9},{10,18},{18,10},{11,19},{19,11},{12,20... | collective-permute-start | bytes 6291464 | tf_op jit(solution)/shard_map/ppermute | solution.py:46
  391.6 50.1 %collective-permute-start.9 = (bf16[512,2048]{1,0:T(8,128)(2,1)}, bf16[512,2048]{1,0:T(8,128)(2,1)}, u32[]{:S(2)}, u32[]{:S(2)}) collective-permute-start(bf16[512,2048]{1,0:T(8,128)(2,1)} %shard_map.293.refs_1_.refs_0_), channel_id=1, source_target_pairs={{8,0},{16,24},{9,1},{17,25},{10,2},{18,26},{11,3},{19,27},{12,4},{... | collective-permute-start | bytes 6291464 | tf_op jit(solution)/shard_map/ppermute | solution.py:50
  392.9 41.8 %all-to-all-start.2 = ((bf16[8,256,512]{2,1,0:T(8,128)(2,1)}), bf16[8,256,512]{2,1,0:T(8,128)(2,1)}, u32[]{:S(2)}, u32[]{:S(2)}) async-start(bf16[8,256,512]{2,1,0:T(8,128)(2,1)} %bitcast.232), calls=%async_computation.2 | async-start | bytes 4194304 | tf_op jit(solution)/shard_map/all_to_all | solution.py:598
  446.1 63.5 %collective-permute-start.12 = (bf16[512,2048]{1,0:T(8,128)(2,1)}, bf16[512,2048]{1,0:T(8,128)(2,1)}, u32[]{:S(2)}, u32[]{:S(2)}) collective-permute-start(bf16[512,2048]{1,0:T(8,128)(2,1)} %shard_map.298.refs_2_), channel_id=1, source_target_pairs={{8,0},{16,24},{9,1},{17,25},{10,2},{18,26},{11,3},{19,27},{12,4},{... | collective-permute-start | bytes 6291464 | tf_op jit(solution)/shard_map/ppermute | solution.py:50
  451.7 57.9 %collective-permute-start.13 = (bf16[8,256,512]{2,1,0:T(8,128)(2,1)}, bf16[8,256,512]{2,1,0:T(8,128)(2,1)}, u32[]{:S(2)}, u32[]{:S(2)}) collective-permute-start(bf16[8,256,512]{2,1,0:T(8,128)(2,1)} %bitcast.51.refs_3_), channel_id=1, source_target_pairs={{8,16},{16,8},{9,17},{17,9},{10,18},{18,10},{11,19},{19,11},{12,20... | collective-permute-start | bytes 6291464 | tf_op jit(solution)/shard_map/ppermute | solution.py:46
  453.7 56.0 %collective-permute-start.14 = (bf16[8,256,512]{2,1,0:T(8,128)(2,1)}, bf16[8,256,512]{2,1,0:T(8,128)(2,1)}, u32[]{:S(2)}, u32[]{:S(2)}) collective-permute-start(bf16[8,256,512]{2,1,0:T(8,128)(2,1)} %all-to-all-done.2.refs_4_), channel_id=1, source_target_pairs={{0,8},{24,16},{1,9},{25,17},{2,10},{26,18},{3,11},{27,19},{4,12},{... | collective-permute-start | bytes 6291464 | tf_op jit(solution)/shard_map/ppermute | solution.py:42
  509.5 44.2 %collective-permute-start.18 = (bf16[4,4096,256]{2,1,0:T(8,128)(2,1)}, bf16[4,4096,256]{2,1,0:T(8,128)(2,1)}, u32[]{:S(2)}, u32[]{:S(2)}) collective-permute-start(bf16[4,4096,256]{2,1,0:T(8,128)(2,1)} %shard_map.302.refs_6_), channel_id=1, source_target_pairs={{0,1},{1,0},{2,3},{3,2},{4,5},{5,4},{6,7},{7,6},{8,9},{9,8},{10,11... | collective-permute-start | bytes 25165832 | tf_op jit(solution)/shard_map/ppermute | solution.py:30
  539.5 78.3 %collective-permute-start.25 = (bf16[4,2,256,2048]{3,2,1,0:T(8,128)(2,1)}, bf16[4,2,256,2048]{3,2,1,0:T(8,128)(2,1)}, u32[]{:S(2)}, u32[]{:S(2)}) collective-permute-start(bf16[4,2,256,2048]{3,2,1,0:T(8,128)(2,1)} %shard_map.306.refs_6_), channel_id=1, source_target_pairs={{0,1},{1,0},{2,3},{3,2},{4,5},{5,4},{6,7},{7,6},{8,9},{9,8},{10,11... | collective-permute-start | bytes 25165832 | tf_op jit(solution)/shard_map/ppermute | solution.py:30
  540.0 42.4 %all-to-all-start.3 = ((bf16[8,256,768]{2,1,0:T(8,128)(2,1)}), bf16[8,256,768]{2,1,0:T(8,128)(2,1)}, u32[]{:S(2)}, u32[]{:S(2)}) async-start(bf16[8,256,768]{2,1,0:T(8,128)(2,1)} %bitcast.195), calls=%async_computation.3 | async-start | bytes 6291456 | tf_op jit(solution)/shard_map/all_to_all | solution.py:598
  544.4 37.9 %collective-permute-start.16 = (bf16[8,256,512]{2,1,0:T(8,128)(2,1)}, bf16[8,256,512]{2,1,0:T(8,128)(2,1)}, u32[]{:S(2)}, u32[]{:S(2)}) collective-permute-start(bf16[8,256,512]{2,1,0:T(8,128)(2,1)} %bitcast.186), channel_id=1, source_target_pairs={{8,16},{16,8},{9,17},{17,9},{10,18},{18,10},{11,19},{19,11},{12,20... | collective-permute-start | bytes 6291464 | tf_op jit(solution)/shard_map/ppermute | solution.py:46
  546.5 49.9 %collective-permute-start.15 = (bf16[8,256,512]{2,1,0:T(8,128)(2,1)S(1)}, bf16[8,256,512]{2,1,0:T(8,128)(2,1)}, u32[]{:S(2)}, u32[]{:S(2)}) collective-permute-start(bf16[8,256,512]{2,1,0:T(8,128)(2,1)S(1)} %bitcast.183), channel_id=1, source_target_pairs={{8,0},{16,24},{9,1},{17,25},{10,2},{18,26},{11,3},{19,27},{12,4},{... | collective-permute-start | bytes 6291464 | tf_op jit(solution)/shard_map/ppermute | solution.py:50
  547.7 28.9 %collective-permute-start.17 = (bf16[256,2048]{1,0:T(8,128)(2,1)}, bf16[256,2048]{1,0:T(8,128)(2,1)S(1)}, u32[]{:S(2)}, u32[]{:S(2)}) collective-permute-start(bf16[256,2048]{1,0:T(8,128)(2,1)} %shard_map.301), channel_id=1, source_target_pairs={{0,8},{24,16},{1,9},{25,17},{2,10},{26,18},{3,11},{27,19},{4,12},{... | collective-permute-start | bytes 3145736 | tf_op jit(solution)/shard_map/ppermute | solution.py:42
  599.1 16.1 %collective-permute-start.23 = (bf16[256,2048]{1,0:T(8,128)(2,1)S(1)}, bf16[256,2048]{1,0:T(8,128)(2,1)S(1)}, u32[]{:S(2)}, u32[]{:S(2)}) collective-permute-start(bf16[256,2048]{1,0:T(8,128)(2,1)S(1)} %shard_map.309.refs_3_), channel_id=1, source_target_pairs={{8,16},{16,8},{9,17},{17,9},{10,18},{18,10},{11,19},{19,11},{12,20... | collective-permute-start | bytes 3145736 | tf_op jit(solution)/shard_map/ppermute | solution.py:46
  603.9 52.2 %collective-permute-start.24 = (bf16[4,256,768]{2,1,0:T(8,128)(2,1)}, bf16[4,256,768]{2,1,0:T(8,128)(2,1)}, u32[]{:S(2)}, u32[]{:S(2)}) collective-permute-start(bf16[4,256,768]{2,1,0:T(8,128)(2,1)} %get-tuple-element.284.refs_4_), channel_id=1, source_target_pairs={{0,8},{24,16},{1,9},{25,17},{2,10},{26,18},{3,11},{27,19},{4,12},{... | collective-permute-start | bytes 4718600 | tf_op jit(solution)/shard_map/ppermute | solution.py:42
  612.2 63.4 %collective-permute-start.22 = (bf16[8,256,512]{2,1,0:T(8,128)(2,1)}, bf16[8,256,512]{2,1,0:T(8,128)(2,1)}, u32[]{:S(2)}, u32[]{:S(2)}) collective-permute-start(bf16[8,256,512]{2,1,0:T(8,128)(2,1)} %bitcast.64.refs_2_), channel_id=1, source_target_pairs={{8,0},{16,24},{9,1},{17,25},{10,2},{18,26},{11,3},{19,27},{12,4},{... | collective-permute-start | bytes 6291464 | tf_op jit(solution)/shard_map/ppermute | solution.py:50
  613.5 63.9 %collective-permute-start.20 = (bf16[2,2048,256]{2,1,0:T(8,128)(2,1)}, bf16[2,2048,256]{2,1,0:T(8,128)(2,1)}, u32[]{:S(2)}, u32[]{:S(2)}) collective-permute-start(bf16[2,2048,256]{2,1,0:T(8,128)(2,1)} %get-tuple-element.210.refs_7_), channel_id=1, source_target_pairs={{0,2},{1,3},{2,0},{3,1},{4,6},{5,7},{6,4},{7,5},{8,10},{9,11},{10,... | collective-permute-start | bytes 6291464 | tf_op jit(solution)/shard_map/ppermute | solution.py:30
  616.3 62.6 %collective-permute-start.21 = (bf16[2,2048,256]{2,1,0:T(8,128)(2,1)}, bf16[2,2048,256]{2,1,0:T(8,128)(2,1)}, u32[]{:S(2)}, u32[]{:S(2)}) collective-permute-start(bf16[2,2048,256]{2,1,0:T(8,128)(2,1)} %get-tuple-element.211), channel_id=1, source_target_pairs={{0,4},{1,5},{2,6},{3,7},{4,0},{5,1},{6,2},{7,3},{8,12},{9,13},{10,... | collective-permute-start | bytes 6291464 | tf_op jit(solution)/shard_map/ppermute | solution.py:30
  617.7 56.4 %collective-permute-start.19 = (bf16[4,256,768]{2,1,0:T(8,128)(2,1)}, bf16[4,256,768]{2,1,0:T(8,128)(2,1)}, u32[]{:S(2)}, u32[]{:S(2)}) collective-permute-start(bf16[4,256,768]{2,1,0:T(8,128)(2,1)} %get-tuple-element.285.refs_5_), channel_id=1, source_target_pairs={{0,8},{24,16},{1,9},{25,17},{2,10},{26,18},{3,11},{27,19},{4,12},{... | collective-permute-start | bytes 4718600 | tf_op jit(solution)/shard_map/ppermute | solution.py:42
  659.0 46.7 %collective-permute-start.31 = (bf16[4,256,768]{2,1,0:T(8,128)(2,1)S(1)}, bf16[4,256,768]{2,1,0:T(8,128)(2,1)S(1)}, u32[]{:S(2)}, u32[]{:S(2)}) collective-permute-start(bf16[4,256,768]{2,1,0:T(8,128)(2,1)S(1)} %bitcast.191), channel_id=1, source_target_pairs={{8,16},{16,8},{9,17},{17,9},{10,18},{18,10},{11,19},{19,11},{12,20... | collective-permute-start | bytes 4718600 | tf_op jit(solution)/shard_map/ppermute | solution.py:46
  674.2 48.9 %collective-permute-start.29 = (bf16[2,256,2048]{2,1,0:T(8,128)(2,1)}, bf16[2,256,2048]{2,1,0:T(8,128)(2,1)}, u32[]{:S(2)}, u32[]{:S(2)}) collective-permute-start(bf16[2,256,2048]{2,1,0:T(8,128)(2,1)} %get-tuple-element.229), channel_id=1, source_target_pairs={{0,2},{1,3},{2,0},{3,1},{4,6},{5,7},{6,4},{7,5},{8,10},{9,11},{10,... | collective-permute-start | bytes 6291464 | tf_op jit(solution)/shard_map/ppermute | solution.py:30
  675.6 56.2 %collective-permute-start.30 = (bf16[2,256,2048]{2,1,0:T(8,128)(2,1)}, bf16[2,256,2048]{2,1,0:T(8,128)(2,1)}, u32[]{:S(2)}, u32[]{:S(2)}) collective-permute-start(bf16[2,256,2048]{2,1,0:T(8,128)(2,1)} %get-tuple-element.230), channel_id=1, source_target_pairs={{0,4},{1,5},{2,6},{3,7},{4,0},{5,1},{6,2},{7,3},{8,12},{9,13},{10,... | collective-permute-start | bytes 6291464 | tf_op jit(solution)/shard_map/ppermute | solution.py:30
  677.4 26.7 %collective-permute-start.32 = (bf16[256,2048]{1,0:T(8,128)(2,1)S(1)}, bf16[256,2048]{1,0:T(8,128)(2,1)S(1)}, u32[]{:S(2)}, u32[]{:S(2)}) collective-permute-start(bf16[256,2048]{1,0:T(8,128)(2,1)S(1)} %shard_map.312.refs_0_), channel_id=1, source_target_pairs={{8,0},{16,24},{9,1},{17,25},{10,2},{18,26},{11,3},{19,27},{12,4},{... | collective-permute-start | bytes 3145736 | tf_op jit(solution)/shard_map/ppermute | solution.py:50
  678.9 23.5 %collective-permute-start.27 = (f32[2048]{0:T(1024)S(1)}, f32[2048]{0:T(1024)S(1)}, u32[]{:S(2)}, u32[]{:S(2)}) collective-permute-start(f32[2048]{0:T(1024)S(1)} %copy-done.45), channel_id=1, source_target_pairs={{0,8},{8,0},{16,24},{24,16},{1,9},{9,1},{17,25},{25,17},{2,10},{10... | collective-permute-start | bytes 24584 | tf_op jit(solution)/shard_map/ppermute | solution.py:758
  702.4 36.5 %collective-permute-start.26 = (bf16[4,256,768]{2,1,0:T(8,128)(2,1)}, bf16[4,256,768]{2,1,0:T(8,128)(2,1)}, u32[]{:S(2)}, u32[]{:S(2)}) collective-permute-start(bf16[4,256,768]{2,1,0:T(8,128)(2,1)} %bitcast.73), channel_id=1, source_target_pairs={{8,16},{16,8},{9,17},{17,9},{10,18},{18,10},{11,19},{19,11},{12,20... | collective-permute-start | bytes 4718600 | tf_op jit(solution)/shard_map/ppermute | solution.py:46
  705.2 39.0 %collective-permute-start.36 = (bf16[2048,256]{1,0:T(8,128)(2,1)}, bf16[2048,256]{1,0:T(8,128)(2,1)}, u32[]{:S(2)}, u32[]{:S(2)}) collective-permute-start(bf16[2048,256]{1,0:T(8,128)(2,1)} %shard_map.314), channel_id=1, source_target_pairs={{0,4},{1,5},{2,6},{3,7},{4,0},{5,1},{6,2},{7,3},{8,12},{9,13},{10,... | collective-permute-start | bytes 3145736 | tf_op jit(solution)/shard_map/ppermute | solution.py:30
  706.8 37.4 %collective-permute-start.37 = (bf16[2048,256]{1,0:T(8,128)(2,1)}, bf16[2048,256]{1,0:T(8,128)(2,1)}, u32[]{:S(2)}, u32[]{:S(2)}) collective-permute-start(bf16[2048,256]{1,0:T(8,128)(2,1)} %shard_map.315), channel_id=1, source_target_pairs={{0,2},{1,3},{2,0},{3,1},{4,6},{5,7},{6,4},{7,5},{8,10},{9,11},{10,... | collective-permute-start | bytes 3145736 | tf_op jit(solution)/shard_map/ppermute | solution.py:30
  723.0 15.8 %collective-permute-start.28 = (f32[2048]{0:T(1024)S(1)}, f32[2048]{0:T(1024)S(1)}, u32[]{:S(2)}, u32[]{:S(2)}) collective-permute-start(f32[2048]{0:T(1024)S(1)} %fusion.36), channel_id=1, source_target_pairs={{0,16},{8,24},{16,0},{24,8},{1,17},{9,25},{17,1},{25,9},{2,18},{10... | collective-permute-start | bytes 24584 | tf_op jit(solution)/shard_map/ppermute | solution.py:816
  731.8 39.7 %collective-permute-start.35 = (bf16[4,256,768]{2,1,0:T(8,128)(2,1)}, bf16[4,256,768]{2,1,0:T(8,128)(2,1)}, u32[]{:S(2)}, u32[]{:S(2)}) collective-permute-start(bf16[4,256,768]{2,1,0:T(8,128)(2,1)} %bitcast.77.refs_0_), channel_id=1, source_target_pairs={{8,0},{16,24},{9,1},{17,25},{10,2},{18,26},{11,3},{19,27},{12,4},{... | collective-permute-start | bytes 4718600 | tf_op jit(solution)/shard_map/ppermute | solution.py:50
  742.9 65.1 %collective-permute-start.38 = (bf16[4,256,768]{2,1,0:T(8,128)(2,1)}, bf16[4,256,768]{2,1,0:T(8,128)(2,1)}, u32[]{:S(2)}, u32[]{:S(2)}) collective-permute-start(bf16[4,256,768]{2,1,0:T(8,128)(2,1)} %bitcast.82.refs_2_), channel_id=1, source_target_pairs={{8,0},{16,24},{9,1},{17,25},{10,2},{18,26},{11,3},{19,27},{12,4},{... | collective-permute-start | bytes 4718600 | tf_op jit(solution)/shard_map/ppermute | solution.py:50
  744.2 24.4 %collective-permute-start.33 = (bf16[256,2048]{1,0:T(8,128)(2,1)}, bf16[256,2048]{1,0:T(8,128)(2,1)}, u32[]{:S(2)}, u32[]{:S(2)}) collective-permute-start(bf16[256,2048]{1,0:T(8,128)(2,1)} %shard_map.320), channel_id=1, source_target_pairs={{0,4},{1,5},{2,6},{3,7},{4,0},{5,1},{6,2},{7,3},{8,12},{9,13},{10,... | collective-permute-start | bytes 3145736 | tf_op jit(solution)/shard_map/ppermute | solution.py:30
  745.7 22.9 %collective-permute-start.34 = (bf16[256,2048]{1,0:T(8,128)(2,1)S(1)}, bf16[256,2048]{1,0:T(8,128)(2,1)}, u32[]{:S(2)}, u32[]{:S(2)}) collective-permute-start(bf16[256,2048]{1,0:T(8,128)(2,1)S(1)} %shard_map.321), channel_id=1, source_target_pairs={{0,2},{1,3},{2,0},{3,1},{4,6},{5,7},{6,4},{7,5},{8,10},{9,11},{10,... | collective-permute-start | bytes 3145736 | tf_op jit(solution)/shard_map/ppermute | solution.py:30
  747.9 19.9 %all-to-all-start.4 = ((f32[8,1,2048]{2,1,0:T(1,128)}), f32[8,1,2048]{2,1,0:T(1,128)}, u32[]{:S(2)}, u32[]{:S(2)}) async-start(f32[8,1,2048]{2,1,0:T(1,128)} %broadcast_in_dim.196), calls=%async_computation.4 | async-start | bytes 131072 | tf_op jit(solution)/shard_map/all_to_all | solution.py:598
  (80 other events, 787.1 us)
Sparse Core Ops, SparseCore 0:
  12.7 117.0 all-gather.4
  132.3 89.8 all-gather.2

commit v3 on v2

--- a/solution.py
+++ b/solution.py
@@ -92,7 +92,7 @@
 def attention_kernel(
     piece_of, inner_of, first_of, end_of,
     qkv_ref, grad_ref, cos_ref, sin_ref,
-    ctx_ref, out_ref,
+    ctx_ref, out_ref, sum_ref,
     q_buf, k_buf, v_buf, g_buf, dk_buf, dv_buf,
 ):
     m = pl.program_id(0)
@@ -102,6 +102,11 @@
 
     def turned(x):
         return jnp.where(lane < ROT // 2, pltpu.roll(x, 128 - ROT // 2, 1), pltpu.roll(x, ROT // 2, 1))
+
+    def store_part(p, i, start, value):
+        low = value.astype(bf16)
+        out_ref[p, 0, i, :, start:start + value.shape[1]] = low
+        sum_ref[0, 0:1, start:start + value.shape[1]] += jnp.sum(low.astype(f32), axis=0, keepdims=True)
 
     def block_rows(g):
         return pl.ds(pl.multiple_of(g * BLK, BLK), BLK)
@@ -122,6 +127,7 @@
     lax.fori_loop(0, blocks, load, 0)
     for buf in (q_buf, k_buf, v_buf, g_buf):
         buf[blocks * BLK:, :] = jnp.zeros((BLK, HD), bf16)
+    sum_ref[...] = jnp.zeros(sum_ref.shape, f32)
     dk_buf[...] = jnp.zeros(dk_buf.shape, f32)
     dv_buf[...] = jnp.zeros(dv_buf.shape, f32)
 
@@ -157,10 +163,8 @@
             at = block - first
             ctx_ref[p, 0, i] = ctx[lo:lo + BLK]
             front = query_grad[lo:lo + BLK, 0:128]
-            out_ref[p, 0, i, :, 0:128] = (
-                front * cos_ref[at] - turned(front) * sin_ref[at]
-            ).astype(bf16)
-            out_ref[p, 0, i, :, 128:HD] = query_grad[lo:lo + BLK, 128:].astype(bf16)
+            store_part(p, i, 0, front * cos_ref[at] - turned(front) * sin_ref[at])
+            store_part(p, i, 128, query_grad[lo:lo + BLK, 128:])
 
         put(g, 0)
         pl.when(second)(lambda: put(after_g, BLK))
@@ -178,11 +182,9 @@
         at = g - first_of[m, g]
         rows = block_rows(g)
         front = dk_buf[rows, 0:128] * SCALE
-        out_ref[p, 0, i, :, HD:HD + 128] = (
-            front * cos_ref[at] - turned(front) * sin_ref[at]
-        ).astype(bf16)
-        out_ref[p, 0, i, :, HD + 128:2 * HD] = (dk_buf[rows, 128:HD] * SCALE).astype(bf16)
-        out_ref[p, 0, i, :, 2 * HD:] = dv_buf[rows, :].astype(bf16)
+        store_part(p, i, HD, front * cos_ref[at] - turned(front) * sin_ref[at])
+        store_part(p, i, HD + 128, dk_buf[rows, 128:HD] * SCALE)
+        store_part(p, i, 2 * HD, dv_buf[rows, :])
         return carry
 
     lax.fori_loop(0, blocks, store, 0)
@@ -203,7 +205,7 @@
             num_scalar_prefetch=4,
             grid=(MB,),
             in_specs=[part(3 * HD), part(HD), whole, whole],
-            out_specs=[part(HD), part(3 * HD)],
+            out_specs=[part(HD), part(3 * HD), spec((1, 8, 3 * HD), lambda m, *_: (m, 0, 0))],
             scratch_shapes=[
                 pltpu.VMEM((rows, HD), bf16),
                 pltpu.VMEM((rows, HD), bf16),
@@ -216,6 +218,7 @@
         out_shape=[
             jax.ShapeDtypeStruct((pieces, MB, own, BLK, HD), bf16),
             jax.ShapeDtypeStruct((pieces, MB, own, BLK, 3 * HD), bf16),
+            jax.ShapeDtypeStruct((MB, 8, 3 * HD), f32),
         ],
         compiler_params=params_of(),
         cost_estimate=cost(0),
@@ -228,14 +231,15 @@
         a, b, index = a[None], b[None], 0
     a, b = [x.reshape(x.shape[0], -1, x.shape[-1]) for x in (a, b)]
     rows, cols = a.shape[1:]
-    block = spec((1, rows // 4, cols), lambda i: (index, i, 0))
+    steps = 2 if rows % 32 == 0 else 1
+    block = spec((1, rows // steps, cols), lambda i: (index, i, 0))
 
     def body(a_ref, b_ref, out_ref):
         out_ref[...] = plus(a_ref[0], b_ref[0]).astype(bf16)
 
     return pl.pallas_call(
-        body, grid=(4,), in_specs=[block, block],
-        out_specs=spec((rows // 4, cols), lambda i: (i, 0)),
+        body, grid=(steps,), in_specs=[block, block],
+        out_specs=spec((rows // steps, cols), lambda i: (i, 0)),
         out_shape=jax.ShapeDtypeStruct((rows, cols), bf16),
         compiler_params=params_of(32), cost_estimate=cost(0),
     )(a, b).reshape(shape)
@@ -364,54 +368,155 @@
     )(owners, *args)
 
 
-def token_dot(left, right, part=0, parts=1):
+def token_dot(left, right, part=0, parts=1, extra=None):
     rows, width = left.shape[0], left.shape[1] // parts
     blocks, _, cols = right.shape
     step = 512 // cols
-
-    def body(left_ref, right_ref, out_ref):
+    more = [] if extra is None else [extra]
+    total = width + sum(m.shape[0] for m in more)
+
+    def body(left_ref, right_ref, *refs):
+        out_ref = refs[-1]
         for b in range(step):
-            out_ref[:, b * cols:(b + 1) * cols] = dot(left_ref[...], right_ref[b], 0, 0).astype(bf16)
+            at = slice(b * cols, (b + 1) * cols)
+            out_ref[0:width, at] = dot(left_ref[...], right_ref[b], 0, 0).astype(bf16)
+        if more:
+            out_ref[width:, :] = refs[0][...]
 
     return pl.pallas_call(
         body, grid=(blocks // step,),
         in_specs=[
             spec((rows, width), lambda i: (0, part)),
             spec((step, rows, cols), lambda i: (i, 0, 0)),
-        ],
-        out_specs=spec((width, step * cols), lambda i: (0, i)),
-        out_shape=jax.ShapeDtypeStruct((width, blocks * cols), bf16),
+        ] + [spec((m.shape[0], step * cols), lambda i: (0, i)) for m in more],
+        out_specs=spec((total, step * cols), lambda i: (0, i)),
+        out_shape=jax.ShapeDtypeStruct((total, blocks * cols), bf16),
         compiler_params=params_of(56), cost_estimate=cost(0),
-    )(left, right)
-
-
-def normed_dot(normed, right, sums=False, part=0, parts=1):
+    )(left, right, *more)
+
+
+EXTRA = 16
+
+
+def normed_dot(spot, shards, normed, right, sums, part=0, parts=1):
     rows, tile = normed.shape[0], 512
-
-    def body(left_ref, right_ref, out_ref, *rest):
-        out_ref[...] = dot(left_ref[...], right_ref[...], 0, 0).astype(bf16)
-        if sums:
-            @pl.when(pl.program_id(0) == 0)
-            def _():
-                rest[0][...] = jnp.sum(right_ref[...].astype(f32), axis=0, keepdims=True)
-
-    width = right.shape[1] // parts
-    out_specs = [spec((tile, width), lambda i: (i, 0))]
-    out_shape = [jax.ShapeDtypeStruct((D, width), bf16)]
-    if sums:
-        out_specs.append(spec((1, width), lambda i: (0, 0)))
-        out_shape.append(jax.ShapeDtypeStruct((1, width), f32))
-    found = pl.pallas_call(
-        body, grid=(D // tile,),
-        in_specs=[spec((rows, tile), lambda i: (0, i)), spec((rows, width), lambda i: (0, part))],
-        out_specs=out_specs, out_shape=out_shape,
+    cols, width = D // shards, right.shape[1] // parts
+    per = tile // cols
+
+    def body(spot_ref, left_ref, right_ref, sum_ref, out_ref):
+        sums = dot(left_ref[...], right_ref[...], 0, 0).astype(bf16)
+        high = sum_ref[...]
+        first = high.astype(bf16).astype(f32)
+        second = (high - first).astype(bf16).astype(f32)
+        third = high - first - second
+        row = lax.broadcasted_iota(jnp.int32, (EXTRA, width), 0) - 3 * spot_ref[0]
+        extra = jnp.where(row == 0, first, jnp.where(row == 1, second, jnp.where(row == 2, third, 0.0)))
+        for b in range(per):
+            out_ref[b, 0:cols, :] = sums[b * cols:(b + 1) * cols]
+            out_ref[b, cols:, :] = extra.astype(bf16)
+
+    return pl.pallas_call(
+        body,
+        grid_spec=pltpu.PrefetchScalarGridSpec(
+            num_scalar_prefetch=1, grid=(D // tile,),
+            in_specs=[
+                spec((rows, tile), lambda i, z: (0, i)),
+                spec((rows, width), lambda i, z: (0, part)),
+                spec((1, width), lambda i, z: (0, part)),
+            ],
+            out_specs=spec((per, cols + EXTRA, width), lambda i, z: (i, 0, 0)),
+        ),
+        out_shape=jax.ShapeDtypeStruct((shards, cols + EXTRA, width), bf16),
         compiler_params=params_of(56), cost_estimate=cost(0),
-    )(normed, right)
-    return found if sums else found[0]
+    )(spot, normed, right, sums)
 
 
 def whole_rows(ref):
     return jnp.concatenate([ref[b] for b in range(ref.shape[0])], axis=1)
+
+
+def out_blocks(piece_of, inner_of, own, parts, bias):
+    blocks = piece_of.shape[1]
+    half, cols = parts[0][2].shape
+
+    def body(piece_ref, inner_ref, *refs):
+        bias_ref, out_ref, all_rows = refs[6:]
+        m = pl.program_id(0)
+
+        @pl.when(m == 0)
+        def _():
+            for h in range(2):
+                keep, came, last = refs[3 * h:3 * h + 3]
+                sums = plus(keep[0], came[0]) + last[...].astype(f32) + bias_ref[...]
+                all_rows[h * half:(h + 1) * half, :] = sums.astype(bf16)
+
+        def one(g, carry):
+            row = ((piece_ref[m, g] * MB + m) * own + inner_ref[m, g]) * BLK
+            out_ref[0, g] = all_rows[pl.ds(pl.multiple_of(row, BLK), BLK), :]
+            return carry
+
+        lax.fori_loop(0, blocks, one, 0)
+
+    first = spec((1, half, cols), lambda m, *_: (0, 0, 0))
+    whole = spec((half, cols), lambda m, *_: (0, 0))
+    return pl.pallas_call(
+        body,
+        grid_spec=pltpu.PrefetchScalarGridSpec(
+            num_scalar_prefetch=2, grid=(MB,),
+            in_specs=[first, first, whole] * 2 + [spec((1, cols), lambda m, *_: (0, 0))],
+            out_specs=spec((1, blocks, BLK, cols), lambda m, *_: (m, 0, 0, 0)),
+            scratch_shapes=[pltpu.VMEM((2 * half, cols), bf16)],
+        ),
+        out_shape=jax.ShapeDtypeStruct((MB, blocks, BLK, cols), bf16),
+        compiler_params=params_of(), cost_estimate=cost(0),
+    )(piece_of, inner_of, *parts[0], *parts[1], bias[None])
+
+
+def token_grads(tokens, grad_rows, parts):
+    rows = tokens.shape[0]
+    n = rows // 4
+
+    def body(tokens_ref, grad_ref, *refs):
+        out_ref = refs[6]
+        x = tokens_ref[...].astype(f32)
+        center = x - jnp.mean(x, axis=1, keepdims=True)
+        inv_std = lax.rsqrt(jnp.mean(center * center, axis=1, keepdims=True) + EPS)
+        normed = center * inv_std
+
+        def finish(keep, came, last):
+            grad = plus(keep[0], came[0]) + last[...].astype(f32)
+            mean = jnp.mean(grad, axis=1, keepdims=True)
+            proj = jnp.mean(grad * normed, axis=1, keepdims=True)
+            grad = inv_std * (grad - mean - normed * proj)
+            out_ref[...] = (grad_ref[...].astype(f32) + grad).astype(bf16)
+
+        pl.when(pl.program_id(0) < 2)(lambda: finish(*refs[0:3]))
+        pl.when(pl.program_id(0) >= 2)(lambda: finish(*refs[3:6]))
+
+    own = spec((n, D), lambda i: (i, 0))
+    in_specs = [own, own]
+    for at in (lambda i: jnp.minimum(i, 1), lambda i: jnp.maximum(i - 2, 0)):
+        first = spec((1, n, D), lambda i, at=at: (0, at(i), 0))
+        in_specs += [first, first, spec((n, D), lambda i, at=at: (at(i), 0))]
+    return pl.pallas_call(
+        body, grid=(4,), in_specs=in_specs, out_specs=own,
+        out_shape=jax.ShapeDtypeStruct((rows, D), bf16),
+        compiler_params=params_of(), cost_estimate=cost(0),
+    )(tokens, grad_rows, *parts[0], *parts[1])
+
+
+def sum_rows(vector, spot):
+    thirds, left = [], vector
+    for _ in range(3):
+        thirds.append(lax.reduce_precision(left, 8, 7))
+        left = left - thirds[-1]
+    mine = jnp.arange(4)[:, None, None] == spot
+    values = jnp.where(mine, jnp.stack(thirds)[None], 0.0).reshape(-1)
+    return jnp.pad(values, (0, 16 * D - values.shape[0])).reshape(16, D).astype(bf16)
+
+
+def sums_of(found, size):
+    return jnp.sum(found.astype(f32).reshape(-1)[:12 * size].reshape(12, size), axis=0)
 
 
 def hidden_back(grad_out, down_w, slope):
@@ -466,8 +571,8 @@
     )(grad_out, out_w)
 
 
-def row_grads(inner, chunks):
-    rows = [c[0].shape[0] for c in chunks]
+def row_grads(inner, chunks, count=None):
+    rows = [count or c[0].shape[0] for c in chunks]
     total, cols = sum(rows), 512
 
     def body(inner_ref, *refs):
@@ -489,7 +594,7 @@
     )(inner, *[a for c in chunks for a in c])
 
 
-def column_grads(inner, chunks, weight, gain, shift, totals, run, step, by_run, token=None):
+def column_grads(inner, chunks, weight, gain, shift, run, step, by_run, token=None):
     rows, each = weight.shape[0], len(chunks[0])
     if by_run:
         groups, per = len(chunks), chunks[0][0].shape[0] // step
@@ -502,7 +607,7 @@
 
     def body(inner_ref, *refs):
         pairs, refs = refs[:each * len(chunks)], refs[each * len(chunks) + len(tokens):]
-        w_ref, t_ref, gain_ref, shift_ref, grads, gain_out, shift_out = refs[-7:]
+        w_ref, gain_ref, shift_ref, grads, gain_out, shift_out, t_out = refs
         i, k = pl.program_id(0), pl.program_id(1)
 
         @pl.when((i == 0) & (k == 0))
@@ -519,7 +624,9 @@
                         other = pairs[2 * c + 1][j].astype(f32)
                         value = jnp.where(inner_ref[0] == 1, value, other)
                     at = slice(j * run, (j + 1) * run)
-                    w, t = w_ref[:, at].astype(f32), t_ref[:, at]
+                    t = jnp.sum(value[rows:], axis=0, keepdims=True)
+                    value, w = value[:rows], w_ref[:, at].astype(f32)
+                    t_out[:, at] = t
                     grads[:, at] = gain_ref[...] * value + shift_ref[...] * t
                     for out, terms in ((gain_out, w * value), (shift_out, w * t)):
                         out[...] += sum(terms[:, lo:lo + 128] for lo in range(0, run, 128))
@@ -534,26 +641,30 @@
 
     column = spec((rows, 1), lambda i, k, *_: (0, 0))
     wide_column = spec((rows, 128), lambda i, k, *_: (0, 0))
-    grads, gain_grad, shift_grad = pl.pallas_call(
+    grads, gain_grad, shift_grad, totals = pl.pallas_call(
         body,
         grid_spec=pltpu.PrefetchScalarGridSpec(
             num_scalar_prefetch=1, grid=(steps, groups),
-            in_specs=[spec((step, rows, run), part_index(c)) for c in range(len(chunks)) for _ in range(each)]
+            in_specs=[spec((step, rows + EXTRA, run), part_index(c)) for c in range(len(chunks)) for _ in range(each)]
             + [pl.BlockSpec(memory_space=pl.ANY)] * len(tokens)
-            + [spec((rows, step * run), columns), spec((1, step * run), columns), column, column],
-            out_specs=[spec((rows, step * run), columns), wide_column, wide_column],
+            + [spec((rows, step * run), columns), column, column],
+            out_specs=[
+                spec((rows, step * run), columns), wide_column, wide_column,
+                spec((1, step * run), columns),
+            ],
         ),
         out_shape=[
             jax.ShapeDtypeStruct(weight.shape, f32),
             jax.ShapeDtypeStruct((rows, 128), f32),
             jax.ShapeDtypeStruct((rows, 128), f32),
+            jax.ShapeDtypeStruct((1, weight.shape[1]), f32),
         ],
         compiler_params=params_of(32), cost_estimate=cost(0),
     )(
-        inner, *[a for c in chunks for a in c], *tokens, weight, totals[None],
+        inner, *[a for c in chunks for a in c], *tokens, weight,
         gain.astype(f32)[:, None], shift.astype(f32)[:, None],
     )
-    return grads, jnp.sum(gain_grad, axis=1), jnp.sum(shift_grad, axis=1)
+    return grads, jnp.sum(gain_grad, axis=1), jnp.sum(shift_grad, axis=1), totals[0]
 
 
 def local(
@@ -649,7 +760,6 @@
     gate(up_send, qkv_send, cot_late)
     found = late(found)
     biases = jnp.sum(found[:, part_rows:part_rows + 2].astype(f32), axis=(0, 1))
-    bias_up, bias_qkv = biases[:wide] + up_bias.astype(f32), biases[wide:]
 
     def exchange(part):
         return [part] + [
@@ -668,10 +778,11 @@
         return array.reshape(D, width)
 
     up_parts = exchange(found[:, :part_rows, :wide])
-    gate(up_parts[0], biases)
-    qkv_parts = exchange(late(found)[:, :part_rows, wide:])
-    normed, up_parts = late((normed, up_parts))
+    normed, up_parts, biases = tie(normed, up_parts, biases)
     up_w = whole(up_parts)
+    found, up_w = tie(found, up_w)
+    qkv_parts = exchange(found[:, :part_rows, wide:])
+    bias_up, bias_qkv = biases[:wide] + up_bias.astype(f32), biases[wide:]
     out_w, down_w, resid = out_weight, down_weight, tokens.reshape(own_rows, D)
 
     hidden = dot(normed, up_w, 1, 0) + bias_up
@@ -681,17 +792,18 @@
     slope = cdf + hidden * density
     grad_out, active = tie(grad_out, active)
 
-    def spread(grads):
-        return swap(grads.reshape(shards, cols, grads.shape[-1]))
+    where_rep = jnp.asarray(spot, jnp.int32).reshape(1)
 
     down_parts = [token_dot(active, grad_out, 0, 2)]
     down_came = [rep_in(down_parts[0])]
     gate(down_parts[0])
-    down_parts.append(token_dot(late(active), grad_out, 1, 2))
-    grad_out, down_parts[1] = tie(grad_out, down_parts[1])
-    hidden_grad, sum_hidden = hidden_back(grad_out, down_w, slope)
-    up_terms = [normed_dot(normed, hidden_grad, False, 0, 2)]
-    up_found = [spread(up_terms[0])]
+    hidden_grad, sum_hidden = hidden_back(late(grad_out), down_w, slope)
+    sum_cot = jnp.sum(cot_own, axis=tuple(range(cot_own.ndim - 1)), dtype=f32)
+    extra = sum_rows(sum_cot, spot) if cube else None
+    down_parts.append(token_dot(active, grad_out, 1, 2, extra))
+    hidden_grad, down_parts[1] = tie(hidden_grad, down_parts[1])
+    up_terms = [normed_dot(where_rep, shards, normed, hidden_grad, sum_hidden, 0, 2)]
+    up_found = [swap(up_terms[0])]
     down_came[0], up_terms[0] = tie(down_came[0], up_terms[0])
     down_pair = [plus_low(down_parts[0], down_came[0])]
     down_other = [rep_over(down_pair[0])]
@@ -702,7 +814,7 @@
     if split > 1:
         pairs = [list(range(h * split, (h + 1) * split)) for h in range(HEADS)]
         context_w = lax.all_gather(out_w, "shard", axis=0, tiled=True, axis_index_groups=pairs)
-    up_terms.append(normed_dot(late(normed), hidden_grad, False, 1, 2))
+    up_terms.append(normed_dot(where_rep, shards, late(normed), hidden_grad, sum_hidden, 1, 2))
     grad_out, up_terms[1] = tie(grad_out, up_terms[1])
     context_grad = head_back(grad_out, context_w)
     qkv_parts, context_grad = tie(qkv_parts, context_grad)
@@ -715,10 +827,10 @@
     down_other.append(rep_over(down_pair[1]))
     up_came = [rep_in(up_found[0])]
     up_terms[1], up_found[0] = tie(up_terms[1], up_found[0])
-    up_found.append(spread(up_terms[1]))
+    up_found.append(swap(up_terms[1]))
     gate(down_total[0], down_pair[1], up_found[0])
     cosine, sine = rotary_tables()
-    context, mixed_grad = attention(
+    context, mixed_grad, sum_mixed = attention(
         tables,
         late(mixed).reshape(shards, MB, own, BLK, 3 * HD),
         context_grad.reshape(shards, MB, own, BLK, HD),
@@ -741,21 +853,11 @@
         context = lax.dynamic_slice_in_dim(context, share * (HD // split), HD // split, 1)
         mixed_grad = lax.dynamic_slice_in_dim(mixed_grad, share * share_cols, share_cols, 1)
         qkv_w = lax.dynamic_slice_in_dim(qkv_w, share * share_cols, share_cols, 1)
-    qkv_terms, sum_mixed = normed_dot(normed, mixed_grad, True)
-    qkv_found = spread(qkv_terms)
-    sum_cot = jnp.sum(cot_own, axis=tuple(range(cot_own.ndim - 1)), dtype=f32)
-    small = jnp.concatenate([sum_mixed[0], sum_hidden[0], sum_cot])
-
-    def bias_grads(small):
-        sum_qkv = small[:, :share_cols].reshape(HEADS, 3, HD).transpose(1, 0, 2).reshape(3 * D)
-        sum_up = small[:, share_cols:share_cols + wide].reshape(FF)
-        out_bias_grad = lax.dynamic_index_in_dim(small[:, share_cols + wide:], place, 0, keepdims=False)
-        qkv_bias_grad = lax.dynamic_slice_in_dim(sum_qkv, place * 3 * cols, 3 * cols)
-        up_bias_grad = lax.dynamic_slice_in_dim(sum_up, place * wide, wide)
-        return sum_qkv, sum_up, out_bias_grad, qkv_bias_grad, up_bias_grad
-
+        sum_mixed = lax.dynamic_slice_in_dim(sum_mixed, share * share_cols, share_cols, 2)
+    sum_mixed = jnp.sum(sum_mixed, axis=(0, 1))[None]
+    qkv_terms = normed_dot(where_rep, shards, normed, mixed_grad, sum_mixed)
+    qkv_found = swap(qkv_terms)
     if cube:
-        small_came = lax.ppermute(small, "rep", [(i, i ^ 1) for i in range(4)])
         context, qkv_terms = tie(context, qkv_terms)
         out_part = token_dot(context, grad_out)
         out_came = rep_in(out_part)
@@ -768,7 +870,7 @@
         up_back = [rep_out(up_total[0])]
         up_pair.append(plus_low(up_found[1], up_came[1]))
         up_other.append(rep_over(up_pair[1]))
-        gate(down_back[1], up_total[0], up_pair[1], small, qkv_terms, odd)
+        gate(down_back[1], up_total[0], up_pair[1], qkv_terms, odd)
 
         norm_odd = norm_terms(owners, late(mixed_grad), hidden_grad, qkv_w, up_w)
         norm_odd_came = flip(norm_odd, 1)
@@ -782,79 +884,76 @@
         )
         up_total.append(plus_low(up_pair[1], up_other[1]))
         up_back.append(rep_out(up_total[1]))
+        qkv_parts = [qkv_found[:shards // 2], qkv_found[shards // 2:]]
+        qkv_came = [rep_in(qkv_parts[0])]
+        gate(up_back[0], up_total[1], out_came, *qkv_parts, norm_odd, send_one)
+
+        norm_send_one, norm_keep_one, norm_send_two, norm_keep_two = norm_terms(
+            owners, mixed_grad, hidden_grad, qkv_w, up_w, late(norm_odd_came)
+        )
+        norm_got_one, norm_got_two = flip(norm_send_one, 2), flip(norm_send_two, 4)
+
+        qkv_came[0], norm_keep_one = tie(qkv_came[0], norm_keep_one)
+        qkv_pair = [plus_low(qkv_parts[0], qkv_came[0])]
+        qkv_other = [rep_over(qkv_pair[0])]
+        qkv_parts[1], out_came, qkv_pair[0] = tie(qkv_parts[1], out_came, qkv_pair[0])
+        qkv_came.append(rep_in(qkv_parts[1]))
+        got_one, got_two, out_came = tie(got_one, got_two, out_came)
         out_pair = plus_low(out_part, out_came)
         out_other = rep_over(out_pair)
-        qkv_parts = [qkv_found[:shards // 2], qkv_found[shards // 2:]]
-        qkv_came = [rep_in(part) for part in qkv_parts]
-        gate(up_back[0], up_total[1], out_pair, *qkv_parts, norm_odd, send_one)
-
-        norm_send_one, norm_keep_one, norm_send_two, norm_keep_two = norm_terms(
-            owners, mixed_grad, hidden_grad, qkv_w, up_w, late(norm_odd_came)
-        )
-        norm_got_one, norm_got_two = flip(norm_send_one, 2), flip(norm_send_two, 4)
-
-        out_other, qkv_came[0], norm_keep_one = tie(out_other, qkv_came[0], norm_keep_one)
-        out_total = plus_low(out_pair, out_other)
-        out_back = rep_out(out_total)
-        qkv_pair = [plus_low(qkv_parts[0], qkv_came[0])]
-        qkv_other = [rep_over(qkv_pair[0])]
-        got_one, got_two, up_back[1], out_total, qkv_pair[0] = tie(
-            got_one, got_two, up_back[1], out_total, qkv_pair[0]
-        )
+        keep_one, keep_two, out_pair = tie(keep_one, keep_two, out_pair)
         last_one = plus_low(keep_one, got_one, 1)
         last_two = plus_low(keep_two, got_two, 1)
-        qkv_came[1], last_one, last_two, up_back[1] = tie(qkv_came[1], last_one, last_two, up_back[1])
-        last_one, last_two = flip(last_one, 4), flip(last_two, 2)
+        down_late, grad_late, last_one, last_two = tie(
+            list(zip(down_total, down_back)), grad_out, last_one, last_two
+        )
+        inner = ((spot == 1) | (spot == 2)).astype(jnp.int32).reshape(1)
+        down_grad = row_grads(inner, down_late, wide // 2)
+        grad_rows = lax.dynamic_slice_in_dim(grad_late, place * own_rows, own_rows, 1)
+        grad_rows = grad_rows.transpose(1, 0, 2).reshape(own_rows, D)
+        qkv_other[0], down_grad, grad_rows = tie(qkv_other[0], down_grad, grad_rows)
+        qkv_total = [plus_low(qkv_pair[0], qkv_other[0])]
+        qkv_back = [rep_out(qkv_total[0])]
+        qkv_came[1], qkv_total[0] = tie(qkv_came[1], qkv_total[0])
         qkv_pair.append(plus_low(qkv_parts[1], qkv_came[1]))
         qkv_other.append(rep_over(qkv_pair[1]))
-        down_late, small_came, qkv_pair[1] = tie(
-            list(zip(down_total, down_back)), small_came, qkv_pair[1]
-        )
-        inner = ((spot == 1) | (spot == 2)).astype(jnp.int32).reshape(1)
-        down_grad = row_grads(inner, down_late)
-        small_pair = small + small_came
-        small_other = lax.ppermute(small_pair, "rep", [(i, i ^ 2) for i in range(4)])
-        qkv_other[0], out_back, down_grad, small_pair = tie(qkv_other[0], out_back, down_grad, small_pair)
-        qkv_total = [plus_low(qkv_pair[0], qkv_other[0])]
-        qkv_back = [rep_out(qkv_total[0])]
-        out_back, grad_late, qkv_total[0] = tie(out_back, grad_out, qkv_total[0])
-        out_grad = row_grads(inner, [(out_total, out_back)])
-        grad_rows = lax.dynamic_slice_in_dim(grad_late, place * own_rows, own_rows, 1)
-        grad_rows = grad_rows.transpose(1, 0, 2).reshape(own_rows, D)
-        norm_got_one, norm_got_two, out_grad, grad_rows = tie(
-            norm_got_one, norm_got_two, out_grad, grad_rows
-        )
+        up_back[1], qkv_pair[1] = tie(up_back[1], qkv_pair[1])
+        up_grad, gain_two_grad, shift_two_grad, sum_up = column_grads(
+            inner, list(zip(up_total, up_back)), up_weight, ln2_gain, ln2_bias, wide // 2, 1, True
+        )
+        norm_got_one, norm_got_two, up_grad = tie(norm_got_one, norm_got_two, up_grad)
         norm_last_one = plus_low(norm_keep_one, norm_got_one, 1)
         norm_last_two = plus_low(norm_keep_two, norm_got_two, 1)
-        qkv_other[1], small_other, norm_last_one, norm_last_two = tie(
-            qkv_other[1], small_other, norm_last_one, norm_last_two
+        qkv_other[1], qkv_back[0], norm_last_one, norm_last_two = tie(
+            qkv_other[1], qkv_back[0], norm_last_one, norm_last_two
         )
         norm_last_one, norm_last_two = flip(norm_last_one, 4), flip(norm_last_two, 2)
         qkv_total.append(plus_low(qkv_pair[1], qkv_other[1]))
         qkv_back.append(rep_out(qkv_total[1]))
-        small_pair = small_pair + small_other
-        small = swap(jnp.broadcast_to(small_pair[None], (shards,) + small_pair.shape))
-        last_one, last_two, qkv_total[1], small_pair = tie(last_one, last_two, qkv_total[1], small_pair)
-        out_own = jnp.concatenate(
-            [
-                plus(keep_one[0], got_one[0]) + last_one.astype(f32),
-                plus(keep_two[0], got_two[0]) + last_two.astype(f32),
-            ],
-            axis=0,
-        )
-        norm_last_one, norm_last_two, qkv_back[0], out_own = tie(
-            norm_last_one, norm_last_two, qkv_back[0], out_own
-        )
-        normed_grad = jnp.concatenate(
-            [
-                plus(norm_keep_one[0], norm_got_one[0]) + norm_last_one.astype(f32),
-                plus(norm_keep_two[0], norm_got_two[0]) + norm_last_two.astype(f32),
-            ],
-            axis=0,
-        )
+        out_other, last_one, last_two, qkv_total[1] = tie(out_other, last_one, last_two, qkv_total[1])
+        last_one, last_two = flip(last_one, 4), flip(last_two, 2)
+        out_total = plus_low(out_pair, out_other)
+        out_back = rep_out(out_total)
+        norm_last_one, norm_last_two, out_total = tie(norm_last_one, norm_last_two, out_total)
+        tokens_grad = token_grads(
+            resid, grad_rows,
+            [(norm_keep_one, norm_got_one, norm_last_one), (norm_keep_two, norm_got_two, norm_last_two)],
+        )
+        last_one, last_two, tokens_grad = tie(last_one, last_two, tokens_grad)
+        out_given = out_blocks(
+            tables[0], tables[1], own, [(keep_one, got_one, last_one), (keep_two, got_two, last_two)],
+            out_bias.astype(f32) + down_bias.astype(f32),
+        )
+        found = jnp.where(inner == 1, down_total[1][wide // 2:], down_back[1][wide // 2:])
+        out_bias_grad = sums_of(found, cols)
+        qkv_back, out_given = tie(qkv_back, out_given)
     else:
-        small = lax.all_gather(lax.psum(small, "rep"), "shard")
-        sum_qkv, sum_up, out_bias_grad, qkv_bias_grad, up_bias_grad = bias_grads(small)
+        sums = jnp.concatenate([sum_mixed[0], sum_hidden[0]])
+        sums, out_bias_grad = lax.psum((sums, sum_cot), "rep")
+        sums = lax.all_gather(sums, "shard")
+        sum_qkv = sums[:, :share_cols].reshape(HEADS, 3, HD).transpose(1, 0, 2).reshape(3 * D)
+        sum_up = sums[:, share_cols:].reshape(FF)
+        qkv_found, up_found = qkv_found[:, :cols], [found[:, :cols] for found in up_found]
         out_sum, qkv_sum, up_sum, down_sum = lax.psum(
             (token_dot(context, grad_out), qkv_found, jnp.concatenate(up_found, axis=2), jnp.concatenate(down_parts)), "rep"
         )
@@ -873,26 +972,21 @@
         grad_rows = lax.dynamic_slice_in_dim(grad_out, place * own_rows, own_rows, 1)
         grad_rows = grad_rows.transpose(1, 0, 2).reshape(own_rows, D)
 
-    out_own = out_own + (out_bias.astype(f32) + down_bias.astype(f32))
-    out_own = out_own.astype(bf16).reshape(shards, MB, own, BLK, cols)
-    out_given = jnp.stack([out_own[piece_of[m], m, inner_of[m]] for m in range(MB)])
-
-    mean_grad = jnp.mean(normed_grad, axis=-1, keepdims=True)
-    mean_proj = jnp.mean(normed_grad * normed_own, axis=-1, keepdims=True)
-    tokens_grad = inv_std * (normed_grad - mean_grad - normed_own * mean_proj)
-    tokens_grad = grad_rows.astype(f32) + tokens_grad
-    tokens_grad = tokens_grad.astype(bf16).reshape(MB, own, BLK, D)
+        out_own = out_own + (out_bias.astype(f32) + down_bias.astype(f32))
+        out_own = out_own.astype(bf16).reshape(shards, MB, own, BLK, cols)
+        out_given = jnp.stack([out_own[piece_of[m], m, inner_of[m]] for m in range(MB)])
+        mean_grad = jnp.mean(normed_grad, axis=-1, keepdims=True)
+        mean_proj = jnp.mean(normed_grad * normed_own, axis=-1, keepdims=True)
+        tokens_grad = inv_std * (normed_grad - mean_grad - normed_own * mean_proj)
+        tokens_grad = (grad_rows.astype(f32) + tokens_grad).astype(bf16)
+    tokens_grad = tokens_grad.reshape(MB, own, BLK, D)
 
     if cube:
-        small, tokens_grad = tie(small, tokens_grad)
-        sum_qkv, sum_up, out_bias_grad, qkv_bias_grad, up_bias_grad = bias_grads(small)
-        up_grad, gain_two_grad, shift_two_grad = column_grads(
-            inner, list(zip(up_total, up_back)), up_weight, ln2_gain, ln2_bias, sum_up, wide // 2, 1, True
-        )
-        qkv_back, up_grad = tie(qkv_back, up_grad)
-        qkv_grad, gain_one_grad, shift_one_grad = column_grads(
-            inner, list(zip(qkv_total, qkv_back)), qkv_weight, ln1_gain, ln1_bias, sum_qkv, HD, 2, False, token
-        )
+        qkv_grad, gain_one_grad, shift_one_grad, sum_qkv = column_grads(
+            inner, list(zip(qkv_total, qkv_back)), qkv_weight, ln1_gain, ln1_bias, HD, 2, False, token
+        )
+        out_back, qkv_grad = tie(out_back, qkv_grad)
+        out_grad = row_grads(inner, [(out_total, out_back)])
     else:
         def finish(sums, weight, gain, shift, total):
             sums = sums.astype(f32)
@@ -912,6 +1006,8 @@
             up_rows, up_weight, ln2_gain, ln2_bias, sum_up
         )
 
+    qkv_bias_grad = lax.dynamic_slice_in_dim(sum_qkv, place * 3 * cols, 3 * cols)
+    up_bias_grad = lax.dynamic_slice_in_dim(sum_up, place * wide, wide)
     return (
         out_given,
         tokens_grad,

time: 842 us -> 787 us (0.935)
  other arithmetic: 49.8 us -> 25.7 us
  starting transfers between devices: 133 us -> 114 us
  local copies, waits for them, and re-layouts: 65 us -> 54.8 us
    ppermute x7, starting transfers between devices: 61.4 us -> 30.4 us  [rep_in(): return lax.ppermute(value, 'rep', [(0, 1), (3, 2)])]
    ppermute x10, waiting for transfers between devices: 1.26 us -> 24.6 us  [flip(): return lax.ppermute(value, 'shard', [(i, i ^ bit) for i in range(8)])]
    ppermute x6, starting transfers between devices: 10.3 us -> 30.2 us  [exchange(): lax.ppermute(part, 'rep', [(i, (i + k) % shares) for i in range(shares)])]
    all_gather x1, waiting for transfers between devices: 34.5 us -> 17.1 us  [local(): grad_out = lax.all_gather(cot_late.reshape(rows, cols), 'shard', axis=0)]
    ppermute x7, waiting for transfers between devices: 23.8 us -> 39.9 us  [rep_out(): return lax.ppermute(value, 'rep', [(1, 0), (2, 3)])]
    add x7 -> x1, other arithmetic: 10.9 us -> 0.01 us  [local(): out_bias.astype(f32) + down_bias.astype(f32)]
    all_to_all x5 -> x4, waiting for transfers between devices: 34.6 us -> 23.8 us  [swap(): lax.all_to_all(value, 'shard', split_axis=0, concat_axis=0, tiled=True)]
    ppermute x2 -> x0, waiting for transfers between devices: 9.75 us -> none  [the longest x1 9.75 us: local(): small_came = lax.ppermute(small, 'rep', [(i, i ^ 1) for i in range(4)])]
  transfers between devices with their start and end apart: 46 -> 43, of which waited for: 13 -> 14; matrix products, arithmetic and copies ran while one was open for 16% -> 13% of each run, Pallas kernels for 39% -> 43%
where the time goes in v3:
time: 787 us; the launch traced here: 776 us
  Pallas kernels  343 us (44%)
  waiting for transfers between devices  176 us (22%)
  starting transfers between devices  114 us (14%)
  local copies, waits for them, and re-layouts  54.8 us (7%)
  matrix products  46.5 us (6%)
  other arithmetic  25.7 us (3%)
  between operations  15.6 us (2%)
    ppermute x6, waiting for transfers between devices, exchange(): lax.ppermute(part, 'rep', [(i, (i + k) % shares) for i in range(shares)])  60.1 us
    pallas_call x18, Pallas kernels, plus_low(): pl.pallas_call(body, grid=(steps,), in_specs=[block, block], out_specs=sp...  50.9 us
    pallas_call x2, Pallas kernels, norm_terms(): pl.pallas_call(body, grid_spec=pltpu.PrefetchScalarGridSpec(num_scalar_pr...  47.4 us
    dot_general x2, matrix products, dot(): lax.dot_general(a, b, (((ca,), (cb,)), ((), ())), preferred_element_type=...  46.5 us
    pallas_call x3, Pallas kernels, normed_dot(): pl.pallas_call(body, grid_spec=pltpu.PrefetchScalarGridSpec(num_scalar_pr...  46.5 us
    ppermute x7, waiting for transfers between devices, rep_out(): return lax.ppermute(value, 'rep', [(1, 0), (2, 3)])  39.9 us
    pallas_call x3, Pallas kernels, token_dot(): pl.pallas_call(body, grid=(blocks // step,), in_specs=[spec((rows, width)...  38 us
    pallas_call x1, Pallas kernels, attention(): pl.pallas_call(attention_kernel, grid_spec=pltpu.PrefetchScalarGridSpec(n...  37.7 us
  transfers between devices with their start and end apart: 43, of which 14 were waited for; matrix products, arithmetic and copies ran while one was open for 13% of the time, Pallas kernels for 43%

profile of v3, /device:TPU:0, one launch (start us, length us, event | category | flops | bytes accessed | tf_op | source)
XLA Modules:
  0.0 776.1 jit_solution(17738716779572549794)
XLA Ops:
  28.4 5.1 all-to-all-start
  50.8 23.8 %all-to-all-done = bf16[8,80,1792]{2,1,0:T(8,128)(2,1)} async-done(((bf16[8,80,1792]{2,1,0:T(8,128)(2,1)}), bf16[8,80,1792]{2,1,0:T(8,128)(2,1)}, u32[]{:S(2)}, u32[]{:S(2)}) %all-to-all-start) | async-done | bytes 2293792 | tf_op jit(solution)/shard_map/all_to_all | solution.py:709
  84.9 19.2 %collective-permute-done = bf16[8,64,1024]{2,1,0:T(8,128)(2,1)S(1)} collective-permute-done((bf16[8,64,1024]{2,1,0:T(8,128)(2,1)S(1)}, bf16[8,64,1024]{2,1,0:T(8,128)(2,1)S(1)}, u32[]{:S(2)}, u32[]{:S(2)}) %collective-permute-start) | collective-permute-done | bytes 1048608 | tf_op jit(solution)/shard_map/ppermute | solution.py:766
  104.1 41.0 %collective-permute-done.1 = bf16[8,64,1024]{2,1,0:T(8,128)(2,1)S(1)} collective-permute-done((bf16[8,64,1024]{2,1,0:T(8,128)(2,1)S(1)}, bf16[8,64,1024]{2,1,0:T(8,128)(2,1)S(1)}, u32[]{:S(2)}, u32[]{:S(2)}) %collective-permute-start.1) | collective-permute-done | bytes 1048608 | tf_op jit(solution)/shard_map/ppermute | solution.py:766
  152.0 22.1 %collective-permute-start.6 = (bf16[8,64,768]{2,1,0:T(8,128)(2,1)}, bf16[8,64,768]{2,1,0:T(8,128)(2,1)}, u32[]{:S(2)}, u32[]{:S(2)}) collective-permute-start(bf16[8,64,768]{2,1,0:T(8,128)(2,1)} %slice.57), channel_id=1, source_target_pairs={{0,8},{8,16},{16,24},{24,0},{1,9},{9,17},{17,25},{25,1},{2,10},{10... | collective-permute-start | bytes 2359304 | tf_op jit(solution)/shard_map/ppermute | solution.py:766
  176.6 27.9 %fusion.3 = (f32[4096,1024]{1,0:T(8,128)}, bf16[4096,1024]{1,0:T(8,128)(2,1)}) fusion(f32[1024]{0:T(1024)S(1)} %convert_add_fusion, bf16[4096,2048]{1,0:T(8,128)(2,1)} %all-gather.5.cloned.1.call-done.left_ref, bf16[2048,1024]{1,0:T(8,128)(2,1)S(1)} %bitcast.153), kind=kOutput, calls=%fused_computation.6 | convolution fusion | flops 17226006528 | bytes 46141440 | tf_op jit(solution)/shard_map/dot_general | solution.py:26
  204.5 17.1 %all-gather.3.cloned.1.call-done.right_ref.grad_ref = bf16[8,4096,256]{2,1,0:T(8,128)(2,1)} async-done(((bf16[1,4096,256]{2,1,0:T(8,128)(2,1)}), bf16[8,4096,256]{2,1,0:T(8,128)(2,1)}) %all-gather.3.cloned.1.call-update) | async-done | bytes 16777232 | tf_op jit(solution)/shard_map/all_gather | solution.py:759
  221.6 13.8 %shard_map.283.refs_1_ = bf16[512,2048]{1,0:T(8,128)(2,1)} custom-call(bf16[4096,1024]{1,0:T(8,128)(2,1)} %get-tuple-element.163.left_ref.refs_1_, bf16[8,4096,256]{2,1,0:T(8,128)(2,1)} %all-gather.3.cloned.1.call-done.right_ref.grad_ref), custom_call_target="tpu_custom_call" | custom-call | flops 1024 | bytes 1024 | tf_op jit(solution)/shard_map/pallas_call | solution.py:386
  235.5 5.0 collective-permute-start.3
  242.0 14.0 %shard_map.286 = bf16[528,2048]{1,0:T(8,128)(2,1)} custom-call(bf16[4096,1024]{1,0:T(8,128)(2,1)} %get-tuple-element.163.left_ref.refs_1_, bf16[8,4096,256]{2,1,0:T(8,128)(2,1)} %all-gather.3.cloned.1.call-done.right_ref.grad_ref, bf16[16,2048]{1,0:T(8,128)(2,1)} %convert_element_type.122.refs_0_), custom_call_target="tpu_custom_call" | custom-call | flops 1024 | bytes 1024 | tf_op jit(solution)/shard_map/pallas_call | solution.py:386
  256.0 25.0 %shard_map.285 = (bf16[4096,1024]{1,0:T(8,128)(2,1)}, f32[1,1024]{1,0:T(1,128)S(1)}) custom-call(bf16[8,4096,256]{2,1,0:T(8,128)(2,1)} %all-gather.3.cloned.1.call-done.right_ref.grad_ref, bf16[1024,2048]{1,0:T(8,128)(2,1)} %refs_9_.3, f32[4096,1024]{1,0:T(8,128)} %get-tuple-element.286.slope_ref), custom_call_target="tpu_custom_call" | custom-call | flops 1024 | bytes 1024 | tf_op jit(solution)/shard_map/pallas_call | solution.py:540
  281.6 13.8 %shard_map.287.refs_2_ = bf16[8,272,512]{2,1,0:T(8,128)(2,1)} custom-call(s32[1]{0:T(128)} %bitcast.20.spot_ref, bf16[4096,2048]{1,0:T(8,128)(2,1)} %all-gather.5.cloned.1.call-done.left_ref, bf16[4096,1024]{1,0:T(8,128)(2,1)} %get-tuple-element.167.right_ref.refs_1_, f32[1,1024]{1,0:T(1,128)} %copy-done.27), custom_call_target="tpu_custom_call" | custom-call | flops 1024 | bytes 1024 | tf_op jit(solution)/shard_map/pallas_call | solution.py:418
  295.3 4.5 all-to-all-start.1
  307.9 13.8 %shard_map.290 = bf16[8,272,512]{2,1,0:T(8,128)(2,1)} custom-call(s32[1]{0:T(128)} %bitcast.20.spot_ref, bf16[4096,2048]{1,0:T(8,128)(2,1)} %all-gather.5.cloned.1.call-done.left_ref, bf16[4096,1024]{1,0:T(8,128)(2,1)} %get-tuple-element.167.right_ref.refs_1_, f32[1,1024]{1,0:T(1,128)} %copy-done.27), custom_call_target="tpu_custom_call" | custom-call | flops 1024 | bytes 1024 | tf_op jit(solution)/shard_map/pallas_call | solution.py:418
  321.8 11.6 %shard_map.291 = bf16[4096,256]{1,0:T(8,128)(2,1)} custom-call(bf16[8,4096,256]{2,1,0:T(8,128)(2,1)} %all-gather.3.cloned.1.call-done.right_ref.grad_ref, bf16[256,2048]{1,0:T(8,128)(2,1)S(1)} %copy-done), custom_call_target="tpu_custom_call" | custom-call | flops 1024 | bytes 1024 | tf_op jit(solution)/shard_map/pallas_call | solution.py:562
  340.2 18.6 %convolution_add_fusion = f32[4096,768]{1,0:T(8,128)} fusion(bf16[4096,2048]{1,0:T(8,128)(2,1)} %all-gather.5.cloned.1.call-done.left_ref, bf16[2048,768]{1,0:T(8,128)(2,1)S(1)} %bitcast.156, f32[768]{0:T(1024)S(1)} %slice-done), kind=kOutput, calls=%fused_computation.10 | convolution fusion | flops 12888047616 | bytes 32508928 | tf_op jit(solution)/shard_map/dot_general | solution.py:26
  361.5 4.1 shard_map.293.refs_2_
  367.6 3.4 shard_map.292.refs_1_.refs_0_
  372.3 4.6 all-to-all-start.2
  377.6 37.7 %shard_map.295 = (bf16[8,2,2,128,256]{4,3,2,1,0:T(8,128)(2,1)}, bf16[8,2,2,128,768]{4,3,2,1,0:T(8,128)(2,1)}, f32[2,8,768]{2,1,0:T(8,128)S(1)}) custom-call(s32[2,16]{1,0:T(2,128)S(1)} %get-tuple-element.300.piece_of.piece_ref, s32[2,16]{1,0:T(2,128)S(1)} %get-tuple-element.299.inner_of.inner_ref, s32[2,16]{1,0:T(2,128)S(1)} %copy-done.33, ...), custom_call_target="tpu_custom_call" | custom-call | flops 1024 | bytes 1024 | tf_op jit(solution)/shard_map/pallas_call | solution.py:202
  415.8 5.3 collective-permute-done.9.refs_1_
  421.2 4.1 shard_map.297.refs_2_
  426.5 3.5 shard_map.296
  432.1 8.7 %collective-permute-start.14 = (bf16[8,272,512]{2,1,0:T(8,128)(2,1)}, bf16[8,272,512]{2,1,0:T(8,128)(2,1)}, u32[]{:S(2)}, u32[]{:S(2)}) collective-permute-start(bf16[8,272,512]{2,1,0:T(8,128)(2,1)} %all-to-all-done.2.refs_4_), channel_id=1, source_target_pairs={{0,8},{24,16},{1,9},{25,17},{2,10},{26,18},{3,11},{27,19},{4,12},{... | collective-permute-start | bytes 6684680 | tf_op jit(solution)/shard_map/ppermute | solution.py:42
  440.8 18.9 %shard_map.299.refs_4_ = bf16[8,272,768]{2,1,0:T(8,128)(2,1)} custom-call(s32[1]{0:T(128)} %bitcast.20.spot_ref, bf16[4096,2048]{1,0:T(8,128)(2,1)} %all-gather.5.cloned.1.call-done.left_ref, bf16[4096,768]{1,0:T(8,128)(2,1)} %bitcast.150, f32[1,768]{1,0:T(1,128)} %broadcast_in_dim.218.sum_ref), custom_call_target="tpu_custom_call" | custom-call | flops 1024 | bytes 1024 | tf_op jit(solution)/shard_map/pallas_call | solution.py:418
  459.7 10.2 %shard_map.300 = bf16[256,2048]{1,0:T(8,128)(2,1)} custom-call(bf16[4096,256]{1,0:T(8,128)(2,1)} %bitcast.159, bf16[8,4096,256]{2,1,0:T(8,128)(2,1)} %all-gather.3.cloned.1.call-done.right_ref.grad_ref), custom_call_target="tpu_custom_call" | custom-call | flops 1024 | bytes 1024 | tf_op jit(solution)/shard_map/pallas_call | solution.py:386
  472.3 4.7 all-to-all-start.3
  477.0 16.8 %shard_map.301.refs_5_ = bf16[4,4096,256]{2,1,0:T(8,128)(2,1)} custom-call(s32[8]{0:T(128)S(1)} %broadcast_xor_fusion.owners_ref, s32[1]{0:T(128)} %bitcast.52.place_ref, bf16[4096,256]{1,0:T(8,128)(2,1)} %bitcast.160, bf16[4096,1024]{1,0:T(8,128)(2,1)} %get-tuple-element.163.left_ref.refs_1_, bf16[256,2048]{1,0:T(8,128)(2,1)S(1)} %copy-done.1, ...), custom_call_target="tpu_custom_call" | custom-call | flops 1024 | bytes 1024 | tf_op jit(solution)/shard_map/pallas_call | solution.py:305
  494.2 3.7 shard_map.303
  500.1 3.7 shard_map.302
  505.1 22.2 %shard_map.305.refs_6_ = bf16[4,2,256,2048]{3,2,1,0:T(8,128)(2,1)} custom-call(s32[8]{0:T(128)S(1)} %broadcast_xor_fusion.owners_ref, bf16[4096,768]{1,0:T(8,128)(2,1)} %bitcast.151, bf16[4096,1024]{1,0:T(8,128)(2,1)} %get-tuple-element.167.right_ref.refs_1_, bf16[2048,768]{1,0:T(8,128)(2,1)} %bitcast.157, bf16[2048,1024]{1,0:T(8,128)(2,1)} %bitcast.154), custom_call_target="tpu_custom_call" | custom-call | flops 1024 | bytes 1024 | tf_op jit(solution)/shard_map/pallas_call | solution.py:362
  527.3 19.1 %shard_map.306 = (bf16[2,2048,256]{2,1,0:T(8,128)(2,1)}, bf16[2,2048,256]{2,1,0:T(8,128)(2,1)}, bf16[2,2048,256]{2,1,0:T(8,128)(2,1)}, bf16[2,2048,256]{2,1,0:T(8,128)(2,1)}) custom-call(s32[8]{0:T(128)S(1)} %broadcast_xor_fusion.owners_ref, s32[1]{0:T(128)} %bitcast.52.place_ref, bf16[4096,256]{1,0:T(8,128)(2,1)} %bitcast.161, ...), custom_call_target="tpu_custom_call" | custom-call | flops 1024 | bytes 1024 | tf_op jit(solution)/shard_map/pallas_call | solution.py:305
  546.5 9.9 %collective-permute-done.15.refs_1_ = bf16[8,272,512]{2,1,0:T(8,128)(2,1)} collective-permute-done((bf16[8,272,512]{2,1,0:T(8,128)(2,1)}, bf16[8,272,512]{2,1,0:T(8,128)(2,1)}, u32[]{:S(2)}, u32[]{:S(2)}) %collective-permute-start.15) | collective-permute-done | bytes 2228256 | tf_op jit(solution)/shard_map/ppermute | solution.py:50
  556.4 4.0 fusion.14
  569.2 25.2 %shard_map.309 = (bf16[2,256,2048]{2,1,0:T(8,128)(2,1)}, bf16[2,256,2048]{2,1,0:T(8,128)(2,1)}, bf16[2,256,2048]{2,1,0:T(8,128)(2,1)}, bf16[2,256,2048]{2,1,0:T(8,128)(2,1)}) custom-call(s32[8]{0:T(128)S(1)} %broadcast_xor_fusion.owners_ref, bf16[4096,768]{1,0:T(8,128)(2,1)} %bitcast.152, bf16[4096,1024]{1,0:T(8,128)(2,1)} %get-tuple-element.167.right_ref.refs_1_, ...), custom_call_target="tpu_custom_call" | custom-call | flops 1024 | bytes 1024 | tf_op jit(solution)/shard_map/pallas_call | solution.py:362
  602.4 6.2 collective-permute-start.21
  620.7 7.1 shard_map.314
  634.2 7.5 collective-permute-done.21
  647.9 14.0 %collective-permute-done.29.refs_3_ = bf16[8,272,512]{2,1,0:T(8,128)(2,1)} collective-permute-done((bf16[8,272,512]{2,1,0:T(8,128)(2,1)S(1)}, bf16[8,272,512]{2,1,0:T(8,128)(2,1)}, u32[]{:S(2)}, u32[]{:S(2)}) %collective-permute-start.29) | collective-permute-done | bytes 2228256 | tf_op jit(solution)/shard_map/ppermute | solution.py:50
  665.4 14.8 %shard_map.317 = (f32[256,8192]{1,0:T(8,128)}, f32[256,128]{1,0:T(8,128)S(1)}, f32[256,128]{1,0:T(8,128)S(1)}, f32[1,8192]{1,0:T(1,128)S(1)}) custom-call(s32[1]{0:T(128)} %bitcast.67.inner_ref, bf16[8,272,512]{2,1,0:T(8,128)(2,1)} %bitcast.55.refs_2_.refs_0_, bf16[8,272,512]{2,1,0:T(8,128)(2,1)} %collective-permute-done.15.refs_1_, ...), custom_call_target="tpu_custom_call" | custom-call | flops 1024 | bytes 1024 | tf_op jit(solution)/shard_map/pallas_call | solution.py:644
  683.9 10.7 %collective-permute-done.26.refs_1_ = bf16[4,272,768]{2,1,0:T(8,128)(2,1)} collective-permute-done((bf16[4,272,768]{2,1,0:T(8,128)(2,1)}, bf16[4,272,768]{2,1,0:T(8,128)(2,1)}, u32[]{:S(2)}, u32[]{:S(2)}) %collective-permute-start.26) | collective-permute-done | bytes 1671200 | tf_op jit(solution)/shard_map/ppermute | solution.py:50
  706.5 14.8 %collective-permute-done.34.refs_2_ = bf16[256,2048]{1,0:T(8,128)(2,1)S(1)} collective-permute-done((bf16[256,2048]{1,0:T(8,128)(2,1)S(1)}, bf16[256,2048]{1,0:T(8,128)(2,1)S(1)}, u32[]{:S(2)}, u32[]{:S(2)}) %collective-permute-start.34) | collective-permute-done | bytes 1048608 | tf_op jit(solution)/shard_map/ppermute | solution.py:30
  728.7 8.1 %shard_map.322 = bf16[512,2048]{1,0:T(8,128)(2,1)} custom-call(bf16[512,2048]{1,0:T(8,128)(2,1)} %bitcast.149, bf16[512,2048]{1,0:T(8,128)(2,1)} %bitcast.168, bf16[2,256,2048]{2,1,0:T(8,128)(2,1)} %get-tuple-element.239.a_ref.refs_0_, bf16[2,256,2048]{2,1,0:T(8,128)(2,1)} %collective-permute-done.27.b_ref.refs_1_, bf16[256,2048]{1,0:T(8,128)(2,1)S(1)} %copy-done.20, ...), custom_call_target="tpu_custom_call" | custom-call | flops 1024 | bytes 1024 | tf_op jit(solution)/shard_map/pallas_call | solution.py:501
  736.8 3.6 collective-permute-done.32.refs_2_
  740.4 5.4 collective-permute-done.33.refs_5_
  745.8 5.8 shard_map.323
  751.6 11.0 %shard_map.324 = (f32[256,6144]{1,0:T(8,128)}, f32[256,128]{1,0:T(8,128)S(1)}, f32[256,128]{1,0:T(8,128)S(1)}, f32[1,6144]{1,0:T(1,128)S(1)}) custom-call(s32[1]{0:T(128)} %bitcast.67.inner_ref, bf16[4,272,768]{2,1,0:T(8,128)(2,1)} %bitcast.72.refs_0_, bf16[4,272,768]{2,1,0:T(8,128)(2,1)} %collective-permute-done.26.refs_1_, ...), custom_call_target="tpu_custom_call" | custom-call | flops 1024 | bytes 1024 | tf_op jit(solution)/shard_map/pallas_call | solution.py:644
  764.6 3.6 shard_map.325
  (315 shorter events, 162.0 us)
Async XLA Ops:
  7.2 138.8 %all-gather.5.cloned.1.call-start = ((), (), s32[]{:S(2)}) async-start(), calls=%async_computation.5 | async-start | bytes 18874368 | tf_op jit(solution)/shard_map/all_gather | solution.py:729
  28.4 46.3 %all-to-all-start = ((bf16[8,80,1792]{2,1,0:T(8,128)(2,1)}), bf16[8,80,1792]{2,1,0:T(8,128)(2,1)}, u32[]{:S(2)}, u32[]{:S(2)}) async-start(bf16[8,80,1792]{2,1,0:T(8,128)(2,1)} %pad_maximum_fusion), calls=%async_computation | async-start | bytes 4587520 | tf_op jit(solution)/shard_map/all_to_all | solution.py:709
  33.5 188.1 %all-gather.3.cloned.1.call-start = ((), (), s32[]{:S(2)}) async-start(), calls=%async_computation.4 | async-start | bytes 18874368 | tf_op jit(solution)/shard_map/all_gather | solution.py:759
  76.0 28.0 %collective-permute-start = (bf16[8,64,1024]{2,1,0:T(8,128)(2,1)S(1)}, bf16[8,64,1024]{2,1,0:T(8,128)(2,1)S(1)}, u32[]{:S(2)}, u32[]{:S(2)}) collective-permute-start(bf16[8,64,1024]{2,1,0:T(8,128)(2,1)S(1)} %slice.54), channel_id=1, source_target_pairs={{0,8},{8,16},{16,24},{24,0},{1,9},{9,17},{17,25},{25,1},{2,10},{10... | collective-permute-start | bytes 3145736 | tf_op jit(solution)/shard_map/ppermute | solution.py:766
  77.5 67.5 %collective-permute-start.1 = (bf16[8,64,1024]{2,1,0:T(8,128)(2,1)S(1)}, bf16[8,64,1024]{2,1,0:T(8,128)(2,1)S(1)}, u32[]{:S(2)}, u32[]{:S(2)}) collective-permute-start(bf16[8,64,1024]{2,1,0:T(8,128)(2,1)S(1)} %slice.54), channel_id=1, source_target_pairs={{0,16},{8,24},{16,0},{24,8},{1,17},{9,25},{17,1},{25,9},{2,18},{10... | collective-permute-start | bytes 3145736 | tf_op jit(solution)/shard_map/ppermute | solution.py:766
  80.0 66.1 %collective-permute-start.2 = (bf16[8,64,1024]{2,1,0:T(8,128)(2,1)S(1)}, bf16[8,64,1024]{2,1,0:T(8,128)(2,1)}, u32[]{:S(2)}, u32[]{:S(2)}) collective-permute-start(bf16[8,64,1024]{2,1,0:T(8,128)(2,1)S(1)} %slice.54), channel_id=1, source_target_pairs={{0,24},{8,0},{16,8},{24,16},{1,25},{9,1},{17,9},{25,17},{2,26},{10... | collective-permute-start | bytes 3145736 | tf_op jit(solution)/shard_map/ppermute | solution.py:766
  81.6 295.3 %copy-start.28 = (s32[2,16]{1,0:T(2,128)}, s32[2,16]{1,0:T(2,128)S(1)}, u32[]{:S(2)}) copy-start(s32[2,16]{1,0:T(2,128)S(1)} %get-tuple-element.299.inner_of.inner_ref) | copy-start | bytes 388
  81.6 295.3 %copy-start.30 = (s32[2,16]{1,0:T(2,128)}, s32[2,16]{1,0:T(2,128)S(1)}, u32[]{:S(2)}) copy-start(s32[2,16]{1,0:T(2,128)S(1)} %get-tuple-element.300.piece_of.piece_ref) | copy-start | bytes 388
  84.9 119.6 %copy-start.42 = (f32[1792]{0:T(1024)}, f32[1792]{0:T(1024)S(1)}, u32[]{:S(2)}) copy-start(f32[1792]{0:T(1024)S(1)} %convert_reduce_fusion.2) | copy-start | bytes 21508
  104.1 41.0 %copy-start.38 = (bf16[8,64,1024]{2,1,0:T(8,128)(2,1)}, bf16[8,64,1024]{2,1,0:T(8,128)(2,1)S(1)}, u32[]{:S(2)}) copy-start(bf16[8,64,1024]{2,1,0:T(8,128)(2,1)S(1)} %collective-permute-done) | copy-start | bytes 3145732
  152.0 181.4 %collective-permute-start.6 = (bf16[8,64,768]{2,1,0:T(8,128)(2,1)}, bf16[8,64,768]{2,1,0:T(8,128)(2,1)}, u32[]{:S(2)}, u32[]{:S(2)}) collective-permute-start(bf16[8,64,768]{2,1,0:T(8,128)(2,1)} %slice.57), channel_id=1, source_target_pairs={{0,8},{8,16},{16,24},{24,0},{1,9},{9,17},{17,25},{25,1},{2,10},{10... | collective-permute-start | bytes 2359304 | tf_op jit(solution)/shard_map/ppermute | solution.py:766
  174.0 159.3 %collective-permute-start.7 = (bf16[8,64,768]{2,1,0:T(8,128)(2,1)}, bf16[8,64,768]{2,1,0:T(8,128)(2,1)}, u32[]{:S(2)}, u32[]{:S(2)}) collective-permute-start(bf16[8,64,768]{2,1,0:T(8,128)(2,1)} %slice.57), channel_id=1, source_target_pairs={{0,16},{8,24},{16,0},{24,8},{1,17},{9,25},{17,1},{25,9},{2,18},{10... | collective-permute-start | bytes 2359304 | tf_op jit(solution)/shard_map/ppermute | solution.py:766
  176.6 156.8 %collective-permute-start.8 = (bf16[8,64,768]{2,1,0:T(8,128)(2,1)}, bf16[8,64,768]{2,1,0:T(8,128)(2,1)}, u32[]{:S(2)}, u32[]{:S(2)}) collective-permute-start(bf16[8,64,768]{2,1,0:T(8,128)(2,1)} %slice.57), channel_id=1, source_target_pairs={{0,24},{8,0},{16,8},{24,16},{1,25},{9,1},{17,9},{25,17},{2,26},{10... | collective-permute-start | bytes 2359304 | tf_op jit(solution)/shard_map/ppermute | solution.py:766
  235.5 67.1 %collective-permute-start.3 = (bf16[512,2048]{1,0:T(8,128)(2,1)}, bf16[512,2048]{1,0:T(8,128)(2,1)}, u32[]{:S(2)}, u32[]{:S(2)}) collective-permute-start(bf16[512,2048]{1,0:T(8,128)(2,1)} %shard_map.283.refs_1_), channel_id=1, source_target_pairs={{0,8},{24,16},{1,9},{25,17},{2,10},{26,18},{3,11},{27,19},{4,12},{... | collective-permute-start | bytes 6291464 | tf_op jit(solution)/shard_map/ppermute | solution.py:42
  295.3 63.5 %all-to-all-start.1 = ((bf16[8,272,512]{2,1,0:T(8,128)(2,1)}), bf16[8,272,512]{2,1,0:T(8,128)(2,1)}, u32[]{:S(2)}, u32[]{:S(2)}) async-start(bf16[8,272,512]{2,1,0:T(8,128)(2,1)} %shard_map.287.refs_2_), calls=%async_computation.1 | async-start | bytes 4456448 | tf_op jit(solution)/shard_map/all_to_all | solution.py:709
  299.8 58.9 %collective-permute-start.5 = (bf16[528,2048]{1,0:T(8,128)(2,1)}, bf16[528,2048]{1,0:T(8,128)(2,1)}, u32[]{:S(2)}, u32[]{:S(2)}) collective-permute-start(bf16[528,2048]{1,0:T(8,128)(2,1)} %shard_map.286), channel_id=1, source_target_pairs={{0,8},{24,16},{1,9},{25,17},{2,10},{26,18},{3,11},{27,19},{4,12},{... | collective-permute-start | bytes 6488072 | tf_op jit(solution)/shard_map/ppermute | solution.py:42
  305.5 53.3 %collective-permute-start.4 = (bf16[512,2048]{1,0:T(8,128)(2,1)}, bf16[512,2048]{1,0:T(8,128)(2,1)}, u32[]{:S(2)}, u32[]{:S(2)}) collective-permute-start(bf16[512,2048]{1,0:T(8,128)(2,1)} %shard_map.288.refs_1_), channel_id=1, source_target_pairs={{8,16},{16,8},{9,17},{17,9},{10,18},{18,10},{11,19},{19,11},{12,20... | collective-permute-start | bytes 6291464 | tf_op jit(solution)/shard_map/ppermute | solution.py:46
  358.8 62.4 %collective-permute-start.11 = (bf16[8,272,512]{2,1,0:T(8,128)(2,1)}, bf16[8,272,512]{2,1,0:T(8,128)(2,1)}, u32[]{:S(2)}, u32[]{:S(2)}) collective-permute-start(bf16[8,272,512]{2,1,0:T(8,128)(2,1)} %all-to-all-done.1.refs_3_), channel_id=1, source_target_pairs={{0,8},{24,16},{1,9},{25,17},{2,10},{26,18},{3,11},{27,19},{4,12},{... | collective-permute-start | bytes 6684680 | tf_op jit(solution)/shard_map/ppermute | solution.py:42
  365.6 55.5 %collective-permute-start.10 = (bf16[528,2048]{1,0:T(8,128)(2,1)}, bf16[528,2048]{1,0:T(8,128)(2,1)}, u32[]{:S(2)}, u32[]{:S(2)}) collective-permute-start(bf16[528,2048]{1,0:T(8,128)(2,1)} %shard_map.293.refs_2_), channel_id=1, source_target_pairs={{8,16},{16,8},{9,17},{17,9},{10,18},{18,10},{11,19},{19,11},{12,20... | collective-permute-start | bytes 6488072 | tf_op jit(solution)/shard_map/ppermute | solution.py:46
  371.0 50.1 %collective-permute-start.9 = (bf16[512,2048]{1,0:T(8,128)(2,1)}, bf16[512,2048]{1,0:T(8,128)(2,1)}, u32[]{:S(2)}, u32[]{:S(2)}) collective-permute-start(bf16[512,2048]{1,0:T(8,128)(2,1)} %shard_map.292.refs_1_.refs_0_), channel_id=1, source_target_pairs={{8,0},{16,24},{9,1},{17,25},{10,2},{18,26},{11,3},{19,27},{12,4},{... | collective-permute-start | bytes 6291464 | tf_op jit(solution)/shard_map/ppermute | solution.py:50
  372.3 43.5 %all-to-all-start.2 = ((bf16[8,272,512]{2,1,0:T(8,128)(2,1)}), bf16[8,272,512]{2,1,0:T(8,128)(2,1)}, u32[]{:S(2)}, u32[]{:S(2)}) async-start(bf16[8,272,512]{2,1,0:T(8,128)(2,1)} %shard_map.290), calls=%async_computation.2 | async-start | bytes 4456448 | tf_op jit(solution)/shard_map/all_to_all | solution.py:709
  425.2 69.0 %collective-permute-start.12 = (bf16[528,2048]{1,0:T(8,128)(2,1)}, bf16[528,2048]{1,0:T(8,128)(2,1)}, u32[]{:S(2)}, u32[]{:S(2)}) collective-permute-start(bf16[528,2048]{1,0:T(8,128)(2,1)} %shard_map.297.refs_2_), channel_id=1, source_target_pairs={{8,0},{16,24},{9,1},{17,25},{10,2},{18,26},{11,3},{19,27},{12,4},{... | collective-permute-start | bytes 6488072 | tf_op jit(solution)/shard_map/ppermute | solution.py:50
  430.0 64.2 %collective-permute-start.13 = (bf16[8,272,512]{2,1,0:T(8,128)(2,1)}, bf16[8,272,512]{2,1,0:T(8,128)(2,1)}, u32[]{:S(2)}, u32[]{:S(2)}) collective-permute-start(bf16[8,272,512]{2,1,0:T(8,128)(2,1)} %bitcast.51.refs_3_), channel_id=1, source_target_pairs={{8,16},{16,8},{9,17},{17,9},{10,18},{18,10},{11,19},{19,11},{12,20... | collective-permute-start | bytes 6684680 | tf_op jit(solution)/shard_map/ppermute | solution.py:46
  432.1 62.1 %collective-permute-start.14 = (bf16[8,272,512]{2,1,0:T(8,128)(2,1)}, bf16[8,272,512]{2,1,0:T(8,128)(2,1)}, u32[]{:S(2)}, u32[]{:S(2)}) collective-permute-start(bf16[8,272,512]{2,1,0:T(8,128)(2,1)} %all-to-all-done.2.refs_4_), channel_id=1, source_target_pairs={{0,8},{24,16},{1,9},{25,17},{2,10},{26,18},{3,11},{27,19},{4,12},{... | collective-permute-start | bytes 6684680 | tf_op jit(solution)/shard_map/ppermute | solution.py:42
  469.9 76.6 %collective-permute-start.17 = (bf16[256,2048]{1,0:T(8,128)(2,1)}, bf16[256,2048]{1,0:T(8,128)(2,1)}, u32[]{:S(2)}, u32[]{:S(2)}) collective-permute-start(bf16[256,2048]{1,0:T(8,128)(2,1)} %shard_map.300), channel_id=1, source_target_pairs={{0,8},{24,16},{1,9},{25,17},{2,10},{26,18},{3,11},{27,19},{4,12},{... | collective-permute-start | bytes 3145736 | tf_op jit(solution)/shard_map/ppermute | solution.py:42
  472.3 74.2 %all-to-all-start.3 = ((bf16[8,272,768]{2,1,0:T(8,128)(2,1)}), bf16[8,272,768]{2,1,0:T(8,128)(2,1)}, u32[]{:S(2)}, u32[]{:S(2)}) async-start(bf16[8,272,768]{2,1,0:T(8,128)(2,1)} %shard_map.299.refs_4_), calls=%async_computation.3 | async-start | bytes 6684672 | tf_op jit(solution)/shard_map/all_to_all | solution.py:709
  493.8 33.6 %collective-permute-start.18 = (bf16[4,4096,256]{2,1,0:T(8,128)(2,1)}, bf16[4,4096,256]{2,1,0:T(8,128)(2,1)}, u32[]{:S(2)}, u32[]{:S(2)}) collective-permute-start(bf16[4,4096,256]{2,1,0:T(8,128)(2,1)} %shard_map.301.refs_5_), channel_id=1, source_target_pairs={{0,1},{1,0},{2,3},{3,2},{4,5},{5,4},{6,7},{7,6},{8,9},{9,8},{10,11... | collective-permute-start | bytes 25165832 | tf_op jit(solution)/shard_map/ppermute | solution.py:30
  497.9 48.6 %collective-permute-start.16 = (bf16[8,272,512]{2,1,0:T(8,128)(2,1)}, bf16[8,272,512]{2,1,0:T(8,128)(2,1)}, u32[]{:S(2)}, u32[]{:S(2)}) collective-permute-start(bf16[8,272,512]{2,1,0:T(8,128)(2,1)} %bitcast.58.refs_3_), channel_id=1, source_target_pairs={{8,16},{16,8},{9,17},{17,9},{10,18},{18,10},{11,19},{19,11},{12,20... | collective-permute-start | bytes 6684680 | tf_op jit(solution)/shard_map/ppermute | solution.py:46
  503.8 52.6 %collective-permute-start.15 = (bf16[8,272,512]{2,1,0:T(8,128)(2,1)}, bf16[8,272,512]{2,1,0:T(8,128)(2,1)}, u32[]{:S(2)}, u32[]{:S(2)}) collective-permute-start(bf16[8,272,512]{2,1,0:T(8,128)(2,1)} %bitcast.55.refs_2_.refs_0_), channel_id=1, source_target_pairs={{8,0},{16,24},{9,1},{17,25},{10,2},{18,26},{11,3},{19,27},{12,4},{... | collective-permute-start | bytes 6684680 | tf_op jit(solution)/shard_map/ppermute | solution.py:50
  527.3 41.9 %collective-permute-start.20 = (bf16[4,2,256,2048]{3,2,1,0:T(8,128)(2,1)}, bf16[4,2,256,2048]{3,2,1,0:T(8,128)(2,1)}, u32[]{:S(2)}, u32[]{:S(2)}) collective-permute-start(bf16[4,2,256,2048]{3,2,1,0:T(8,128)(2,1)} %shard_map.305.refs_6_), channel_id=1, source_target_pairs={{0,1},{1,0},{2,3},{3,2},{4,5},{5,4},{6,7},{7,6},{8,9},{9,8},{10,11... | collective-permute-start | bytes 25165832 | tf_op jit(solution)/shard_map/ppermute | solution.py:30
  560.4 37.2 %collective-permute-start.19 = (bf16[4,272,768]{2,1,0:T(8,128)(2,1)}, bf16[4,272,768]{2,1,0:T(8,128)(2,1)}, u32[]{:S(2)}, u32[]{:S(2)}) collective-permute-start(bf16[4,272,768]{2,1,0:T(8,128)(2,1)} %get-tuple-element.288.refs_4_), channel_id=1, source_target_pairs={{0,8},{24,16},{1,9},{25,17},{2,10},{26,18},{3,11},{27,19},{4,12},{... | collective-permute-start | bytes 5013512 | tf_op jit(solution)/shard_map/ppermute | solution.py:42
  563.2 47.5 %collective-permute-start.23 = (bf16[2,2048,256]{2,1,0:T(8,128)(2,1)}, bf16[2,2048,256]{2,1,0:T(8,128)(2,1)}, u32[]{:S(2)}, u32[]{:S(2)}) collective-permute-start(bf16[2,2048,256]{2,1,0:T(8,128)(2,1)} %get-tuple-element.216.refs_7_), channel_id=1, source_target_pairs={{0,2},{1,3},{2,0},{3,1},{4,6},{5,7},{6,4},{7,5},{8,10},{9,11},{10,... | collective-permute-start | bytes 6291464 | tf_op jit(solution)/shard_map/ppermute | solution.py:30
  565.2 47.2 %collective-permute-start.24 = (bf16[2,2048,256]{2,1,0:T(8,128)(2,1)}, bf16[2,2048,256]{2,1,0:T(8,128)(2,1)}, u32[]{:S(2)}, u32[]{:S(2)}) collective-permute-start(bf16[2,2048,256]{2,1,0:T(8,128)(2,1)} %get-tuple-element.225), channel_id=1, source_target_pairs={{0,4},{1,5},{2,6},{3,7},{4,0},{5,1},{6,2},{7,3},{8,12},{9,13},{10,... | collective-permute-start | bytes 6291464 | tf_op jit(solution)/shard_map/ppermute | solution.py:30
  600.6 30.6 %collective-permute-start.22 = (bf16[4,272,768]{2,1,0:T(8,128)(2,1)}, bf16[4,272,768]{2,1,0:T(8,128)(2,1)}, u32[]{:S(2)}, u32[]{:S(2)}) collective-permute-start(bf16[4,272,768]{2,1,0:T(8,128)(2,1)} %bitcast.64), channel_id=1, source_target_pairs={{8,16},{16,8},{9,17},{17,9},{10,18},{18,10},{11,19},{19,11},{12,20... | collective-permute-start | bytes 5013512 | tf_op jit(solution)/shard_map/ppermute | solution.py:46
  602.4 39.4 %collective-permute-start.21 = (bf16[4,272,768]{2,1,0:T(8,128)(2,1)}, bf16[4,272,768]{2,1,0:T(8,128)(2,1)}, u32[]{:S(2)}, u32[]{:S(2)}) collective-permute-start(bf16[4,272,768]{2,1,0:T(8,128)(2,1)} %get-tuple-element.220.refs_5_), channel_id=1, source_target_pairs={{0,8},{24,16},{1,9},{25,17},{2,10},{26,18},{3,11},{27,19},{4,12},{... | collective-permute-start | bytes 5013512 | tf_op jit(solution)/shard_map/ppermute | solution.py:42
  608.6 53.4 %collective-permute-start.29 = (bf16[8,272,512]{2,1,0:T(8,128)(2,1)S(1)}, bf16[8,272,512]{2,1,0:T(8,128)(2,1)}, u32[]{:S(2)}, u32[]{:S(2)}) collective-permute-start(bf16[8,272,512]{2,1,0:T(8,128)(2,1)S(1)} %bitcast.132), channel_id=1, source_target_pairs={{8,0},{16,24},{9,1},{17,25},{10,2},{18,26},{11,3},{19,27},{12,4},{... | collective-permute-start | bytes 6684680 | tf_op jit(solution)/shard_map/ppermute | solution.py:50
  610.7 69.6 %collective-permute-start.27 = (bf16[2,256,2048]{2,1,0:T(8,128)(2,1)}, bf16[2,256,2048]{2,1,0:T(8,128)(2,1)}, u32[]{:S(2)}, u32[]{:S(2)}) collective-permute-start(bf16[2,256,2048]{2,1,0:T(8,128)(2,1)} %get-tuple-element.240), channel_id=1, source_target_pairs={{0,2},{1,3},{2,0},{3,1},{4,6},{5,7},{6,4},{7,5},{8,10},{9,11},{10,... | collective-permute-start | bytes 6291464 | tf_op jit(solution)/shard_map/ppermute | solution.py:30
  612.4 67.9 %collective-permute-start.28 = (bf16[2,256,2048]{2,1,0:T(8,128)(2,1)}, bf16[2,256,2048]{2,1,0:T(8,128)(2,1)}, u32[]{:S(2)}, u32[]{:S(2)}) collective-permute-start(bf16[2,256,2048]{2,1,0:T(8,128)(2,1)} %get-tuple-element.241), channel_id=1, source_target_pairs={{0,4},{1,5},{2,6},{3,7},{4,0},{5,1},{6,2},{7,3},{8,12},{9,13},{10,... | collective-permute-start | bytes 6291464 | tf_op jit(solution)/shard_map/ppermute | solution.py:30
  644.8 39.2 %collective-permute-start.25 = (bf16[4,272,768]{2,1,0:T(8,128)(2,1)}, bf16[4,272,768]{2,1,0:T(8,128)(2,1)}, u32[]{:S(2)}, u32[]{:S(2)}) collective-permute-start(bf16[4,272,768]{2,1,0:T(8,128)(2,1)} %bitcast.74), channel_id=1, source_target_pairs={{8,16},{16,8},{9,17},{17,9},{10,18},{18,10},{11,19},{19,11},{12,20... | collective-permute-start | bytes 5013512 | tf_op jit(solution)/shard_map/ppermute | solution.py:46
  646.6 48.0 %collective-permute-start.26 = (bf16[4,272,768]{2,1,0:T(8,128)(2,1)}, bf16[4,272,768]{2,1,0:T(8,128)(2,1)}, u32[]{:S(2)}, u32[]{:S(2)}) collective-permute-start(bf16[4,272,768]{2,1,0:T(8,128)(2,1)} %bitcast.72.refs_0_), channel_id=1, source_target_pairs={{8,0},{16,24},{9,1},{17,25},{10,2},{18,26},{11,3},{19,27},{12,4},{... | collective-permute-start | bytes 5013512 | tf_op jit(solution)/shard_map/ppermute | solution.py:50
  661.9 40.5 %collective-permute-start.31 = (bf16[256,2048]{1,0:T(8,128)(2,1)}, bf16[256,2048]{1,0:T(8,128)(2,1)S(1)}, u32[]{:S(2)}, u32[]{:S(2)}) collective-permute-start(bf16[256,2048]{1,0:T(8,128)(2,1)} %shard_map.311), channel_id=1, source_target_pairs={{8,16},{16,8},{9,17},{17,9},{10,18},{18,10},{11,19},{19,11},{12,20... | collective-permute-start | bytes 3145736 | tf_op jit(solution)/shard_map/ppermute | solution.py:46
  694.6 26.7 %collective-permute-start.34 = (bf16[256,2048]{1,0:T(8,128)(2,1)S(1)}, bf16[256,2048]{1,0:T(8,128)(2,1)S(1)}, u32[]{:S(2)}, u32[]{:S(2)}) collective-permute-start(bf16[256,2048]{1,0:T(8,128)(2,1)S(1)} %shard_map.318), channel_id=1, source_target_pairs={{0,4},{1,5},{2,6},{3,7},{4,0},{5,1},{6,2},{7,3},{8,12},{9,13},{10,... | collective-permute-start | bytes 3145736 | tf_op jit(solution)/shard_map/ppermute | solution.py:30
  699.4 52.2 %collective-permute-start.30 = (bf16[4,272,768]{2,1,0:T(8,128)(2,1)S(1)}, bf16[4,272,768]{2,1,0:T(8,128)(2,1)}, u32[]{:S(2)}, u32[]{:S(2)}) collective-permute-start(bf16[4,272,768]{2,1,0:T(8,128)(2,1)S(1)} %bitcast.136), channel_id=1, source_target_pairs={{8,0},{16,24},{9,1},{17,25},{10,2},{18,26},{11,3},{19,27},{12,4},{... | collective-permute-start | bytes 5013512 | tf_op jit(solution)/shard_map/ppermute | solution.py:50
  700.9 26.6 %collective-permute-start.35 = (bf16[256,2048]{1,0:T(8,128)(2,1)}, bf16[256,2048]{1,0:T(8,128)(2,1)}, u32[]{:S(2)}, u32[]{:S(2)}) collective-permute-start(bf16[256,2048]{1,0:T(8,128)(2,1)} %shard_map.319), channel_id=1, source_target_pairs={{0,2},{1,3},{2,0},{3,1},{4,6},{5,7},{6,4},{7,5},{8,10},{9,11},{10,... | collective-permute-start | bytes 3145736 | tf_op jit(solution)/shard_map/ppermute | solution.py:30
  703.4 37.0 %collective-permute-start.32 = (bf16[2048,256]{1,0:T(8,128)(2,1)}, bf16[2048,256]{1,0:T(8,128)(2,1)}, u32[]{:S(2)}, u32[]{:S(2)}) collective-permute-start(bf16[2048,256]{1,0:T(8,128)(2,1)} %shard_map.312), channel_id=1, source_target_pairs={{0,4},{1,5},{2,6},{3,7},{4,0},{5,1},{6,2},{7,3},{8,12},{9,13},{10,... | collective-permute-start | bytes 3145736 | tf_op jit(solution)/shard_map/ppermute | solution.py:30
  703.9 41.9 %collective-permute-start.33 = (bf16[2048,256]{1,0:T(8,128)(2,1)}, bf16[2048,256]{1,0:T(8,128)(2,1)}, u32[]{:S(2)}, u32[]{:S(2)}) collective-permute-start(bf16[2048,256]{1,0:T(8,128)(2,1)} %shard_map.313), channel_id=1, source_target_pairs={{0,2},{1,3},{2,0},{3,1},{4,6},{5,7},{6,4},{7,5},{8,10},{9,11},{10,... | collective-permute-start | bytes 3145736 | tf_op jit(solution)/shard_map/ppermute | solution.py:30
  722.3 40.4 %collective-permute-start.36 = (bf16[256,2048]{1,0:T(8,128)(2,1)S(1)}, bf16[256,2048]{1,0:T(8,128)(2,1)}, u32[]{:S(2)}, u32[]{:S(2)}) collective-permute-start(bf16[256,2048]{1,0:T(8,128)(2,1)S(1)} %shard_map.321.refs_0_), channel_id=1, source_target_pairs={{8,0},{16,24},{9,1},{17,25},{10,2},{18,26},{11,3},{19,27},{12,4},{... | collective-permute-start | bytes 3145736 | tf_op jit(solution)/shard_map/ppermute | solution.py:50
  724.9 43.4 %copy-start.48 = (f32[256]{0:T(256)}, f32[256]{0:T(256)S(1)}, u32[]{:S(2)}) copy-start(f32[256]{0:T(256)S(1)} %convert_reduce_fusion.3) | copy-start | bytes 3076
  (59 other events, 537.5 us)
Sparse Core Ops, SparseCore 0:
  12.1 117.0 all-gather.4
  131.7 89.8 all-gather.2

commit v4 on v3

--- a/solution.py
+++ b/solution.py
@@ -38,16 +38,20 @@
     return a.astype(f32) + b.astype(f32)
 
 
+def rep_move(value, pairs):
+    return lax.ppermute(value, "rep", pairs) if lax.axis_size("rep") == 4 else value
+
+
 def rep_in(value):
-    return lax.ppermute(value, "rep", [(0, 1), (3, 2)])
+    return rep_move(value, [(0, 1), (3, 2)])
 
 
 def rep_over(value):
-    return lax.ppermute(value, "rep", [(1, 2), (2, 1)])
+    return rep_move(value, [(1, 2), (2, 1)])
 
 
 def rep_out(value):
-    return lax.ppermute(value, "rep", [(1, 0), (2, 3)])
+    return rep_move(value, [(1, 0), (2, 3)])
 
 
 def rotary_tables():
@@ -124,7 +128,7 @@
         g_buf[rows, :] = grad_ref[p, 0, i]
         return carry
 
-    lax.fori_loop(0, blocks, load, 0)
+    lax.fori_loop(0, blocks, load, 0, unroll=4)
     for buf in (q_buf, k_buf, v_buf, g_buf):
         buf[blocks * BLK:, :] = jnp.zeros((BLK, HD), bf16)
     sum_ref[...] = jnp.zeros(sum_ref.shape, f32)
@@ -187,7 +191,7 @@
         store_part(p, i, 2 * HD, dv_buf[rows, :])
         return carry
 
-    lax.fori_loop(0, blocks, store, 0)
+    lax.fori_loop(0, blocks, store, 0, unroll=4)
 
 
 def attention(tables, qkv, grad, cosine, sine):
@@ -225,24 +229,31 @@
     )(*tables, qkv, grad, cosine, sine)
 
 
-def plus_low(a, b, index=None):
+def plus_low(a, b, index=None, needed=None):
     shape = a.shape if index is None else a.shape[1:]
     if index is None:
         a, b, index = a[None], b[None], 0
+    if needed is None:
+        needed = jnp.ones((1,), jnp.int32)
     a, b = [x.reshape(x.shape[0], -1, x.shape[-1]) for x in (a, b)]
     rows, cols = a.shape[1:]
-    steps = 2 if rows % 32 == 0 else 1
-    block = spec((1, rows // steps, cols), lambda i: (index, i, 0))
-
-    def body(a_ref, b_ref, out_ref):
-        out_ref[...] = plus(a_ref[0], b_ref[0]).astype(bf16)
-
-    return pl.pallas_call(
-        body, grid=(steps,), in_specs=[block, block],
-        out_specs=spec((rows // steps, cols), lambda i: (i, 0)),
+    steps = next(n for n in (2, 3, 1) if rows % (16 * n) == 0)
+    block = spec((1, rows // steps, cols), lambda i, needed_ref: (index, i * needed_ref[0], 0))
+
+    def body(needed_ref, a_ref, b_ref, out_ref):
+        @pl.when((needed_ref[0] == 1) | (pl.program_id(0) == 0))
+        def _():
+            out_ref[...] = plus(a_ref[0], b_ref[0]).astype(bf16)
+
+    return pl.pallas_call(
+        body,
+        grid_spec=pltpu.PrefetchScalarGridSpec(
+            num_scalar_prefetch=1, grid=(steps,), in_specs=[block, block],
+            out_specs=spec((rows // steps, cols), lambda i, needed_ref: (i * needed_ref[0], 0)),
+        ),
         out_shape=jax.ShapeDtypeStruct((rows, cols), bf16),
         compiler_params=params_of(32), cost_estimate=cost(0),
-    )(a, b).reshape(shape)
+    )(needed, a, b).reshape(shape)
 
 
 def out_terms(owners, place, context, active, out_w, down_w, resid, came=None):
@@ -793,6 +804,7 @@
     grad_out, active = tie(grad_out, active)
 
     where_rep = jnp.asarray(spot, jnp.int32).reshape(1)
+    inner = ((where_rep == 1) | (where_rep == 2)).astype(jnp.int32)
 
     down_parts = [token_dot(active, grad_out, 0, 2)]
     down_came = [rep_in(down_parts[0])]
@@ -805,7 +817,7 @@
     up_terms = [normed_dot(where_rep, shards, normed, hidden_grad, sum_hidden, 0, 2)]
     up_found = [swap(up_terms[0])]
     down_came[0], up_terms[0] = tie(down_came[0], up_terms[0])
-    down_pair = [plus_low(down_parts[0], down_came[0])]
+    down_pair = [plus_low(down_parts[0], down_came[0], needed=inner)]
     down_other = [rep_over(down_pair[0])]
     down_came.append(rep_in(down_parts[1]))
     gate(down_pair[0], up_terms[0])
@@ -821,9 +833,9 @@
     qkv_w = whole(qkv_parts)
     mixed = dot(normed, qkv_w, 1, 0) + bias_qkv
     down_other[0], down_came[1], up_found[0], mixed = tie(down_other[0], down_came[1], up_found[0], mixed)
-    down_total = [plus_low(down_pair[0], down_other[0])]
+    down_total = [plus_low(down_pair[0], down_other[0], needed=inner)]
     down_back = [rep_out(down_total[0])]
-    down_pair.append(plus_low(down_parts[1], down_came[1]))
+    down_pair.append(plus_low(down_parts[1], down_came[1], needed=inner))
     down_other.append(rep_over(down_pair[1]))
     up_came = [rep_in(up_found[0])]
     up_terms[1], up_found[0] = tie(up_terms[1], up_found[0])
@@ -842,9 +854,9 @@
     down_back[0], down_other[1], up_came[0], up_found[1], context = tie(
         down_back[0], down_other[1], up_came[0], up_found[1], context
     )
-    down_total.append(plus_low(down_pair[1], down_other[1]))
+    down_total.append(plus_low(down_pair[1], down_other[1], needed=inner))
     down_back.append(rep_out(down_total[1]))
-    up_pair = [plus_low(up_found[0], up_came[0])]
+    up_pair = [plus_low(up_found[0], up_came[0], needed=inner)]
     up_other = [rep_over(up_pair[0])]
     up_came.append(rep_in(up_found[1]))
     gate(down_back[0], down_total[1], up_pair[0], up_found[1])
@@ -866,9 +878,9 @@
         odd = out_terms(owners, place, context, active, out_w, down_w, resid)
         odd_came = flip(odd, 1)
         down_back[1], up_other[0], up_came[1], odd = tie(down_back[1], up_other[0], up_came[1], odd)
-        up_total = [plus_low(up_pair[0], up_other[0])]
+        up_total = [plus_low(up_pair[0], up_other[0], needed=inner)]
         up_back = [rep_out(up_total[0])]
-        up_pair.append(plus_low(up_found[1], up_came[1]))
+        up_pair.append(plus_low(up_found[1], up_came[1], needed=inner))
         up_other.append(rep_over(up_pair[1]))
         gate(down_back[1], up_total[0], up_pair[1], qkv_terms, odd)
 
@@ -882,10 +894,10 @@
         up_back[0], up_other[1], out_came, qkv_found, keep_one = tie(
             up_back[0], up_other[1], out_came, qkv_found, keep_one
         )
-        up_total.append(plus_low(up_pair[1], up_other[1]))
+        up_total.append(plus_low(up_pair[1], up_other[1], needed=inner))
         up_back.append(rep_out(up_total[1]))
         qkv_parts = [qkv_found[:shards // 2], qkv_found[shards // 2:]]
-        qkv_came = [rep_in(qkv_parts[0])]
+        qkv_came = [rep_in(part) for part in qkv_parts]
         gate(up_back[0], up_total[1], out_came, *qkv_parts, norm_odd, send_one)
 
         norm_send_one, norm_keep_one, norm_send_two, norm_keep_two = norm_terms(
@@ -894,59 +906,62 @@
         norm_got_one, norm_got_two = flip(norm_send_one, 2), flip(norm_send_two, 4)
 
         qkv_came[0], norm_keep_one = tie(qkv_came[0], norm_keep_one)
-        qkv_pair = [plus_low(qkv_parts[0], qkv_came[0])]
+        qkv_pair = [plus_low(qkv_parts[0], qkv_came[0], needed=inner)]
         qkv_other = [rep_over(qkv_pair[0])]
-        qkv_parts[1], out_came, qkv_pair[0] = tie(qkv_parts[1], out_came, qkv_pair[0])
-        qkv_came.append(rep_in(qkv_parts[1]))
+        out_came, qkv_pair[0] = tie(out_came, qkv_pair[0])
         got_one, got_two, out_came = tie(got_one, got_two, out_came)
-        out_pair = plus_low(out_part, out_came)
+        out_pair = plus_low(out_part, out_came, needed=inner)
         out_other = rep_over(out_pair)
         keep_one, keep_two, out_pair = tie(keep_one, keep_two, out_pair)
         last_one = plus_low(keep_one, got_one, 1)
         last_two = plus_low(keep_two, got_two, 1)
-        down_late, grad_late, last_one, last_two = tie(
-            list(zip(down_total, down_back)), grad_out, last_one, last_two
-        )
-        inner = ((spot == 1) | (spot == 2)).astype(jnp.int32).reshape(1)
+        qkv_came[1], last_one, last_two = tie(qkv_came[1], last_one, last_two)
+        qkv_pair.append(plus_low(qkv_parts[1], qkv_came[1], needed=inner))
+        qkv_other.append(rep_over(qkv_pair[1]))
+        down_late, grad_late, qkv_pair[1] = tie(list(zip(down_total, down_back)), grad_out, qkv_pair[1])
         down_grad = row_grads(inner, down_late, wide // 2)
+        found = jnp.where(inner == 1, down_late[1][0][wide // 2:], down_late[1][1][wide // 2:])
+        out_bias_grad = sums_of(found, cols)
         grad_rows = lax.dynamic_slice_in_dim(grad_late, place * own_rows, own_rows, 1)
         grad_rows = grad_rows.transpose(1, 0, 2).reshape(own_rows, D)
-        qkv_other[0], down_grad, grad_rows = tie(qkv_other[0], down_grad, grad_rows)
-        qkv_total = [plus_low(qkv_pair[0], qkv_other[0])]
+        qkv_other[0], down_grad, grad_rows, out_bias_grad = tie(
+            qkv_other[0], down_grad, grad_rows, out_bias_grad
+        )
+        qkv_total = [plus_low(qkv_pair[0], qkv_other[0], needed=inner)]
         qkv_back = [rep_out(qkv_total[0])]
-        qkv_came[1], qkv_total[0] = tie(qkv_came[1], qkv_total[0])
-        qkv_pair.append(plus_low(qkv_parts[1], qkv_came[1]))
-        qkv_other.append(rep_over(qkv_pair[1]))
-        up_back[1], qkv_pair[1] = tie(up_back[1], qkv_pair[1])
+        norm_got_one, norm_got_two, qkv_total[0] = tie(norm_got_one, norm_got_two, qkv_total[0])
+        norm_last_one = plus_low(norm_keep_one, norm_got_one, 1)
+        norm_last_two = plus_low(norm_keep_two, norm_got_two, 1)
+        up_back[1], norm_last_one, norm_last_two = tie(up_back[1], norm_last_one, norm_last_two)
+        norm_last_one, norm_last_two = flip(norm_last_one, 4), flip(norm_last_two, 2)
         up_grad, gain_two_grad, shift_two_grad, sum_up = column_grads(
             inner, list(zip(up_total, up_back)), up_weight, ln2_gain, ln2_bias, wide // 2, 1, True
         )
-        norm_got_one, norm_got_two, up_grad = tie(norm_got_one, norm_got_two, up_grad)
-        norm_last_one = plus_low(norm_keep_one, norm_got_one, 1)
-        norm_last_two = plus_low(norm_keep_two, norm_got_two, 1)
-        qkv_other[1], qkv_back[0], norm_last_one, norm_last_two = tie(
-            qkv_other[1], qkv_back[0], norm_last_one, norm_last_two
-        )
-        norm_last_one, norm_last_two = flip(norm_last_one, 4), flip(norm_last_two, 2)
-        qkv_total.append(plus_low(qkv_pair[1], qkv_other[1]))
+        qkv_other[1], up_grad = tie(qkv_other[1], up_grad)
+        qkv_total.append(plus_low(qkv_pair[1], qkv_other[1], needed=inner))
         qkv_back.append(rep_out(qkv_total[1]))
-        out_other, last_one, last_two, qkv_total[1] = tie(out_other, last_one, last_two, qkv_total[1])
+        out_other, qkv_back[0], norm_last_one, norm_last_two, last_one, last_two, qkv_total[1] = tie(
+            out_other, qkv_back[0], norm_last_one, norm_last_two, last_one, last_two, qkv_total[1]
+        )
         last_one, last_two = flip(last_one, 4), flip(last_two, 2)
-        out_total = plus_low(out_pair, out_other)
+        out_total = plus_low(out_pair, out_other, needed=inner)
         out_back = rep_out(out_total)
         norm_last_one, norm_last_two, out_total = tie(norm_last_one, norm_last_two, out_total)
         tokens_grad = token_grads(
             resid, grad_rows,
             [(norm_keep_one, norm_got_one, norm_last_one), (norm_keep_two, norm_got_two, norm_last_two)],
         )
-        last_one, last_two, tokens_grad = tie(last_one, last_two, tokens_grad)
+        qkv_back, tokens_grad = tie(qkv_back, tokens_grad)
+        qkv_grad, gain_one_grad, shift_one_grad, sum_qkv = column_grads(
+            inner, list(zip(qkv_total, qkv_back)), qkv_weight, ln1_gain, ln1_bias, HD, 2, False, token
+        )
+        last_one, last_two, qkv_grad = tie(last_one, last_two, qkv_grad)
         out_given = out_blocks(
             tables[0], tables[1], own, [(keep_one, got_one, last_one), (keep_two, got_two, last_two)],
             out_bias.astype(f32) + down_bias.astype(f32),
         )
-        found = jnp.where(inner == 1, down_total[1][wide // 2:], down_back[1][wide // 2:])
-        out_bias_grad = sums_of(found, cols)
-        qkv_back, out_given = tie(qkv_back, out_given)
+        out_back, out_given = tie(out_back, out_given)
+        out_grad = row_grads(inner, [(out_total, out_back)])
     else:
         sums = jnp.concatenate([sum_mixed[0], sum_hidden[0]])
         sums, out_bias_grad = lax.psum((sums, sum_cot), "rep")
@@ -981,13 +996,7 @@
         tokens_grad = (grad_rows.astype(f32) + tokens_grad).astype(bf16)
     tokens_grad = tokens_grad.reshape(MB, own, BLK, D)
 
-    if cube:
-        qkv_grad, gain_one_grad, shift_one_grad, sum_qkv = column_grads(
-            inner, list(zip(qkv_total, qkv_back)), qkv_weight, ln1_gain, ln1_bias, HD, 2, False, token
-        )
-        out_back, qkv_grad = tie(out_back, qkv_grad)
-        out_grad = row_grads(inner, [(out_total, out_back)])
-    else:
+    if not cube:
         def finish(sums, weight, gain, shift, total):
             sums = sums.astype(f32)
             grads = gain.astype(f32)[:, None] * sums + shift.astype(f32)[:, None] * total

time: 787 us -> 767 us (0.975)
  Pallas kernels: 343 us -> 331 us
    ppermute x10, waiting for transfers between devices: 24.6 us -> 10.4 us  [flip(): return lax.ppermute(value, 'shard', [(i, i ^ bit) for i in range(8)])]
    ppermute x21, waiting for transfers between devices: 50.7 us -> 59.4 us  [rep_move(): lax.ppermute(value, 'rep', pairs)]
    pallas_call x18, Pallas kernels: 50.9 us -> 42.2 us  [plus_low(): pl.pallas_call(body, grid_spec=pltpu.PrefetchScalarGridSpec(num_scalar_pr...]
    unnamed x129 -> x123, local copies, waits for them, and re-layouts: 22.2 us -> 18.8 us
  transfers between devices with their start and end apart: 43 -> 43, of which waited for: 14 -> 14; matrix products, arithmetic and copies ran while one was open for 13% -> 14% of each run, Pallas kernels for 43% -> 43%
where the time goes in v4:
time: 767 us; the launch traced here: 757 us
  Pallas kernels  331 us (43%)
  waiting for transfers between devices  171 us (22%)
  starting transfers between devices  114 us (15%)
  local copies, waits for them, and re-layouts  51.4 us (7%)
  matrix products  46.5 us (6%)
  other arithmetic  27.5 us (4%)
  between operations  15.6 us (2%)
    ppermute x6, waiting for transfers between devices, exchange(): lax.ppermute(part, 'rep', [(i, (i + k) % shares) for i in range(shares)])  60.1 us
    ppermute x21, waiting for transfers between devices, rep_move(): lax.ppermute(value, 'rep', pairs)  59.4 us
    ppermute x21, starting transfers between devices, rep_move(): lax.ppermute(value, 'rep', pairs)  50.8 us
    pallas_call x2, Pallas kernels, norm_terms(): pl.pallas_call(body, grid_spec=pltpu.PrefetchScalarGridSpec(num_scalar_pr...  47.4 us
    pallas_call x3, Pallas kernels, normed_dot(): pl.pallas_call(body, grid_spec=pltpu.PrefetchScalarGridSpec(num_scalar_pr...  46.5 us
    dot_general x2, matrix products, dot(): lax.dot_general(a, b, (((ca,), (cb,)), ((), ())), preferred_element_type=...  46.5 us
    pallas_call x18, Pallas kernels, plus_low(): pl.pallas_call(body, grid_spec=pltpu.PrefetchScalarGridSpec(num_scalar_pr...  42.2 us
    pallas_call x3, Pallas kernels, token_dot(): pl.pallas_call(body, grid=(blocks // step,), in_specs=[spec((rows, width)...  37.9 us
  transfers between devices with their start and end apart: 43, of which 14 were waited for; matrix products, arithmetic and copies ran while one was open for 14% of the time, Pallas kernels for 43%

profile of v4, /device:TPU:0, one launch (start us, length us, event | category | flops | bytes accessed | tf_op | source)
XLA Modules:
  0.0 756.6 jit_solution(11105156267203040513)
XLA Ops:
  28.4 5.1 all-to-all-start
  33.9 3.1 slice_bitcast_fusion.1
  42.6 3.1 pad_maximum_fusion.1.refs_3_
  50.8 23.8 %all-to-all-done = bf16[8,80,1792]{2,1,0:T(8,128)(2,1)} async-done(((bf16[8,80,1792]{2,1,0:T(8,128)(2,1)}), bf16[8,80,1792]{2,1,0:T(8,128)(2,1)}, u32[]{:S(2)}, u32[]{:S(2)}) %all-to-all-start) | async-done | bytes 2293792 | tf_op jit(solution)/shard_map/all_to_all | solution.py:720
  84.9 19.2 %collective-permute-done = bf16[8,64,1024]{2,1,0:T(8,128)(2,1)S(1)} collective-permute-done((bf16[8,64,1024]{2,1,0:T(8,128)(2,1)S(1)}, bf16[8,64,1024]{2,1,0:T(8,128)(2,1)S(1)}, u32[]{:S(2)}, u32[]{:S(2)}) %collective-permute-start) | collective-permute-done | bytes 1048608 | tf_op jit(solution)/shard_map/ppermute | solution.py:777
  104.1 41.0 %collective-permute-done.1 = bf16[8,64,1024]{2,1,0:T(8,128)(2,1)S(1)} collective-permute-done((bf16[8,64,1024]{2,1,0:T(8,128)(2,1)S(1)}, bf16[8,64,1024]{2,1,0:T(8,128)(2,1)S(1)}, u32[]{:S(2)}, u32[]{:S(2)}) %collective-permute-start.1) | collective-permute-done | bytes 1048608 | tf_op jit(solution)/shard_map/ppermute | solution.py:777
  152.0 22.1 %collective-permute-start.6 = (bf16[8,64,768]{2,1,0:T(8,128)(2,1)}, bf16[8,64,768]{2,1,0:T(8,128)(2,1)}, u32[]{:S(2)}, u32[]{:S(2)}) collective-permute-start(bf16[8,64,768]{2,1,0:T(8,128)(2,1)} %slice.57), channel_id=1, source_target_pairs={{0,8},{8,16},{16,24},{24,0},{1,9},{9,17},{17,25},{25,1},{2,10},{10... | collective-permute-start | bytes 2359304 | tf_op jit(solution)/shard_map/ppermute | solution.py:777
  176.6 27.9 %fusion.3 = (f32[4096,1024]{1,0:T(8,128)}, bf16[4096,1024]{1,0:T(8,128)(2,1)}) fusion(f32[1024]{0:T(1024)S(1)} %convert_add_fusion, bf16[4096,2048]{1,0:T(8,128)(2,1)} %all-gather.5.cloned.1.call-done.left_ref, bf16[2048,1024]{1,0:T(8,128)(2,1)S(1)} %bitcast.152), kind=kOutput, calls=%fused_computation.6 | convolution fusion | flops 17226006528 | bytes 46141440 | tf_op jit(solution)/shard_map/dot_general | solution.py:26
  204.5 17.1 %all-gather.3.cloned.1.call-done.right_ref.grad_ref = bf16[8,4096,256]{2,1,0:T(8,128)(2,1)} async-done(((bf16[1,4096,256]{2,1,0:T(8,128)(2,1)}), bf16[8,4096,256]{2,1,0:T(8,128)(2,1)}) %all-gather.3.cloned.1.call-update) | async-done | bytes 16777232 | tf_op jit(solution)/shard_map/all_gather | solution.py:770
  221.6 13.8 %shard_map.283.refs_1_ = bf16[512,2048]{1,0:T(8,128)(2,1)} custom-call(bf16[4096,1024]{1,0:T(8,128)(2,1)} %get-tuple-element.165.left_ref.refs_1_, bf16[8,4096,256]{2,1,0:T(8,128)(2,1)} %all-gather.3.cloned.1.call-done.right_ref.grad_ref), custom_call_target="tpu_custom_call" | custom-call | flops 1024 | bytes 1024 | tf_op jit(solution)/shard_map/pallas_call | solution.py:397
  235.5 5.0 collective-permute-start.3
  242.0 13.9 %shard_map.286 = bf16[528,2048]{1,0:T(8,128)(2,1)} custom-call(bf16[4096,1024]{1,0:T(8,128)(2,1)} %get-tuple-element.165.left_ref.refs_1_, bf16[8,4096,256]{2,1,0:T(8,128)(2,1)} %all-gather.3.cloned.1.call-done.right_ref.grad_ref, bf16[16,2048]{1,0:T(8,128)(2,1)} %convert_element_type.125.refs_0_), custom_call_target="tpu_custom_call" | custom-call | flops 1024 | bytes 1024 | tf_op jit(solution)/shard_map/pallas_call | solution.py:397
  256.0 24.9 %shard_map.285 = (bf16[4096,1024]{1,0:T(8,128)(2,1)}, f32[1,1024]{1,0:T(1,128)S(1)}) custom-call(bf16[8,4096,256]{2,1,0:T(8,128)(2,1)} %all-gather.3.cloned.1.call-done.right_ref.grad_ref, bf16[1024,2048]{1,0:T(8,128)(2,1)} %refs_9_.3, f32[4096,1024]{1,0:T(8,128)} %get-tuple-element.290.slope_ref), custom_call_target="tpu_custom_call" | custom-call | flops 1024 | bytes 1024 | tf_op jit(solution)/shard_map/pallas_call | solution.py:551
  281.5 13.8 %shard_map.287.refs_2_ = bf16[8,272,512]{2,1,0:T(8,128)(2,1)} custom-call(s32[1]{0:T(128)} %bitcast.spot_ref, bf16[4096,2048]{1,0:T(8,128)(2,1)} %all-gather.5.cloned.1.call-done.left_ref, bf16[4096,1024]{1,0:T(8,128)(2,1)} %get-tuple-element.169.right_ref.refs_1_, f32[1,1024]{1,0:T(1,128)} %copy-done.24), custom_call_target="tpu_custom_call" | custom-call | flops 1024 | bytes 1024 | tf_op jit(solution)/shard_map/pallas_call | solution.py:429
  295.3 4.5 all-to-all-start.1
  307.6 13.8 %shard_map.290 = bf16[8,272,512]{2,1,0:T(8,128)(2,1)} custom-call(s32[1]{0:T(128)} %bitcast.spot_ref, bf16[4096,2048]{1,0:T(8,128)(2,1)} %all-gather.5.cloned.1.call-done.left_ref, bf16[4096,1024]{1,0:T(8,128)(2,1)} %get-tuple-element.169.right_ref.refs_1_, f32[1,1024]{1,0:T(1,128)} %copy-done.24), custom_call_target="tpu_custom_call" | custom-call | flops 1024 | bytes 1024 | tf_op jit(solution)/shard_map/pallas_call | solution.py:429
  321.4 11.6 %shard_map.291 = bf16[4096,256]{1,0:T(8,128)(2,1)} custom-call(bf16[8,4096,256]{2,1,0:T(8,128)(2,1)} %all-gather.3.cloned.1.call-done.right_ref.grad_ref, bf16[256,2048]{1,0:T(8,128)(2,1)S(1)} %copy-done), custom_call_target="tpu_custom_call" | custom-call | flops 1024 | bytes 1024 | tf_op jit(solution)/shard_map/pallas_call | solution.py:573
  339.8 18.6 %convolution_add_fusion = f32[4096,768]{1,0:T(8,128)} fusion(bf16[4096,2048]{1,0:T(8,128)(2,1)} %all-gather.5.cloned.1.call-done.left_ref, bf16[2048,768]{1,0:T(8,128)(2,1)S(1)} %bitcast.155, f32[768]{0:T(1024)S(1)} %slice-done), kind=kOutput, calls=%fused_computation.10 | convolution fusion | flops 12888047616 | bytes 32508928 | tf_op jit(solution)/shard_map/dot_general | solution.py:26
  365.6 2.8 shard_map.292.refs_1_.refs_0_
  369.7 4.5 all-to-all-start.2
  374.9 33.9 %shard_map.295 = (bf16[8,2,2,128,256]{4,3,2,1,0:T(8,128)(2,1)}, bf16[8,2,2,128,768]{4,3,2,1,0:T(8,128)(2,1)}, f32[2,8,768]{2,1,0:T(8,128)S(1)}) custom-call(s32[2,16]{1,0:T(2,128)S(1)} %get-tuple-element.304.piece_of.piece_ref, s32[2,16]{1,0:T(2,128)S(1)} %get-tuple-element.303.inner_of.inner_ref, s32[2,16]{1,0:T(2,128)S(1)} %copy-done.30, ...), custom_call_target="tpu_custom_call" | custom-call | flops 1024 | bytes 1024 | tf_op jit(solution)/shard_map/pallas_call | solution.py:206
  409.4 9.1 %collective-permute-done.9.refs_1_ = bf16[512,2048]{1,0:T(8,128)(2,1)} collective-permute-done((bf16[512,2048]{1,0:T(8,128)(2,1)}, bf16[512,2048]{1,0:T(8,128)(2,1)}, u32[]{:S(2)}, u32[]{:S(2)}) %collective-permute-start.9) | collective-permute-done | bytes 2097184 | tf_op jit(solution)/shard_map/ppermute | solution.py:42
  422.3 2.9 shard_map.296
  427.2 9.2 %collective-permute-start.14 = (bf16[8,272,512]{2,1,0:T(8,128)(2,1)}, bf16[8,272,512]{2,1,0:T(8,128)(2,1)}, u32[]{:S(2)}, u32[]{:S(2)}) collective-permute-start(bf16[8,272,512]{2,1,0:T(8,128)(2,1)} %all-to-all-done.2.refs_4_), channel_id=1, source_target_pairs={{0,8},{24,16},{1,9},{25,17},{2,10},{26,18},{3,11},{27,19},{4,12},{... | collective-permute-start | bytes 6684680 | tf_op jit(solution)/shard_map/ppermute | solution.py:42
  436.5 18.9 %shard_map.299.refs_4_ = bf16[8,272,768]{2,1,0:T(8,128)(2,1)} custom-call(s32[1]{0:T(128)} %bitcast.spot_ref, bf16[4096,2048]{1,0:T(8,128)(2,1)} %all-gather.5.cloned.1.call-done.left_ref, bf16[4096,768]{1,0:T(8,128)(2,1)} %bitcast.149, f32[1,768]{1,0:T(1,128)} %broadcast_in_dim.218.sum_ref), custom_call_target="tpu_custom_call" | custom-call | flops 1024 | bytes 1024 | tf_op jit(solution)/shard_map/pallas_call | solution.py:429
  455.4 10.1 %shard_map.300 = bf16[256,2048]{1,0:T(8,128)(2,1)} custom-call(bf16[4096,256]{1,0:T(8,128)(2,1)} %bitcast.158, bf16[8,4096,256]{2,1,0:T(8,128)(2,1)} %all-gather.3.cloned.1.call-done.right_ref.grad_ref), custom_call_target="tpu_custom_call" | custom-call | flops 1024 | bytes 1024 | tf_op jit(solution)/shard_map/pallas_call | solution.py:397
  467.8 4.7 all-to-all-start.3
  472.5 16.8 %shard_map.301.refs_5_ = bf16[4,4096,256]{2,1,0:T(8,128)(2,1)} custom-call(s32[8]{0:T(128)S(1)} %broadcast_xor_fusion.owners_ref, s32[1]{0:T(128)} %bitcast.52.place_ref, bf16[4096,256]{1,0:T(8,128)(2,1)} %bitcast.159, bf16[4096,1024]{1,0:T(8,128)(2,1)} %get-tuple-element.165.left_ref.refs_1_, bf16[256,2048]{1,0:T(8,128)(2,1)S(1)} %copy-done.1, ...), custom_call_target="tpu_custom_call" | custom-call | flops 1024 | bytes 1024 | tf_op jit(solution)/shard_map/pallas_call | solution.py:316
  489.8 3.1 shard_map.303
  495.1 3.0 shard_map.302
  499.4 22.2 %shard_map.305.refs_6_ = bf16[4,2,256,2048]{3,2,1,0:T(8,128)(2,1)} custom-call(s32[8]{0:T(128)S(1)} %broadcast_xor_fusion.owners_ref, bf16[4096,768]{1,0:T(8,128)(2,1)} %bitcast.150, bf16[4096,1024]{1,0:T(8,128)(2,1)} %get-tuple-element.169.right_ref.refs_1_, bf16[2048,768]{1,0:T(8,128)(2,1)} %bitcast.156, bf16[2048,1024]{1,0:T(8,128)(2,1)} %bitcast.153), custom_call_target="tpu_custom_call" | custom-call | flops 1024 | bytes 1024 | tf_op jit(solution)/shard_map/pallas_call | solution.py:373
  521.7 19.1 %shard_map.306 = (bf16[2,2048,256]{2,1,0:T(8,128)(2,1)}, bf16[2,2048,256]{2,1,0:T(8,128)(2,1)}, bf16[2,2048,256]{2,1,0:T(8,128)(2,1)}, bf16[2,2048,256]{2,1,0:T(8,128)(2,1)}) custom-call(s32[8]{0:T(128)S(1)} %broadcast_xor_fusion.owners_ref, s32[1]{0:T(128)} %bitcast.52.place_ref, bf16[4096,256]{1,0:T(8,128)(2,1)} %bitcast.160, ...), custom_call_target="tpu_custom_call" | custom-call | flops 1024 | bytes 1024 | tf_op jit(solution)/shard_map/pallas_call | solution.py:316
  540.8 9.9 %collective-permute-done.15.refs_1_ = bf16[8,272,512]{2,1,0:T(8,128)(2,1)} collective-permute-done((bf16[8,272,512]{2,1,0:T(8,128)(2,1)}, bf16[8,272,512]{2,1,0:T(8,128)(2,1)}, u32[]{:S(2)}, u32[]{:S(2)}) %collective-permute-start.15) | collective-permute-done | bytes 2228256 | tf_op jit(solution)/shard_map/ppermute | solution.py:42
  550.7 4.0 fusion.14
  554.7 2.8 collective-permute-start.21
  565.4 25.2 %shard_map.309 = (bf16[2,256,2048]{2,1,0:T(8,128)(2,1)}, bf16[2,256,2048]{2,1,0:T(8,128)(2,1)}, bf16[2,256,2048]{2,1,0:T(8,128)(2,1)}, bf16[2,256,2048]{2,1,0:T(8,128)(2,1)}) custom-call(s32[8]{0:T(128)S(1)} %broadcast_xor_fusion.owners_ref, bf16[4096,768]{1,0:T(8,128)(2,1)} %bitcast.151, bf16[4096,1024]{1,0:T(8,128)(2,1)} %get-tuple-element.169.right_ref.refs_1_, ...), custom_call_target="tpu_custom_call" | custom-call | flops 1024 | bytes 1024 | tf_op jit(solution)/shard_map/pallas_call | solution.py:373
  590.6 3.0 collective-permute-done.21
  599.2 5.8 collective-permute-done.19.b_ref.refs_1_
  615.1 12.6 %collective-permute-done.25 = bf16[4,272,768]{2,1,0:T(8,128)(2,1)} collective-permute-done((bf16[4,272,768]{2,1,0:T(8,128)(2,1)}, bf16[4,272,768]{2,1,0:T(8,128)(2,1)}, u32[]{:S(2)}, u32[]{:S(2)}) %collective-permute-start.25) | collective-permute-done | bytes 1671200 | tf_op jit(solution)/shard_map/ppermute | solution.py:42
  632.1 7.1 shard_map.315
  647.7 3.9 collective-permute-done.28.b_ref.refs_1_
  663.3 14.7 %shard_map.319 = (f32[256,8192]{1,0:T(8,128)}, f32[256,128]{1,0:T(8,128)S(1)}, f32[256,128]{1,0:T(8,128)S(1)}, f32[1,8192]{1,0:T(1,128)S(1)}) custom-call(s32[1]{0:T(128)S(6)} %convert_element_type.102.needed_ref.inner_ref, bf16[8,272,512]{2,1,0:T(8,128)(2,1)} %bitcast.55.refs_2_.refs_0_, bf16[8,272,512]{2,1,0:T(8,128)(2,1)} %collective-permute-done.15.refs_1_, ...), custom_call_target="tpu_custom_call" | custom-call | flops 1024 | bytes 1024 | tf_op jit(solution)/shard_map/pallas_call | solution.py:655
  682.0 7.4 collective-permute-done.26.refs_1_
  700.5 8.4 %shard_map.322 = bf16[512,2048]{1,0:T(8,128)(2,1)} custom-call(bf16[512,2048]{1,0:T(8,128)(2,1)} %bitcast.148, bf16[512,2048]{1,0:T(8,128)(2,1)} %bitcast.167, bf16[2,256,2048]{2,1,0:T(8,128)(2,1)} %get-tuple-element.241.a_ref.refs_0_, bf16[2,256,2048]{2,1,0:T(8,128)(2,1)} %collective-permute-done.28.b_ref.refs_1_, ...), custom_call_target="tpu_custom_call" | custom-call | flops 1024 | bytes 1024 | tf_op jit(solution)/shard_map/pallas_call | solution.py:512
  708.9 16.3 %collective-permute-done.36.refs_3_ = bf16[4,272,768]{2,1,0:T(8,128)(2,1)} collective-permute-done((bf16[4,272,768]{2,1,0:T(8,128)(2,1)S(1)}, bf16[4,272,768]{2,1,0:T(8,128)(2,1)}, u32[]{:S(2)}, u32[]{:S(2)}) %collective-permute-start.36) | collective-permute-done | bytes 1671200 | tf_op jit(solution)/shard_map/ppermute | solution.py:42
  725.2 11.0 %shard_map.323 = (f32[256,6144]{1,0:T(8,128)}, f32[256,128]{1,0:T(8,128)S(1)}, f32[256,128]{1,0:T(8,128)S(1)}, f32[1,6144]{1,0:T(1,128)S(1)}) custom-call(s32[1]{0:T(128)S(6)} %convert_element_type.102.needed_ref.inner_ref, bf16[4,272,768]{2,1,0:T(8,128)(2,1)} %bitcast.75.refs_0_, bf16[4,272,768]{2,1,0:T(8,128)(2,1)} %collective-permute-done.26.refs_1_, ...), custom_call_target="tpu_custom_call" | custom-call | flops 1024 | bytes 1024 | tf_op jit(solution)/shard_map/pallas_call | solution.py:655
  738.1 5.8 shard_map.324
  745.1 3.6 shard_map.325
  (309 shorter events, 157.1 us)
Async XLA Ops:
  7.2 138.8 %all-gather.5.cloned.1.call-start = ((), (), s32[]{:S(2)}) async-start(), calls=%async_computation.5 | async-start | bytes 18874368 | tf_op jit(solution)/shard_map/all_gather | solution.py:740
  28.4 46.3 %all-to-all-start = ((bf16[8,80,1792]{2,1,0:T(8,128)(2,1)}), bf16[8,80,1792]{2,1,0:T(8,128)(2,1)}, u32[]{:S(2)}, u32[]{:S(2)}) async-start(bf16[8,80,1792]{2,1,0:T(8,128)(2,1)} %pad_maximum_fusion), calls=%async_computation | async-start | bytes 4587520 | tf_op jit(solution)/shard_map/all_to_all | solution.py:720
  33.5 188.1 %all-gather.3.cloned.1.call-start = ((), (), s32[]{:S(2)}) async-start(), calls=%async_computation.4 | async-start | bytes 18874368 | tf_op jit(solution)/shard_map/all_gather | solution.py:770
  76.0 28.0 %collective-permute-start = (bf16[8,64,1024]{2,1,0:T(8,128)(2,1)S(1)}, bf16[8,64,1024]{2,1,0:T(8,128)(2,1)S(1)}, u32[]{:S(2)}, u32[]{:S(2)}) collective-permute-start(bf16[8,64,1024]{2,1,0:T(8,128)(2,1)S(1)} %slice.54), channel_id=1, source_target_pairs={{0,8},{8,16},{16,24},{24,0},{1,9},{9,17},{17,25},{25,1},{2,10},{10... | collective-permute-start | bytes 3145736 | tf_op jit(solution)/shard_map/ppermute | solution.py:777
  77.5 67.5 %collective-permute-start.1 = (bf16[8,64,1024]{2,1,0:T(8,128)(2,1)S(1)}, bf16[8,64,1024]{2,1,0:T(8,128)(2,1)S(1)}, u32[]{:S(2)}, u32[]{:S(2)}) collective-permute-start(bf16[8,64,1024]{2,1,0:T(8,128)(2,1)S(1)} %slice.54), channel_id=1, source_target_pairs={{0,16},{8,24},{16,0},{24,8},{1,17},{9,25},{17,1},{25,9},{2,18},{10... | collective-permute-start | bytes 3145736 | tf_op jit(solution)/shard_map/ppermute | solution.py:777
  80.0 66.1 %collective-permute-start.2 = (bf16[8,64,1024]{2,1,0:T(8,128)(2,1)S(1)}, bf16[8,64,1024]{2,1,0:T(8,128)(2,1)}, u32[]{:S(2)}, u32[]{:S(2)}) collective-permute-start(bf16[8,64,1024]{2,1,0:T(8,128)(2,1)S(1)} %slice.54), channel_id=1, source_target_pairs={{0,24},{8,0},{16,8},{24,16},{1,25},{9,1},{17,9},{25,17},{2,26},{10... | collective-permute-start | bytes 3145736 | tf_op jit(solution)/shard_map/ppermute | solution.py:777
  81.6 292.7 %copy-start.25 = (s32[2,16]{1,0:T(2,128)}, s32[2,16]{1,0:T(2,128)S(1)}, u32[]{:S(2)}) copy-start(s32[2,16]{1,0:T(2,128)S(1)} %get-tuple-element.303.inner_of.inner_ref) | copy-start | bytes 388
  81.6 292.7 %copy-start.27 = (s32[2,16]{1,0:T(2,128)}, s32[2,16]{1,0:T(2,128)S(1)}, u32[]{:S(2)}) copy-start(s32[2,16]{1,0:T(2,128)S(1)} %get-tuple-element.304.piece_of.piece_ref) | copy-start | bytes 388
  84.9 119.6 %copy-start.39 = (f32[1792]{0:T(1024)}, f32[1792]{0:T(1024)S(1)}, u32[]{:S(2)}) copy-start(f32[1792]{0:T(1024)S(1)} %convert_reduce_fusion.2) | copy-start | bytes 21508
  104.1 41.0 %copy-start.35 = (bf16[8,64,1024]{2,1,0:T(8,128)(2,1)}, bf16[8,64,1024]{2,1,0:T(8,128)(2,1)S(1)}, u32[]{:S(2)}) copy-start(bf16[8,64,1024]{2,1,0:T(8,128)(2,1)S(1)} %collective-permute-done) | copy-start | bytes 3145732
  152.0 181.0 %collective-permute-start.6 = (bf16[8,64,768]{2,1,0:T(8,128)(2,1)}, bf16[8,64,768]{2,1,0:T(8,128)(2,1)}, u32[]{:S(2)}, u32[]{:S(2)}) collective-permute-start(bf16[8,64,768]{2,1,0:T(8,128)(2,1)} %slice.57), channel_id=1, source_target_pairs={{0,8},{8,16},{16,24},{24,0},{1,9},{9,17},{17,25},{25,1},{2,10},{10... | collective-permute-start | bytes 2359304 | tf_op jit(solution)/shard_map/ppermute | solution.py:777
  174.0 159.0 %collective-permute-start.7 = (bf16[8,64,768]{2,1,0:T(8,128)(2,1)}, bf16[8,64,768]{2,1,0:T(8,128)(2,1)}, u32[]{:S(2)}, u32[]{:S(2)}) collective-permute-start(bf16[8,64,768]{2,1,0:T(8,128)(2,1)} %slice.57), channel_id=1, source_target_pairs={{0,16},{8,24},{16,0},{24,8},{1,17},{9,25},{17,1},{25,9},{2,18},{10... | collective-permute-start | bytes 2359304 | tf_op jit(solution)/shard_map/ppermute | solution.py:777
  176.6 156.4 %collective-permute-start.8 = (bf16[8,64,768]{2,1,0:T(8,128)(2,1)}, bf16[8,64,768]{2,1,0:T(8,128)(2,1)}, u32[]{:S(2)}, u32[]{:S(2)}) collective-permute-start(bf16[8,64,768]{2,1,0:T(8,128)(2,1)} %slice.57), channel_id=1, source_target_pairs={{0,24},{8,0},{16,8},{24,16},{1,25},{9,1},{17,9},{25,17},{2,26},{10... | collective-permute-start | bytes 2359304 | tf_op jit(solution)/shard_map/ppermute | solution.py:777
  235.5 67.0 %collective-permute-start.3 = (bf16[512,2048]{1,0:T(8,128)(2,1)}, bf16[512,2048]{1,0:T(8,128)(2,1)}, u32[]{:S(2)}, u32[]{:S(2)}) collective-permute-start(bf16[512,2048]{1,0:T(8,128)(2,1)} %shard_map.283.refs_1_), channel_id=1, source_target_pairs={{0,8},{24,16},{1,9},{25,17},{2,10},{26,18},{3,11},{27,19},{4,12},{... | collective-permute-start | bytes 6291464 | tf_op jit(solution)/shard_map/ppermute | solution.py:42
  295.3 63.1 %all-to-all-start.1 = ((bf16[8,272,512]{2,1,0:T(8,128)(2,1)}), bf16[8,272,512]{2,1,0:T(8,128)(2,1)}, u32[]{:S(2)}, u32[]{:S(2)}) async-start(bf16[8,272,512]{2,1,0:T(8,128)(2,1)} %shard_map.287.refs_2_), calls=%async_computation.1 | async-start | bytes 4456448 | tf_op jit(solution)/shard_map/all_to_all | solution.py:720
  299.8 58.6 %collective-permute-start.5 = (bf16[528,2048]{1,0:T(8,128)(2,1)}, bf16[528,2048]{1,0:T(8,128)(2,1)}, u32[]{:S(2)}, u32[]{:S(2)}) collective-permute-start(bf16[528,2048]{1,0:T(8,128)(2,1)} %shard_map.286), channel_id=1, source_target_pairs={{0,8},{24,16},{1,9},{25,17},{2,10},{26,18},{3,11},{27,19},{4,12},{... | collective-permute-start | bytes 6488072 | tf_op jit(solution)/shard_map/ppermute | solution.py:42
  305.1 53.3 %collective-permute-start.4 = (bf16[512,2048]{1,0:T(8,128)(2,1)}, bf16[512,2048]{1,0:T(8,128)(2,1)}, u32[]{:S(2)}, u32[]{:S(2)}) collective-permute-start(bf16[512,2048]{1,0:T(8,128)(2,1)} %shard_map.288.refs_1_), channel_id=1, source_target_pairs={{8,16},{16,8},{9,17},{17,9},{10,18},{18,10},{11,19},{19,11},{12,20... | collective-permute-start | bytes 6291464 | tf_op jit(solution)/shard_map/ppermute | solution.py:42
  358.4 60.1 %collective-permute-start.11 = (bf16[8,272,512]{2,1,0:T(8,128)(2,1)}, bf16[8,272,512]{2,1,0:T(8,128)(2,1)}, u32[]{:S(2)}, u32[]{:S(2)}) collective-permute-start(bf16[8,272,512]{2,1,0:T(8,128)(2,1)} %all-to-all-done.1.refs_3_), channel_id=1, source_target_pairs={{0,8},{24,16},{1,9},{25,17},{2,10},{26,18},{3,11},{27,19},{4,12},{... | collective-permute-start | bytes 6684680 | tf_op jit(solution)/shard_map/ppermute | solution.py:42
  363.6 55.0 %collective-permute-start.10 = (bf16[528,2048]{1,0:T(8,128)(2,1)}, bf16[528,2048]{1,0:T(8,128)(2,1)}, u32[]{:S(2)}, u32[]{:S(2)}) collective-permute-start(bf16[528,2048]{1,0:T(8,128)(2,1)} %shard_map.293.refs_2_), channel_id=1, source_target_pairs={{8,16},{16,8},{9,17},{17,9},{10,18},{18,10},{11,19},{19,11},{12,20... | collective-permute-start | bytes 6488072 | tf_op jit(solution)/shard_map/ppermute | solution.py:42
  368.4 50.1 %collective-permute-start.9 = (bf16[512,2048]{1,0:T(8,128)(2,1)}, bf16[512,2048]{1,0:T(8,128)(2,1)}, u32[]{:S(2)}, u32[]{:S(2)}) collective-permute-start(bf16[512,2048]{1,0:T(8,128)(2,1)} %shard_map.292.refs_1_.refs_0_), channel_id=1, source_target_pairs={{8,0},{16,24},{9,1},{17,25},{10,2},{18,26},{11,3},{19,27},{12,4},{... | collective-permute-start | bytes 6291464 | tf_op jit(solution)/shard_map/ppermute | solution.py:42
  369.7 39.7 %all-to-all-start.2 = ((bf16[8,272,512]{2,1,0:T(8,128)(2,1)}), bf16[8,272,512]{2,1,0:T(8,128)(2,1)}, u32[]{:S(2)}, u32[]{:S(2)}) async-start(bf16[8,272,512]{2,1,0:T(8,128)(2,1)} %shard_map.290), calls=%async_computation.2 | async-start | bytes 4456448 | tf_op jit(solution)/shard_map/all_to_all | solution.py:720
  421.0 68.8 %collective-permute-start.12 = (bf16[528,2048]{1,0:T(8,128)(2,1)}, bf16[528,2048]{1,0:T(8,128)(2,1)}, u32[]{:S(2)}, u32[]{:S(2)}) collective-permute-start(bf16[528,2048]{1,0:T(8,128)(2,1)} %shard_map.297.refs_2_), channel_id=1, source_target_pairs={{8,0},{16,24},{9,1},{17,25},{10,2},{18,26},{11,3},{19,27},{12,4},{... | collective-permute-start | bytes 6488072 | tf_op jit(solution)/shard_map/ppermute | solution.py:42
  425.2 64.6 %collective-permute-start.13 = (bf16[8,272,512]{2,1,0:T(8,128)(2,1)}, bf16[8,272,512]{2,1,0:T(8,128)(2,1)}, u32[]{:S(2)}, u32[]{:S(2)}) collective-permute-start(bf16[8,272,512]{2,1,0:T(8,128)(2,1)} %bitcast.51.refs_3_), channel_id=1, source_target_pairs={{8,16},{16,8},{9,17},{17,9},{10,18},{18,10},{11,19},{19,11},{12,20... | collective-permute-start | bytes 6684680 | tf_op jit(solution)/shard_map/ppermute | solution.py:42
  427.2 62.6 %collective-permute-start.14 = (bf16[8,272,512]{2,1,0:T(8,128)(2,1)}, bf16[8,272,512]{2,1,0:T(8,128)(2,1)}, u32[]{:S(2)}, u32[]{:S(2)}) collective-permute-start(bf16[8,272,512]{2,1,0:T(8,128)(2,1)} %all-to-all-done.2.refs_4_), channel_id=1, source_target_pairs={{0,8},{24,16},{1,9},{25,17},{2,10},{26,18},{3,11},{27,19},{4,12},{... | collective-permute-start | bytes 6684680 | tf_op jit(solution)/shard_map/ppermute | solution.py:42
  465.4 75.3 %collective-permute-start.17 = (bf16[256,2048]{1,0:T(8,128)(2,1)}, bf16[256,2048]{1,0:T(8,128)(2,1)}, u32[]{:S(2)}, u32[]{:S(2)}) collective-permute-start(bf16[256,2048]{1,0:T(8,128)(2,1)} %shard_map.300), channel_id=1, source_target_pairs={{0,8},{24,16},{1,9},{25,17},{2,10},{26,18},{3,11},{27,19},{4,12},{... | collective-permute-start | bytes 3145736 | tf_op jit(solution)/shard_map/ppermute | solution.py:42
  467.8 72.9 %all-to-all-start.3 = ((bf16[8,272,768]{2,1,0:T(8,128)(2,1)}), bf16[8,272,768]{2,1,0:T(8,128)(2,1)}, u32[]{:S(2)}, u32[]{:S(2)}) async-start(bf16[8,272,768]{2,1,0:T(8,128)(2,1)} %shard_map.299.refs_4_), calls=%async_computation.3 | async-start | bytes 6684672 | tf_op jit(solution)/shard_map/all_to_all | solution.py:720
  489.3 32.3 %collective-permute-start.18 = (bf16[4,4096,256]{2,1,0:T(8,128)(2,1)}, bf16[4,4096,256]{2,1,0:T(8,128)(2,1)}, u32[]{:S(2)}, u32[]{:S(2)}) collective-permute-start(bf16[4,4096,256]{2,1,0:T(8,128)(2,1)} %shard_map.301.refs_5_), channel_id=1, source_target_pairs={{0,1},{1,0},{2,3},{3,2},{4,5},{5,4},{6,7},{7,6},{8,9},{9,8},{10,11... | collective-permute-start | bytes 25165832 | tf_op jit(solution)/shard_map/ppermute | solution.py:30
  492.9 47.9 %collective-permute-start.16 = (bf16[8,272,512]{2,1,0:T(8,128)(2,1)}, bf16[8,272,512]{2,1,0:T(8,128)(2,1)}, u32[]{:S(2)}, u32[]{:S(2)}) collective-permute-start(bf16[8,272,512]{2,1,0:T(8,128)(2,1)} %bitcast.58.refs_3_), channel_id=1, source_target_pairs={{8,16},{16,8},{9,17},{17,9},{10,18},{18,10},{11,19},{19,11},{12,20... | collective-permute-start | bytes 6684680 | tf_op jit(solution)/shard_map/ppermute | solution.py:42
  498.1 52.6 %collective-permute-start.15 = (bf16[8,272,512]{2,1,0:T(8,128)(2,1)}, bf16[8,272,512]{2,1,0:T(8,128)(2,1)}, u32[]{:S(2)}, u32[]{:S(2)}) collective-permute-start(bf16[8,272,512]{2,1,0:T(8,128)(2,1)} %bitcast.55.refs_2_.refs_0_), channel_id=1, source_target_pairs={{8,0},{16,24},{9,1},{17,25},{10,2},{18,26},{11,3},{19,27},{12,4},{... | collective-permute-start | bytes 6684680 | tf_op jit(solution)/shard_map/ppermute | solution.py:42
  521.6 43.8 %collective-permute-start.22 = (bf16[4,2,256,2048]{3,2,1,0:T(8,128)(2,1)}, bf16[4,2,256,2048]{3,2,1,0:T(8,128)(2,1)}, u32[]{:S(2)}, u32[]{:S(2)}) collective-permute-start(bf16[4,2,256,2048]{3,2,1,0:T(8,128)(2,1)} %shard_map.305.refs_6_), channel_id=1, source_target_pairs={{0,1},{1,0},{2,3},{3,2},{4,5},{5,4},{6,7},{7,6},{8,9},{9,8},{10,11... | collective-permute-start | bytes 25165832 | tf_op jit(solution)/shard_map/ppermute | solution.py:30
  554.7 38.8 %collective-permute-start.21 = (bf16[4,272,768]{2,1,0:T(8,128)(2,1)}, bf16[4,272,768]{2,1,0:T(8,128)(2,1)}, u32[]{:S(2)}, u32[]{:S(2)}) collective-permute-start(bf16[4,272,768]{2,1,0:T(8,128)(2,1)} %get-tuple-element.293.refs_4_), channel_id=1, source_target_pairs={{0,8},{24,16},{1,9},{25,17},{2,10},{26,18},{3,11},{27,19},{4,12},{... | collective-permute-start | bytes 5013512 | tf_op jit(solution)/shard_map/ppermute | solution.py:42
  557.6 47.5 %collective-permute-start.19 = (bf16[2,2048,256]{2,1,0:T(8,128)(2,1)}, bf16[2,2048,256]{2,1,0:T(8,128)(2,1)}, u32[]{:S(2)}, u32[]{:S(2)}) collective-permute-start(bf16[2,2048,256]{2,1,0:T(8,128)(2,1)} %get-tuple-element.215.refs_7_), channel_id=1, source_target_pairs={{0,2},{1,3},{2,0},{3,1},{4,6},{5,7},{6,4},{7,5},{8,10},{9,11},{10,... | collective-permute-start | bytes 6291464 | tf_op jit(solution)/shard_map/ppermute | solution.py:30
  559.5 47.2 %collective-permute-start.20 = (bf16[2,2048,256]{2,1,0:T(8,128)(2,1)}, bf16[2,2048,256]{2,1,0:T(8,128)(2,1)}, u32[]{:S(2)}, u32[]{:S(2)}) collective-permute-start(bf16[2,2048,256]{2,1,0:T(8,128)(2,1)} %get-tuple-element.216), channel_id=1, source_target_pairs={{0,4},{1,5},{2,6},{3,7},{4,0},{5,1},{6,2},{7,3},{8,12},{9,13},{10,... | collective-permute-start | bytes 6291464 | tf_op jit(solution)/shard_map/ppermute | solution.py:30
  561.0 66.7 %collective-permute-start.25 = (bf16[4,272,768]{2,1,0:T(8,128)(2,1)}, bf16[4,272,768]{2,1,0:T(8,128)(2,1)}, u32[]{:S(2)}, u32[]{:S(2)}) collective-permute-start(bf16[4,272,768]{2,1,0:T(8,128)(2,1)} %get-tuple-element.292.refs_5_), channel_id=1, source_target_pairs={{0,8},{24,16},{1,9},{25,17},{2,10},{26,18},{3,11},{27,19},{4,12},{... | collective-permute-start | bytes 5013512 | tf_op jit(solution)/shard_map/ppermute | solution.py:42
  596.1 47.4 %collective-permute-start.24 = (bf16[4,272,768]{2,1,0:T(8,128)(2,1)}, bf16[4,272,768]{2,1,0:T(8,128)(2,1)}, u32[]{:S(2)}, u32[]{:S(2)}) collective-permute-start(bf16[4,272,768]{2,1,0:T(8,128)(2,1)} %bitcast.65), channel_id=1, source_target_pairs={{8,16},{16,8},{9,17},{17,9},{10,18},{18,10},{11,19},{19,11},{12,20... | collective-permute-start | bytes 5013512 | tf_op jit(solution)/shard_map/ppermute | solution.py:42
  598.0 59.8 %collective-permute-start.27 = (bf16[8,272,512]{2,1,0:T(8,128)(2,1)S(1)}, bf16[8,272,512]{2,1,0:T(8,128)(2,1)}, u32[]{:S(2)}, u32[]{:S(2)}) collective-permute-start(bf16[8,272,512]{2,1,0:T(8,128)(2,1)S(1)} %bitcast.131), channel_id=1, source_target_pairs={{8,0},{16,24},{9,1},{17,25},{10,2},{18,26},{11,3},{19,27},{12,4},{... | collective-permute-start | bytes 6684680 | tf_op jit(solution)/shard_map/ppermute | solution.py:42
  605.0 46.6 %collective-permute-start.28 = (bf16[2,256,2048]{2,1,0:T(8,128)(2,1)}, bf16[2,256,2048]{2,1,0:T(8,128)(2,1)}, u32[]{:S(2)}, u32[]{:S(2)}) collective-permute-start(bf16[2,256,2048]{2,1,0:T(8,128)(2,1)} %get-tuple-element.242), channel_id=1, source_target_pairs={{0,2},{1,3},{2,0},{3,1},{4,6},{5,7},{6,4},{7,5},{8,10},{9,11},{10,... | collective-permute-start | bytes 6291464 | tf_op jit(solution)/shard_map/ppermute | solution.py:30
  606.8 46.7 %collective-permute-start.29 = (bf16[2,256,2048]{2,1,0:T(8,128)(2,1)}, bf16[2,256,2048]{2,1,0:T(8,128)(2,1)}, u32[]{:S(2)}, u32[]{:S(2)}) collective-permute-start(bf16[2,256,2048]{2,1,0:T(8,128)(2,1)} %get-tuple-element.243), channel_id=1, source_target_pairs={{0,4},{1,5},{2,6},{3,7},{4,0},{5,1},{6,2},{7,3},{8,12},{9,13},{10,... | collective-permute-start | bytes 6291464 | tf_op jit(solution)/shard_map/ppermute | solution.py:30
  630.3 47.7 %collective-permute-start.32 = (bf16[4,272,768]{2,1,0:T(8,128)(2,1)}, bf16[4,272,768]{2,1,0:T(8,128)(2,1)}, u32[]{:S(2)}, u32[]{:S(2)}) collective-permute-start(bf16[4,272,768]{2,1,0:T(8,128)(2,1)} %bitcast.71), channel_id=1, source_target_pairs={{8,16},{16,8},{9,17},{17,9},{10,18},{18,10},{11,19},{19,11},{12,20... | collective-permute-start | bytes 5013512 | tf_op jit(solution)/shard_map/ppermute | solution.py:42
  643.5 105.2 %copy-start.45 = (f32[256]{0:T(256)}, f32[256]{0:T(256)S(1)}, u32[]{:S(2)}) copy-start(f32[256]{0:T(256)S(1)} %convert_reduce_fusion.3) | copy-start | bytes 3076
  646.3 43.1 %collective-permute-start.26 = (bf16[4,272,768]{2,1,0:T(8,128)(2,1)}, bf16[4,272,768]{2,1,0:T(8,128)(2,1)}, u32[]{:S(2)}, u32[]{:S(2)}) collective-permute-start(bf16[4,272,768]{2,1,0:T(8,128)(2,1)} %bitcast.75.refs_0_), channel_id=1, source_target_pairs={{8,0},{16,24},{9,1},{17,25},{10,2},{18,26},{11,3},{19,27},{12,4},{... | collective-permute-start | bytes 5013512 | tf_op jit(solution)/shard_map/ppermute | solution.py:42
  651.6 29.7 %collective-permute-start.23 = (bf16[256,2048]{1,0:T(8,128)(2,1)S(1)}, bf16[256,2048]{1,0:T(8,128)(2,1)}, u32[]{:S(2)}, u32[]{:S(2)}) collective-permute-start(bf16[256,2048]{1,0:T(8,128)(2,1)S(1)} %copy-done.20), channel_id=1, source_target_pairs={{8,16},{16,8},{9,17},{17,9},{10,18},{18,10},{11,19},{19,11},{12,20... | collective-permute-start | bytes 3145736 | tf_op jit(solution)/shard_map/ppermute | solution.py:42
  657.8 23.5 %collective-permute-start.30 = (bf16[256,2048]{1,0:T(8,128)(2,1)}, bf16[256,2048]{1,0:T(8,128)(2,1)}, u32[]{:S(2)}, u32[]{:S(2)}) collective-permute-start(bf16[256,2048]{1,0:T(8,128)(2,1)} %shard_map.317), channel_id=1, source_target_pairs={{0,4},{1,5},{2,6},{3,7},{4,0},{5,1},{6,2},{7,3},{8,12},{9,13},{10,... | collective-permute-start | bytes 3145736 | tf_op jit(solution)/shard_map/ppermute | solution.py:30
  659.3 22.6 %collective-permute-start.31 = (bf16[256,2048]{1,0:T(8,128)(2,1)}, bf16[256,2048]{1,0:T(8,128)(2,1)}, u32[]{:S(2)}, u32[]{:S(2)}) collective-permute-start(bf16[256,2048]{1,0:T(8,128)(2,1)} %shard_map.318), channel_id=1, source_target_pairs={{0,2},{1,3},{2,0},{3,1},{4,6},{5,7},{6,4},{7,5},{8,10},{9,11},{10,... | collective-permute-start | bytes 3145736 | tf_op jit(solution)/shard_map/ppermute | solution.py:30
  679.8 45.3 %collective-permute-start.36 = (bf16[4,272,768]{2,1,0:T(8,128)(2,1)S(1)}, bf16[4,272,768]{2,1,0:T(8,128)(2,1)}, u32[]{:S(2)}, u32[]{:S(2)}) collective-permute-start(bf16[4,272,768]{2,1,0:T(8,128)(2,1)S(1)} %bitcast.135), channel_id=1, source_target_pairs={{8,0},{16,24},{9,1},{17,25},{10,2},{18,26},{11,3},{19,27},{12,4},{... | collective-permute-start | bytes 5013512 | tf_op jit(solution)/shard_map/ppermute | solution.py:42
  689.4 48.8 %collective-permute-start.34 = (bf16[2048,256]{1,0:T(8,128)(2,1)}, bf16[2048,256]{1,0:T(8,128)(2,1)}, u32[]{:S(2)}, u32[]{:S(2)}) collective-permute-start(bf16[2048,256]{1,0:T(8,128)(2,1)} %shard_map.312), channel_id=1, source_target_pairs={{0,4},{1,5},{2,6},{3,7},{4,0},{5,1},{6,2},{7,3},{8,12},{9,13},{10,... | collective-permute-start | bytes 3145736 | tf_op jit(solution)/shard_map/ppermute | solution.py:30
  691.7 46.4 %collective-permute-start.35 = (bf16[2048,256]{1,0:T(8,128)(2,1)}, bf16[2048,256]{1,0:T(8,128)(2,1)}, u32[]{:S(2)}, u32[]{:S(2)}) collective-permute-start(bf16[2048,256]{1,0:T(8,128)(2,1)} %shard_map.313), channel_id=1, source_target_pairs={{0,2},{1,3},{2,0},{3,1},{4,6},{5,7},{6,4},{7,5},{8,10},{9,11},{10,... | collective-permute-start | bytes 3145736 | tf_op jit(solution)/shard_map/ppermute | solution.py:30
  694.4 50.7 %collective-permute-start.33 = (bf16[256,2048]{1,0:T(8,128)(2,1)S(1)}, bf16[256,2048]{1,0:T(8,128)(2,1)}, u32[]{:S(2)}, u32[]{:S(2)}) collective-permute-start(bf16[256,2048]{1,0:T(8,128)(2,1)S(1)} %shard_map.321.refs_0_), channel_id=1, source_target_pairs={{8,0},{16,24},{9,1},{17,25},{10,2},{18,26},{11,3},{19,27},{12,4},{... | collective-permute-start | bytes 3145736 | tf_op jit(solution)/shard_map/ppermute | solution.py:42
  (56 other events, 513.3 us)
Sparse Core Ops, SparseCore 0:
  12.1 117.0 all-gather.4
  131.7 89.8 all-gather.2

commit v5 on v4

--- a/solution.py
+++ b/solution.py
@@ -951,16 +951,16 @@
             resid, grad_rows,
             [(norm_keep_one, norm_got_one, norm_last_one), (norm_keep_two, norm_got_two, norm_last_two)],
         )
-        qkv_back, tokens_grad = tie(qkv_back, tokens_grad)
-        qkv_grad, gain_one_grad, shift_one_grad, sum_qkv = column_grads(
-            inner, list(zip(qkv_total, qkv_back)), qkv_weight, ln1_gain, ln1_bias, HD, 2, False, token
-        )
-        last_one, last_two, qkv_grad = tie(last_one, last_two, qkv_grad)
+        last_one, last_two, tokens_grad = tie(last_one, last_two, tokens_grad)
         out_given = out_blocks(
             tables[0], tables[1], own, [(keep_one, got_one, last_one), (keep_two, got_two, last_two)],
             out_bias.astype(f32) + down_bias.astype(f32),
         )
-        out_back, out_given = tie(out_back, out_given)
+        qkv_back, out_given = tie(qkv_back, out_given)
+        qkv_grad, gain_one_grad, shift_one_grad, sum_qkv = column_grads(
+            inner, list(zip(qkv_total, qkv_back)), qkv_weight, ln1_gain, ln1_bias, HD, 2, False, token
+        )
+        out_back, qkv_grad = tie(out_back, qkv_grad)
         out_grad = row_grads(inner, [(out_total, out_back)])
     else:
         sums = jnp.concatenate([sum_mixed[0], sum_hidden[0]])

time: 767 us -> 772 us (level)
  waiting for transfers between devices: 171 us -> 179 us
  transfers between devices with their start and end apart: 43 -> 43, of which waited for: 14 -> 16; matrix products, arithmetic and copies ran while one was open for 14% -> 13% of each run, Pallas kernels for 43% -> 42%
where the time goes in v5:
time: 772 us; the launch traced here: 762 us
  Pallas kernels  329 us (43%)
  waiting for transfers between devices  179 us (23%)
  starting transfers between devices  113 us (15%)
  local copies, waits for them, and re-layouts  51.4 us (7%)
  matrix products  46.5 us (6%)
  other arithmetic  27.5 us (4%)
  between operations  15.6 us (2%)
    ppermute x21, waiting for transfers between devices, rep_move(): lax.ppermute(value, 'rep', pairs)  63.6 us
    ppermute x6, waiting for transfers between devices, exchange(): lax.ppermute(part, 'rep', [(i, (i + k) % shares) for i in range(shares)])  60.1 us
    ppermute x21, starting transfers between devices, rep_move(): lax.ppermute(value, 'rep', pairs)  49.8 us
    pallas_call x2, Pallas kernels, norm_terms(): pl.pallas_call(body, grid_spec=pltpu.PrefetchScalarGridSpec(num_scalar_pr...  47.3 us
    pallas_call x3, Pallas kernels, normed_dot(): pl.pallas_call(body, grid_spec=pltpu.PrefetchScalarGridSpec(num_scalar_pr...  46.5 us
    dot_general x2, matrix products, dot(): lax.dot_general(a, b, (((ca,), (cb,)), ((), ())), preferred_element_type=...  46.5 us
    pallas_call x18, Pallas kernels, plus_low(): pl.pallas_call(body, grid_spec=pltpu.PrefetchScalarGridSpec(num_scalar_pr...  42.2 us
    pallas_call x3, Pallas kernels, token_dot(): pl.pallas_call(body, grid=(blocks // step,), in_specs=[spec((rows, width)...  37.9 us
  transfers between devices with their start and end apart: 43, of which 16 were waited for; matrix products, arithmetic and copies ran while one was open for 13% of the time, Pallas kernels for 42%

profile of v5, /device:TPU:0, one launch (start us, length us, event | category | flops | bytes accessed | tf_op | source)
XLA Modules:
  0.0 761.8 jit_solution(16724642909854242721)
XLA Ops:
  28.4 5.1 all-to-all-start
  33.9 3.1 slice_bitcast_fusion.1
  42.6 3.1 pad_maximum_fusion.1.refs_3_
  50.8 23.8 %all-to-all-done = bf16[8,80,1792]{2,1,0:T(8,128)(2,1)} async-done(((bf16[8,80,1792]{2,1,0:T(8,128)(2,1)}), bf16[8,80,1792]{2,1,0:T(8,128)(2,1)}, u32[]{:S(2)}, u32[]{:S(2)}) %all-to-all-start) | async-done | bytes 2293792 | tf_op jit(solution)/shard_map/all_to_all | solution.py:720
  84.9 19.2 %collective-permute-done = bf16[8,64,1024]{2,1,0:T(8,128)(2,1)S(1)} collective-permute-done((bf16[8,64,1024]{2,1,0:T(8,128)(2,1)S(1)}, bf16[8,64,1024]{2,1,0:T(8,128)(2,1)S(1)}, u32[]{:S(2)}, u32[]{:S(2)}) %collective-permute-start) | collective-permute-done | bytes 1048608 | tf_op jit(solution)/shard_map/ppermute | solution.py:777
  104.1 41.0 %collective-permute-done.1 = bf16[8,64,1024]{2,1,0:T(8,128)(2,1)S(1)} collective-permute-done((bf16[8,64,1024]{2,1,0:T(8,128)(2,1)S(1)}, bf16[8,64,1024]{2,1,0:T(8,128)(2,1)S(1)}, u32[]{:S(2)}, u32[]{:S(2)}) %collective-permute-start.1) | collective-permute-done | bytes 1048608 | tf_op jit(solution)/shard_map/ppermute | solution.py:777
  152.0 22.1 %collective-permute-start.6 = (bf16[8,64,768]{2,1,0:T(8,128)(2,1)}, bf16[8,64,768]{2,1,0:T(8,128)(2,1)}, u32[]{:S(2)}, u32[]{:S(2)}) collective-permute-start(bf16[8,64,768]{2,1,0:T(8,128)(2,1)} %slice.57), channel_id=1, source_target_pairs={{0,8},{8,16},{16,24},{24,0},{1,9},{9,17},{17,25},{25,1},{2,10},{10... | collective-permute-start | bytes 2359304 | tf_op jit(solution)/shard_map/ppermute | solution.py:777
  176.6 27.9 %fusion.3 = (f32[4096,1024]{1,0:T(8,128)}, bf16[4096,1024]{1,0:T(8,128)(2,1)}) fusion(f32[1024]{0:T(1024)S(1)} %convert_add_fusion, bf16[4096,2048]{1,0:T(8,128)(2,1)} %all-gather.5.cloned.1.call-done.left_ref, bf16[2048,1024]{1,0:T(8,128)(2,1)S(1)} %bitcast.152), kind=kOutput, calls=%fused_computation.6 | convolution fusion | flops 17226006528 | bytes 46141440 | tf_op jit(solution)/shard_map/dot_general | solution.py:26
  204.5 17.1 %all-gather.3.cloned.1.call-done.right_ref.grad_ref = bf16[8,4096,256]{2,1,0:T(8,128)(2,1)} async-done(((bf16[1,4096,256]{2,1,0:T(8,128)(2,1)}), bf16[8,4096,256]{2,1,0:T(8,128)(2,1)}) %all-gather.3.cloned.1.call-update) | async-done | bytes 16777232 | tf_op jit(solution)/shard_map/all_gather | solution.py:770
  221.6 13.8 %shard_map.283.refs_1_ = bf16[512,2048]{1,0:T(8,128)(2,1)} custom-call(bf16[4096,1024]{1,0:T(8,128)(2,1)} %get-tuple-element.163.left_ref.refs_1_, bf16[8,4096,256]{2,1,0:T(8,128)(2,1)} %all-gather.3.cloned.1.call-done.right_ref.grad_ref), custom_call_target="tpu_custom_call" | custom-call | flops 1024 | bytes 1024 | tf_op jit(solution)/shard_map/pallas_call | solution.py:397
  235.5 4.9 collective-permute-start.3
  242.0 13.9 %shard_map.286 = bf16[528,2048]{1,0:T(8,128)(2,1)} custom-call(bf16[4096,1024]{1,0:T(8,128)(2,1)} %get-tuple-element.163.left_ref.refs_1_, bf16[8,4096,256]{2,1,0:T(8,128)(2,1)} %all-gather.3.cloned.1.call-done.right_ref.grad_ref, bf16[16,2048]{1,0:T(8,128)(2,1)} %convert_element_type.125.refs_0_), custom_call_target="tpu_custom_call" | custom-call | flops 1024 | bytes 1024 | tf_op jit(solution)/shard_map/pallas_call | solution.py:397
  255.9 24.9 %shard_map.285 = (bf16[4096,1024]{1,0:T(8,128)(2,1)}, f32[1,1024]{1,0:T(1,128)S(1)}) custom-call(bf16[8,4096,256]{2,1,0:T(8,128)(2,1)} %all-gather.3.cloned.1.call-done.right_ref.grad_ref, bf16[1024,2048]{1,0:T(8,128)(2,1)} %refs_9_.3, f32[4096,1024]{1,0:T(8,128)} %get-tuple-element.290.slope_ref), custom_call_target="tpu_custom_call" | custom-call | flops 1024 | bytes 1024 | tf_op jit(solution)/shard_map/pallas_call | solution.py:551
  281.5 13.8 %shard_map.287.refs_2_ = bf16[8,272,512]{2,1,0:T(8,128)(2,1)} custom-call(s32[1]{0:T(128)} %bitcast.spot_ref, bf16[4096,2048]{1,0:T(8,128)(2,1)} %all-gather.5.cloned.1.call-done.left_ref, bf16[4096,1024]{1,0:T(8,128)(2,1)} %get-tuple-element.168.right_ref.refs_1_, f32[1,1024]{1,0:T(1,128)} %copy-done.24), custom_call_target="tpu_custom_call" | custom-call | flops 1024 | bytes 1024 | tf_op jit(solution)/shard_map/pallas_call | solution.py:429
  295.2 4.5 all-to-all-start.1
  307.5 13.8 %shard_map.290 = bf16[8,272,512]{2,1,0:T(8,128)(2,1)} custom-call(s32[1]{0:T(128)} %bitcast.spot_ref, bf16[4096,2048]{1,0:T(8,128)(2,1)} %all-gather.5.cloned.1.call-done.left_ref, bf16[4096,1024]{1,0:T(8,128)(2,1)} %get-tuple-element.168.right_ref.refs_1_, f32[1,1024]{1,0:T(1,128)} %copy-done.24), custom_call_target="tpu_custom_call" | custom-call | flops 1024 | bytes 1024 | tf_op jit(solution)/shard_map/pallas_call | solution.py:429
  321.4 11.6 %shard_map.291 = bf16[4096,256]{1,0:T(8,128)(2,1)} custom-call(bf16[8,4096,256]{2,1,0:T(8,128)(2,1)} %all-gather.3.cloned.1.call-done.right_ref.grad_ref, bf16[256,2048]{1,0:T(8,128)(2,1)S(1)} %copy-done), custom_call_target="tpu_custom_call" | custom-call | flops 1024 | bytes 1024 | tf_op jit(solution)/shard_map/pallas_call | solution.py:573
  339.8 18.6 %convolution_add_fusion = f32[4096,768]{1,0:T(8,128)} fusion(bf16[4096,2048]{1,0:T(8,128)(2,1)} %all-gather.5.cloned.1.call-done.left_ref, bf16[2048,768]{1,0:T(8,128)(2,1)S(1)} %bitcast.155, f32[768]{0:T(1024)S(1)} %slice-done), kind=kOutput, calls=%fused_computation.10 | convolution fusion | flops 12888047616 | bytes 32508928 | tf_op jit(solution)/shard_map/dot_general | solution.py:26
  361.1 4.4 all-to-all-start.2
  369.9 2.8 shard_map.292.refs_1_.refs_0_
  374.9 32.6 %shard_map.295 = (bf16[8,2,2,128,256]{4,3,2,1,0:T(8,128)(2,1)}, bf16[8,2,2,128,768]{4,3,2,1,0:T(8,128)(2,1)}, f32[2,8,768]{2,1,0:T(8,128)S(1)}) custom-call(s32[2,16]{1,0:T(2,128)S(1)} %get-tuple-element.304.piece_of.piece_ref, s32[2,16]{1,0:T(2,128)S(1)} %get-tuple-element.303.inner_of.inner_ref, s32[2,16]{1,0:T(2,128)S(1)} %copy-done.30, ...), custom_call_target="tpu_custom_call" | custom-call | flops 1024 | bytes 1024 | tf_op jit(solution)/shard_map/pallas_call | solution.py:206
  408.1 14.8 %collective-permute-done.9.refs_1_ = bf16[512,2048]{1,0:T(8,128)(2,1)} collective-permute-done((bf16[512,2048]{1,0:T(8,128)(2,1)}, bf16[512,2048]{1,0:T(8,128)(2,1)}, u32[]{:S(2)}, u32[]{:S(2)}) %collective-permute-start.9) | collective-permute-done | bytes 2097184 | tf_op jit(solution)/shard_map/ppermute | solution.py:42
  422.8 2.9 shard_map.297
  431.5 8.2 %collective-permute-start.15 = (bf16[8,272,512]{2,1,0:T(8,128)(2,1)}, bf16[8,272,512]{2,1,0:T(8,128)(2,1)}, u32[]{:S(2)}, u32[]{:S(2)}) collective-permute-start(bf16[8,272,512]{2,1,0:T(8,128)(2,1)} %all-to-all-done.2.refs_4_), channel_id=1, source_target_pairs={{0,8},{24,16},{1,9},{25,17},{2,10},{26,18},{3,11},{27,19},{4,12},{... | collective-permute-start | bytes 6684680 | tf_op jit(solution)/shard_map/ppermute | solution.py:42
  439.7 18.9 %shard_map.299.refs_4_ = bf16[8,272,768]{2,1,0:T(8,128)(2,1)} custom-call(s32[1]{0:T(128)} %bitcast.spot_ref, bf16[4096,2048]{1,0:T(8,128)(2,1)} %all-gather.5.cloned.1.call-done.left_ref, bf16[4096,768]{1,0:T(8,128)(2,1)} %bitcast.149, f32[1,768]{1,0:T(1,128)} %broadcast_in_dim.218.sum_ref), custom_call_target="tpu_custom_call" | custom-call | flops 1024 | bytes 1024 | tf_op jit(solution)/shard_map/pallas_call | solution.py:429
  458.6 10.1 %shard_map.300 = bf16[256,2048]{1,0:T(8,128)(2,1)} custom-call(bf16[4096,256]{1,0:T(8,128)(2,1)} %bitcast.158, bf16[8,4096,256]{2,1,0:T(8,128)(2,1)} %all-gather.3.cloned.1.call-done.right_ref.grad_ref), custom_call_target="tpu_custom_call" | custom-call | flops 1024 | bytes 1024 | tf_op jit(solution)/shard_map/pallas_call | solution.py:397
  471.1 4.7 all-to-all-start.3
  475.8 16.8 %shard_map.301.refs_5_ = bf16[4,4096,256]{2,1,0:T(8,128)(2,1)} custom-call(s32[8]{0:T(128)S(1)} %broadcast_xor_fusion.owners_ref, s32[1]{0:T(128)} %bitcast.53.place_ref, bf16[4096,256]{1,0:T(8,128)(2,1)} %bitcast.159, bf16[4096,1024]{1,0:T(8,128)(2,1)} %get-tuple-element.163.left_ref.refs_1_, bf16[256,2048]{1,0:T(8,128)(2,1)S(1)} %copy-done.1, ...), custom_call_target="tpu_custom_call" | custom-call | flops 1024 | bytes 1024 | tf_op jit(solution)/shard_map/pallas_call | solution.py:316
  493.1 3.1 shard_map.303
  498.3 3.0 shard_map.302
  502.6 22.2 %shard_map.305.refs_6_ = bf16[4,2,256,2048]{3,2,1,0:T(8,128)(2,1)} custom-call(s32[8]{0:T(128)S(1)} %broadcast_xor_fusion.owners_ref, bf16[4096,768]{1,0:T(8,128)(2,1)} %bitcast.150, bf16[4096,1024]{1,0:T(8,128)(2,1)} %get-tuple-element.168.right_ref.refs_1_, bf16[2048,768]{1,0:T(8,128)(2,1)} %bitcast.156, bf16[2048,1024]{1,0:T(8,128)(2,1)} %bitcast.153), custom_call_target="tpu_custom_call" | custom-call | flops 1024 | bytes 1024 | tf_op jit(solution)/shard_map/pallas_call | solution.py:373
  524.9 19.1 %shard_map.306 = (bf16[2,2048,256]{2,1,0:T(8,128)(2,1)}, bf16[2,2048,256]{2,1,0:T(8,128)(2,1)}, bf16[2,2048,256]{2,1,0:T(8,128)(2,1)}, bf16[2,2048,256]{2,1,0:T(8,128)(2,1)}) custom-call(s32[8]{0:T(128)S(1)} %broadcast_xor_fusion.owners_ref, s32[1]{0:T(128)} %bitcast.53.place_ref, bf16[4096,256]{1,0:T(8,128)(2,1)} %bitcast.160, ...), custom_call_target="tpu_custom_call" | custom-call | flops 1024 | bytes 1024 | tf_op jit(solution)/shard_map/pallas_call | solution.py:316
  544.0 9.9 %collective-permute-done.18.refs_1_ = bf16[8,272,512]{2,1,0:T(8,128)(2,1)} collective-permute-done((bf16[8,272,512]{2,1,0:T(8,128)(2,1)}, bf16[8,272,512]{2,1,0:T(8,128)(2,1)}, u32[]{:S(2)}, u32[]{:S(2)}) %collective-permute-start.18) | collective-permute-done | bytes 2228256 | tf_op jit(solution)/shard_map/ppermute | solution.py:42
  553.9 4.0 fusion.14
  568.6 25.1 %shard_map.309 = (bf16[2,256,2048]{2,1,0:T(8,128)(2,1)}, bf16[2,256,2048]{2,1,0:T(8,128)(2,1)}, bf16[2,256,2048]{2,1,0:T(8,128)(2,1)}, bf16[2,256,2048]{2,1,0:T(8,128)(2,1)}) custom-call(s32[8]{0:T(128)S(1)} %broadcast_xor_fusion.owners_ref, bf16[4096,768]{1,0:T(8,128)(2,1)} %bitcast.151, bf16[4096,1024]{1,0:T(8,128)(2,1)} %get-tuple-element.168.right_ref.refs_1_, ...), custom_call_target="tpu_custom_call" | custom-call | flops 1024 | bytes 1024 | tf_op jit(solution)/shard_map/pallas_call | solution.py:373
  593.8 3.0 collective-permute-done.21
  602.5 5.8 collective-permute-done.16.b_ref.refs_1_
  618.3 12.6 %collective-permute-done.25 = bf16[4,272,768]{2,1,0:T(8,128)(2,1)} collective-permute-done((bf16[4,272,768]{2,1,0:T(8,128)(2,1)}, bf16[4,272,768]{2,1,0:T(8,128)(2,1)}, u32[]{:S(2)}, u32[]{:S(2)}) %collective-permute-start.25) | collective-permute-done | bytes 1671200 | tf_op jit(solution)/shard_map/ppermute | solution.py:42
  635.4 7.1 shard_map.315
  650.9 3.8 collective-permute-done.28.b_ref.refs_1_
  666.5 14.7 %shard_map.319 = (f32[256,8192]{1,0:T(8,128)}, f32[256,128]{1,0:T(8,128)S(1)}, f32[256,128]{1,0:T(8,128)S(1)}, f32[1,8192]{1,0:T(1,128)S(1)}) custom-call(s32[1]{0:T(128)S(6)} %convert_element_type.102.needed_ref.inner_ref, bf16[8,272,512]{2,1,0:T(8,128)(2,1)} %bitcast.56.refs_2_.refs_0_, bf16[8,272,512]{2,1,0:T(8,128)(2,1)} %collective-permute-done.18.refs_1_, ...), custom_call_target="tpu_custom_call" | custom-call | flops 1024 | bytes 1024 | tf_op jit(solution)/shard_map/pallas_call | solution.py:655
  685.2 7.4 collective-permute-done.26.refs_1_
  703.7 8.2 %shard_map.322 = bf16[512,2048]{1,0:T(8,128)(2,1)} custom-call(bf16[512,2048]{1,0:T(8,128)(2,1)} %bitcast.148, bf16[512,2048]{1,0:T(8,128)(2,1)} %bitcast.167, bf16[2,256,2048]{2,1,0:T(8,128)(2,1)} %get-tuple-element.240.a_ref.refs_0_, bf16[2,256,2048]{2,1,0:T(8,128)(2,1)} %collective-permute-done.28.b_ref.refs_1_, ...), custom_call_target="tpu_custom_call" | custom-call | flops 1024 | bytes 1024 | tf_op jit(solution)/shard_map/pallas_call | solution.py:512
  715.6 5.8 shard_map.323
  721.4 7.0 collective-permute-done.33.refs_3_
  728.4 11.0 %shard_map.324 = (f32[256,6144]{1,0:T(8,128)}, f32[256,128]{1,0:T(8,128)S(1)}, f32[256,128]{1,0:T(8,128)S(1)}, f32[1,6144]{1,0:T(1,128)S(1)}) custom-call(s32[1]{0:T(128)S(6)} %convert_element_type.102.needed_ref.inner_ref, bf16[4,272,768]{2,1,0:T(8,128)(2,1)} %bitcast.74.refs_0_, bf16[4,272,768]{2,1,0:T(8,128)(2,1)} %collective-permute-done.26.refs_1_, ...), custom_call_target="tpu_custom_call" | custom-call | flops 1024 | bytes 1024 | tf_op jit(solution)/shard_map/pallas_call | solution.py:655
  739.3 8.9 %collective-permute-done.36.refs_1_ = bf16[256,2048]{1,0:T(8,128)(2,1)} collective-permute-done((bf16[256,2048]{1,0:T(8,128)(2,1)S(1)}, bf16[256,2048]{1,0:T(8,128)(2,1)}, u32[]{:S(2)}, u32[]{:S(2)}) %collective-permute-start.36) | collective-permute-done | bytes 1048608 | tf_op jit(solution)/shard_map/ppermute | solution.py:42
  750.3 3.6 shard_map.325
  (309 shorter events, 162.5 us)
Async XLA Ops:
  7.2 138.8 %all-gather.5.cloned.1.call-start = ((), (), s32[]{:S(2)}) async-start(), calls=%async_computation.5 | async-start | bytes 18874368 | tf_op jit(solution)/shard_map/all_gather | solution.py:740
  28.4 46.3 %all-to-all-start = ((bf16[8,80,1792]{2,1,0:T(8,128)(2,1)}), bf16[8,80,1792]{2,1,0:T(8,128)(2,1)}, u32[]{:S(2)}, u32[]{:S(2)}) async-start(bf16[8,80,1792]{2,1,0:T(8,128)(2,1)} %pad_maximum_fusion), calls=%async_computation | async-start | bytes 4587520 | tf_op jit(solution)/shard_map/all_to_all | solution.py:720
  33.5 188.1 %all-gather.3.cloned.1.call-start = ((), (), s32[]{:S(2)}) async-start(), calls=%async_computation.4 | async-start | bytes 18874368 | tf_op jit(solution)/shard_map/all_gather | solution.py:770
  76.0 28.0 %collective-permute-start = (bf16[8,64,1024]{2,1,0:T(8,128)(2,1)S(1)}, bf16[8,64,1024]{2,1,0:T(8,128)(2,1)S(1)}, u32[]{:S(2)}, u32[]{:S(2)}) collective-permute-start(bf16[8,64,1024]{2,1,0:T(8,128)(2,1)S(1)} %slice.54), channel_id=1, source_target_pairs={{0,8},{8,16},{16,24},{24,0},{1,9},{9,17},{17,25},{25,1},{2,10},{10... | collective-permute-start | bytes 3145736 | tf_op jit(solution)/shard_map/ppermute | solution.py:777
  77.5 67.5 %collective-permute-start.1 = (bf16[8,64,1024]{2,1,0:T(8,128)(2,1)S(1)}, bf16[8,64,1024]{2,1,0:T(8,128)(2,1)S(1)}, u32[]{:S(2)}, u32[]{:S(2)}) collective-permute-start(bf16[8,64,1024]{2,1,0:T(8,128)(2,1)S(1)} %slice.54), channel_id=1, source_target_pairs={{0,16},{8,24},{16,0},{24,8},{1,17},{9,25},{17,1},{25,9},{2,18},{10... | collective-permute-start | bytes 3145736 | tf_op jit(solution)/shard_map/ppermute | solution.py:777
  80.0 66.1 %collective-permute-start.2 = (bf16[8,64,1024]{2,1,0:T(8,128)(2,1)S(1)}, bf16[8,64,1024]{2,1,0:T(8,128)(2,1)}, u32[]{:S(2)}, u32[]{:S(2)}) collective-permute-start(bf16[8,64,1024]{2,1,0:T(8,128)(2,1)S(1)} %slice.54), channel_id=1, source_target_pairs={{0,24},{8,0},{16,8},{24,16},{1,25},{9,1},{17,9},{25,17},{2,26},{10... | collective-permute-start | bytes 3145736 | tf_op jit(solution)/shard_map/ppermute | solution.py:777
  81.6 292.6 %copy-start.25 = (s32[2,16]{1,0:T(2,128)}, s32[2,16]{1,0:T(2,128)S(1)}, u32[]{:S(2)}) copy-start(s32[2,16]{1,0:T(2,128)S(1)} %get-tuple-element.303.inner_of.inner_ref) | copy-start | bytes 388
  81.6 292.6 %copy-start.27 = (s32[2,16]{1,0:T(2,128)}, s32[2,16]{1,0:T(2,128)S(1)}, u32[]{:S(2)}) copy-start(s32[2,16]{1,0:T(2,128)S(1)} %get-tuple-element.304.piece_of.piece_ref) | copy-start | bytes 388
  84.9 119.6 %copy-start.39 = (f32[1792]{0:T(1024)}, f32[1792]{0:T(1024)S(1)}, u32[]{:S(2)}) copy-start(f32[1792]{0:T(1024)S(1)} %convert_reduce_fusion.2) | copy-start | bytes 21508
  104.1 41.0 %copy-start.35 = (bf16[8,64,1024]{2,1,0:T(8,128)(2,1)}, bf16[8,64,1024]{2,1,0:T(8,128)(2,1)S(1)}, u32[]{:S(2)}) copy-start(bf16[8,64,1024]{2,1,0:T(8,128)(2,1)S(1)} %collective-permute-done) | copy-start | bytes 3145732
  152.0 181.0 %collective-permute-start.6 = (bf16[8,64,768]{2,1,0:T(8,128)(2,1)}, bf16[8,64,768]{2,1,0:T(8,128)(2,1)}, u32[]{:S(2)}, u32[]{:S(2)}) collective-permute-start(bf16[8,64,768]{2,1,0:T(8,128)(2,1)} %slice.57), channel_id=1, source_target_pairs={{0,8},{8,16},{16,24},{24,0},{1,9},{9,17},{17,25},{25,1},{2,10},{10... | collective-permute-start | bytes 2359304 | tf_op jit(solution)/shard_map/ppermute | solution.py:777
  174.0 158.9 %collective-permute-start.7 = (bf16[8,64,768]{2,1,0:T(8,128)(2,1)}, bf16[8,64,768]{2,1,0:T(8,128)(2,1)}, u32[]{:S(2)}, u32[]{:S(2)}) collective-permute-start(bf16[8,64,768]{2,1,0:T(8,128)(2,1)} %slice.57), channel_id=1, source_target_pairs={{0,16},{8,24},{16,0},{24,8},{1,17},{9,25},{17,1},{25,9},{2,18},{10... | collective-permute-start | bytes 2359304 | tf_op jit(solution)/shard_map/ppermute | solution.py:777
  176.6 156.4 %collective-permute-start.8 = (bf16[8,64,768]{2,1,0:T(8,128)(2,1)}, bf16[8,64,768]{2,1,0:T(8,128)(2,1)}, u32[]{:S(2)}, u32[]{:S(2)}) collective-permute-start(bf16[8,64,768]{2,1,0:T(8,128)(2,1)} %slice.57), channel_id=1, source_target_pairs={{0,24},{8,0},{16,8},{24,16},{1,25},{9,1},{17,9},{25,17},{2,26},{10... | collective-permute-start | bytes 2359304 | tf_op jit(solution)/shard_map/ppermute | solution.py:777
  235.5 67.0 %collective-permute-start.3 = (bf16[512,2048]{1,0:T(8,128)(2,1)}, bf16[512,2048]{1,0:T(8,128)(2,1)}, u32[]{:S(2)}, u32[]{:S(2)}) collective-permute-start(bf16[512,2048]{1,0:T(8,128)(2,1)} %shard_map.283.refs_1_), channel_id=1, source_target_pairs={{0,8},{24,16},{1,9},{25,17},{2,10},{26,18},{3,11},{27,19},{4,12},{... | collective-permute-start | bytes 6291464 | tf_op jit(solution)/shard_map/ppermute | solution.py:42
  295.2 63.1 %all-to-all-start.1 = ((bf16[8,272,512]{2,1,0:T(8,128)(2,1)}), bf16[8,272,512]{2,1,0:T(8,128)(2,1)}, u32[]{:S(2)}, u32[]{:S(2)}) async-start(bf16[8,272,512]{2,1,0:T(8,128)(2,1)} %shard_map.287.refs_2_), calls=%async_computation.1 | async-start | bytes 4456448 | tf_op jit(solution)/shard_map/all_to_all | solution.py:720
  299.8 58.6 %collective-permute-start.5 = (bf16[528,2048]{1,0:T(8,128)(2,1)}, bf16[528,2048]{1,0:T(8,128)(2,1)}, u32[]{:S(2)}, u32[]{:S(2)}) collective-permute-start(bf16[528,2048]{1,0:T(8,128)(2,1)} %shard_map.286), channel_id=1, source_target_pairs={{0,8},{24,16},{1,9},{25,17},{2,10},{26,18},{3,11},{27,19},{4,12},{... | collective-permute-start | bytes 6488072 | tf_op jit(solution)/shard_map/ppermute | solution.py:42
  305.1 53.3 %collective-permute-start.4 = (bf16[512,2048]{1,0:T(8,128)(2,1)}, bf16[512,2048]{1,0:T(8,128)(2,1)}, u32[]{:S(2)}, u32[]{:S(2)}) collective-permute-start(bf16[512,2048]{1,0:T(8,128)(2,1)} %shard_map.288.refs_1_), channel_id=1, source_target_pairs={{8,16},{16,8},{9,17},{17,9},{10,18},{18,10},{11,19},{19,11},{12,20... | collective-permute-start | bytes 6291464 | tf_op jit(solution)/shard_map/ppermute | solution.py:42
  358.4 64.5 %collective-permute-start.11 = (bf16[8,272,512]{2,1,0:T(8,128)(2,1)}, bf16[8,272,512]{2,1,0:T(8,128)(2,1)}, u32[]{:S(2)}, u32[]{:S(2)}) collective-permute-start(bf16[8,272,512]{2,1,0:T(8,128)(2,1)} %all-to-all-done.1.refs_3_), channel_id=1, source_target_pairs={{0,8},{24,16},{1,9},{25,17},{2,10},{26,18},{3,11},{27,19},{4,12},{... | collective-permute-start | bytes 6684680 | tf_op jit(solution)/shard_map/ppermute | solution.py:42
  361.1 47.0 %all-to-all-start.2 = ((bf16[8,272,512]{2,1,0:T(8,128)(2,1)}), bf16[8,272,512]{2,1,0:T(8,128)(2,1)}, u32[]{:S(2)}, u32[]{:S(2)}) async-start(bf16[8,272,512]{2,1,0:T(8,128)(2,1)} %shard_map.290), calls=%async_computation.2 | async-start | bytes 4456448 | tf_op jit(solution)/shard_map/all_to_all | solution.py:720
  367.9 54.9 %collective-permute-start.10 = (bf16[528,2048]{1,0:T(8,128)(2,1)}, bf16[528,2048]{1,0:T(8,128)(2,1)}, u32[]{:S(2)}, u32[]{:S(2)}) collective-permute-start(bf16[528,2048]{1,0:T(8,128)(2,1)} %shard_map.293.refs_2_), channel_id=1, source_target_pairs={{8,16},{16,8},{9,17},{17,9},{10,18},{18,10},{11,19},{19,11},{12,20... | collective-permute-start | bytes 6488072 | tf_op jit(solution)/shard_map/ppermute | solution.py:42
  372.7 50.1 %collective-permute-start.9 = (bf16[512,2048]{1,0:T(8,128)(2,1)}, bf16[512,2048]{1,0:T(8,128)(2,1)}, u32[]{:S(2)}, u32[]{:S(2)}) collective-permute-start(bf16[512,2048]{1,0:T(8,128)(2,1)} %shard_map.292.refs_1_.refs_0_), channel_id=1, source_target_pairs={{8,0},{16,24},{9,1},{17,25},{10,2},{18,26},{11,3},{19,27},{12,4},{... | collective-permute-start | bytes 6291464 | tf_op jit(solution)/shard_map/ppermute | solution.py:42
  425.7 67.3 %collective-permute-start.14 = (bf16[8,272,512]{2,1,0:T(8,128)(2,1)}, bf16[8,272,512]{2,1,0:T(8,128)(2,1)}, u32[]{:S(2)}, u32[]{:S(2)}) collective-permute-start(bf16[8,272,512]{2,1,0:T(8,128)(2,1)} %bitcast.51.refs_3_), channel_id=1, source_target_pairs={{8,16},{16,8},{9,17},{17,9},{10,18},{18,10},{11,19},{19,11},{12,20... | collective-permute-start | bytes 6684680 | tf_op jit(solution)/shard_map/ppermute | solution.py:42
  430.2 62.8 %collective-permute-start.13 = (bf16[528,2048]{1,0:T(8,128)(2,1)}, bf16[528,2048]{1,0:T(8,128)(2,1)}, u32[]{:S(2)}, u32[]{:S(2)}) collective-permute-start(bf16[528,2048]{1,0:T(8,128)(2,1)} %shard_map.296.refs_2_), channel_id=1, source_target_pairs={{8,0},{16,24},{9,1},{17,25},{10,2},{18,26},{11,3},{19,27},{12,4},{... | collective-permute-start | bytes 6488072 | tf_op jit(solution)/shard_map/ppermute | solution.py:42
  431.5 61.5 %collective-permute-start.15 = (bf16[8,272,512]{2,1,0:T(8,128)(2,1)}, bf16[8,272,512]{2,1,0:T(8,128)(2,1)}, u32[]{:S(2)}, u32[]{:S(2)}) collective-permute-start(bf16[8,272,512]{2,1,0:T(8,128)(2,1)} %all-to-all-done.2.refs_4_), channel_id=1, source_target_pairs={{0,8},{24,16},{1,9},{25,17},{2,10},{26,18},{3,11},{27,19},{4,12},{... | collective-permute-start | bytes 6684680 | tf_op jit(solution)/shard_map/ppermute | solution.py:42
  468.7 75.3 %collective-permute-start.20 = (bf16[256,2048]{1,0:T(8,128)(2,1)}, bf16[256,2048]{1,0:T(8,128)(2,1)}, u32[]{:S(2)}, u32[]{:S(2)}) collective-permute-start(bf16[256,2048]{1,0:T(8,128)(2,1)} %shard_map.300), channel_id=1, source_target_pairs={{0,8},{24,16},{1,9},{25,17},{2,10},{26,18},{3,11},{27,19},{4,12},{... | collective-permute-start | bytes 3145736 | tf_op jit(solution)/shard_map/ppermute | solution.py:42
  471.1 72.9 %all-to-all-start.3 = ((bf16[8,272,768]{2,1,0:T(8,128)(2,1)}), bf16[8,272,768]{2,1,0:T(8,128)(2,1)}, u32[]{:S(2)}, u32[]{:S(2)}) async-start(bf16[8,272,768]{2,1,0:T(8,128)(2,1)} %shard_map.299.refs_4_), calls=%async_computation.3 | async-start | bytes 6684672 | tf_op jit(solution)/shard_map/all_to_all | solution.py:720
  492.6 32.3 %collective-permute-start.12 = (bf16[4,4096,256]{2,1,0:T(8,128)(2,1)}, bf16[4,4096,256]{2,1,0:T(8,128)(2,1)}, u32[]{:S(2)}, u32[]{:S(2)}) collective-permute-start(bf16[4,4096,256]{2,1,0:T(8,128)(2,1)} %shard_map.301.refs_5_), channel_id=1, source_target_pairs={{0,1},{1,0},{2,3},{3,2},{4,5},{5,4},{6,7},{7,6},{8,9},{9,8},{10,11... | collective-permute-start | bytes 25165832 | tf_op jit(solution)/shard_map/ppermute | solution.py:30
  496.1 47.9 %collective-permute-start.19 = (bf16[8,272,512]{2,1,0:T(8,128)(2,1)}, bf16[8,272,512]{2,1,0:T(8,128)(2,1)}, u32[]{:S(2)}, u32[]{:S(2)}) collective-permute-start(bf16[8,272,512]{2,1,0:T(8,128)(2,1)} %bitcast.59.refs_3_), channel_id=1, source_target_pairs={{8,16},{16,8},{9,17},{17,9},{10,18},{18,10},{11,19},{19,11},{12,20... | collective-permute-start | bytes 6684680 | tf_op jit(solution)/shard_map/ppermute | solution.py:42
  501.3 52.6 %collective-permute-start.18 = (bf16[8,272,512]{2,1,0:T(8,128)(2,1)}, bf16[8,272,512]{2,1,0:T(8,128)(2,1)}, u32[]{:S(2)}, u32[]{:S(2)}) collective-permute-start(bf16[8,272,512]{2,1,0:T(8,128)(2,1)} %bitcast.56.refs_2_.refs_0_), channel_id=1, source_target_pairs={{8,0},{16,24},{9,1},{17,25},{10,2},{18,26},{11,3},{19,27},{12,4},{... | collective-permute-start | bytes 6684680 | tf_op jit(solution)/shard_map/ppermute | solution.py:42
  524.8 43.8 %collective-permute-start.22 = (bf16[4,2,256,2048]{3,2,1,0:T(8,128)(2,1)}, bf16[4,2,256,2048]{3,2,1,0:T(8,128)(2,1)}, u32[]{:S(2)}, u32[]{:S(2)}) collective-permute-start(bf16[4,2,256,2048]{3,2,1,0:T(8,128)(2,1)} %shard_map.305.refs_6_), channel_id=1, source_target_pairs={{0,1},{1,0},{2,3},{3,2},{4,5},{5,4},{6,7},{7,6},{8,9},{9,8},{10,11... | collective-permute-start | bytes 25165832 | tf_op jit(solution)/shard_map/ppermute | solution.py:30
  557.9 38.8 %collective-permute-start.21 = (bf16[4,272,768]{2,1,0:T(8,128)(2,1)}, bf16[4,272,768]{2,1,0:T(8,128)(2,1)}, u32[]{:S(2)}, u32[]{:S(2)}) collective-permute-start(bf16[4,272,768]{2,1,0:T(8,128)(2,1)} %get-tuple-element.293.refs_4_), channel_id=1, source_target_pairs={{0,8},{24,16},{1,9},{25,17},{2,10},{26,18},{3,11},{27,19},{4,12},{... | collective-permute-start | bytes 5013512 | tf_op jit(solution)/shard_map/ppermute | solution.py:42
  560.8 47.5 %collective-permute-start.16 = (bf16[2,2048,256]{2,1,0:T(8,128)(2,1)}, bf16[2,2048,256]{2,1,0:T(8,128)(2,1)}, u32[]{:S(2)}, u32[]{:S(2)}) collective-permute-start(bf16[2,2048,256]{2,1,0:T(8,128)(2,1)} %get-tuple-element.212.refs_7_), channel_id=1, source_target_pairs={{0,2},{1,3},{2,0},{3,1},{4,6},{5,7},{6,4},{7,5},{8,10},{9,11},{10,... | collective-permute-start | bytes 6291464 | tf_op jit(solution)/shard_map/ppermute | solution.py:30
  562.7 47.2 %collective-permute-start.17 = (bf16[2,2048,256]{2,1,0:T(8,128)(2,1)}, bf16[2,2048,256]{2,1,0:T(8,128)(2,1)}, u32[]{:S(2)}, u32[]{:S(2)}) collective-permute-start(bf16[2,2048,256]{2,1,0:T(8,128)(2,1)} %get-tuple-element.213), channel_id=1, source_target_pairs={{0,4},{1,5},{2,6},{3,7},{4,0},{5,1},{6,2},{7,3},{8,12},{9,13},{10,... | collective-permute-start | bytes 6291464 | tf_op jit(solution)/shard_map/ppermute | solution.py:30
  564.2 66.7 %collective-permute-start.25 = (bf16[4,272,768]{2,1,0:T(8,128)(2,1)}, bf16[4,272,768]{2,1,0:T(8,128)(2,1)}, u32[]{:S(2)}, u32[]{:S(2)}) collective-permute-start(bf16[4,272,768]{2,1,0:T(8,128)(2,1)} %get-tuple-element.292.refs_5_), channel_id=1, source_target_pairs={{0,8},{24,16},{1,9},{25,17},{2,10},{26,18},{3,11},{27,19},{4,12},{... | collective-permute-start | bytes 5013512 | tf_op jit(solution)/shard_map/ppermute | solution.py:42
  599.3 47.5 %collective-permute-start.24 = (bf16[4,272,768]{2,1,0:T(8,128)(2,1)}, bf16[4,272,768]{2,1,0:T(8,128)(2,1)}, u32[]{:S(2)}, u32[]{:S(2)}) collective-permute-start(bf16[4,272,768]{2,1,0:T(8,128)(2,1)} %bitcast.65), channel_id=1, source_target_pairs={{8,16},{16,8},{9,17},{17,9},{10,18},{18,10},{11,19},{19,11},{12,20... | collective-permute-start | bytes 5013512 | tf_op jit(solution)/shard_map/ppermute | solution.py:42
  601.2 59.8 %collective-permute-start.27 = (bf16[8,272,512]{2,1,0:T(8,128)(2,1)S(1)}, bf16[8,272,512]{2,1,0:T(8,128)(2,1)}, u32[]{:S(2)}, u32[]{:S(2)}) collective-permute-start(bf16[8,272,512]{2,1,0:T(8,128)(2,1)S(1)} %bitcast.131), channel_id=1, source_target_pairs={{8,0},{16,24},{9,1},{17,25},{10,2},{18,26},{11,3},{19,27},{12,4},{... | collective-permute-start | bytes 6684680 | tf_op jit(solution)/shard_map/ppermute | solution.py:42
  608.2 46.6 %collective-permute-start.28 = (bf16[2,256,2048]{2,1,0:T(8,128)(2,1)}, bf16[2,256,2048]{2,1,0:T(8,128)(2,1)}, u32[]{:S(2)}, u32[]{:S(2)}) collective-permute-start(bf16[2,256,2048]{2,1,0:T(8,128)(2,1)} %get-tuple-element.241), channel_id=1, source_target_pairs={{0,2},{1,3},{2,0},{3,1},{4,6},{5,7},{6,4},{7,5},{8,10},{9,11},{10,... | collective-permute-start | bytes 6291464 | tf_op jit(solution)/shard_map/ppermute | solution.py:30
  610.0 46.7 %collective-permute-start.29 = (bf16[2,256,2048]{2,1,0:T(8,128)(2,1)}, bf16[2,256,2048]{2,1,0:T(8,128)(2,1)}, u32[]{:S(2)}, u32[]{:S(2)}) collective-permute-start(bf16[2,256,2048]{2,1,0:T(8,128)(2,1)} %get-tuple-element.242), channel_id=1, source_target_pairs={{0,4},{1,5},{2,6},{3,7},{4,0},{5,1},{6,2},{7,3},{8,12},{9,13},{10,... | collective-permute-start | bytes 6291464 | tf_op jit(solution)/shard_map/ppermute | solution.py:30
  633.5 47.7 %collective-permute-start.32 = (bf16[4,272,768]{2,1,0:T(8,128)(2,1)}, bf16[4,272,768]{2,1,0:T(8,128)(2,1)}, u32[]{:S(2)}, u32[]{:S(2)}) collective-permute-start(bf16[4,272,768]{2,1,0:T(8,128)(2,1)} %bitcast.70), channel_id=1, source_target_pairs={{8,16},{16,8},{9,17},{17,9},{10,18},{18,10},{11,19},{19,11},{12,20... | collective-permute-start | bytes 5013512 | tf_op jit(solution)/shard_map/ppermute | solution.py:42
  646.8 107.1 %copy-start.45 = (f32[256]{0:T(256)}, f32[256]{0:T(256)S(1)}, u32[]{:S(2)}) copy-start(f32[256]{0:T(256)S(1)} %convert_reduce_fusion.3) | copy-start | bytes 3076
  649.5 43.0 %collective-permute-start.26 = (bf16[4,272,768]{2,1,0:T(8,128)(2,1)}, bf16[4,272,768]{2,1,0:T(8,128)(2,1)}, u32[]{:S(2)}, u32[]{:S(2)}) collective-permute-start(bf16[4,272,768]{2,1,0:T(8,128)(2,1)} %bitcast.74.refs_0_), channel_id=1, source_target_pairs={{8,0},{16,24},{9,1},{17,25},{10,2},{18,26},{11,3},{19,27},{12,4},{... | collective-permute-start | bytes 5013512 | tf_op jit(solution)/shard_map/ppermute | solution.py:42
  654.8 29.7 %collective-permute-start.23 = (bf16[256,2048]{1,0:T(8,128)(2,1)S(1)}, bf16[256,2048]{1,0:T(8,128)(2,1)}, u32[]{:S(2)}, u32[]{:S(2)}) collective-permute-start(bf16[256,2048]{1,0:T(8,128)(2,1)S(1)} %copy-done.20), channel_id=1, source_target_pairs={{8,16},{16,8},{9,17},{17,9},{10,18},{18,10},{11,19},{19,11},{12,20... | collective-permute-start | bytes 3145736 | tf_op jit(solution)/shard_map/ppermute | solution.py:42
  661.0 23.5 %collective-permute-start.30 = (bf16[256,2048]{1,0:T(8,128)(2,1)}, bf16[256,2048]{1,0:T(8,128)(2,1)}, u32[]{:S(2)}, u32[]{:S(2)}) collective-permute-start(bf16[256,2048]{1,0:T(8,128)(2,1)} %shard_map.317), channel_id=1, source_target_pairs={{0,4},{1,5},{2,6},{3,7},{4,0},{5,1},{6,2},{7,3},{8,12},{9,13},{10,... | collective-permute-start | bytes 3145736 | tf_op jit(solution)/shard_map/ppermute | solution.py:30
  662.5 22.6 %collective-permute-start.31 = (bf16[256,2048]{1,0:T(8,128)(2,1)}, bf16[256,2048]{1,0:T(8,128)(2,1)}, u32[]{:S(2)}, u32[]{:S(2)}) collective-permute-start(bf16[256,2048]{1,0:T(8,128)(2,1)} %shard_map.318), channel_id=1, source_target_pairs={{0,2},{1,3},{2,0},{3,1},{4,6},{5,7},{6,4},{7,5},{8,10},{9,11},{10,... | collective-permute-start | bytes 3145736 | tf_op jit(solution)/shard_map/ppermute | solution.py:30
  683.0 45.3 %collective-permute-start.33 = (bf16[4,272,768]{2,1,0:T(8,128)(2,1)S(1)}, bf16[4,272,768]{2,1,0:T(8,128)(2,1)}, u32[]{:S(2)}, u32[]{:S(2)}) collective-permute-start(bf16[4,272,768]{2,1,0:T(8,128)(2,1)S(1)} %bitcast.135), channel_id=1, source_target_pairs={{8,0},{16,24},{9,1},{17,25},{10,2},{18,26},{11,3},{19,27},{12,4},{... | collective-permute-start | bytes 5013512 | tf_op jit(solution)/shard_map/ppermute | solution.py:42
  692.5 21.6 %collective-permute-start.34 = (bf16[2048,256]{1,0:T(8,128)(2,1)}, bf16[2048,256]{1,0:T(8,128)(2,1)}, u32[]{:S(2)}, u32[]{:S(2)}) collective-permute-start(bf16[2048,256]{1,0:T(8,128)(2,1)} %shard_map.312), channel_id=1, source_target_pairs={{0,4},{1,5},{2,6},{3,7},{4,0},{5,1},{6,2},{7,3},{8,12},{9,13},{10,... | collective-permute-start | bytes 3145736 | tf_op jit(solution)/shard_map/ppermute | solution.py:30
  694.9 20.7 %collective-permute-start.35 = (bf16[2048,256]{1,0:T(8,128)(2,1)}, bf16[2048,256]{1,0:T(8,128)(2,1)}, u32[]{:S(2)}, u32[]{:S(2)}) collective-permute-start(bf16[2048,256]{1,0:T(8,128)(2,1)} %shard_map.313), channel_id=1, source_target_pairs={{0,2},{1,3},{2,0},{3,1},{4,6},{5,7},{6,4},{7,5},{8,10},{9,11},{10,... | collective-permute-start | bytes 3145736 | tf_op jit(solution)/shard_map/ppermute | solution.py:30
  697.6 50.7 %collective-permute-start.36 = (bf16[256,2048]{1,0:T(8,128)(2,1)S(1)}, bf16[256,2048]{1,0:T(8,128)(2,1)}, u32[]{:S(2)}, u32[]{:S(2)}) collective-permute-start(bf16[256,2048]{1,0:T(8,128)(2,1)S(1)} %shard_map.321.refs_0_), channel_id=1, source_target_pairs={{8,0},{16,24},{9,1},{17,25},{10,2},{18,26},{11,3},{19,27},{12,4},{... | collective-permute-start | bytes 3145736 | tf_op jit(solution)/shard_map/ppermute | solution.py:42
  (56 other events, 470.2 us)
Sparse Core Ops, SparseCore 0:
  12.1 117.0 all-gather.4
  131.7 89.8 all-gather.2
